TPU v7x, 32 devices: a whole 2x2x4 slice. The times are simulated.
32 devices in a mesh: fib: 16 (over z, x, core), pln: 2 (over y).
Axes of the slice: x: 2, y: 2, z: 4, core: 2. Of those that a mesh axis runs over, the one named last changes fastest.
Arguments:
- nodal_values: float32 [2, 16, 288, 1000], P('pln', 'fib'), may hold values from -6 to 6
- interp_matrix: float32 [1000, 512], replicated, may hold values from -0.1875 to 0.1875
- count_table: int32 [2, 16, 3], P('pln'), may hold values from 1 to 96, as said below
- slot_order: int32 [2, 16, 192], P('pln', 'fib'), may hold values from 0 to 191, each once within a row
- start_basis: float32 [768, 128], replicated, may hold values from -6 to 6
Outputs:
- core_values: float32 [2, 16, 128, 128], P('pln', 'fib')
Inputs may be any that keep to these rules, and one draw needn't show every extreme that they name: count_table[j, o, d] elements of owner o come from the source d places before it along fib, cyclically; for every owner the 3 entries sum to 192 and one equals 96. `slot_order`: each owner's row is a permutation.
All inputs are finite; a program needn't handle non-finite values.
Results may differ from a plain program's by a relative error of at most 0.0003.
Values sent between devices are 32-bit elements; how exact they have to be, the bound alone decides.
No kernel may reach another device: no remote copies, remote signals or barrier semaphores. Data moves between devices by JAX's collectives and lax.ppermute only.
A program may use at most 64 MiB of HBM per device.

v0:
```python
import jax
import jax.numpy as jnp
from jax import lax
from jax.sharding import PartitionSpec as P

NX = 768
TILES_DEV = 1


def shifted(value, axis, by):
    peers = lax.axis_size(axis)
    return lax.ppermute(value, axis, [(i, (i + by) % peers) for i in range(peers)])


def per_device(nodal_values, interp_matrix, count_table, slot_order, start_basis):
    full_precision = lax.Precision.HIGHEST
    node_rows = nodal_values[0, 0]
    owner_table = count_table[0]
    brick_order = slot_order[0, 0]
    owners = lax.axis_size("fib")
    own_index = lax.axis_index("fib")
    window = owner_table.shape[1]
    capacity = node_rows.shape[0] // window
    elements = brick_order.shape[0]
    tiles_total = TILES_DEV * owners
    block_width = NX // owners
    send_start = []
    running = jnp.int32(0)
    for distance in range(window):
        send_start.append(running)
        column = owner_table[:, distance]
        running = running + lax.dynamic_index_in_dim(
            column, (own_index + distance) % owners, 0, keepdims=False
        )
    own_counts = lax.dynamic_index_in_dim(owner_table, own_index, 0, keepdims=False)
    positions = jnp.arange(elements, dtype=jnp.int32)
    combined_index = jnp.zeros((elements,), jnp.int32)
    offset = jnp.int32(0)
    for distance in range(window - 1, -1, -1):
        taken_count = own_counts[distance]
        inside = (positions >= offset) & (positions < offset + taken_count)
        combined_index = jnp.where(inside, distance * capacity + positions - offset, combined_index)
        offset = offset + taken_count
    brick_source = jnp.zeros((elements,), jnp.int32).at[brick_order].set(combined_index)
    grid_rows = jnp.dot(
        node_rows, interp_matrix, precision=full_precision, preferred_element_type=jnp.float32
    )
    received = []
    for distance in range(window):
        send_piece = lax.dynamic_slice_in_dim(grid_rows, send_start[distance], capacity, 0)
        if distance > 0:
            send_piece = shifted(send_piece, "fib", distance)
        received.append(send_piece)
    brick_values = jnp.concatenate(received, axis=0)[brick_source]
    brick_grid = brick_values.reshape(tiles_total, block_width, brick_values.shape[1] // 4)
    fibre_field = lax.all_to_all(brick_grid, "fib", split_axis=0, concat_axis=1, tiled=True)
    gram_share = lax.psum_scatter(
        jnp.einsum("txf,tyf->xy", fibre_field, fibre_field, precision=full_precision),
        "fib",
        scatter_dimension=0,
        tiled=True,
    )
    gram_share = lax.psum(gram_share, "pln")
    image_share = jnp.dot(gram_share, start_basis, precision=full_precision)
    image_matrix = lax.all_gather(image_share, "fib", axis=0, tiled=True)
    normal_matrix = jnp.dot(image_matrix.T, image_matrix, precision=full_precision)
    lower_factor = jnp.linalg.cholesky(normal_matrix)
    new_basis = jax.scipy.linalg.solve_triangular(lower_factor, image_matrix.T, lower=True).T
    core_values = jnp.einsum("xk,txf->tkf", new_basis, fibre_field, precision=full_precision)
    return core_values[None]


def solution(mesh):
    placed = (P("pln", "fib", None, None), P(), P("pln", None, None), P("pln", "fib", None), P())
    return jax.shard_map(
        per_device,
        mesh=mesh,
        in_specs=placed,
        out_specs=P("pln", "fib", None, None),
        check_vma=False,
    )
```

profile of v0, /device:TPU:0, one launch (start us, length us, event | category | flops | bytes accessed | tf_op | source)
XLA Modules:
  0.0 189.0 jit_solution(12188578795357635)
XLA Ops:
  6.5 0.0 copy-start
  6.5 0.0 reduce-scatter.2.cloned.1.call-start
  6.5 0.8 copy.12
  7.4 0.7 constant_dynamic-slice_fusion.4
  11.2 0.0 copy-done
  11.2 0.0 copy-start.2
  11.2 0.0 copy-start.3
  11.2 3.4 %fusion = f32[288,512]{1,0:T(8,128)S(1)} fusion(f32[1000,512]{1,0:T(8,128)S(1)} %copy-done, f32[1,1,288,1000]{3,2,1,0:T(8,128)} %param.5), kind=kOutput, calls=%fused_computation.2 | convolution fusion | flops 1769472000 | bytes 3789824 | tf_op jit(solution)/shard_map/dot_general | solution.py:45
  14.7 0.1 fusion.8
  14.7 3.0 %collective-permute-start.1 = (f32[96,512]{1,0:T(8,128)S(1)}, f32[96,512]{1,0:T(8,128)S(1)}, u32[]{:S(2)}, u32[]{:S(2)}) collective-permute-start(f32[96,512]{1,0:T(8,128)S(1)} %get-tuple-element.6), channel_id=1, source_target_pairs={{0,4},{2,6},{4,8},{6,10},{8,12},{10,14},{12,16},{14,18},{16,20},{1... | collective-permute-start | bytes 589832 | tf_op jit(solution)/shard_map/ppermute | solution.py:12
  17.7 0.0 collective-permute-start
  17.7 0.0 copy-done.2
  17.7 0.6 constant_dynamic-slice_fusion.2
  20.3 0.6 and_select_fusion.1
  20.9 0.0 copy-done.3
  20.9 1.2 scatter_custom_fusion
  22.1 4.4 %collective-permute-done.1 = f32[96,512]{1,0:T(8,128)S(1)} collective-permute-done((f32[96,512]{1,0:T(8,128)S(1)}, f32[96,512]{1,0:T(8,128)S(1)}, u32[]{:S(2)}, u32[]{:S(2)}) %collective-permute-start.1) | collective-permute-done | bytes 196640 | tf_op jit(solution)/shard_map/ppermute | solution.py:12
  26.5 1.3 collective-permute-done
  27.8 0.9 gather_fusion
  28.7 15.1 %all_to_all.4 = f32[16,48,128]{2,1,0:T(8,128)S(1)} all-to-all(f32[16,48,128]{2,1,0:T(8,128)S(1)} %reshape.65), channel_id=1, replica_groups=mesh['fib'=16,'pln'=2] {'fib'}, dimensions={0} | all-to-all | bytes 786432 | tf_op jit(solution)/shard_map/all_to_all | solution.py:56
  43.8 0.0 copy-start.1
  43.8 3.4 %fusion.10 = f32[768,768]{1,0:T(8,128)} fusion(f32[768,128]{1,0:T(8,128)S(1)} %bitcast.41), kind=kOutput, calls=%fused_computation.34 | convolution fusion | flops 905969664 | bytes 2752512 | tf_op jit(solution)/shard_map/txf,tyf->xy/dot_general | solution.py:58
  47.2 0.0 reduce-scatter.2.cloned.1.call-update
  47.3 0.0 all-reduce.2.cloned.1.call-start
  47.3 62.0 %reduce-scatter.2.cloned.1.call-done = f32[48,768]{1,0:T(8,128)} async-done(((f32[768,768]{1,0:T(8,128)}), f32[48,768]{1,0:T(8,128)}) %reduce-scatter.2.cloned.1.call-update) | async-done | bytes 147472 | tf_op jit(solution)/shard_map/reduce_scatter | solution.py:57
  109.3 0.0 all-reduce.2.cloned.1.call-update
  109.3 23.1 %all-reduce.2.cloned.1.call-done = f32[48,768]{1,0:T(8,128)} async-done(((f32[48,768]{1,0:T(8,128)}), f32[48,768]{1,0:T(8,128)}) %all-reduce.2.cloned.1.call-update) | async-done | bytes 147472 | tf_op jit(solution)/shard_map/psum | solution.py:63
  132.4 0.0 copy-done.1
  132.4 1.2 fusion.11
  133.6 22.7 %all_gather.3 = f32[768,128]{1,0:T(8,128)S(1)} all-gather(f32[48,128]{1,0:T(8,128)S(1)} %fusion.11), channel_id=1, replica_groups=mesh['fib'=16,'pln'=2] {'fib'}, dimensions={0}, use_global_device_ids=true | all-gather | bytes 417792 | tf_op jit(solution)/shard_map/all_gather | solution.py:65
  156.3 0.8 fusion.12
  157.1 0.1 copy.8
  157.2 11.7 %cholesky.16 = f32[128,128]{1,0:T(8,128)S(1)} custom-call(f32[128,128]{1,0:T(8,128)S(1)} %fusion.5), custom_call_target="Cholesky" | custom-call | tf_op jit(solution)/shard_map/jit(cholesky)/cholesky | solution.py:67
  169.0 0.6 compare_reduce_fusion
  169.6 0.7 fusion.2
  170.3 9.8 %custom-call.7 = f32[1,128,128]{1,2,0:T(8,128)S(1)} custom-call(f32[1,128,128]{2,1,0:T(8,128)S(1)} %fusion.2), custom_call_target="InvertDiagBlocksLowerTriangular" | custom-call | tf_op jit(solution)/shard_map/jit(_solve_triangular)/triangular_solve | solution.py:68
  180.1 0.5 fusion.3
  180.6 0.8 convolution_bitcast_fusion
  181.4 0.7 copy.9
  (8 shorter events, 0.1 us)
Async XLA Ops:
  6.5 4.7 %copy-start = (f32[1000,512]{1,0:T(8,128)S(1)}, f32[1000,512]{1,0:T(8,128)}, u32[]{:S(2)}) copy-start(f32[1000,512]{1,0:T(8,128)} %param.6) | copy-start | bytes 6144004
  6.5 102.7 %reduce-scatter.2.cloned.1.call-start = ((), (), s32[]{:S(2)}) async-start(), calls=%async_computation.2 | async-start | bytes 2506752 | tf_op jit(solution)/shard_map/reduce_scatter | solution.py:57
  11.2 6.5 %copy-start.2 = (s32[1,16,3]{1,0,2:T(1,128)S(1)}, s32[1,16,3]{1,0,2:T(1,128)}, u32[]{:S(2)}) copy-start(s32[1,16,3]{1,0,2:T(1,128)} %param.7) | copy-start | bytes 580
  11.2 9.6 %copy-start.3 = (s32[1,1,192]{2,1,0:T(1,128)S(1)}, s32[1,1,192]{2,1,0:T(1,128)}, u32[]{:S(2)}) copy-start(s32[1,1,192]{2,1,0:T(1,128)} %param.8) | copy-start | bytes 2308
  14.7 11.8 %collective-permute-start.1 = (f32[96,512]{1,0:T(8,128)S(1)}, f32[96,512]{1,0:T(8,128)S(1)}, u32[]{:S(2)}, u32[]{:S(2)}) collective-permute-start(f32[96,512]{1,0:T(8,128)S(1)} %get-tuple-element.6), channel_id=1, source_target_pairs={{0,4},{2,6},{4,8},{6,10},{8,12},{10,14},{12,16},{14,18},{16,20},{1... | collective-permute-start | bytes 589832 | tf_op jit(solution)/shard_map/ppermute | solution.py:12
  17.7 10.0 %collective-permute-start = (f32[96,512]{1,0:T(8,128)S(1)}, f32[96,512]{1,0:T(8,128)S(1)}, u32[]{:S(2)}, u32[]{:S(2)}) collective-permute-start(f32[96,512]{1,0:T(8,128)S(1)} %get-tuple-element.7), channel_id=1, source_target_pairs={{0,2},{2,4},{4,6},{6,8},{8,10},{10,12},{12,14},{14,16},{16,18},{18... | collective-permute-start | bytes 589832 | tf_op jit(solution)/shard_map/ppermute | solution.py:12
  43.8 88.5 %copy-start.1 = (f32[768,128]{1,0:T(8,128)S(1)}, f32[768,128]{1,0:T(8,128)}, u32[]{:S(2)}) copy-start(f32[768,128]{1,0:T(8,128)} %param.9) | copy-start | bytes 1179652
  47.3 85.1 %all-reduce.2.cloned.1.call-start = ((), (), s32[]{:S(2)}) async-start(), calls=%async_computation.3 | async-start | bytes 294912 | tf_op jit(solution)/shard_map/psum | solution.py:63
Sparse Core Ops, SparseCore 0:
  47.4 61.8 reduce-scatter.1
  111.6 20.6 all-reduce.1
where the time goes:
time: 189 us
  waiting for transfers between devices  90.7 us (48%)
  blocking collectives  37.8 us (20%)
  other arithmetic  23.5 us (12%)
  between operations  18.6 us (10%)
  matrix products  10.2 us (5%)
  local copies, waits for them, and re-layouts  5.12 us (3%)
  starting transfers between devices  3.04 us (2%)
    reduce_scatter x1, waiting for transfers between devices, per_device(): lax.psum_scatter(jnp.einsum('txf,tyf->xy', fibre_field, fibre_field, prec...  62 us
    psum x1, waiting for transfers between devices, per_device(): gram_share = lax.psum(gram_share, 'pln')  23.1 us
    all_gather x1, blocking collectives, per_device(): image_matrix = lax.all_gather(image_share, 'fib', axis=0, tiled=True)  22.7 us
    all_to_all x1, blocking collectives, per_device(): lax.all_to_all(brick_grid, 'fib', split_axis=0, concat_axis=1, tiled=True)  15.1 us
    another operation x3, other arithmetic, per_device(): lower_factor = jnp.linalg.cholesky(normal_matrix)  12.4 us
    another operation x2, other arithmetic, per_device(): jax.scipy.linalg.solve_triangular(lower_factor, image_matrix.T, lower=True)  10.5 us
    ppermute x2, waiting for transfers between devices, shifted(): lax.ppermute(value, axis, [(i, (i + by) % peers) for i in range(peers)])  5.63 us
  transfers between devices with their start and end apart: 4, of which 4 were waited for; matrix products, arithmetic and copies ran while one was open for 1% of the time, Pallas kernels for 0%

commit v1 on v0

v1 whole, which is shorter than its diff:
```python
import functools

import jax
import jax.numpy as jnp
from jax import lax
from jax.experimental import pallas as pl
from jax.experimental.pallas import tpu as pltpu
from jax.sharding import PartitionSpec as P

F32 = jnp.float32
BF16 = jnp.bfloat16
SLAB = 8
VMEM = pl.BlockSpec(memory_space=pltpu.VMEM)
SMEM = pl.BlockSpec(memory_space=pltpu.SMEM)
BIG = pltpu.CompilerParams(vmem_limit_bytes=32 * 1024 * 1024)


def halves(value):
    high = value.astype(BF16)
    return high, (value - high.astype(F32)).astype(BF16)


def dot3(left, right, contract):
    dims = (contract, ((), ()))
    lh, ll = left
    rh, rl = right
    out = lax.dot_general(lh, rl, dims, preferred_element_type=F32)
    out += lax.dot_general(ll, rh, dims, preferred_element_type=F32)
    return out + lax.dot_general(lh, rh, dims, preferred_element_type=F32)


def interp_kernel(owners, table_ref, node_ref, interp_ref, *refs):
    outs, grid_scr = refs[:-1], refs[-1]
    window = len(outs)
    rows = outs[0].shape[0]
    slots = node_ref.shape[0]
    own = lax.axis_index("fib")
    grid_scr[:slots, :] = dot3(halves(node_ref[...]), halves(interp_ref[...]), ((1,), (0,)))
    outs[0][...] = grid_scr[:rows, :]
    start = table_ref[0, own]
    for distance in range(1, window):
        shift = lax.rem(start, SLAB)
        at = pl.multiple_of(start - shift, SLAB)
        wide = grid_scr[pl.ds(at, rows + SLAB), :]
        outs[distance][...] = pltpu.roll(wide, lax.rem(rows + SLAB - shift, rows + SLAB), 0)[:rows, :]
        start = start + table_ref[distance, lax.rem(own + distance, owners)]


def pick_kernel(rows, table_ref, order_ref, out_ref):
    elements, slots = out_ref.shape
    window = slots // rows
    own = lax.axis_index("fib")
    rank_at = lax.broadcasted_iota(jnp.int32, (elements, slots), 0)
    slot_at = lax.broadcasted_iota(jnp.int32, (elements, slots), 1)
    from_slot = jnp.zeros((elements, slots), jnp.bool_)
    start = 0
    for distance in range(window - 1, -1, -1):
        count = table_ref[distance, own]
        inside = (rank_at >= start) & (rank_at < start + count)
        from_slot = from_slot | (inside & (slot_at - distance * rows == rank_at - start))
        start = start + count
    place = jnp.broadcast_to(order_ref[...], (elements, elements))
    row = lax.broadcasted_iota(jnp.int32, (elements, elements), 0)
    to_place = jnp.where(place == row, 1.0, 0.0).astype(BF16)
    out_ref[...] = jnp.dot(
        to_place, jnp.where(from_slot, 1.0, 0.0).astype(BF16), preferred_element_type=F32
    )


def order_kernel(pick_ref, *refs):
    pieces, out_ref = refs[:-1], refs[-1]
    pick = pick_ref[...].astype(BF16)
    line = jnp.concatenate([piece[...] for piece in pieces], axis=0)
    high = line.astype(BF16)
    rest = line - high.astype(F32)
    mid = rest.astype(BF16)
    low = (rest - mid.astype(F32)).astype(BF16)
    out = jnp.dot(pick, low, preferred_element_type=F32)
    out += jnp.dot(pick, mid, preferred_element_type=F32)
    out_ref[...] = out + jnp.dot(pick, high, preferred_element_type=F32)


def plane_index(inner):
    return lax.rem(lax.axis_index("fib"), inner) * lax.axis_size("pln") + lax.axis_index("pln")


def image_kernel(inner, field_ref, start_ref, *refs):
    outs, image_scr = refs[:-1], refs[-1]
    rows = outs[0].shape[0]
    field = halves(field_ref[...])
    mixed = dot3(field, halves(start_ref[...]), ((0,), (0,)))
    image_scr[...] = dot3(field, halves(mixed), ((1,), (0,)))
    mine = plane_index(inner)
    for step, out in enumerate(outs):
        at = pl.multiple_of((mine ^ step) * rows, rows)
        out[...] = image_scr[pl.ds(at, rows), :]


def factor_kernel(inner, field_ref, *refs):
    chunks, out_ref, image_scr, work, line_scr = refs[:-4], refs[-4], refs[-3], refs[-2], refs[-1]
    rows = chunks[0].shape[0]
    rank = out_ref.shape[0]
    mine = plane_index(inner)
    for step, chunk in enumerate(chunks):
        at = pl.multiple_of((mine ^ step) * rows, rows)
        image_scr[pl.ds(at, rows), :] = chunk[...]
    image = halves(image_scr[...])
    work[:, :rank] = dot3(image, image, ((0,), (0,)))
    work[:, rank:] = dot3(image, halves(field_ref[...]), ((0,), (0,)))
    shape = (1, rank)
    for base in range(0, rank, SLAB):
        left = [work[base + k : base + k + 1, :rank] for k in range(SLAB)]
        right = [work[base + k : base + k + 1, rank:] for k in range(SLAB)]
        entry = [
            [jnp.broadcast_to(left[k][:, base + i : base + i + 1], shape) for i in range(SLAB)]
            for k in range(SLAB)
        ]
        for k in range(SLAB):
            scale = lax.rsqrt(entry[k][k])
            left[k] = left[k] * scale
            right[k] = right[k] * scale
            factor = {i: entry[k][i] * scale for i in range(k + 1, SLAB)}
            for i in range(k + 1, SLAB):
                for j in range(i, SLAB):
                    entry[i][j] = entry[i][j] - factor[i] * factor[j]
                left[i] = left[i] - factor[i] * left[k]
                right[i] = right[i] - factor[i] * right[k]
            out_ref[base + k : base + k + 1, :] = right[k]
            line_scr[k : k + 1, :rank] = left[k]
            line_scr[k : k + 1, rank:] = right[k]
        after = base + SLAB
        if after < rank:
            line = line_scr[...]
            high = line.astype(BF16).astype(F32)
            rest = line - high
            mid = rest.astype(BF16).astype(F32)
            low = rest - mid
            first = jnp.concatenate([high, high, mid, high, low, mid], axis=0).astype(BF16)
            second = jnp.concatenate([high, mid, high, low, high, mid], axis=0).astype(BF16)
            drop = lax.dot_general(
                first[:, :rank], second, (((0,), (0,)), ((), ())), preferred_element_type=F32
            )
            work[after:, :] = work[after:, :] - drop[after:, :]


def pairs_by(sizes, move):
    owners, planes = sizes
    out = []
    for fib in range(owners):
        for pln in range(planes):
            to_fib, to_pln = move(fib, pln)
            out.append((fib * planes + pln, to_fib * planes + to_pln))
    return out


def per_device(nodal_values, interp_matrix, count_table, slot_order, start_basis):
    nodes = nodal_values[0, 0]
    table = count_table[0].T
    owners = lax.axis_size("fib")
    planes = lax.axis_size("pln")
    sizes = (owners, planes)
    both = ("fib", "pln")
    window = table.shape[0]
    capacity = nodes.shape[0] // window
    points = interp_matrix.shape[1]
    elements = slot_order.shape[2]
    length, rank = start_basis.shape
    tile = points * elements // length
    piece = jax.ShapeDtypeStruct((capacity, points), F32)

    pieces = pl.pallas_call(
        functools.partial(interp_kernel, owners),
        out_shape=[piece] * window,
        in_specs=[SMEM, VMEM, VMEM],
        out_specs=[VMEM] * window,
        scratch_shapes=[pltpu.VMEM((nodes.shape[0] + SLAB, points), F32)],
        compiler_params=BIG,
        name="interp",
    )(table, nodes, interp_matrix)
    received = [pieces[0]] + [
        lax.ppermute(pieces[d], "fib", [(i, (i + d) % owners) for i in range(owners)])
        for d in range(1, window)
    ]
    pick = pl.pallas_call(
        functools.partial(pick_kernel, capacity),
        out_shape=jax.ShapeDtypeStruct((elements, capacity * window), F32),
        in_specs=[SMEM, VMEM],
        out_specs=VMEM,
        compiler_params=BIG,
        name="pick",
    )(table, slot_order[0])
    brick = pl.pallas_call(
        order_kernel,
        out_shape=jax.ShapeDtypeStruct((elements, points), F32),
        in_specs=[VMEM] * (1 + window),
        out_specs=VMEM,
        compiler_params=BIG,
        name="order",
    )(pick, *received)
    brick = brick.reshape(owners, length // owners, tile)
    field = lax.all_to_all(brick, "fib", split_axis=0, concat_axis=0, tiled=True)
    field = field.reshape(length, tile)

    inner = 4
    group = inner * planes
    rows = length // group
    steps = range(group)

    def plane_move(step):
        def move(fib, pln):
            to = ((fib % inner) * planes + pln) ^ step
            return fib - fib % inner + to // planes, to % planes

        return pairs_by(sizes, move)

    chunk = jax.ShapeDtypeStruct((rows, rank), F32)
    chunks = pl.pallas_call(
        functools.partial(image_kernel, inner),
        out_shape=[chunk] * group,
        in_specs=[VMEM] * 2,
        out_specs=[VMEM] * group,
        scratch_shapes=[pltpu.VMEM((length, rank), F32)],
        compiler_params=BIG,
        name="image",
    )(field, start_basis)
    total = chunks[0]
    for step in steps[1:]:
        total = total + lax.ppermute(chunks[step], both, plane_move(step))
    own_sum = total
    for step in range(1, owners // inner):
        moves = pairs_by(sizes, lambda fib, pln: ((fib + step * inner) % owners, pln))
        total = total + lax.ppermute(own_sum, both, moves)
    gathered = [total] + [lax.ppermute(total, both, plane_move(step)) for step in steps[1:]]
    core_values = pl.pallas_call(
        functools.partial(factor_kernel, inner),
        out_shape=jax.ShapeDtypeStruct((rank, tile), F32),
        in_specs=[VMEM] * (1 + group),
        out_specs=VMEM,
        scratch_shapes=[
            pltpu.VMEM((length, rank), F32),
            pltpu.VMEM((rank, rank + tile), F32),
            pltpu.VMEM((SLAB, rank + tile), F32),
        ],
        compiler_params=BIG,
        name="factor",
    )(field, *gathered)
    return core_values[None, None]


def solution(mesh):
    placed = (P("pln", "fib", None, None), P(), P("pln", None, None), P("pln", "fib", None), P())
    return jax.shard_map(
        per_device,
        mesh=mesh,
        in_specs=placed,
        out_specs=P("pln", "fib", None, None),
        check_vma=False,
    )
```

time: 189 us -> 69.8 us (0.37)
  waiting for transfers between devices: 90.7 us -> 18.3 us
  other arithmetic: 23.5 us -> 0.04 us
  blocking collectives: 37.8 us -> 16.3 us
  between operations: 18.6 us -> 0.08 us
  starting transfers between devices: 3.04 us -> 21 us
  matrix products: 10.2 us -> 0 us
  Pallas kernels: 0 us -> 10.2 us
    reduce_scatter x1 -> x0, waiting for transfers between devices: 62 us -> none  [per_device(): lax.psum_scatter(jnp.einsum('txf,tyf->xy', fibre_field, fibre_field, prec...]
    psum x1 -> x0, waiting for transfers between devices: 23.1 us -> none  [per_device(): gram_share = lax.psum(gram_share, 'pln')]
    another operation x5 -> x0, other arithmetic: 22.9 us -> none  [the longest x3 12.4 us: per_device(): lower_factor = jnp.linalg.cholesky(normal_matrix)]
    all_gather x1 -> x0, blocking collectives: 22.7 us -> none  [per_device(): image_matrix = lax.all_gather(image_share, 'fib', axis=0, tiled=True)]
    ppermute x2 -> x19, starting transfers between devices: 2.99 us -> 21 us  [the longest x7 7.31 us: per_device(): total = total + lax.ppermute(chunks[step], both, plane_move(step))]
    ppermute x2 -> x19, waiting for transfers between devices: 5.63 us -> 18.3 us  [the longest x2 7.83 us: per_device(): lax.ppermute(pieces[d], 'fib', [(i, (i + d) % owners) for i in range(owne...]
    pallas_call x0 -> x5, Pallas kernels: none -> 10.2 us  [the longest x1 6.23 us: per_device(): pl.pallas_call(functools.partial(factor_kernel, inner), out_shape=jax.Sha...]
    dot_general x5 -> x0, matrix products: 9.67 us -> none  [the longest x1 3.42 us: per_device(): jnp.einsum('txf,tyf->xy', fibre_field, fibre_field, precision=full_precis...]
  transfers between devices with their start and end apart: 4 -> 19, of which waited for: 4 -> 12; matrix products, arithmetic and copies ran while one was open for 1% -> 0% of each run, Pallas kernels for 0% -> 1%
where the time goes in v1:
time: 69.8 us; the launch traced here: 69.6 us
  starting transfers between devices  21 us (30%)
  waiting for transfers between devices  18.3 us (26%)
  blocking collectives  16.3 us (23%)
  Pallas kernels  10.2 us (15%)
  local copies, waits for them, and re-layouts  3.58 us (5%)
    all_to_all x1, blocking collectives, per_device(): lax.all_to_all(brick, 'fib', split_axis=0, concat_axis=0, tiled=True)  16.3 us
    ppermute x2, waiting for transfers between devices, per_device(): lax.ppermute(pieces[d], 'fib', [(i, (i + d) % owners) for i in range(owne...  7.83 us
    ppermute x7, starting transfers between devices, per_device(): total = total + lax.ppermute(chunks[step], both, plane_move(step))  7.31 us
    ppermute x7, starting transfers between devices, per_device(): lax.ppermute(total, both, plane_move(step))  6.76 us
    pallas_call x1, Pallas kernels, per_device(): pl.pallas_call(functools.partial(factor_kernel, inner), out_shape=jax.Sha...  6.23 us
    ppermute x3, waiting for transfers between devices, per_device(): total = total + lax.ppermute(own_sum, both, moves)  4.61 us
    ppermute x3, starting transfers between devices, per_device(): total = total + lax.ppermute(own_sum, both, moves)  3.9 us
    unnamed x9, local copies, waits for them, and re-layouts  3.55 us
  transfers between devices with their start and end apart: 19, of which 12 were waited for; matrix products, arithmetic and copies ran while one was open for 0% of the time, Pallas kernels for 1%

profile of v1, /device:TPU:0, one launch (start us, length us, event | category | flops | bytes accessed | tf_op | source)
XLA Modules:
  0.0 69.6 jit_solution(7595535868112887770)
XLA Ops:
  0.0 0.0 copy-start.3
  0.0 0.7 copy.8
  0.7 0.0 copy-start
  0.7 1.6 %copy-done = f32[1000,512]{1,0:T(8,128)S(1)} copy-done((f32[1000,512]{1,0:T(8,128)S(1)}, f32[1000,512]{1,0:T(8,128)}, u32[]{:S(2)}) %copy-start) | copy-done | bytes 2048024
  2.3 0.0 copy-start.1
  2.3 1.3 %copy-done.1 = f32[1,1,288,1000]{3,2,1,0:T(8,128)S(1)} copy-done((f32[1,1,288,1000]{3,2,1,0:T(8,128)S(1)}, f32[1,1,288,1000]{3,2,1,0:T(8,128)}, u32[]{:S(2)}) %copy-start.1) | copy-done | bytes 1152024
  3.5 1.8 %interp.1 = (f32[96,512]{1,0:T(8,128)S(1)}, f32[96,512]{1,0:T(8,128)S(1)}, f32[96,512]{1,0:T(8,128)S(1)}) custom-call(s32[3,16]{1,0:T(4,128)S(1)} %bitcast.12, f32[288,1000]{1,0:T(8,128)S(1)} %bitcast.11, f32[1000,512]{1,0:T(8,128)S(1)} %copy-done), custom_call_target="tpu_custom_call" | custom-call | tf_op jit(solution)/shard_map/interp/pallas_call | solution.py:171
  5.4 0.0 copy-start.2
  5.4 0.5 collective-permute-start
  5.9 2.6 %collective-permute-start.1 = (f32[96,512]{1,0:T(8,128)S(1)}, f32[96,512]{1,0:T(8,128)S(1)}, u32[]{:S(2)}, u32[]{:S(2)}) collective-permute-start(f32[96,512]{1,0:T(8,128)S(1)} %get-tuple-element.18), channel_id=1, source_target_pairs={{0,4},{2,6},{4,8},{6,10},{8,12},{10,14},{12,16},{14,18},{16,20},{1... | collective-permute-start | bytes 589832 | tf_op jit(solution)/shard_map/ppermute | solution.py:181
  8.4 0.0 copy-done.3
  8.4 0.9 %pick.1.pick_ref = f32[192,288]{1,0:T(8,128)S(1)} custom-call(s32[3,16]{1,0:T(4,128)S(1)} %bitcast.13, s32[1,192]{1,0:T(1,128)S(1)} %bitcast.14), custom_call_target="tpu_custom_call" | custom-call | tf_op jit(solution)/shard_map/pick/pallas_call | solution.py:184
  9.4 6.0 %collective-permute-done.refs_1_ = f32[96,512]{1,0:T(8,128)S(1)} collective-permute-done((f32[96,512]{1,0:T(8,128)S(1)}, f32[96,512]{1,0:T(8,128)S(1)}, u32[]{:S(2)}, u32[]{:S(2)}) %collective-permute-start) | collective-permute-done | bytes 196640 | tf_op jit(solution)/shard_map/ppermute | solution.py:181
  15.4 1.8 %collective-permute-done.1.refs_2_ = f32[96,512]{1,0:T(8,128)S(1)} collective-permute-done((f32[96,512]{1,0:T(8,128)S(1)}, f32[96,512]{1,0:T(8,128)S(1)}, u32[]{:S(2)}, u32[]{:S(2)}) %collective-permute-start.1) | collective-permute-done | bytes 196640 | tf_op jit(solution)/shard_map/ppermute | solution.py:181
  17.2 0.5 order.1
  17.8 16.3 %all_to_all.5 = f32[16,48,128]{2,1,0:T(8,128)S(1)} all-to-all(f32[16,48,128]{2,1,0:T(8,128)S(1)} %reshape.6), channel_id=1, replica_groups=mesh['fib'=16,'pln'=2] {'fib'}, dimensions={0} | all-to-all | bytes 786432 | tf_op jit(solution)/shard_map/all_to_all | solution.py:201
  34.1 0.0 copy-done.2
  34.1 0.7 %image.1 = (f32[96,128]{1,0:T(8,128)S(1)}, f32[96,128]{1,0:T(8,128)S(1)}, f32[96,128]{1,0:T(8,128)S(1)}, f32[96,128]{1,0:T(8,128)S(1)}, f32[96,128]{1,0:T(8,128)...) custom-call(f32[768,128]{1,0:T(8,128)S(1)} %bitcast.9, f32[768,128]{1,0:T(8,128)S(1)} %copy-done.2), custom_call_target="tpu_custom_call" | custom-call | tf_op jit(solution)/shard_map/image/pallas_call | solution.py:217
  34.8 1.6 %collective-permute-start.2 = (f32[96,128]{1,0:T(8,128)S(1)}, f32[96,128]{1,0:T(8,128)S(1)}, u32[]{:S(2)}, u32[]{:S(2)}) collective-permute-start(f32[96,128]{1,0:T(8,128)S(1)} %get-tuple-element.20), channel_id=1, source_target_pairs={{0,1},{1,0},{2,3},{3,2},{4,5},{5,4},{6,7},{7,6},{8,9},{9,8},{10,11... | collective-permute-start | bytes 147464 | tf_op jit(solution)/shard_map/ppermute | solution.py:228
  36.4 0.0 collective-permute-start.3
  36.4 0.6 collective-permute-start.4
  37.0 0.2 collective-permute-start.5
  37.2 2.8 %collective-permute-start.6 = (f32[96,128]{1,0:T(8,128)S(1)}, f32[96,128]{1,0:T(8,128)S(1)}, u32[]{:S(2)}, u32[]{:S(2)}) collective-permute-start(f32[96,128]{1,0:T(8,128)S(1)} %get-tuple-element.24), channel_id=1, source_target_pairs={{0,5},{1,4},{2,7},{3,6},{4,1},{5,0},{6,3},{7,2},{8,13},{9,12},{10,... | collective-permute-start | bytes 147464 | tf_op jit(solution)/shard_map/ppermute | solution.py:228
  40.0 0.0 collective-permute-done.2
  40.0 0.0 collective-permute-start.7
  40.0 0.0 collective-permute-done.3
  40.0 2.1 %collective-permute-start.8 = (f32[96,128]{1,0:T(8,128)S(1)}, f32[96,128]{1,0:T(8,128)S(1)}, u32[]{:S(2)}, u32[]{:S(2)}) collective-permute-start(f32[96,128]{1,0:T(8,128)S(1)} %get-tuple-element.26), channel_id=1, source_target_pairs={{0,7},{1,6},{2,5},{3,4},{4,3},{5,2},{6,1},{7,0},{8,15},{9,14},{10,... | collective-permute-start | bytes 147464 | tf_op jit(solution)/shard_map/ppermute | solution.py:228
  42.2 0.0 collective-permute-done.4
  42.2 0.0 collective-permute-done.5
  42.2 0.5 collective-permute-done.6
  42.7 1.0 %collective-permute-done.7 = f32[96,128]{1,0:T(8,128)S(1)} collective-permute-done((f32[96,128]{1,0:T(8,128)S(1)}, f32[96,128]{1,0:T(8,128)S(1)}, u32[]{:S(2)}, u32[]{:S(2)}) %collective-permute-start.7) | collective-permute-done | bytes 49184 | tf_op jit(solution)/shard_map/ppermute | solution.py:228
  43.7 1.0 %collective-permute-done.8 = f32[96,128]{1,0:T(8,128)S(1)} collective-permute-done((f32[96,128]{1,0:T(8,128)S(1)}, f32[96,128]{1,0:T(8,128)S(1)}, u32[]{:S(2)}, u32[]{:S(2)}) %collective-permute-start.8) | collective-permute-done | bytes 49184 | tf_op jit(solution)/shard_map/ppermute | solution.py:228
  44.7 1.7 %collective-permute-start.11 = (f32[96,128]{1,0:T(8,128)S(1)}, f32[96,128]{1,0:T(8,128)S(1)}, u32[]{:S(2)}, u32[]{:S(2)}) collective-permute-start(f32[96,128]{1,0:T(8,128)S(1)} %add_add_fusion.1), channel_id=1, source_target_pairs={{0,24},{1,25},{2,26},{3,27},{4,28},{5,29},{6,30},{7,31},{8,0},{9,1... | collective-permute-start | bytes 147464 | tf_op jit(solution)/shard_map/ppermute | solution.py:232
  46.4 0.6 collective-permute-start.10
  47.0 1.7 %collective-permute-start.9 = (f32[96,128]{1,0:T(8,128)S(1)}, f32[96,128]{1,0:T(8,128)S(1)}, u32[]{:S(2)}, u32[]{:S(2)}) collective-permute-start(f32[96,128]{1,0:T(8,128)S(1)} %add_add_fusion.1), channel_id=1, source_target_pairs={{0,8},{1,9},{2,10},{3,11},{4,12},{5,13},{6,14},{7,15},{8,16},{9,17... | collective-permute-start | bytes 147464 | tf_op jit(solution)/shard_map/ppermute | solution.py:232
  48.6 0.2 collective-permute-done.11
  48.9 4.4 %collective-permute-done.10 = f32[96,128]{1,0:T(8,128)S(1)} collective-permute-done((f32[96,128]{1,0:T(8,128)S(1)}, f32[96,128]{1,0:T(8,128)S(1)}, u32[]{:S(2)}, u32[]{:S(2)}) %collective-permute-start.10) | collective-permute-done | bytes 49184 | tf_op jit(solution)/shard_map/ppermute | solution.py:232
  53.2 0.0 collective-permute-done.9
  53.3 0.3 collective-permute-start.18
  53.6 2.1 %collective-permute-start.17 = (f32[96,128]{1,0:T(8,128)S(1)}, f32[96,128]{1,0:T(8,128)S(1)}, u32[]{:S(2)}, u32[]{:S(2)}) collective-permute-start(f32[96,128]{1,0:T(8,128)S(1)} %add_add_fusion.refs_0_), channel_id=1, source_target_pairs={{0,6},{1,7},{2,4},{3,5},{4,2},{5,3},{6,0},{7,1},{8,14},{9,15},{10,... | collective-permute-start | bytes 147464 | tf_op jit(solution)/shard_map/ppermute | solution.py:233
  55.7 1.4 %collective-permute-start.16 = (f32[96,128]{1,0:T(8,128)S(1)}, f32[96,128]{1,0:T(8,128)S(1)}, u32[]{:S(2)}, u32[]{:S(2)}) collective-permute-start(f32[96,128]{1,0:T(8,128)S(1)} %add_add_fusion.refs_0_), channel_id=1, source_target_pairs={{0,5},{1,4},{2,7},{3,6},{4,1},{5,0},{6,3},{7,2},{8,13},{9,12},{10,... | collective-permute-start | bytes 147464 | tf_op jit(solution)/shard_map/ppermute | solution.py:233
  57.0 1.0 %collective-permute-start.15 = (f32[96,128]{1,0:T(8,128)S(1)}, f32[96,128]{1,0:T(8,128)S(1)}, u32[]{:S(2)}, u32[]{:S(2)}) collective-permute-start(f32[96,128]{1,0:T(8,128)S(1)} %add_add_fusion.refs_0_), channel_id=1, source_target_pairs={{0,4},{1,5},{2,6},{3,7},{4,0},{5,1},{6,2},{7,3},{8,12},{9,13},{10,... | collective-permute-start | bytes 147464 | tf_op jit(solution)/shard_map/ppermute | solution.py:233
  58.0 0.0 collective-permute-start.14
  58.0 0.1 collective-permute-done.18.refs_7_
  58.1 1.1 %collective-permute-start.13 = (f32[96,128]{1,0:T(8,128)S(1)}, f32[96,128]{1,0:T(8,128)S(1)}, u32[]{:S(2)}, u32[]{:S(2)}) collective-permute-start(f32[96,128]{1,0:T(8,128)S(1)} %add_add_fusion.refs_0_), channel_id=1, source_target_pairs={{0,2},{1,3},{2,0},{3,1},{4,6},{5,7},{6,4},{7,5},{8,10},{9,11},{10,... | collective-permute-start | bytes 147464 | tf_op jit(solution)/shard_map/ppermute | solution.py:233
  59.3 0.0 collective-permute-done.17.refs_6_
  59.3 0.9 %collective-permute-start.12 = (f32[96,128]{1,0:T(8,128)S(1)}, f32[96,128]{1,0:T(8,128)S(1)}, u32[]{:S(2)}, u32[]{:S(2)}) collective-permute-start(f32[96,128]{1,0:T(8,128)S(1)} %add_add_fusion.refs_0_), channel_id=1, source_target_pairs={{0,1},{1,0},{2,3},{3,2},{4,5},{5,4},{6,7},{7,6},{8,9},{9,8},{10,11... | collective-permute-start | bytes 147464 | tf_op jit(solution)/shard_map/ppermute | solution.py:233
  60.2 0.8 %collective-permute-done.16.refs_5_ = f32[96,128]{1,0:T(8,128)S(1)} collective-permute-done((f32[96,128]{1,0:T(8,128)S(1)}, f32[96,128]{1,0:T(8,128)S(1)}, u32[]{:S(2)}, u32[]{:S(2)}) %collective-permute-start.16) | collective-permute-done | bytes 49184 | tf_op jit(solution)/shard_map/ppermute | solution.py:233
  60.9 0.2 collective-permute-done.15.refs_4_
  61.1 0.8 %collective-permute-done.14.refs_3_ = f32[96,128]{1,0:T(8,128)S(1)} collective-permute-done((f32[96,128]{1,0:T(8,128)S(1)}, f32[96,128]{1,0:T(8,128)S(1)}, u32[]{:S(2)}, u32[]{:S(2)}) %collective-permute-start.14) | collective-permute-done | bytes 49184 | tf_op jit(solution)/shard_map/ppermute | solution.py:233
  62.0 0.0 collective-permute-done.13.refs_2_
  62.0 1.4 %collective-permute-done.12.refs_1_ = f32[96,128]{1,0:T(8,128)S(1)} collective-permute-done((f32[96,128]{1,0:T(8,128)S(1)}, f32[96,128]{1,0:T(8,128)S(1)}, u32[]{:S(2)}, u32[]{:S(2)}) %collective-permute-start.12) | collective-permute-done | bytes 49184 | tf_op jit(solution)/shard_map/ppermute | solution.py:233
  63.4 6.2 %factor.1 = f32[128,128]{1,0:T(8,128)} custom-call(f32[768,128]{1,0:T(8,128)S(1)} %bitcast.10, f32[96,128]{1,0:T(8,128)S(1)} %add_add_fusion.refs_0_, f32[96,128]{1,0:T(8,128)S(1)} %collective-permute-done.12.refs_1_, f32[96,128]{1,0:T(8,128)S(1)} %collective-permute-done.13.refs_2_, f32[96,128]{1,0:T(8,128)S(1)} %collective-permute-done.14.refs_3_, ...), custom_call_target="tpu_custom_call" | custom-call | tf_op jit(solution)/shard_map/factor/pallas_call | solution.py:234
  (3 shorter events, 0.1 us)
Async XLA Ops:
  0.0 8.4 %copy-start.3 = (s32[1,1,192]{2,1,0:T(1,128)S(1)}, s32[1,1,192]{2,1,0:T(1,128)}, u32[]{:S(2)}) copy-start(s32[1,1,192]{2,1,0:T(1,128)} %param.8) | copy-start | bytes 2308
  0.7 1.6 %copy-start = (f32[1000,512]{1,0:T(8,128)S(1)}, f32[1000,512]{1,0:T(8,128)}, u32[]{:S(2)}) copy-start(f32[1000,512]{1,0:T(8,128)} %interp_ref.1) | copy-start | bytes 6144004
  2.3 1.3 %copy-start.1 = (f32[1,1,288,1000]{3,2,1,0:T(8,128)S(1)}, f32[1,1,288,1000]{3,2,1,0:T(8,128)}, u32[]{:S(2)}) copy-start(f32[1,1,288,1000]{3,2,1,0:T(8,128)} %param.5) | copy-start | bytes 3456004
  5.4 28.7 %copy-start.2 = (f32[768,128]{1,0:T(8,128)S(1)}, f32[768,128]{1,0:T(8,128)}, u32[]{:S(2)}) copy-start(f32[768,128]{1,0:T(8,128)} %start_ref.1) | copy-start | bytes 1179652
  5.4 10.0 %collective-permute-start = (f32[96,512]{1,0:T(8,128)S(1)}, f32[96,512]{1,0:T(8,128)S(1)}, u32[]{:S(2)}, u32[]{:S(2)}) collective-permute-start(f32[96,512]{1,0:T(8,128)S(1)} %get-tuple-element.17), channel_id=1, source_target_pairs={{0,2},{2,4},{4,6},{6,8},{8,10},{10,12},{12,14},{14,16},{16,18},{18... | collective-permute-start | bytes 589832 | tf_op jit(solution)/shard_map/ppermute | solution.py:181
  5.9 11.3 %collective-permute-start.1 = (f32[96,512]{1,0:T(8,128)S(1)}, f32[96,512]{1,0:T(8,128)S(1)}, u32[]{:S(2)}, u32[]{:S(2)}) collective-permute-start(f32[96,512]{1,0:T(8,128)S(1)} %get-tuple-element.18), channel_id=1, source_target_pairs={{0,4},{2,6},{4,8},{6,10},{8,12},{10,14},{12,16},{14,18},{16,20},{1... | collective-permute-start | bytes 589832 | tf_op jit(solution)/shard_map/ppermute | solution.py:181
  34.8 5.2 %collective-permute-start.2 = (f32[96,128]{1,0:T(8,128)S(1)}, f32[96,128]{1,0:T(8,128)S(1)}, u32[]{:S(2)}, u32[]{:S(2)}) collective-permute-start(f32[96,128]{1,0:T(8,128)S(1)} %get-tuple-element.20), channel_id=1, source_target_pairs={{0,1},{1,0},{2,3},{3,2},{4,5},{5,4},{6,7},{7,6},{8,9},{9,8},{10,11... | collective-permute-start | bytes 147464 | tf_op jit(solution)/shard_map/ppermute | solution.py:228
  36.4 3.6 %collective-permute-start.3 = (f32[96,128]{1,0:T(8,128)S(1)}, f32[96,128]{1,0:T(8,128)S(1)}, u32[]{:S(2)}, u32[]{:S(2)}) collective-permute-start(f32[96,128]{1,0:T(8,128)S(1)} %get-tuple-element.21), channel_id=1, source_target_pairs={{0,2},{1,3},{2,0},{3,1},{4,6},{5,7},{6,4},{7,5},{8,10},{9,11},{10,... | collective-permute-start | bytes 147464 | tf_op jit(solution)/shard_map/ppermute | solution.py:228
  36.4 5.7 %collective-permute-start.4 = (f32[96,128]{1,0:T(8,128)S(1)}, f32[96,128]{1,0:T(8,128)S(1)}, u32[]{:S(2)}, u32[]{:S(2)}) collective-permute-start(f32[96,128]{1,0:T(8,128)S(1)} %get-tuple-element.22), channel_id=1, source_target_pairs={{0,3},{1,2},{2,1},{3,0},{4,7},{5,6},{6,5},{7,4},{8,11},{9,10},{10,... | collective-permute-start | bytes 147464 | tf_op jit(solution)/shard_map/ppermute | solution.py:228
  37.0 5.1 %collective-permute-start.5 = (f32[96,128]{1,0:T(8,128)S(1)}, f32[96,128]{1,0:T(8,128)S(1)}, u32[]{:S(2)}, u32[]{:S(2)}) collective-permute-start(f32[96,128]{1,0:T(8,128)S(1)} %get-tuple-element.23), channel_id=1, source_target_pairs={{0,4},{1,5},{2,6},{3,7},{4,0},{5,1},{6,2},{7,3},{8,12},{9,13},{10,... | collective-permute-start | bytes 147464 | tf_op jit(solution)/shard_map/ppermute | solution.py:228
  37.2 5.5 %collective-permute-start.6 = (f32[96,128]{1,0:T(8,128)S(1)}, f32[96,128]{1,0:T(8,128)S(1)}, u32[]{:S(2)}, u32[]{:S(2)}) collective-permute-start(f32[96,128]{1,0:T(8,128)S(1)} %get-tuple-element.24), channel_id=1, source_target_pairs={{0,5},{1,4},{2,7},{3,6},{4,1},{5,0},{6,3},{7,2},{8,13},{9,12},{10,... | collective-permute-start | bytes 147464 | tf_op jit(solution)/shard_map/ppermute | solution.py:228
  40.0 3.7 %collective-permute-start.7 = (f32[96,128]{1,0:T(8,128)S(1)}, f32[96,128]{1,0:T(8,128)S(1)}, u32[]{:S(2)}, u32[]{:S(2)}) collective-permute-start(f32[96,128]{1,0:T(8,128)S(1)} %get-tuple-element.25), channel_id=1, source_target_pairs={{0,6},{1,7},{2,4},{3,5},{4,2},{5,3},{6,0},{7,1},{8,14},{9,15},{10,... | collective-permute-start | bytes 147464 | tf_op jit(solution)/shard_map/ppermute | solution.py:228
  40.0 4.7 %collective-permute-start.8 = (f32[96,128]{1,0:T(8,128)S(1)}, f32[96,128]{1,0:T(8,128)S(1)}, u32[]{:S(2)}, u32[]{:S(2)}) collective-permute-start(f32[96,128]{1,0:T(8,128)S(1)} %get-tuple-element.26), channel_id=1, source_target_pairs={{0,7},{1,6},{2,5},{3,4},{4,3},{5,2},{6,1},{7,0},{8,15},{9,14},{10,... | collective-permute-start | bytes 147464 | tf_op jit(solution)/shard_map/ppermute | solution.py:228
  44.7 4.1 %collective-permute-start.11 = (f32[96,128]{1,0:T(8,128)S(1)}, f32[96,128]{1,0:T(8,128)S(1)}, u32[]{:S(2)}, u32[]{:S(2)}) collective-permute-start(f32[96,128]{1,0:T(8,128)S(1)} %add_add_fusion.1), channel_id=1, source_target_pairs={{0,24},{1,25},{2,26},{3,27},{4,28},{5,29},{6,30},{7,31},{8,0},{9,1... | collective-permute-start | bytes 147464 | tf_op jit(solution)/shard_map/ppermute | solution.py:232
  46.4 6.9 %collective-permute-start.10 = (f32[96,128]{1,0:T(8,128)S(1)}, f32[96,128]{1,0:T(8,128)S(1)}, u32[]{:S(2)}, u32[]{:S(2)}) collective-permute-start(f32[96,128]{1,0:T(8,128)S(1)} %add_add_fusion.1), channel_id=1, source_target_pairs={{0,16},{1,17},{2,18},{3,19},{4,20},{5,21},{6,22},{7,23},{8,24},{9,... | collective-permute-start | bytes 147464 | tf_op jit(solution)/shard_map/ppermute | solution.py:232
  47.0 6.3 %collective-permute-start.9 = (f32[96,128]{1,0:T(8,128)S(1)}, f32[96,128]{1,0:T(8,128)S(1)}, u32[]{:S(2)}, u32[]{:S(2)}) collective-permute-start(f32[96,128]{1,0:T(8,128)S(1)} %add_add_fusion.1), channel_id=1, source_target_pairs={{0,8},{1,9},{2,10},{3,11},{4,12},{5,13},{6,14},{7,15},{8,16},{9,17... | collective-permute-start | bytes 147464 | tf_op jit(solution)/shard_map/ppermute | solution.py:232
  53.3 4.9 %collective-permute-start.18 = (f32[96,128]{1,0:T(8,128)S(1)}, f32[96,128]{1,0:T(8,128)S(1)}, u32[]{:S(2)}, u32[]{:S(2)}) collective-permute-start(f32[96,128]{1,0:T(8,128)S(1)} %add_add_fusion.refs_0_), channel_id=1, source_target_pairs={{0,7},{1,6},{2,5},{3,4},{4,3},{5,2},{6,1},{7,0},{8,15},{9,14},{10,... | collective-permute-start | bytes 147464 | tf_op jit(solution)/shard_map/ppermute | solution.py:233
  53.6 5.7 %collective-permute-start.17 = (f32[96,128]{1,0:T(8,128)S(1)}, f32[96,128]{1,0:T(8,128)S(1)}, u32[]{:S(2)}, u32[]{:S(2)}) collective-permute-start(f32[96,128]{1,0:T(8,128)S(1)} %add_add_fusion.refs_0_), channel_id=1, source_target_pairs={{0,6},{1,7},{2,4},{3,5},{4,2},{5,3},{6,0},{7,1},{8,14},{9,15},{10,... | collective-permute-start | bytes 147464 | tf_op jit(solution)/shard_map/ppermute | solution.py:233
  55.7 5.3 %collective-permute-start.16 = (f32[96,128]{1,0:T(8,128)S(1)}, f32[96,128]{1,0:T(8,128)S(1)}, u32[]{:S(2)}, u32[]{:S(2)}) collective-permute-start(f32[96,128]{1,0:T(8,128)S(1)} %add_add_fusion.refs_0_), channel_id=1, source_target_pairs={{0,5},{1,4},{2,7},{3,6},{4,1},{5,0},{6,3},{7,2},{8,13},{9,12},{10,... | collective-permute-start | bytes 147464 | tf_op jit(solution)/shard_map/ppermute | solution.py:233
  57.0 4.1 %collective-permute-start.15 = (f32[96,128]{1,0:T(8,128)S(1)}, f32[96,128]{1,0:T(8,128)S(1)}, u32[]{:S(2)}, u32[]{:S(2)}) collective-permute-start(f32[96,128]{1,0:T(8,128)S(1)} %add_add_fusion.refs_0_), channel_id=1, source_target_pairs={{0,4},{1,5},{2,6},{3,7},{4,0},{5,1},{6,2},{7,3},{8,12},{9,13},{10,... | collective-permute-start | bytes 147464 | tf_op jit(solution)/shard_map/ppermute | solution.py:233
  58.0 4.0 %collective-permute-start.14 = (f32[96,128]{1,0:T(8,128)S(1)}, f32[96,128]{1,0:T(8,128)S(1)}, u32[]{:S(2)}, u32[]{:S(2)}) collective-permute-start(f32[96,128]{1,0:T(8,128)S(1)} %add_add_fusion.refs_0_), channel_id=1, source_target_pairs={{0,3},{1,2},{2,1},{3,0},{4,7},{5,6},{6,5},{7,4},{8,11},{9,10},{10,... | collective-permute-start | bytes 147464 | tf_op jit(solution)/shard_map/ppermute | solution.py:233
  58.1 3.8 %collective-permute-start.13 = (f32[96,128]{1,0:T(8,128)S(1)}, f32[96,128]{1,0:T(8,128)S(1)}, u32[]{:S(2)}, u32[]{:S(2)}) collective-permute-start(f32[96,128]{1,0:T(8,128)S(1)} %add_add_fusion.refs_0_), channel_id=1, source_target_pairs={{0,2},{1,3},{2,0},{3,1},{4,6},{5,7},{6,4},{7,5},{8,10},{9,11},{10,... | collective-permute-start | bytes 147464 | tf_op jit(solution)/shard_map/ppermute | solution.py:233
  59.3 4.1 %collective-permute-start.12 = (f32[96,128]{1,0:T(8,128)S(1)}, f32[96,128]{1,0:T(8,128)S(1)}, u32[]{:S(2)}, u32[]{:S(2)}) collective-permute-start(f32[96,128]{1,0:T(8,128)S(1)} %add_add_fusion.refs_0_), channel_id=1, source_target_pairs={{0,1},{1,0},{2,3},{3,2},{4,5},{5,4},{6,7},{7,6},{8,9},{9,8},{10,11... | collective-permute-start | bytes 147464 | tf_op jit(solution)/shard_map/ppermute | solution.py:233

commit v2 on v1

--- a/solution.py
+++ b/solution.py
@@ -37,13 +37,13 @@
     own = lax.axis_index("fib")
     grid_scr[:slots, :] = dot3(halves(node_ref[...]), halves(interp_ref[...]), ((1,), (0,)))
     outs[0][...] = grid_scr[:rows, :]
-    start = table_ref[0, own]
+    start = table_ref[0, 0, own]
     for distance in range(1, window):
         shift = lax.rem(start, SLAB)
         at = pl.multiple_of(start - shift, SLAB)
         wide = grid_scr[pl.ds(at, rows + SLAB), :]
         outs[distance][...] = pltpu.roll(wide, lax.rem(rows + SLAB - shift, rows + SLAB), 0)[:rows, :]
-        start = start + table_ref[distance, lax.rem(own + distance, owners)]
+        start = start + table_ref[distance, 0, lax.rem(own + distance, owners)]
 
 
 def pick_kernel(rows, table_ref, order_ref, out_ref):
@@ -55,7 +55,7 @@
     from_slot = jnp.zeros((elements, slots), jnp.bool_)
     start = 0
     for distance in range(window - 1, -1, -1):
-        count = table_ref[distance, own]
+        count = table_ref[distance, 0, own]
         inside = (rank_at >= start) & (rank_at < start + count)
         from_slot = from_slot | (inside & (slot_at - distance * rows == rank_at - start))
         start = start + count
@@ -80,31 +80,15 @@
     out_ref[...] = out + jnp.dot(pick, high, preferred_element_type=F32)
 
 
-def plane_index(inner):
-    return lax.rem(lax.axis_index("fib"), inner) * lax.axis_size("pln") + lax.axis_index("pln")
-
-
-def image_kernel(inner, field_ref, start_ref, *refs):
-    outs, image_scr = refs[:-1], refs[-1]
-    rows = outs[0].shape[0]
+def image_kernel(field_ref, start_ref, out_ref):
     field = halves(field_ref[...])
     mixed = dot3(field, halves(start_ref[...]), ((0,), (0,)))
-    image_scr[...] = dot3(field, halves(mixed), ((1,), (0,)))
-    mine = plane_index(inner)
-    for step, out in enumerate(outs):
-        at = pl.multiple_of((mine ^ step) * rows, rows)
-        out[...] = image_scr[pl.ds(at, rows), :]
-
-
-def factor_kernel(inner, field_ref, *refs):
-    chunks, out_ref, image_scr, work, line_scr = refs[:-4], refs[-4], refs[-3], refs[-2], refs[-1]
-    rows = chunks[0].shape[0]
+    out_ref[...] = dot3(field, halves(mixed), ((1,), (0,)))
+
+
+def factor_kernel(field_ref, image_ref, out_ref, work, line_scr):
     rank = out_ref.shape[0]
-    mine = plane_index(inner)
-    for step, chunk in enumerate(chunks):
-        at = pl.multiple_of((mine ^ step) * rows, rows)
-        image_scr[pl.ds(at, rows), :] = chunk[...]
-    image = halves(image_scr[...])
+    image = halves(image_ref[...])
     work[:, :rank] = dot3(image, image, ((0,), (0,)))
     work[:, rank:] = dot3(image, halves(field_ref[...]), ((0,), (0,)))
     shape = (1, rank)
@@ -155,7 +139,7 @@
 
 def per_device(nodal_values, interp_matrix, count_table, slot_order, start_basis):
     nodes = nodal_values[0, 0]
-    table = count_table[0].T
+    table = jnp.transpose(count_table, (2, 0, 1))
     owners = lax.axis_size("fib")
     planes = lax.axis_size("pln")
     sizes = (owners, planes)
@@ -204,46 +188,45 @@
     inner = 4
     group = inner * planes
     rows = length // group
-    steps = range(group)
-
-    def plane_move(step):
-        def move(fib, pln):
-            to = ((fib % inner) * planes + pln) ^ step
-            return fib - fib % inner + to // planes, to % planes
-
-        return pairs_by(sizes, move)
-
-    chunk = jax.ShapeDtypeStruct((rows, rank), F32)
-    chunks = pl.pallas_call(
-        functools.partial(image_kernel, inner),
-        out_shape=[chunk] * group,
+    planes_of = [
+        [
+            (base + i // planes) * planes + i % planes
+            for i in range(group)
+        ]
+        for base in range(0, owners, inner)
+    ]
+
+    def plane_exchange(value):
+        return lax.all_to_all(
+            value, both, split_axis=0, concat_axis=0, axis_index_groups=planes_of, tiled=True
+        )
+
+    image = pl.pallas_call(
+        image_kernel,
+        out_shape=jax.ShapeDtypeStruct((length, rank), F32),
         in_specs=[VMEM] * 2,
-        out_specs=[VMEM] * group,
-        scratch_shapes=[pltpu.VMEM((length, rank), F32)],
+        out_specs=VMEM,
         compiler_params=BIG,
         name="image",
     )(field, start_basis)
-    total = chunks[0]
-    for step in steps[1:]:
-        total = total + lax.ppermute(chunks[step], both, plane_move(step))
-    own_sum = total
+    own_sum = jnp.sum(plane_exchange(image).reshape(group, rows, rank), axis=0)
+    total = own_sum
     for step in range(1, owners // inner):
         moves = pairs_by(sizes, lambda fib, pln: ((fib + step * inner) % owners, pln))
         total = total + lax.ppermute(own_sum, both, moves)
-    gathered = [total] + [lax.ppermute(total, both, plane_move(step)) for step in steps[1:]]
+    image = plane_exchange(jnp.tile(total, (group, 1)))
     core_values = pl.pallas_call(
-        functools.partial(factor_kernel, inner),
+        factor_kernel,
         out_shape=jax.ShapeDtypeStruct((rank, tile), F32),
-        in_specs=[VMEM] * (1 + group),
+        in_specs=[VMEM] * 2,
         out_specs=VMEM,
         scratch_shapes=[
-            pltpu.VMEM((length, rank), F32),
             pltpu.VMEM((rank, rank + tile), F32),
             pltpu.VMEM((SLAB, rank + tile), F32),
         ],
         compiler_params=BIG,
         name="factor",
-    )(field, *gathered)
+    )(field, image)
     return core_values[None, None]
 
 

time: 69.8 us -> 70.5 us (1.010)
  blocking collectives: 16.3 us -> 36.8 us
  starting transfers between devices: 21 us -> 6.85 us
  waiting for transfers between devices: 18.3 us -> 12.7 us
    all_to_all x0 -> x2, blocking collectives: none -> 20.5 us  [plane_exchange(): lax.all_to_all(value, both, split_axis=0, concat_axis=0, axis_index_group...]
    ppermute x14 -> x0, starting transfers between devices: 14.1 us -> none  [the longest x7 7.31 us: per_device(): total = total + lax.ppermute(chunks[step], both, plane_move(step))]
    ppermute x14 -> x0, waiting for transfers between devices: 5.88 us -> none  [the longest x7 3.33 us: per_device(): lax.ppermute(total, both, plane_move(step))]
    unnamed x9 -> x10, local copies, waits for them, and re-layouts: 3.55 us -> 3.55 us
  transfers between devices with their start and end apart: 19 -> 5, of which waited for: 12 -> 5; matrix products, arithmetic and copies ran while one was open for 0% -> 0% of each run, Pallas kernels for 1% -> 1%
where the time goes in v2:
time: 70.5 us; the launch traced here: 70.2 us
  blocking collectives  36.8 us (52%)
  waiting for transfers between devices  12.7 us (18%)
  Pallas kernels  10.2 us (14%)
  starting transfers between devices  6.85 us (10%)
  local copies, waits for them, and re-layouts  3.6 us (5%)
    all_to_all x2, blocking collectives, plane_exchange(): lax.all_to_all(value, both, split_axis=0, concat_axis=0, axis_index_group...  20.5 us
    all_to_all x1, blocking collectives, per_device(): lax.all_to_all(brick, 'fib', split_axis=0, concat_axis=0, tiled=True)  16.3 us
    ppermute x2, waiting for transfers between devices, per_device(): lax.ppermute(pieces[d], 'fib', [(i, (i + d) % owners) for i in range(owne...  7.84 us
    pallas_call x1, Pallas kernels, per_device(): pl.pallas_call(factor_kernel, out_shape=jax.ShapeDtypeStruct((rank, tile)...  6.19 us
    ppermute x3, waiting for transfers between devices, per_device(): total = total + lax.ppermute(own_sum, both, moves)  4.85 us
    ppermute x3, starting transfers between devices, per_device(): total = total + lax.ppermute(own_sum, both, moves)  3.79 us
    unnamed x10, local copies, waits for them, and re-layouts  3.55 us
    ppermute x2, starting transfers between devices, per_device(): lax.ppermute(pieces[d], 'fib', [(i, (i + d) % owners) for i in range(owne...  3.06 us
  transfers between devices with their start and end apart: 5, of which 5 were waited for; matrix products, arithmetic and copies ran while one was open for 0% of the time, Pallas kernels for 1%

profile of v2, /device:TPU:0, one launch (start us, length us, event | category | flops | bytes accessed | tf_op | source)
XLA Modules:
  0.0 70.2 jit_solution(13314966890774283231)
XLA Ops:
  0.0 0.0 copy-start.4
  0.0 0.0 copy-start
  0.0 1.6 %copy-done = f32[1000,512]{1,0:T(8,128)S(1)} copy-done((f32[1000,512]{1,0:T(8,128)S(1)}, f32[1000,512]{1,0:T(8,128)}, u32[]{:S(2)}) %copy-start) | copy-done | bytes 2048024
  1.6 0.0 copy-start.1
  1.6 1.3 %copy-done.1 = f32[1,1,288,1000]{3,2,1,0:T(8,128)S(1)} copy-done((f32[1,1,288,1000]{3,2,1,0:T(8,128)S(1)}, f32[1,1,288,1000]{3,2,1,0:T(8,128)}, u32[]{:S(2)}) %copy-start.1) | copy-done | bytes 1152024
  2.9 0.0 copy-start.3
  2.9 0.7 copy-done.3
  3.5 1.8 %interp.1 = (f32[96,512]{1,0:T(8,128)S(1)}, f32[96,512]{1,0:T(8,128)S(1)}, f32[96,512]{1,0:T(8,128)S(1)}) custom-call(s32[3,1,16]{2,1,0:T(1,128)S(1)} %bitcast.12, f32[288,1000]{1,0:T(8,128)S(1)} %bitcast.11, f32[1000,512]{1,0:T(8,128)S(1)} %copy-done), custom_call_target="tpu_custom_call" | custom-call | tf_op jit(solution)/shard_map/interp/pallas_call | solution.py:155
  5.4 0.0 copy-start.2
  5.4 0.5 collective-permute-start
  5.9 2.6 %collective-permute-start.1 = (f32[96,512]{1,0:T(8,128)S(1)}, f32[96,512]{1,0:T(8,128)S(1)}, u32[]{:S(2)}, u32[]{:S(2)}) collective-permute-start(f32[96,512]{1,0:T(8,128)S(1)} %get-tuple-element.10), channel_id=1, source_target_pairs={{0,4},{2,6},{4,8},{6,10},{8,12},{10,14},{12,16},{14,18},{16,20},{1... | collective-permute-start | bytes 589832 | tf_op jit(solution)/shard_map/ppermute | solution.py:165
  8.4 0.0 copy-done.4
  8.4 0.9 %pick.1.pick_ref = f32[192,288]{1,0:T(8,128)S(1)} custom-call(s32[3,1,16]{2,1,0:T(1,128)S(1)} %bitcast.13, s32[1,192]{1,0:T(1,128)S(1)} %bitcast.14), custom_call_target="tpu_custom_call" | custom-call | tf_op jit(solution)/shard_map/pick/pallas_call | solution.py:168
  9.4 6.0 %collective-permute-done.refs_1_ = f32[96,512]{1,0:T(8,128)S(1)} collective-permute-done((f32[96,512]{1,0:T(8,128)S(1)}, f32[96,512]{1,0:T(8,128)S(1)}, u32[]{:S(2)}, u32[]{:S(2)}) %collective-permute-start) | collective-permute-done | bytes 196640 | tf_op jit(solution)/shard_map/ppermute | solution.py:165
  15.4 1.8 %collective-permute-done.1.refs_2_ = f32[96,512]{1,0:T(8,128)S(1)} collective-permute-done((f32[96,512]{1,0:T(8,128)S(1)}, f32[96,512]{1,0:T(8,128)S(1)}, u32[]{:S(2)}, u32[]{:S(2)}) %collective-permute-start.1) | collective-permute-done | bytes 196640 | tf_op jit(solution)/shard_map/ppermute | solution.py:165
  17.2 0.5 order.1
  17.8 16.3 %all_to_all.22 = f32[16,48,128]{2,1,0:T(8,128)S(1)} all-to-all(f32[16,48,128]{2,1,0:T(8,128)S(1)} %reshape.17), channel_id=1, replica_groups=mesh['fib'=16,'pln'=2] {'fib'}, dimensions={0} | all-to-all | bytes 786432 | tf_op jit(solution)/shard_map/all_to_all | solution.py:185
  34.1 0.0 copy-done.2
  34.1 0.7 %image.1 = f32[768,128]{1,0:T(8,128)S(1)} custom-call(f32[768,128]{1,0:T(8,128)S(1)} %bitcast.7, f32[768,128]{1,0:T(8,128)S(1)} %copy-done.2), custom_call_target="tpu_custom_call" | custom-call | tf_op jit(solution)/shard_map/image/pallas_call | solution.py:204
  34.8 10.4 %all_to_all.23 = f32[8,96,128]{2,1,0:T(8,128)S(1)} all-to-all(f32[8,96,128]{2,1,0:T(8,128)S(1)} %bitcast.10), channel_id=1, replica_groups={{0,1,2,3,4,5,6,7},{8,9,10,11,12,13,14,15},{16,17,18,19,20,21,22,23},{24..., dimensions={0} | all-to-all | bytes 786432 | tf_op jit(solution)/shard_map/all_to_all | solution.py:200
  45.2 2.2 %collective-permute-start.4 = (f32[96,128]{1,0:T(8,128)S(1)}, f32[96,128]{1,0:T(8,128)S(1)}, u32[]{:S(2)}, u32[]{:S(2)}) collective-permute-start(f32[96,128]{1,0:T(8,128)S(1)} %reduce_sum.9), channel_id=1, source_target_pairs={{0,24},{1,25},{2,26},{3,27},{4,28},{5,29},{6,30},{7,31},{8,0},{9,1... | collective-permute-start | bytes 147464 | tf_op jit(solution)/shard_map/ppermute | solution.py:216
  47.4 0.6 collective-permute-start.3
  47.9 1.0 %collective-permute-start.2 = (f32[96,128]{1,0:T(8,128)S(1)}, f32[96,128]{1,0:T(8,128)S(1)}, u32[]{:S(2)}, u32[]{:S(2)}) collective-permute-start(f32[96,128]{1,0:T(8,128)S(1)} %reduce_sum.9), channel_id=1, source_target_pairs={{0,8},{1,9},{2,10},{3,11},{4,12},{5,13},{6,14},{7,15},{8,16},{9,17... | collective-permute-start | bytes 147464 | tf_op jit(solution)/shard_map/ppermute | solution.py:216
  49.0 0.5 collective-permute-done.4
  49.5 3.6 %collective-permute-done.3 = f32[96,128]{1,0:T(8,128)S(1)} collective-permute-done((f32[96,128]{1,0:T(8,128)S(1)}, f32[96,128]{1,0:T(8,128)S(1)}, u32[]{:S(2)}, u32[]{:S(2)}) %collective-permute-start.3) | collective-permute-done | bytes 49184 | tf_op jit(solution)/shard_map/ppermute | solution.py:216
  53.1 0.7 %collective-permute-done.2 = f32[96,128]{1,0:T(8,128)S(1)} collective-permute-done((f32[96,128]{1,0:T(8,128)S(1)}, f32[96,128]{1,0:T(8,128)S(1)}, u32[]{:S(2)}, u32[]{:S(2)}) %collective-permute-start.2) | collective-permute-done | bytes 49184 | tf_op jit(solution)/shard_map/ppermute | solution.py:216
  53.9 10.1 %all_to_all.24 = f32[8,96,128]{2,1,0:T(8,128)S(1)} all-to-all(f32[8,96,128]{2,1,0:T(8,128)S(1)} %tile.2), channel_id=1, replica_groups={{0,1,2,3,4,5,6,7},{8,9,10,11,12,13,14,15},{16,17,18,19,20,21,22,23},{24..., dimensions={0} | all-to-all | bytes 786432 | tf_op jit(solution)/shard_map/all_to_all | solution.py:200
  64.0 6.2 %factor.1 = f32[128,128]{1,0:T(8,128)} custom-call(f32[768,128]{1,0:T(8,128)S(1)} %bitcast.8, f32[768,128]{1,0:T(8,128)S(1)} %bitcast.9), custom_call_target="tpu_custom_call" | custom-call | tf_op jit(solution)/shard_map/factor/pallas_call | solution.py:218
  (4 shorter events, 0.1 us)
Async XLA Ops:
  0.0 8.4 %copy-start.4 = (s32[1,1,192]{2,1,0:T(1,128)S(1)}, s32[1,1,192]{2,1,0:T(1,128)}, u32[]{:S(2)}) copy-start(s32[1,1,192]{2,1,0:T(1,128)} %param.8) | copy-start | bytes 2308
  0.0 1.6 %copy-start = (f32[1000,512]{1,0:T(8,128)S(1)}, f32[1000,512]{1,0:T(8,128)}, u32[]{:S(2)}) copy-start(f32[1000,512]{1,0:T(8,128)} %interp_ref.1) | copy-start | bytes 6144004
  1.6 1.3 %copy-start.1 = (f32[1,1,288,1000]{3,2,1,0:T(8,128)S(1)}, f32[1,1,288,1000]{3,2,1,0:T(8,128)}, u32[]{:S(2)}) copy-start(f32[1,1,288,1000]{3,2,1,0:T(8,128)} %param.5) | copy-start | bytes 3456004
  2.9 0.7 copy-start.3
  5.4 28.7 %copy-start.2 = (f32[768,128]{1,0:T(8,128)S(1)}, f32[768,128]{1,0:T(8,128)}, u32[]{:S(2)}) copy-start(f32[768,128]{1,0:T(8,128)} %start_ref.1) | copy-start | bytes 1179652
  5.4 10.0 %collective-permute-start = (f32[96,512]{1,0:T(8,128)S(1)}, f32[96,512]{1,0:T(8,128)S(1)}, u32[]{:S(2)}, u32[]{:S(2)}) collective-permute-start(f32[96,512]{1,0:T(8,128)S(1)} %get-tuple-element.9), channel_id=1, source_target_pairs={{0,2},{2,4},{4,6},{6,8},{8,10},{10,12},{12,14},{14,16},{16,18},{18... | collective-permute-start | bytes 589832 | tf_op jit(solution)/shard_map/ppermute | solution.py:165
  5.9 11.3 %collective-permute-start.1 = (f32[96,512]{1,0:T(8,128)S(1)}, f32[96,512]{1,0:T(8,128)S(1)}, u32[]{:S(2)}, u32[]{:S(2)}) collective-permute-start(f32[96,512]{1,0:T(8,128)S(1)} %get-tuple-element.10), channel_id=1, source_target_pairs={{0,4},{2,6},{4,8},{6,10},{8,12},{10,14},{12,16},{14,18},{16,20},{1... | collective-permute-start | bytes 589832 | tf_op jit(solution)/shard_map/ppermute | solution.py:165
  45.2 4.3 %collective-permute-start.4 = (f32[96,128]{1,0:T(8,128)S(1)}, f32[96,128]{1,0:T(8,128)S(1)}, u32[]{:S(2)}, u32[]{:S(2)}) collective-permute-start(f32[96,128]{1,0:T(8,128)S(1)} %reduce_sum.9), channel_id=1, source_target_pairs={{0,24},{1,25},{2,26},{3,27},{4,28},{5,29},{6,30},{7,31},{8,0},{9,1... | collective-permute-start | bytes 147464 | tf_op jit(solution)/shard_map/ppermute | solution.py:216
  47.4 5.7 %collective-permute-start.3 = (f32[96,128]{1,0:T(8,128)S(1)}, f32[96,128]{1,0:T(8,128)S(1)}, u32[]{:S(2)}, u32[]{:S(2)}) collective-permute-start(f32[96,128]{1,0:T(8,128)S(1)} %reduce_sum.9), channel_id=1, source_target_pairs={{0,16},{1,17},{2,18},{3,19},{4,20},{5,21},{6,22},{7,23},{8,24},{9,... | collective-permute-start | bytes 147464 | tf_op jit(solution)/shard_map/ppermute | solution.py:216
  47.9 5.9 %collective-permute-start.2 = (f32[96,128]{1,0:T(8,128)S(1)}, f32[96,128]{1,0:T(8,128)S(1)}, u32[]{:S(2)}, u32[]{:S(2)}) collective-permute-start(f32[96,128]{1,0:T(8,128)S(1)} %reduce_sum.9), channel_id=1, source_target_pairs={{0,8},{1,9},{2,10},{3,11},{4,12},{5,13},{6,14},{7,15},{8,16},{9,17... | collective-permute-start | bytes 147464 | tf_op jit(solution)/shard_map/ppermute | solution.py:216

commit v3 on v2

--- a/solution.py
+++ b/solution.py
@@ -80,15 +80,43 @@
     out_ref[...] = out + jnp.dot(pick, high, preferred_element_type=F32)
 
 
-def image_kernel(field_ref, start_ref, out_ref):
+def bit_place(order):
+    index = 0
+    for axis, mask in order:
+        index = index * 2 + lax.rem(lax.div(lax.axis_index(axis), mask), 2)
+    return index
+
+
+def image_kernel(orders, field_ref, start_ref, *refs):
+    outs, image_scr = refs[:-1], refs[-1]
+    length = field_ref.shape[0]
     field = halves(field_ref[...])
     mixed = dot3(field, halves(start_ref[...]), ((0,), (0,)))
-    out_ref[...] = dot3(field, halves(mixed), ((1,), (0,)))
-
-
-def factor_kernel(field_ref, image_ref, out_ref, work, line_scr):
-    rank = out_ref.shape[0]
-    image = halves(image_ref[...])
+    image_scr[...] = dot3(field, halves(mixed), ((1,), (0,)))
+    share = length // len(orders)
+    for chain, order in enumerate(orders):
+        count = 2 ** len(order)
+        rows = share // count
+        mine = bit_place(order)
+        for step in range(count):
+            at = pl.multiple_of(chain * share + (mine ^ step) * rows, rows)
+            half, place = divmod(step, count // 2)
+            outs[2 * chain + half][place * rows : (place + 1) * rows, :] = image_scr[pl.ds(at, rows), :]
+
+
+def factor_kernel(orders, field_ref, *refs):
+    parts, out_ref, image_scr, work, line_scr = refs[:-4], refs[-4], refs[-3], refs[-2], refs[-1]
+    length, rank = image_scr.shape
+    share = length // len(orders)
+    for chain, order in enumerate(orders):
+        count = 2 ** len(order)
+        rows = share // count
+        mine = bit_place(order)
+        for step in range(count):
+            at = pl.multiple_of(chain * share + (mine ^ step) * rows, rows)
+            half, place = divmod(step, count // 2)
+            image_scr[pl.ds(at, rows), :] = parts[2 * chain + half][place * rows : (place + 1) * rows, :]
+    image = halves(image_scr[...])
     work[:, :rank] = dot3(image, image, ((0,), (0,)))
     work[:, rank:] = dot3(image, halves(field_ref[...]), ((0,), (0,)))
     shape = (1, rank)
@@ -127,13 +155,16 @@
             work[after:, :] = work[after:, :] - drop[after:, :]
 
 
-def pairs_by(sizes, move):
-    owners, planes = sizes
+def swapped(value, bit):
+    axis, mask = bit
+    return lax.ppermute(value, axis, [(i, i ^ mask) for i in range(lax.axis_size(axis))])
+
+
+def masks(axis, low, high):
     out = []
-    for fib in range(owners):
-        for pln in range(planes):
-            to_fib, to_pln = move(fib, pln)
-            out.append((fib * planes + pln, to_fib * planes + to_pln))
+    while low < high:
+        out.append((axis, low))
+        low *= 2
     return out
 
 
@@ -142,8 +173,6 @@
     table = jnp.transpose(count_table, (2, 0, 1))
     owners = lax.axis_size("fib")
     planes = lax.axis_size("pln")
-    sizes = (owners, planes)
-    both = ("fib", "pln")
     window = table.shape[0]
     capacity = nodes.shape[0] // window
     points = interp_matrix.shape[1]
@@ -186,47 +215,56 @@
     field = field.reshape(length, tile)
 
     inner = 4
-    group = inner * planes
-    rows = length // group
-    planes_of = [
-        [
-            (base + i // planes) * planes + i % planes
-            for i in range(group)
-        ]
-        for base in range(0, owners, inner)
-    ]
-
-    def plane_exchange(value):
-        return lax.all_to_all(
-            value, both, split_axis=0, concat_axis=0, axis_index_groups=planes_of, tiled=True
-        )
-
-    image = pl.pallas_call(
-        image_kernel,
-        out_shape=jax.ShapeDtypeStruct((length, rank), F32),
+    near = masks("fib", 1, inner)
+    across = masks("pln", 1, planes)
+    far = masks("fib", inner, owners)
+    orders = [near + across, near[:1] + across + near[1:]]
+    if length % (16 * inner * planes) != 0:
+        orders = orders[:1]
+    half = jax.ShapeDtypeStruct((length // len(orders) // 2, rank), F32)
+    halves_out = pl.pallas_call(
+        functools.partial(image_kernel, orders),
+        out_shape=[half] * (2 * len(orders)),
         in_specs=[VMEM] * 2,
-        out_specs=VMEM,
+        out_specs=[VMEM] * (2 * len(orders)),
+        scratch_shapes=[pltpu.VMEM((length, rank), F32)],
         compiler_params=BIG,
         name="image",
     )(field, start_basis)
-    own_sum = jnp.sum(plane_exchange(image).reshape(group, rows, rank), axis=0)
-    total = own_sum
-    for step in range(1, owners // inner):
-        moves = pairs_by(sizes, lambda fib, pln: ((fib + step * inner) % owners, pln))
-        total = total + lax.ppermute(own_sum, both, moves)
-    image = plane_exchange(jnp.tile(total, (group, 1)))
+    keep = list(halves_out[0::2])
+    send = list(halves_out[1::2])
+    chains = range(len(orders))
+    depth = len(orders[0])
+    for level in range(depth):
+        got = [swapped(send[c], orders[c][level]) for c in chains]
+        for c in chains:
+            total = keep[c] + got[c]
+            if level + 1 < depth:
+                middle = total.shape[0] // 2
+                keep[c], send[c] = total[:middle], total[middle:]
+            else:
+                keep[c] = total
+    for bit in far:
+        got = [swapped(keep[c], bit) for c in chains]
+        keep = [keep[c] + got[c] for c in chains]
+    for level in range(depth - 1, -1, -1):
+        got = [swapped(keep[c], orders[c][level]) for c in chains]
+        if level:
+            keep = [jnp.concatenate([keep[c], got[c]], axis=0) for c in chains]
+    parts = [part for c in chains for part in (keep[c], got[c])]
     core_values = pl.pallas_call(
-        factor_kernel,
+        functools.partial(factor_kernel, orders),
         out_shape=jax.ShapeDtypeStruct((rank, tile), F32),
-        in_specs=[VMEM] * 2,
+        in_specs=[VMEM] * (1 + len(parts)),
         out_specs=VMEM,
         scratch_shapes=[
+            pltpu.VMEM((length, rank), F32),
             pltpu.VMEM((rank, rank + tile), F32),
             pltpu.VMEM((SLAB, rank + tile), F32),
         ],
         compiler_params=BIG,
         name="factor",
-    )(field, image)
+    )(field, *parts)
     return core_values[None, None]
 
 

time: 70.5 us -> 70.5 us (level)
  blocking collectives: 36.8 us -> 16.3 us
  starting transfers between devices: 6.85 us -> 17.4 us
  waiting for transfers between devices: 12.7 us -> 22.6 us
    all_to_all x2 -> x0, blocking collectives: 20.5 us -> none  [plane_exchange(): lax.all_to_all(value, both, split_axis=0, concat_axis=0, axis_index_group...]
    ppermute x3 -> x16, starting transfers between devices: 3.79 us -> 14.3 us  [swapped(): lax.ppermute(value, axis, [(i, i ^ mask) for i in range(lax.axis_size(axi...]
    ppermute x3 -> x16, waiting for transfers between devices: 4.85 us -> 14.8 us  [swapped(): lax.ppermute(value, axis, [(i, i ^ mask) for i in range(lax.axis_size(axi...]
  transfers between devices with their start and end apart: 5 -> 18, of which waited for: 5 -> 14; matrix products, arithmetic and copies ran while one was open for 0% -> 0% of each run, Pallas kernels for 1% -> 1%
where the time goes in v3:
time: 70.5 us; the launch traced here: 70.3 us
  waiting for transfers between devices  22.6 us (32%)
  starting transfers between devices  17.4 us (25%)
  blocking collectives  16.3 us (23%)
  Pallas kernels  10.2 us (14%)
  local copies, waits for them, and re-layouts  3.59 us (5%)
    all_to_all x1, blocking collectives, per_device(): lax.all_to_all(brick, 'fib', split_axis=0, concat_axis=0, tiled=True)  16.3 us
    ppermute x16, waiting for transfers between devices, swapped(): lax.ppermute(value, axis, [(i, i ^ mask) for i in range(lax.axis_size(axi...  14.8 us
    ppermute x16, starting transfers between devices, swapped(): lax.ppermute(value, axis, [(i, i ^ mask) for i in range(lax.axis_size(axi...  14.3 us
    ppermute x2, waiting for transfers between devices, per_device(): lax.ppermute(pieces[d], 'fib', [(i, (i + d) % owners) for i in range(owne...  7.84 us
    pallas_call x1, Pallas kernels, per_device(): pl.pallas_call(functools.partial(factor_kernel, orders), out_shape=jax.Sh...  6.22 us
    unnamed x10, local copies, waits for them, and re-layouts  3.55 us
    ppermute x2, starting transfers between devices, per_device(): lax.ppermute(pieces[d], 'fib', [(i, (i + d) % owners) for i in range(owne...  3.06 us
    pallas_call x1, Pallas kernels, per_device(): pl.pallas_call(functools.partial(interp_kernel, owners), out_shape=[piece...  1.8 us
  transfers between devices with their start and end apart: 18, of which 14 were waited for; matrix products, arithmetic and copies ran while one was open for 0% of the time, Pallas kernels for 1%

profile of v3, /device:TPU:0, one launch (start us, length us, event | category | flops | bytes accessed | tf_op | source)
XLA Modules:
  0.0 70.3 jit_solution(1141716098443946784)
XLA Ops:
  0.0 0.0 copy-start.4
  0.0 0.0 copy-start
  0.0 1.6 %copy-done = f32[1000,512]{1,0:T(8,128)S(1)} copy-done((f32[1000,512]{1,0:T(8,128)S(1)}, f32[1000,512]{1,0:T(8,128)}, u32[]{:S(2)}) %copy-start) | copy-done | bytes 2048024
  1.6 0.0 copy-start.1
  1.6 1.3 %copy-done.1 = f32[1,1,288,1000]{3,2,1,0:T(8,128)S(1)} copy-done((f32[1,1,288,1000]{3,2,1,0:T(8,128)S(1)}, f32[1,1,288,1000]{3,2,1,0:T(8,128)}, u32[]{:S(2)}) %copy-start.1) | copy-done | bytes 1152024
  2.9 0.0 copy-start.3
  2.9 0.7 copy-done.3
  3.5 1.8 %interp.1 = (f32[96,512]{1,0:T(8,128)S(1)}, f32[96,512]{1,0:T(8,128)S(1)}, f32[96,512]{1,0:T(8,128)S(1)}) custom-call(s32[3,1,16]{2,1,0:T(1,128)S(1)} %bitcast.8, f32[288,1000]{1,0:T(8,128)S(1)} %bitcast.7, f32[1000,512]{1,0:T(8,128)S(1)} %copy-done), custom_call_target="tpu_custom_call" | custom-call | tf_op jit(solution)/shard_map/interp/pallas_call | solution.py:184
  5.4 0.0 copy-start.2
  5.4 0.5 collective-permute-start
  5.9 2.6 %collective-permute-start.1 = (f32[96,512]{1,0:T(8,128)S(1)}, f32[96,512]{1,0:T(8,128)S(1)}, u32[]{:S(2)}, u32[]{:S(2)}) collective-permute-start(f32[96,512]{1,0:T(8,128)S(1)} %get-tuple-element.14), channel_id=1, source_target_pairs={{0,4},{2,6},{4,8},{6,10},{8,12},{10,14},{12,16},{14,18},{16,20},{1... | collective-permute-start | bytes 589832 | tf_op jit(solution)/shard_map/ppermute | solution.py:194
  8.4 0.0 copy-done.4
  8.4 0.9 %pick.1.pick_ref = f32[192,288]{1,0:T(8,128)S(1)} custom-call(s32[3,1,16]{2,1,0:T(1,128)S(1)} %bitcast.9, s32[1,192]{1,0:T(1,128)S(1)} %bitcast.10), custom_call_target="tpu_custom_call" | custom-call | tf_op jit(solution)/shard_map/pick/pallas_call | solution.py:197
  9.4 6.0 %collective-permute-done.refs_1_ = f32[96,512]{1,0:T(8,128)S(1)} collective-permute-done((f32[96,512]{1,0:T(8,128)S(1)}, f32[96,512]{1,0:T(8,128)S(1)}, u32[]{:S(2)}, u32[]{:S(2)}) %collective-permute-start) | collective-permute-done | bytes 196640 | tf_op jit(solution)/shard_map/ppermute | solution.py:194
  15.4 1.8 %collective-permute-done.1.refs_2_ = f32[96,512]{1,0:T(8,128)S(1)} collective-permute-done((f32[96,512]{1,0:T(8,128)S(1)}, f32[96,512]{1,0:T(8,128)S(1)}, u32[]{:S(2)}, u32[]{:S(2)}) %collective-permute-start.1) | collective-permute-done | bytes 196640 | tf_op jit(solution)/shard_map/ppermute | solution.py:194
  17.2 0.5 order.1
  17.8 16.3 %all_to_all.5 = f32[16,48,128]{2,1,0:T(8,128)S(1)} all-to-all(f32[16,48,128]{2,1,0:T(8,128)S(1)} %reshape.6), channel_id=1, replica_groups=mesh['fib'=16,'pln'=2] {'fib'}, dimensions={0} | all-to-all | bytes 786432 | tf_op jit(solution)/shard_map/all_to_all | solution.py:214
  34.1 0.0 copy-done.2
  34.1 0.7 %image.1 = (f32[192,128]{1,0:T(8,128)S(1)}, f32[192,128]{1,0:T(8,128)S(1)}, f32[192,128]{1,0:T(8,128)S(1)}, f32[192,128]{1,0:T(8,128)S(1)}) custom-call(f32[768,128]{1,0:T(8,128)S(1)} %bitcast.5, f32[768,128]{1,0:T(8,128)S(1)} %copy-done.2), custom_call_target="tpu_custom_call" | custom-call | tf_op jit(solution)/shard_map/image/pallas_call | solution.py:225
  34.8 0.2 collective-permute-start.2
  35.0 0.4 collective-permute-start.10
  35.4 0.8 %collective-permute-done.2 = f32[192,128]{1,0:T(8,128)S(1)} collective-permute-done((f32[192,128]{1,0:T(8,128)S(1)}, f32[192,128]{1,0:T(8,128)S(1)}, u32[]{:S(2)}, u32[]{:S(2)}) %collective-permute-start.2) | collective-permute-done | bytes 98336 | tf_op jit(solution)/shard_map/ppermute | solution.py:160
  36.2 0.7 collective-permute-start.3
  36.9 0.0 collective-permute-done.10
  36.9 1.6 %collective-permute-start.11 = (f32[96,128]{1,0:T(8,128)S(1)}, f32[96,128]{1,0:T(8,128)S(1)}, u32[]{:S(2)}, u32[]{:S(2)}) collective-permute-start(f32[96,128]{1,0:T(8,128)S(1)} %slice.37), channel_id=1, source_target_pairs={{0,1},{1,0},{2,3},{3,2},{4,5},{5,4},{6,7},{7,6},{8,9},{9,8},{10,11... | collective-permute-start | bytes 147464 | tf_op jit(solution)/shard_map/ppermute | solution.py:160
  38.5 1.9 %collective-permute-done.3 = f32[96,128]{1,0:T(8,128)S(1)} collective-permute-done((f32[96,128]{1,0:T(8,128)S(1)}, f32[96,128]{1,0:T(8,128)S(1)}, u32[]{:S(2)}, u32[]{:S(2)}) %collective-permute-start.3) | collective-permute-done | bytes 49184 | tf_op jit(solution)/shard_map/ppermute | solution.py:160
  40.4 1.6 %collective-permute-start.4 = (f32[48,128]{1,0:T(8,128)S(1)}, f32[48,128]{1,0:T(8,128)S(1)}, u32[]{:S(2)}, u32[]{:S(2)}) collective-permute-start(f32[48,128]{1,0:T(8,128)S(1)} %slice.35), channel_id=1, source_target_pairs={{0,1},{1,0},{2,3},{3,2},{4,5},{5,4},{6,7},{7,6},{8,9},{9,8},{10,11... | collective-permute-start | bytes 73736 | tf_op jit(solution)/shard_map/ppermute | solution.py:160
  42.0 0.0 collective-permute-done.11
  42.0 0.7 collective-permute-start.12
  42.7 1.6 %collective-permute-done.4 = f32[48,128]{1,0:T(8,128)S(1)} collective-permute-done((f32[48,128]{1,0:T(8,128)S(1)}, f32[48,128]{1,0:T(8,128)S(1)}, u32[]{:S(2)}, u32[]{:S(2)}) %collective-permute-start.4) | collective-permute-done | bytes 24608 | tf_op jit(solution)/shard_map/ppermute | solution.py:160
  44.3 0.9 %collective-permute-start.5 = (f32[48,128]{1,0:T(8,128)S(1)}, f32[48,128]{1,0:T(8,128)S(1)}, u32[]{:S(2)}, u32[]{:S(2)}) collective-permute-start(f32[48,128]{1,0:T(8,128)S(1)} %slice_add_fusion.3), channel_id=1, source_target_pairs={{0,8},{2,10},{4,12},{6,14},{8,0},{10,2},{12,4},{14,6},{16,24},{18,... | collective-permute-start | bytes 73736 | tf_op jit(solution)/shard_map/ppermute | solution.py:160
  45.2 0.7 collective-permute-done.12
  45.9 0.9 %collective-permute-start.13 = (f32[48,128]{1,0:T(8,128)S(1)}, f32[48,128]{1,0:T(8,128)S(1)}, u32[]{:S(2)}, u32[]{:S(2)}) collective-permute-start(f32[48,128]{1,0:T(8,128)S(1)} %slice_add_fusion.2), channel_id=1, source_target_pairs={{0,8},{2,10},{4,12},{6,14},{8,0},{10,2},{12,4},{14,6},{16,24},{18,... | collective-permute-start | bytes 73736 | tf_op jit(solution)/shard_map/ppermute | solution.py:160
  46.8 1.3 %collective-permute-done.5 = f32[48,128]{1,0:T(8,128)S(1)} collective-permute-done((f32[48,128]{1,0:T(8,128)S(1)}, f32[48,128]{1,0:T(8,128)S(1)}, u32[]{:S(2)}, u32[]{:S(2)}) %collective-permute-start.5) | collective-permute-done | bytes 24608 | tf_op jit(solution)/shard_map/ppermute | solution.py:160
  48.1 1.9 %collective-permute-start.6 = (f32[48,128]{1,0:T(8,128)S(1)}, f32[48,128]{1,0:T(8,128)S(1)}, u32[]{:S(2)}, u32[]{:S(2)}) collective-permute-start(f32[48,128]{1,0:T(8,128)S(1)} %add.33), channel_id=1, source_target_pairs={{0,16},{2,18},{4,20},{6,22},{8,24},{10,26},{12,28},{14,30},{16,0},... | collective-permute-start | bytes 73736 | tf_op jit(solution)/shard_map/ppermute | solution.py:160
  50.0 0.0 collective-permute-done.13
  50.0 1.5 %collective-permute-start.14 = (f32[48,128]{1,0:T(8,128)S(1)}, f32[48,128]{1,0:T(8,128)S(1)}, u32[]{:S(2)}, u32[]{:S(2)}) collective-permute-start(f32[48,128]{1,0:T(8,128)S(1)} %add.38), channel_id=1, source_target_pairs={{0,16},{2,18},{4,20},{6,22},{8,24},{10,26},{12,28},{14,30},{16,0},... | collective-permute-start | bytes 73736 | tf_op jit(solution)/shard_map/ppermute | solution.py:160
  51.4 1.4 %collective-permute-done.6 = f32[48,128]{1,0:T(8,128)S(1)} collective-permute-done((f32[48,128]{1,0:T(8,128)S(1)}, f32[48,128]{1,0:T(8,128)S(1)}, u32[]{:S(2)}, u32[]{:S(2)}) %collective-permute-start.6) | collective-permute-done | bytes 24608 | tf_op jit(solution)/shard_map/ppermute | solution.py:160
  52.9 1.5 %collective-permute-start.7 = (f32[48,128]{1,0:T(8,128)S(1)}, f32[48,128]{1,0:T(8,128)S(1)}, u32[]{:S(2)}, u32[]{:S(2)}) collective-permute-start(f32[48,128]{1,0:T(8,128)S(1)} %add.34), channel_id=1, source_target_pairs={{0,1},{1,0},{2,3},{3,2},{4,5},{5,4},{6,7},{7,6},{8,9},{9,8},{10,11... | collective-permute-start | bytes 73736 | tf_op jit(solution)/shard_map/ppermute | solution.py:160
  54.4 0.4 collective-permute-done.14
  54.8 0.3 collective-permute-start.15
  55.1 1.6 %collective-permute-done.7 = f32[48,128]{1,0:T(8,128)S(1)} collective-permute-done((f32[48,128]{1,0:T(8,128)S(1)}, f32[48,128]{1,0:T(8,128)S(1)}, u32[]{:S(2)}, u32[]{:S(2)}) %collective-permute-start.7) | collective-permute-done | bytes 24608 | tf_op jit(solution)/shard_map/ppermute | solution.py:160
  56.7 0.6 collective-permute-start.8
  57.3 1.3 %collective-permute-done.15 = f32[48,128]{1,0:T(8,128)S(1)} collective-permute-done((f32[48,128]{1,0:T(8,128)S(1)}, f32[48,128]{1,0:T(8,128)S(1)}, u32[]{:S(2)}, u32[]{:S(2)}) %collective-permute-start.15) | collective-permute-done | bytes 24608 | tf_op jit(solution)/shard_map/ppermute | solution.py:160
  58.6 1.5 %collective-permute-start.16 = (f32[96,128]{1,0:T(8,128)S(1)}, f32[96,128]{1,0:T(8,128)S(1)}, u32[]{:S(2)}, u32[]{:S(2)}) collective-permute-start(f32[96,128]{1,0:T(8,128)S(1)} %pad_maximum_fusion.3), channel_id=1, source_target_pairs={{0,1},{1,0},{2,3},{3,2},{4,5},{5,4},{6,7},{7,6},{8,9},{9,8},{10,11... | collective-permute-start | bytes 147464 | tf_op jit(solution)/shard_map/ppermute | solution.py:160
  60.1 0.7 collective-permute-done.8
  60.8 0.1 collective-permute-start.9
  60.9 1.9 %collective-permute-done.16 = f32[96,128]{1,0:T(8,128)S(1)} collective-permute-done((f32[96,128]{1,0:T(8,128)S(1)}, f32[96,128]{1,0:T(8,128)S(1)}, u32[]{:S(2)}, u32[]{:S(2)}) %collective-permute-start.16) | collective-permute-done | bytes 49184 | tf_op jit(solution)/shard_map/ppermute | solution.py:160
  62.7 0.1 collective-permute-start.17
  62.8 0.0 collective-permute-done.9.refs_1_
  62.8 1.3 %collective-permute-done.17.refs_3_ = f32[192,128]{1,0:T(8,128)S(1)} collective-permute-done((f32[192,128]{1,0:T(8,128)S(1)}, f32[192,128]{1,0:T(8,128)S(1)}, u32[]{:S(2)}, u32[]{:S(2)}) %collective-permute-start.17) | collective-permute-done | bytes 98336 | tf_op jit(solution)/shard_map/ppermute | solution.py:160
  64.1 6.2 %factor.1 = f32[128,128]{1,0:T(8,128)} custom-call(f32[768,128]{1,0:T(8,128)S(1)} %bitcast.6, f32[192,128]{1,0:T(8,128)S(1)} %pad_maximum_fusion.refs_0_, f32[192,128]{1,0:T(8,128)S(1)} %collective-permute-done.9.refs_1_, f32[192,128]{1,0:T(8,128)S(1)} %pad_maximum_fusion.1.refs_2_, f32[192,128]{1,0:T(8,128)S(1)} %collective-permute-done.17.refs_3_), custom_call_target="tpu_custom_call" | custom-call | tf_op jit(solution)/shard_map/factor/pallas_call | solution.py:255
  (19 shorter events, 0.1 us)
Async XLA Ops:
  0.0 8.4 %copy-start.4 = (s32[1,1,192]{2,1,0:T(1,128)S(1)}, s32[1,1,192]{2,1,0:T(1,128)}, u32[]{:S(2)}) copy-start(s32[1,1,192]{2,1,0:T(1,128)} %param.8) | copy-start | bytes 2308
  0.0 1.6 %copy-start = (f32[1000,512]{1,0:T(8,128)S(1)}, f32[1000,512]{1,0:T(8,128)}, u32[]{:S(2)}) copy-start(f32[1000,512]{1,0:T(8,128)} %interp_ref.1) | copy-start | bytes 6144004
  1.6 1.3 %copy-start.1 = (f32[1,1,288,1000]{3,2,1,0:T(8,128)S(1)}, f32[1,1,288,1000]{3,2,1,0:T(8,128)}, u32[]{:S(2)}) copy-start(f32[1,1,288,1000]{3,2,1,0:T(8,128)} %param.5) | copy-start | bytes 3456004
  2.9 0.7 copy-start.3
  5.4 28.7 %copy-start.2 = (f32[768,128]{1,0:T(8,128)S(1)}, f32[768,128]{1,0:T(8,128)}, u32[]{:S(2)}) copy-start(f32[768,128]{1,0:T(8,128)} %start_ref.1) | copy-start | bytes 1179652
  5.4 10.0 %collective-permute-start = (f32[96,512]{1,0:T(8,128)S(1)}, f32[96,512]{1,0:T(8,128)S(1)}, u32[]{:S(2)}, u32[]{:S(2)}) collective-permute-start(f32[96,512]{1,0:T(8,128)S(1)} %get-tuple-element.13), channel_id=1, source_target_pairs={{0,2},{2,4},{4,6},{6,8},{8,10},{10,12},{12,14},{14,16},{16,18},{18... | collective-permute-start | bytes 589832 | tf_op jit(solution)/shard_map/ppermute | solution.py:194
  5.9 11.3 %collective-permute-start.1 = (f32[96,512]{1,0:T(8,128)S(1)}, f32[96,512]{1,0:T(8,128)S(1)}, u32[]{:S(2)}, u32[]{:S(2)}) collective-permute-start(f32[96,512]{1,0:T(8,128)S(1)} %get-tuple-element.14), channel_id=1, source_target_pairs={{0,4},{2,6},{4,8},{6,10},{8,12},{10,14},{12,16},{14,18},{16,20},{1... | collective-permute-start | bytes 589832 | tf_op jit(solution)/shard_map/ppermute | solution.py:194
  34.8 1.4 %collective-permute-start.2 = (f32[192,128]{1,0:T(8,128)S(1)}, f32[192,128]{1,0:T(8,128)S(1)}, u32[]{:S(2)}, u32[]{:S(2)}) collective-permute-start(f32[192,128]{1,0:T(8,128)S(1)} %get-tuple-element.16), channel_id=1, source_target_pairs={{0,2},{2,0},{4,6},{6,4},{8,10},{10,8},{12,14},{14,12},{16,18},{18,... | collective-permute-start | bytes 294920 | tf_op jit(solution)/shard_map/ppermute | solution.py:160
  35.0 1.9 %collective-permute-start.10 = (f32[192,128]{1,0:T(8,128)S(1)}, f32[192,128]{1,0:T(8,128)S(1)}, u32[]{:S(2)}, u32[]{:S(2)}) collective-permute-start(f32[192,128]{1,0:T(8,128)S(1)} %get-tuple-element.18), channel_id=1, source_target_pairs={{0,2},{2,0},{4,6},{6,4},{8,10},{10,8},{12,14},{14,12},{16,18},{18,... | collective-permute-start | bytes 294920 | tf_op jit(solution)/shard_map/ppermute | solution.py:160
  36.2 4.2 %collective-permute-start.3 = (f32[96,128]{1,0:T(8,128)S(1)}, f32[96,128]{1,0:T(8,128)S(1)}, u32[]{:S(2)}, u32[]{:S(2)}) collective-permute-start(f32[96,128]{1,0:T(8,128)S(1)} %slice.33), channel_id=1, source_target_pairs={{0,4},{2,6},{4,0},{6,2},{8,12},{10,14},{12,8},{14,10},{16,20},{18,... | collective-permute-start | bytes 147464 | tf_op jit(solution)/shard_map/ppermute | solution.py:160
  36.9 5.0 %collective-permute-start.11 = (f32[96,128]{1,0:T(8,128)S(1)}, f32[96,128]{1,0:T(8,128)S(1)}, u32[]{:S(2)}, u32[]{:S(2)}) collective-permute-start(f32[96,128]{1,0:T(8,128)S(1)} %slice.37), channel_id=1, source_target_pairs={{0,1},{1,0},{2,3},{3,2},{4,5},{5,4},{6,7},{7,6},{8,9},{9,8},{10,11... | collective-permute-start | bytes 147464 | tf_op jit(solution)/shard_map/ppermute | solution.py:160
  40.4 3.9 %collective-permute-start.4 = (f32[48,128]{1,0:T(8,128)S(1)}, f32[48,128]{1,0:T(8,128)S(1)}, u32[]{:S(2)}, u32[]{:S(2)}) collective-permute-start(f32[48,128]{1,0:T(8,128)S(1)} %slice.35), channel_id=1, source_target_pairs={{0,1},{1,0},{2,3},{3,2},{4,5},{5,4},{6,7},{7,6},{8,9},{9,8},{10,11... | collective-permute-start | bytes 73736 | tf_op jit(solution)/shard_map/ppermute | solution.py:160
  42.0 3.9 %collective-permute-start.12 = (f32[48,128]{1,0:T(8,128)S(1)}, f32[48,128]{1,0:T(8,128)S(1)}, u32[]{:S(2)}, u32[]{:S(2)}) collective-permute-start(f32[48,128]{1,0:T(8,128)S(1)} %slice.39), channel_id=1, source_target_pairs={{0,4},{2,6},{4,0},{6,2},{8,12},{10,14},{12,8},{14,10},{16,20},{18,... | collective-permute-start | bytes 73736 | tf_op jit(solution)/shard_map/ppermute | solution.py:160
  44.3 3.8 %collective-permute-start.5 = (f32[48,128]{1,0:T(8,128)S(1)}, f32[48,128]{1,0:T(8,128)S(1)}, u32[]{:S(2)}, u32[]{:S(2)}) collective-permute-start(f32[48,128]{1,0:T(8,128)S(1)} %slice_add_fusion.3), channel_id=1, source_target_pairs={{0,8},{2,10},{4,12},{6,14},{8,0},{10,2},{12,4},{14,6},{16,24},{18,... | collective-permute-start | bytes 73736 | tf_op jit(solution)/shard_map/ppermute | solution.py:160
  45.9 4.1 %collective-permute-start.13 = (f32[48,128]{1,0:T(8,128)S(1)}, f32[48,128]{1,0:T(8,128)S(1)}, u32[]{:S(2)}, u32[]{:S(2)}) collective-permute-start(f32[48,128]{1,0:T(8,128)S(1)} %slice_add_fusion.2), channel_id=1, source_target_pairs={{0,8},{2,10},{4,12},{6,14},{8,0},{10,2},{12,4},{14,6},{16,24},{18,... | collective-permute-start | bytes 73736 | tf_op jit(solution)/shard_map/ppermute | solution.py:160
  48.1 4.7 %collective-permute-start.6 = (f32[48,128]{1,0:T(8,128)S(1)}, f32[48,128]{1,0:T(8,128)S(1)}, u32[]{:S(2)}, u32[]{:S(2)}) collective-permute-start(f32[48,128]{1,0:T(8,128)S(1)} %add.33), channel_id=1, source_target_pairs={{0,16},{2,18},{4,20},{6,22},{8,24},{10,26},{12,28},{14,30},{16,0},... | collective-permute-start | bytes 73736 | tf_op jit(solution)/shard_map/ppermute | solution.py:160
  50.0 4.8 %collective-permute-start.14 = (f32[48,128]{1,0:T(8,128)S(1)}, f32[48,128]{1,0:T(8,128)S(1)}, u32[]{:S(2)}, u32[]{:S(2)}) collective-permute-start(f32[48,128]{1,0:T(8,128)S(1)} %add.38), channel_id=1, source_target_pairs={{0,16},{2,18},{4,20},{6,22},{8,24},{10,26},{12,28},{14,30},{16,0},... | collective-permute-start | bytes 73736 | tf_op jit(solution)/shard_map/ppermute | solution.py:160
  52.9 3.8 %collective-permute-start.7 = (f32[48,128]{1,0:T(8,128)S(1)}, f32[48,128]{1,0:T(8,128)S(1)}, u32[]{:S(2)}, u32[]{:S(2)}) collective-permute-start(f32[48,128]{1,0:T(8,128)S(1)} %add.34), channel_id=1, source_target_pairs={{0,1},{1,0},{2,3},{3,2},{4,5},{5,4},{6,7},{7,6},{8,9},{9,8},{10,11... | collective-permute-start | bytes 73736 | tf_op jit(solution)/shard_map/ppermute | solution.py:160
  54.8 3.8 %collective-permute-start.15 = (f32[48,128]{1,0:T(8,128)S(1)}, f32[48,128]{1,0:T(8,128)S(1)}, u32[]{:S(2)}, u32[]{:S(2)}) collective-permute-start(f32[48,128]{1,0:T(8,128)S(1)} %add.39), channel_id=1, source_target_pairs={{0,4},{2,6},{4,0},{6,2},{8,12},{10,14},{12,8},{14,10},{16,20},{18,... | collective-permute-start | bytes 73736 | tf_op jit(solution)/shard_map/ppermute | solution.py:160
  56.7 4.1 %collective-permute-start.8 = (f32[96,128]{1,0:T(8,128)S(1)}, f32[96,128]{1,0:T(8,128)S(1)}, u32[]{:S(2)}, u32[]{:S(2)}) collective-permute-start(f32[96,128]{1,0:T(8,128)S(1)} %pad_maximum_fusion.2), channel_id=1, source_target_pairs={{0,4},{2,6},{4,0},{6,2},{8,12},{10,14},{12,8},{14,10},{16,20},{18,... | collective-permute-start | bytes 147464 | tf_op jit(solution)/shard_map/ppermute | solution.py:160
  58.6 4.1 %collective-permute-start.16 = (f32[96,128]{1,0:T(8,128)S(1)}, f32[96,128]{1,0:T(8,128)S(1)}, u32[]{:S(2)}, u32[]{:S(2)}) collective-permute-start(f32[96,128]{1,0:T(8,128)S(1)} %pad_maximum_fusion.3), channel_id=1, source_target_pairs={{0,1},{1,0},{2,3},{3,2},{4,5},{5,4},{6,7},{7,6},{8,9},{9,8},{10,11... | collective-permute-start | bytes 147464 | tf_op jit(solution)/shard_map/ppermute | solution.py:160
  60.8 2.0 %collective-permute-start.9 = (f32[192,128]{1,0:T(8,128)S(1)}, f32[192,128]{1,0:T(8,128)S(1)}, u32[]{:S(2)}, u32[]{:S(2)}) collective-permute-start(f32[192,128]{1,0:T(8,128)S(1)} %pad_maximum_fusion.refs_0_), channel_id=1, source_target_pairs={{0,2},{2,0},{4,6},{6,4},{8,10},{10,8},{12,14},{14,12},{16,18},{18,... | collective-permute-start | bytes 294920 | tf_op jit(solution)/shard_map/ppermute | solution.py:160
  62.7 1.4 %collective-permute-start.17 = (f32[192,128]{1,0:T(8,128)S(1)}, f32[192,128]{1,0:T(8,128)S(1)}, u32[]{:S(2)}, u32[]{:S(2)}) collective-permute-start(f32[192,128]{1,0:T(8,128)S(1)} %pad_maximum_fusion.1.refs_2_), channel_id=1, source_target_pairs={{0,2},{2,0},{4,6},{6,4},{8,10},{10,8},{12,14},{14,12},{16,18},{18,... | collective-permute-start | bytes 294920 | tf_op jit(solution)/shard_map/ppermute | solution.py:160

commit v4 on v2

--- a/solution.py
+++ b/solution.py
@@ -46,7 +46,7 @@
         start = start + table_ref[distance, 0, lax.rem(own + distance, owners)]
 
 
-def pick_kernel(rows, table_ref, order_ref, out_ref):
+def pick_kernel(rows, per_tile, relative, table_ref, order_ref, out_ref):
     elements, slots = out_ref.shape
     window = slots // rows
     own = lax.axis_index("fib")
@@ -59,7 +59,13 @@
         inside = (rank_at >= start) & (rank_at < start + count)
         from_slot = from_slot | (inside & (slot_at - distance * rows == rank_at - start))
         start = start + count
-    place = jnp.broadcast_to(order_ref[...], (elements, elements))
+    place = order_ref[...]
+    if relative:
+        tile = lax.div(place, jnp.full_like(place, per_tile))
+        inside = place - tile * per_tile
+        apart = tile ^ own
+        place = ((apart & 1) * (elements // per_tile // 2) + (apart >> 1)) * per_tile + inside
+    place = jnp.broadcast_to(place, (elements, elements))
     row = lax.broadcasted_iota(jnp.int32, (elements, elements), 0)
     to_place = jnp.where(place == row, 1.0, 0.0).astype(BF16)
     out_ref[...] = jnp.dot(
@@ -68,7 +74,7 @@
 
 
 def order_kernel(pick_ref, *refs):
-    pieces, out_ref = refs[:-1], refs[-1]
+    pieces, outs = refs[:-2], refs[-2:]
     pick = pick_ref[...].astype(BF16)
     line = jnp.concatenate([piece[...] for piece in pieces], axis=0)
     high = line.astype(BF16)
@@ -77,18 +83,55 @@
     low = (rest - mid.astype(F32)).astype(BF16)
     out = jnp.dot(pick, low, preferred_element_type=F32)
     out += jnp.dot(pick, mid, preferred_element_type=F32)
-    out_ref[...] = out + jnp.dot(pick, high, preferred_element_type=F32)
-
-
-def image_kernel(field_ref, start_ref, out_ref):
+    out += jnp.dot(pick, high, preferred_element_type=F32)
+    half = out.shape[0] // 2
+    outs[0][...] = out[:half]
+    outs[1][...] = out[half:]
+
+
+def bit_place(order):
+    index = 0
+    for axis, mask in order:
+        index = index * 2 + lax.rem(lax.div(lax.axis_index(axis), mask), 2)
+    return index
+
+
+def image_kernel(near, mid, blocks, *refs):
+    block_refs, start_ref, keep_ref, send_ref, field_ref, image_scr = refs[:blocks], *refs[blocks:]
+    length = field_ref.shape[0]
+    if blocks > 1:
+        own = lax.axis_index("fib")
+        each = length // (2 * blocks)
+        for step, block in enumerate(block_refs):
+            for core in range(2):
+                at = pl.multiple_of((own ^ (2 * step + core)) * each, each)
+                field_ref[pl.ds(at, each), :] = block[core * each : (core + 1) * each, :]
+    else:
+        field_ref[...] = block_refs[0][...]
     field = halves(field_ref[...])
     mixed = dot3(field, halves(start_ref[...]), ((0,), (0,)))
-    out_ref[...] = dot3(field, halves(mixed), ((1,), (0,)))
-
-
-def factor_kernel(field_ref, image_ref, out_ref, work, line_scr):
-    rank = out_ref.shape[0]
-    image = halves(image_ref[...])
+    image_scr[...] = dot3(field, halves(mixed), ((1,), (0,)))
+    count = 2 ** len(mid)
+    rows = length // (2 * count)
+    core, place = bit_place(near), bit_place(mid)
+    for step in range(count):
+        at = pl.multiple_of((core * count + (place ^ step)) * rows, rows)
+        keep_ref[step * rows : (step + 1) * rows, :] = image_scr[pl.ds(at, rows), :]
+        at = pl.multiple_of(((1 - core) * count + (place ^ step)) * rows, rows)
+        send_ref[step * rows : (step + 1) * rows, :] = image_scr[pl.ds(at, rows), :]
+
+
+def factor_kernel(near, mid, field_ref, own_ref, other_ref, out_ref, image_scr, work, line_scr):
+    length, rank = image_scr.shape
+    count = 2 ** len(mid)
+    rows = length // (2 * count)
+    core, place = bit_place(near), bit_place(mid)
+    for step in range(count):
+        at = pl.multiple_of((core * count + (place ^ step)) * rows, rows)
+        image_scr[pl.ds(at, rows), :] = own_ref[step * rows : (step + 1) * rows, :]
+        at = pl.multiple_of(((1 - core) * count + (place ^ step)) * rows, rows)
+        image_scr[pl.ds(at, rows), :] = other_ref[step * rows : (step + 1) * rows, :]
+    image = halves(image_scr[...])
     work[:, :rank] = dot3(image, image, ((0,), (0,)))
     work[:, rank:] = dot3(image, halves(field_ref[...]), ((0,), (0,)))
     shape = (1, rank)
@@ -127,13 +170,22 @@
             work[after:, :] = work[after:, :] - drop[after:, :]
 
 
-def pairs_by(sizes, move):
-    owners, planes = sizes
+def swapped(value, bits, step=1):
+    apart = [bit for at, bit in enumerate(reversed(bits)) if step >> at & 1]
+    peers = {axis: sum(mask for name, mask in apart if name == axis) for axis in ("fib", "pln")}
+    owners, planes = lax.axis_size("fib"), lax.axis_size("pln")
+    pairs = []
+    for i in range(owners * planes):
+        fib, pln = divmod(i, planes)
+        pairs.append((i, (fib ^ peers["fib"]) * planes + (pln ^ peers["pln"])))
+    return lax.ppermute(value, ("fib", "pln"), pairs)
+
+
+def masks(axis, low, high):
     out = []
-    for fib in range(owners):
-        for pln in range(planes):
-            to_fib, to_pln = move(fib, pln)
-            out.append((fib * planes + pln, to_fib * planes + to_pln))
+    while low < high:
+        out.append((axis, low))
+        low *= 2
     return out
 
 
@@ -142,8 +194,6 @@
     table = jnp.transpose(count_table, (2, 0, 1))
     owners = lax.axis_size("fib")
     planes = lax.axis_size("pln")
-    sizes = (owners, planes)
-    both = ("fib", "pln")
     window = table.shape[0]
     capacity = nodes.shape[0] // window
     points = interp_matrix.shape[1]
@@ -151,6 +201,7 @@
     length, rank = start_basis.shape
     tile = points * elements // length
     piece = jax.ShapeDtypeStruct((capacity, points), F32)
+    direct = length // owners % SLAB == 0
 
     pieces = pl.pallas_call(
         functools.partial(interp_kernel, owners),
@@ -166,7 +217,7 @@
         for d in range(1, window)
     ]
     pick = pl.pallas_call(
-        functools.partial(pick_kernel, capacity),
+        functools.partial(pick_kernel, capacity, elements // owners, direct),
         out_shape=jax.ShapeDtypeStruct((elements, capacity * window), F32),
         in_specs=[SMEM, VMEM],
         out_specs=VMEM,
@@ -175,58 +226,63 @@
     )(table, slot_order[0])
     brick = pl.pallas_call(
         order_kernel,
-        out_shape=jax.ShapeDtypeStruct((elements, points), F32),
+        out_shape=[jax.ShapeDtypeStruct((elements // 2, points), F32)] * 2,
         in_specs=[VMEM] * (1 + window),
-        out_specs=VMEM,
+        out_specs=[VMEM] * 2,
         compiler_params=BIG,
         name="order",
     )(pick, *received)
-    brick = brick.reshape(owners, length // owners, tile)
-    field = lax.all_to_all(brick, "fib", split_axis=0, concat_axis=0, tiled=True)
-    field = field.reshape(length, tile)
-
-    inner = 4
-    group = inner * planes
-    rows = length // group
-    planes_of = [
-        [
-            (base + i // planes) * planes + i % planes
-            for i in range(group)
-        ]
-        for base in range(0, owners, inner)
-    ]
-
-    def plane_exchange(value):
-        return lax.all_to_all(
-            value, both, split_axis=0, concat_axis=0, axis_index_groups=planes_of, tiled=True
-        )
-
-    image = pl.pallas_call(
-        image_kernel,
-        out_shape=jax.ShapeDtypeStruct((length, rank), F32),
-        in_specs=[VMEM] * 2,
-        out_specs=VMEM,
+    near = masks("fib", 1, 2)
+    mid = masks("fib", 2, 4) + masks("pln", 1, planes)
+    far = masks("fib", 4, owners)
+    if direct:
+        chips = masks("fib", 2, owners)[::-1]
+        blocks = owners // 2
+        shape = (blocks, length // owners, tile)
+        own, other = (half.reshape(shape) for half in brick)
+        both = jnp.concatenate([own, swapped(other, near)], axis=1)
+        order = sorted(range(1, blocks), reverse=True)
+        got = {step: swapped(both[step], chips, step) for step in order}
+        got[0] = both[0]
+        field_parts = [got[step] for step in range(blocks)]
+    else:
+        whole = jnp.concatenate(brick, axis=0).reshape(owners, length // owners, tile)
+        whole = lax.all_to_all(whole, "fib", split_axis=0, concat_axis=0, tiled=True)
+        field_parts = [whole.reshape(length, tile)]
+
+    half = jax.ShapeDtypeStruct((length // 2, rank), F32)
+    keep, send, field = pl.pallas_call(
+        functools.partial(image_kernel, near, mid, len(field_parts)),
+        out_shape=[half, half, jax.ShapeDtypeStruct((length, tile), F32)],
+        in_specs=[VMEM] * (len(field_parts) + 1),
+        out_specs=[VMEM] * 3,
+        scratch_shapes=[pltpu.VMEM((length, rank), F32)],
         compiler_params=BIG,
         name="image",
-    )(field, start_basis)
-    own_sum = jnp.sum(plane_exchange(image).reshape(group, rows, rank), axis=0)
-    total = own_sum
-    for step in range(1, owners // inner):
-        moves = pairs_by(sizes, lambda fib, pln: ((fib + step * inner) % owners, pln))
-        total = total + lax.ppermute(own_sum, both, moves)
-    image = plane_exchange(jnp.tile(total, (group, 1)))
+    )(*field_parts, start_basis)
+    count = 2 ** len(mid)
+    chunks = (keep + swapped(send, near)).reshape(count, length // (2 * count), rank)
+    total = chunks[0]
+    for got in [swapped(chunks[step], mid, step) for step in range(count - 1, 0, -1)]:
+        total = total + got
+    own = total
+    for got in [swapped(own, far, step) for step in range(2 ** len(far) - 1, 0, -1)]:
+        total = total + got
+    own = jnp.concatenate([total] + [swapped(total, mid, step) for step in range(1, count)], axis=0)
+    other = swapped(own, near)
     core_values = pl.pallas_call(
-        factor_kernel,
+        functools.partial(factor_kernel, near, mid),
         out_shape=jax.ShapeDtypeStruct((rank, tile), F32),
-        in_specs=[VMEM] * 2,
+        in_specs=[VMEM] * 3,
         out_specs=VMEM,
         scratch_shapes=[
+            pltpu.VMEM((length, rank), F32),
             pltpu.VMEM((rank, rank + tile), F32),
             pltpu.VMEM((SLAB, rank + tile), F32),
         ],
         compiler_params=BIG,
         name="factor",
-    )(field, image)
+    )(field, own, other)
     return core_values[None, None]
 
 

time: 70.5 us -> 67.2 us (0.953)
  blocking collectives: 36.8 us -> 0 us
  starting transfers between devices: 6.85 us -> 27.2 us
  waiting for transfers between devices: 12.7 us -> 25.7 us
    all_to_all x3 -> x0, blocking collectives: 36.8 us -> none  [the longest x2 20.5 us: plane_exchange(): lax.all_to_all(value, both, split_axis=0, concat_axis=0, axis_index_group...]
    ppermute x3 -> x19, starting transfers between devices: 3.79 us -> 24.1 us  [swapped(): return lax.ppermute(value, ('fib', 'pln'), pairs)]
    ppermute x3 -> x19, waiting for transfers between devices: 4.85 us -> 17.8 us  [swapped(): return lax.ppermute(value, ('fib', 'pln'), pairs)]
    unnamed x10 -> x11, local copies, waits for them, and re-layouts: 3.55 us -> 3.56 us
  transfers between devices with their start and end apart: 5 -> 21, of which waited for: 5 -> 17; matrix products, arithmetic and copies ran while one was open for 0% -> 0% of each run, Pallas kernels for 1% -> 1%
where the time goes in v4:
time: 67.2 us; the launch traced here: 67 us
  starting transfers between devices  27.2 us (40%)
  waiting for transfers between devices  25.7 us (38%)
  Pallas kernels  10.3 us (15%)
  local copies, waits for them, and re-layouts  3.65 us (5%)
    ppermute x19, starting transfers between devices, swapped(): return lax.ppermute(value, ('fib', 'pln'), pairs)  24.1 us
    ppermute x19, waiting for transfers between devices, swapped(): return lax.ppermute(value, ('fib', 'pln'), pairs)  17.8 us
    ppermute x2, waiting for transfers between devices, per_device(): lax.ppermute(pieces[d], 'fib', [(i, (i + d) % owners) for i in range(owne...  7.84 us
    pallas_call x1, Pallas kernels, per_device(): pl.pallas_call(functools.partial(factor_kernel, near, mid), out_shape=jax...  6.22 us
    unnamed x11, local copies, waits for them, and re-layouts  3.56 us
    ppermute x2, starting transfers between devices, per_device(): lax.ppermute(pieces[d], 'fib', [(i, (i + d) % owners) for i in range(owne...  3.06 us
    pallas_call x1, Pallas kernels, per_device(): pl.pallas_call(functools.partial(interp_kernel, owners), out_shape=[piece...  1.8 us
  transfers between devices with their start and end apart: 21, of which 17 were waited for; matrix products, arithmetic and copies ran while one was open for 0% of the time, Pallas kernels for 1%

profile of v4, /device:TPU:0, one launch (start us, length us, event | category | flops | bytes accessed | tf_op | source)
XLA Modules:
  0.0 67.0 jit_solution(10604054595339636912)
XLA Ops:
  0.0 0.0 copy-start.4
  0.0 0.0 copy-start
  0.0 1.6 %copy-done = f32[1000,512]{1,0:T(8,128)S(1)} copy-done((f32[1000,512]{1,0:T(8,128)S(1)}, f32[1000,512]{1,0:T(8,128)}, u32[]{:S(2)}) %copy-start) | copy-done | bytes 2048024
  1.6 0.0 copy-start.1
  1.6 1.3 %copy-done.1 = f32[1,1,288,1000]{3,2,1,0:T(8,128)S(1)} copy-done((f32[1,1,288,1000]{3,2,1,0:T(8,128)S(1)}, f32[1,1,288,1000]{3,2,1,0:T(8,128)}, u32[]{:S(2)}) %copy-start.1) | copy-done | bytes 1152024
  2.9 0.0 copy-start.3
  2.9 0.7 %copy-done.3 = s32[1,16,3]{1,0,2:T(1,128)S(1)} copy-done((s32[1,16,3]{1,0,2:T(1,128)S(1)}, s32[1,16,3]{1,0,2:T(1,128)}, u32[]{:S(2)}) %copy-start.3) | copy-done | bytes 216
  3.5 1.8 %interp.1 = (f32[96,512]{1,0:T(8,128)S(1)}, f32[96,512]{1,0:T(8,128)S(1)}, f32[96,512]{1,0:T(8,128)S(1)}) custom-call(s32[3,1,16]{2,1,0:T(1,128)S(1)} %bitcast.21, f32[288,1000]{1,0:T(8,128)S(1)} %bitcast.20, f32[1000,512]{1,0:T(8,128)S(1)} %copy-done), custom_call_target="tpu_custom_call" | custom-call | tf_op jit(solution)/shard_map/interp/pallas_call | solution.py:206
  5.4 0.0 copy-start.2
  5.4 0.5 collective-permute-start
  5.9 2.6 %collective-permute-start.1 = (f32[96,512]{1,0:T(8,128)S(1)}, f32[96,512]{1,0:T(8,128)S(1)}, u32[]{:S(2)}, u32[]{:S(2)}) collective-permute-start(f32[96,512]{1,0:T(8,128)S(1)} %get-tuple-element.15), channel_id=1, source_target_pairs={{0,4},{2,6},{4,8},{6,10},{8,12},{10,14},{12,16},{14,18},{16,20},{1... | collective-permute-start | bytes 589832 | tf_op jit(solution)/shard_map/ppermute | solution.py:216
  8.4 0.0 copy-done.4
  8.4 0.9 %pick.1.pick_ref = f32[192,288]{1,0:T(8,128)S(1)} custom-call(s32[3,1,16]{2,1,0:T(1,128)S(1)} %bitcast.22, s32[1,192]{1,0:T(1,128)S(1)} %bitcast.23), custom_call_target="tpu_custom_call" | custom-call | tf_op jit(solution)/shard_map/pick/pallas_call | solution.py:219
  9.4 6.0 %collective-permute-done.refs_1_ = f32[96,512]{1,0:T(8,128)S(1)} collective-permute-done((f32[96,512]{1,0:T(8,128)S(1)}, f32[96,512]{1,0:T(8,128)S(1)}, u32[]{:S(2)}, u32[]{:S(2)}) %collective-permute-start) | collective-permute-done | bytes 196640 | tf_op jit(solution)/shard_map/ppermute | solution.py:216
  15.4 1.8 %collective-permute-done.1.refs_2_ = f32[96,512]{1,0:T(8,128)S(1)} collective-permute-done((f32[96,512]{1,0:T(8,128)S(1)}, f32[96,512]{1,0:T(8,128)S(1)}, u32[]{:S(2)}, u32[]{:S(2)}) %collective-permute-start.1) | collective-permute-done | bytes 196640 | tf_op jit(solution)/shard_map/ppermute | solution.py:216
  17.2 0.5 order.1
  17.8 1.1 %collective-permute-start.2 = (f32[8,48,128]{2,1,0:T(8,128)S(1)}, f32[8,48,128]{2,1,0:T(8,128)S(1)}, u32[]{:S(2)}, u32[]{:S(2)}) collective-permute-start(f32[8,48,128]{2,1,0:T(8,128)S(1)} %reshape.16), channel_id=1, source_target_pairs={{0,2},{1,3},{2,0},{3,1},{4,6},{5,7},{6,4},{7,5},{8,10},{9,11},{10,... | collective-permute-start | bytes 589832 | tf_op jit(solution)/shard_map/ppermute | solution.py:181
  18.9 1.0 %collective-permute-done.2 = f32[8,48,128]{2,1,0:T(8,128)S(1)} collective-permute-done((f32[8,48,128]{2,1,0:T(8,128)S(1)}, f32[8,48,128]{2,1,0:T(8,128)S(1)}, u32[]{:S(2)}, u32[]{:S(2)}) %collective-permute-start.2) | collective-permute-done | bytes 196640 | tf_op jit(solution)/shard_map/ppermute | solution.py:181
  20.0 2.4 %collective-permute-start.9 = (f32[96,128]{1,0:T(8,128)S(1)}, f32[96,128]{1,0:T(8,128)S(1)}, u32[]{:S(2)}, u32[]{:S(2)}) collective-permute-start(f32[96,128]{1,0:T(8,128)S(1)} %get-tuple-element.21), channel_id=1, source_target_pairs={{0,28},{1,29},{2,30},{3,31},{4,24},{5,25},{6,26},{7,27},{8,20},{9,... | collective-permute-start | bytes 147464 | tf_op jit(solution)/shard_map/ppermute | solution.py:181
  22.3 0.2 collective-permute-start.8
  22.6 1.7 %collective-permute-start.7 = (f32[96,128]{1,0:T(8,128)S(1)}, f32[96,128]{1,0:T(8,128)S(1)}, u32[]{:S(2)}, u32[]{:S(2)}) collective-permute-start(f32[96,128]{1,0:T(8,128)S(1)} %get-tuple-element.23), channel_id=1, source_target_pairs={{0,20},{1,21},{2,22},{3,23},{4,16},{5,17},{6,18},{7,19},{8,28},{9,... | collective-permute-start | bytes 147464 | tf_op jit(solution)/shard_map/ppermute | solution.py:181
  24.2 3.5 %collective-permute-start.6 = (f32[96,128]{1,0:T(8,128)S(1)}, f32[96,128]{1,0:T(8,128)S(1)}, u32[]{:S(2)}, u32[]{:S(2)}) collective-permute-start(f32[96,128]{1,0:T(8,128)S(1)} %get-tuple-element.24), channel_id=1, source_target_pairs={{0,16},{1,17},{2,18},{3,19},{4,20},{5,21},{6,22},{7,23},{8,24},{9,... | collective-permute-start | bytes 147464 | tf_op jit(solution)/shard_map/ppermute | solution.py:181
  27.7 0.0 collective-permute-start.5
  27.7 0.0 collective-permute-done.9.refs_7_
  27.7 0.7 %collective-permute-start.4 = (f32[96,128]{1,0:T(8,128)S(1)}, f32[96,128]{1,0:T(8,128)S(1)}, u32[]{:S(2)}, u32[]{:S(2)}) collective-permute-start(f32[96,128]{1,0:T(8,128)S(1)} %get-tuple-element.26), channel_id=1, source_target_pairs={{0,8},{1,9},{2,10},{3,11},{4,12},{5,13},{6,14},{7,15},{8,0},{9,1},... | collective-permute-start | bytes 147464 | tf_op jit(solution)/shard_map/ppermute | solution.py:181
  28.4 0.0 collective-permute-done.8.refs_6_
  28.4 2.8 %collective-permute-start.3 = (f32[96,128]{1,0:T(8,128)S(1)}, f32[96,128]{1,0:T(8,128)S(1)}, u32[]{:S(2)}, u32[]{:S(2)}) collective-permute-start(f32[96,128]{1,0:T(8,128)S(1)} %get-tuple-element.27), channel_id=1, source_target_pairs={{0,4},{1,5},{2,6},{3,7},{4,0},{5,1},{6,2},{7,3},{8,12},{9,13},{10,... | collective-permute-start | bytes 147464 | tf_op jit(solution)/shard_map/ppermute | solution.py:181
  31.2 0.4 collective-permute-done.7.refs_5_
  31.6 0.1 collective-permute-done.6.refs_4_
  31.7 1.9 %collective-permute-done.5.refs_3_ = f32[96,128]{1,0:T(8,128)S(1)} collective-permute-done((f32[96,128]{1,0:T(8,128)S(1)}, f32[96,128]{1,0:T(8,128)S(1)}, u32[]{:S(2)}, u32[]{:S(2)}) %collective-permute-start.5) | collective-permute-done | bytes 49184 | tf_op jit(solution)/shard_map/ppermute | solution.py:181
  33.5 0.0 collective-permute-done.4.refs_2_
  33.5 0.2 collective-permute-done.3.refs_1_
  33.7 0.0 copy-done.2
  33.7 0.8 %image.1 = (f32[384,128]{1,0:T(8,128)S(1)}, f32[384,128]{1,0:T(8,128)S(1)}, f32[768,128]{1,0:T(8,128)S(1)}) custom-call(f32[96,128]{1,0:T(8,128)S(1)} %get-tuple-element.28.refs_0_, f32[96,128]{1,0:T(8,128)S(1)} %collective-permute-done.3.refs_1_, f32[96,128]{1,0:T(8,128)S(1)} %collective-permute-done.4.refs_2_, ...), custom_call_target="tpu_custom_call" | custom-call | tf_op jit(solution)/shard_map/image/pallas_call | solution.py:254
  34.5 0.1 collective-permute-start.10
  34.6 1.4 %collective-permute-done.10 = f32[384,128]{1,0:T(8,128)S(1)} collective-permute-done((f32[384,128]{1,0:T(8,128)S(1)}, f32[384,128]{1,0:T(8,128)S(1)}, u32[]{:S(2)}, u32[]{:S(2)}) %collective-permute-start.10) | collective-permute-done | bytes 196640 | tf_op jit(solution)/shard_map/ppermute | solution.py:181
  36.1 3.0 %collective-permute-start.11 = (f32[96,128]{1,0:T(8,128)S(1)}, f32[96,128]{1,0:T(8,128)S(1)}, u32[]{:S(2)}, u32[]{:S(2)}) collective-permute-start(f32[96,128]{1,0:T(8,128)S(1)} %get-tuple-element.29), channel_id=1, source_target_pairs={{0,5},{1,4},{2,7},{3,6},{4,1},{5,0},{6,3},{7,2},{8,13},{9,12},{10,... | collective-permute-start | bytes 147464 | tf_op jit(solution)/shard_map/ppermute | solution.py:181
  39.1 0.0 collective-permute-start.13
  39.2 0.6 collective-permute-start.12
  39.8 1.4 %collective-permute-done.11 = f32[96,128]{1,0:T(8,128)S(1)} collective-permute-done((f32[96,128]{1,0:T(8,128)S(1)}, f32[96,128]{1,0:T(8,128)S(1)}, u32[]{:S(2)}, u32[]{:S(2)}) %collective-permute-start.11) | collective-permute-done | bytes 49184 | tf_op jit(solution)/shard_map/ppermute | solution.py:181
  41.2 2.0 %collective-permute-done.13 = f32[96,128]{1,0:T(8,128)S(1)} collective-permute-done((f32[96,128]{1,0:T(8,128)S(1)}, f32[96,128]{1,0:T(8,128)S(1)}, u32[]{:S(2)}, u32[]{:S(2)}) %collective-permute-start.13) | collective-permute-done | bytes 49184 | tf_op jit(solution)/shard_map/ppermute | solution.py:181
  43.2 0.0 collective-permute-done.12
  43.3 0.9 %collective-permute-start.16 = (f32[96,128]{1,0:T(8,128)S(1)}, f32[96,128]{1,0:T(8,128)S(1)}, u32[]{:S(2)}, u32[]{:S(2)}) collective-permute-start(f32[96,128]{1,0:T(8,128)S(1)} %fusion.1), channel_id=1, source_target_pairs={{0,16},{1,17},{2,18},{3,19},{4,20},{5,21},{6,22},{7,23},{8,24},{9,... | collective-permute-start | bytes 147464 | tf_op jit(solution)/shard_map/ppermute | solution.py:181
  44.2 2.0 %collective-permute-start.15 = (f32[96,128]{1,0:T(8,128)S(1)}, f32[96,128]{1,0:T(8,128)S(1)}, u32[]{:S(2)}, u32[]{:S(2)}) collective-permute-start(f32[96,128]{1,0:T(8,128)S(1)} %fusion.1), channel_id=1, source_target_pairs={{0,8},{1,9},{2,10},{3,11},{4,12},{5,13},{6,14},{7,15},{8,0},{9,1},... | collective-permute-start | bytes 147464 | tf_op jit(solution)/shard_map/ppermute | solution.py:181
  46.2 1.6 %collective-permute-start.14 = (f32[96,128]{1,0:T(8,128)S(1)}, f32[96,128]{1,0:T(8,128)S(1)}, u32[]{:S(2)}, u32[]{:S(2)}) collective-permute-start(f32[96,128]{1,0:T(8,128)S(1)} %fusion.1), channel_id=1, source_target_pairs={{0,24},{1,25},{2,26},{3,27},{4,28},{5,29},{6,30},{7,31},{8,16},{9,... | collective-permute-start | bytes 147464 | tf_op jit(solution)/shard_map/ppermute | solution.py:181
  47.7 0.7 %collective-permute-done.16 = f32[96,128]{1,0:T(8,128)S(1)} collective-permute-done((f32[96,128]{1,0:T(8,128)S(1)}, f32[96,128]{1,0:T(8,128)S(1)}, u32[]{:S(2)}, u32[]{:S(2)}) %collective-permute-start.16) | collective-permute-done | bytes 49184 | tf_op jit(solution)/shard_map/ppermute | solution.py:181
  48.5 0.9 %collective-permute-done.15 = f32[96,128]{1,0:T(8,128)S(1)} collective-permute-done((f32[96,128]{1,0:T(8,128)S(1)}, f32[96,128]{1,0:T(8,128)S(1)}, u32[]{:S(2)}, u32[]{:S(2)}) %collective-permute-start.15) | collective-permute-done | bytes 49184 | tf_op jit(solution)/shard_map/ppermute | solution.py:181
  49.4 2.7 %collective-permute-done.14 = f32[96,128]{1,0:T(8,128)S(1)} collective-permute-done((f32[96,128]{1,0:T(8,128)S(1)}, f32[96,128]{1,0:T(8,128)S(1)}, u32[]{:S(2)}, u32[]{:S(2)}) %collective-permute-start.14) | collective-permute-done | bytes 49184 | tf_op jit(solution)/shard_map/ppermute | solution.py:181
  52.1 1.9 %collective-permute-start.19 = (f32[96,128]{1,0:T(8,128)S(1)}, f32[96,128]{1,0:T(8,128)S(1)}, u32[]{:S(2)}, u32[]{:S(2)}) collective-permute-start(f32[96,128]{1,0:T(8,128)S(1)} %add_add_fusion), channel_id=1, source_target_pairs={{0,5},{1,4},{2,7},{3,6},{4,1},{5,0},{6,3},{7,2},{8,13},{9,12},{10,... | collective-permute-start | bytes 147464 | tf_op jit(solution)/shard_map/ppermute | solution.py:181
  54.0 1.1 %collective-permute-start.18 = (f32[96,128]{1,0:T(8,128)S(1)}, f32[96,128]{1,0:T(8,128)S(1)}, u32[]{:S(2)}, u32[]{:S(2)}) collective-permute-start(f32[96,128]{1,0:T(8,128)S(1)} %add_add_fusion), channel_id=1, source_target_pairs={{0,4},{1,5},{2,6},{3,7},{4,0},{5,1},{6,2},{7,3},{8,12},{9,13},{10,... | collective-permute-start | bytes 147464 | tf_op jit(solution)/shard_map/ppermute | solution.py:181
  55.1 0.5 collective-permute-start.17
  55.6 1.5 %collective-permute-done.19 = f32[96,128]{1,0:T(8,128)S(1)} collective-permute-done((f32[96,128]{1,0:T(8,128)S(1)}, f32[96,128]{1,0:T(8,128)S(1)}, u32[]{:S(2)}, u32[]{:S(2)}) %collective-permute-start.19) | collective-permute-done | bytes 49184 | tf_op jit(solution)/shard_map/ppermute | solution.py:181
  57.1 0.9 %collective-permute-done.18 = f32[96,128]{1,0:T(8,128)S(1)} collective-permute-done((f32[96,128]{1,0:T(8,128)S(1)}, f32[96,128]{1,0:T(8,128)S(1)}, u32[]{:S(2)}, u32[]{:S(2)}) %collective-permute-start.18) | collective-permute-done | bytes 49184 | tf_op jit(solution)/shard_map/ppermute | solution.py:181
  58.1 1.1 %collective-permute-done.17 = f32[96,128]{1,0:T(8,128)S(1)} collective-permute-done((f32[96,128]{1,0:T(8,128)S(1)}, f32[96,128]{1,0:T(8,128)S(1)}, u32[]{:S(2)}, u32[]{:S(2)}) %collective-permute-start.17) | collective-permute-done | bytes 49184 | tf_op jit(solution)/shard_map/ppermute | solution.py:181
  59.2 0.1 collective-permute-start.20
  59.3 1.4 %collective-permute-done.20.other_ref = f32[384,128]{1,0:T(8,128)S(1)} collective-permute-done((f32[384,128]{1,0:T(8,128)S(1)}, f32[384,128]{1,0:T(8,128)S(1)}, u32[]{:S(2)}, u32[]{:S(2)}) %collective-permute-start.20) | collective-permute-done | bytes 196640 | tf_op jit(solution)/shard_map/ppermute | solution.py:181
  60.7 6.2 %factor.1 = f32[128,128]{1,0:T(8,128)} custom-call(f32[768,128]{1,0:T(8,128)S(1)} %get-tuple-element.18.field_ref, f32[384,128]{1,0:T(8,128)S(1)} %pad_maximum_fusion.own_ref, f32[384,128]{1,0:T(8,128)S(1)} %collective-permute-done.20.other_ref), custom_call_target="tpu_custom_call" | custom-call | tf_op jit(solution)/shard_map/factor/pallas_call | solution.py:273
  (10 shorter events, 0.2 us)
Async XLA Ops:
  0.0 8.4 %copy-start.4 = (s32[1,1,192]{2,1,0:T(1,128)S(1)}, s32[1,1,192]{2,1,0:T(1,128)}, u32[]{:S(2)}) copy-start(s32[1,1,192]{2,1,0:T(1,128)} %param.8) | copy-start | bytes 2308
  0.0 1.6 %copy-start = (f32[1000,512]{1,0:T(8,128)S(1)}, f32[1000,512]{1,0:T(8,128)}, u32[]{:S(2)}) copy-start(f32[1000,512]{1,0:T(8,128)} %interp_ref.1) | copy-start | bytes 6144004
  1.6 1.3 %copy-start.1 = (f32[1,1,288,1000]{3,2,1,0:T(8,128)S(1)}, f32[1,1,288,1000]{3,2,1,0:T(8,128)}, u32[]{:S(2)}) copy-start(f32[1,1,288,1000]{3,2,1,0:T(8,128)} %param.5) | copy-start | bytes 3456004
  2.9 0.7 %copy-start.3 = (s32[1,16,3]{1,0,2:T(1,128)S(1)}, s32[1,16,3]{1,0,2:T(1,128)}, u32[]{:S(2)}) copy-start(s32[1,16,3]{1,0,2:T(1,128)} %param.7) | copy-start | bytes 580
  5.4 28.4 %copy-start.2 = (f32[768,128]{1,0:T(8,128)S(1)}, f32[768,128]{1,0:T(8,128)}, u32[]{:S(2)}) copy-start(f32[768,128]{1,0:T(8,128)} %refs_8_.1) | copy-start | bytes 1179652
  5.4 10.0 %collective-permute-start = (f32[96,512]{1,0:T(8,128)S(1)}, f32[96,512]{1,0:T(8,128)S(1)}, u32[]{:S(2)}, u32[]{:S(2)}) collective-permute-start(f32[96,512]{1,0:T(8,128)S(1)} %get-tuple-element.14), channel_id=1, source_target_pairs={{0,2},{2,4},{4,6},{6,8},{8,10},{10,12},{12,14},{14,16},{16,18},{18... | collective-permute-start | bytes 589832 | tf_op jit(solution)/shard_map/ppermute | solution.py:216
  5.9 11.3 %collective-permute-start.1 = (f32[96,512]{1,0:T(8,128)S(1)}, f32[96,512]{1,0:T(8,128)S(1)}, u32[]{:S(2)}, u32[]{:S(2)}) collective-permute-start(f32[96,512]{1,0:T(8,128)S(1)} %get-tuple-element.15), channel_id=1, source_target_pairs={{0,4},{2,6},{4,8},{6,10},{8,12},{10,14},{12,16},{14,18},{16,20},{1... | collective-permute-start | bytes 589832 | tf_op jit(solution)/shard_map/ppermute | solution.py:216
  17.8 2.2 %collective-permute-start.2 = (f32[8,48,128]{2,1,0:T(8,128)S(1)}, f32[8,48,128]{2,1,0:T(8,128)S(1)}, u32[]{:S(2)}, u32[]{:S(2)}) collective-permute-start(f32[8,48,128]{2,1,0:T(8,128)S(1)} %reshape.16), channel_id=1, source_target_pairs={{0,2},{1,3},{2,0},{3,1},{4,6},{5,7},{6,4},{7,5},{8,10},{9,11},{10,... | collective-permute-start | bytes 589832 | tf_op jit(solution)/shard_map/ppermute | solution.py:181
  20.0 7.7 %collective-permute-start.9 = (f32[96,128]{1,0:T(8,128)S(1)}, f32[96,128]{1,0:T(8,128)S(1)}, u32[]{:S(2)}, u32[]{:S(2)}) collective-permute-start(f32[96,128]{1,0:T(8,128)S(1)} %get-tuple-element.21), channel_id=1, source_target_pairs={{0,28},{1,29},{2,30},{3,31},{4,24},{5,25},{6,26},{7,27},{8,20},{9,... | collective-permute-start | bytes 147464 | tf_op jit(solution)/shard_map/ppermute | solution.py:181
  22.3 6.1 %collective-permute-start.8 = (f32[96,128]{1,0:T(8,128)S(1)}, f32[96,128]{1,0:T(8,128)S(1)}, u32[]{:S(2)}, u32[]{:S(2)}) collective-permute-start(f32[96,128]{1,0:T(8,128)S(1)} %get-tuple-element.22), channel_id=1, source_target_pairs={{0,24},{1,25},{2,26},{3,27},{4,28},{5,29},{6,30},{7,31},{8,16},{9,... | collective-permute-start | bytes 147464 | tf_op jit(solution)/shard_map/ppermute | solution.py:181
  22.6 9.0 %collective-permute-start.7 = (f32[96,128]{1,0:T(8,128)S(1)}, f32[96,128]{1,0:T(8,128)S(1)}, u32[]{:S(2)}, u32[]{:S(2)}) collective-permute-start(f32[96,128]{1,0:T(8,128)S(1)} %get-tuple-element.23), channel_id=1, source_target_pairs={{0,20},{1,21},{2,22},{3,23},{4,16},{5,17},{6,18},{7,19},{8,28},{9,... | collective-permute-start | bytes 147464 | tf_op jit(solution)/shard_map/ppermute | solution.py:181
  24.2 7.4 %collective-permute-start.6 = (f32[96,128]{1,0:T(8,128)S(1)}, f32[96,128]{1,0:T(8,128)S(1)}, u32[]{:S(2)}, u32[]{:S(2)}) collective-permute-start(f32[96,128]{1,0:T(8,128)S(1)} %get-tuple-element.24), channel_id=1, source_target_pairs={{0,16},{1,17},{2,18},{3,19},{4,20},{5,21},{6,22},{7,23},{8,24},{9,... | collective-permute-start | bytes 147464 | tf_op jit(solution)/shard_map/ppermute | solution.py:181
  27.7 5.8 %collective-permute-start.5 = (f32[96,128]{1,0:T(8,128)S(1)}, f32[96,128]{1,0:T(8,128)S(1)}, u32[]{:S(2)}, u32[]{:S(2)}) collective-permute-start(f32[96,128]{1,0:T(8,128)S(1)} %get-tuple-element.25), channel_id=1, source_target_pairs={{0,12},{1,13},{2,14},{3,15},{4,8},{5,9},{6,10},{7,11},{8,4},{9,5},... | collective-permute-start | bytes 147464 | tf_op jit(solution)/shard_map/ppermute | solution.py:181
  27.7 5.8 %collective-permute-start.4 = (f32[96,128]{1,0:T(8,128)S(1)}, f32[96,128]{1,0:T(8,128)S(1)}, u32[]{:S(2)}, u32[]{:S(2)}) collective-permute-start(f32[96,128]{1,0:T(8,128)S(1)} %get-tuple-element.26), channel_id=1, source_target_pairs={{0,8},{1,9},{2,10},{3,11},{4,12},{5,13},{6,14},{7,15},{8,0},{9,1},... | collective-permute-start | bytes 147464 | tf_op jit(solution)/shard_map/ppermute | solution.py:181
  28.4 5.3 %collective-permute-start.3 = (f32[96,128]{1,0:T(8,128)S(1)}, f32[96,128]{1,0:T(8,128)S(1)}, u32[]{:S(2)}, u32[]{:S(2)}) collective-permute-start(f32[96,128]{1,0:T(8,128)S(1)} %get-tuple-element.27), channel_id=1, source_target_pairs={{0,4},{1,5},{2,6},{3,7},{4,0},{5,1},{6,2},{7,3},{8,12},{9,13},{10,... | collective-permute-start | bytes 147464 | tf_op jit(solution)/shard_map/ppermute | solution.py:181
  34.5 1.5 %collective-permute-start.10 = (f32[384,128]{1,0:T(8,128)S(1)}, f32[384,128]{1,0:T(8,128)S(1)}, u32[]{:S(2)}, u32[]{:S(2)}) collective-permute-start(f32[384,128]{1,0:T(8,128)S(1)} %get-tuple-element.20), channel_id=1, source_target_pairs={{0,2},{1,3},{2,0},{3,1},{4,6},{5,7},{6,4},{7,5},{8,10},{9,11},{10,... | collective-permute-start | bytes 589832 | tf_op jit(solution)/shard_map/ppermute | solution.py:181
  36.1 5.1 %collective-permute-start.11 = (f32[96,128]{1,0:T(8,128)S(1)}, f32[96,128]{1,0:T(8,128)S(1)}, u32[]{:S(2)}, u32[]{:S(2)}) collective-permute-start(f32[96,128]{1,0:T(8,128)S(1)} %get-tuple-element.29), channel_id=1, source_target_pairs={{0,5},{1,4},{2,7},{3,6},{4,1},{5,0},{6,3},{7,2},{8,13},{9,12},{10,... | collective-permute-start | bytes 147464 | tf_op jit(solution)/shard_map/ppermute | solution.py:181
  39.1 4.1 %collective-permute-start.13 = (f32[96,128]{1,0:T(8,128)S(1)}, f32[96,128]{1,0:T(8,128)S(1)}, u32[]{:S(2)}, u32[]{:S(2)}) collective-permute-start(f32[96,128]{1,0:T(8,128)S(1)} %get-tuple-element.30), channel_id=1, source_target_pairs={{0,1},{1,0},{2,3},{3,2},{4,5},{5,4},{6,7},{7,6},{8,9},{9,8},{10,11... | collective-permute-start | bytes 147464 | tf_op jit(solution)/shard_map/ppermute | solution.py:181
  39.2 4.1 %collective-permute-start.12 = (f32[96,128]{1,0:T(8,128)S(1)}, f32[96,128]{1,0:T(8,128)S(1)}, u32[]{:S(2)}, u32[]{:S(2)}) collective-permute-start(f32[96,128]{1,0:T(8,128)S(1)} %get-tuple-element.31), channel_id=1, source_target_pairs={{0,4},{1,5},{2,6},{3,7},{4,0},{5,1},{6,2},{7,3},{8,12},{9,13},{10,... | collective-permute-start | bytes 147464 | tf_op jit(solution)/shard_map/ppermute | solution.py:181
  43.3 5.2 %collective-permute-start.16 = (f32[96,128]{1,0:T(8,128)S(1)}, f32[96,128]{1,0:T(8,128)S(1)}, u32[]{:S(2)}, u32[]{:S(2)}) collective-permute-start(f32[96,128]{1,0:T(8,128)S(1)} %fusion.1), channel_id=1, source_target_pairs={{0,16},{1,17},{2,18},{3,19},{4,20},{5,21},{6,22},{7,23},{8,24},{9,... | collective-permute-start | bytes 147464 | tf_op jit(solution)/shard_map/ppermute | solution.py:181
  44.2 5.1 %collective-permute-start.15 = (f32[96,128]{1,0:T(8,128)S(1)}, f32[96,128]{1,0:T(8,128)S(1)}, u32[]{:S(2)}, u32[]{:S(2)}) collective-permute-start(f32[96,128]{1,0:T(8,128)S(1)} %fusion.1), channel_id=1, source_target_pairs={{0,8},{1,9},{2,10},{3,11},{4,12},{5,13},{6,14},{7,15},{8,0},{9,1},... | collective-permute-start | bytes 147464 | tf_op jit(solution)/shard_map/ppermute | solution.py:181
  46.2 5.9 %collective-permute-start.14 = (f32[96,128]{1,0:T(8,128)S(1)}, f32[96,128]{1,0:T(8,128)S(1)}, u32[]{:S(2)}, u32[]{:S(2)}) collective-permute-start(f32[96,128]{1,0:T(8,128)S(1)} %fusion.1), channel_id=1, source_target_pairs={{0,24},{1,25},{2,26},{3,27},{4,28},{5,29},{6,30},{7,31},{8,16},{9,... | collective-permute-start | bytes 147464 | tf_op jit(solution)/shard_map/ppermute | solution.py:181
  52.1 5.1 %collective-permute-start.19 = (f32[96,128]{1,0:T(8,128)S(1)}, f32[96,128]{1,0:T(8,128)S(1)}, u32[]{:S(2)}, u32[]{:S(2)}) collective-permute-start(f32[96,128]{1,0:T(8,128)S(1)} %add_add_fusion), channel_id=1, source_target_pairs={{0,5},{1,4},{2,7},{3,6},{4,1},{5,0},{6,3},{7,2},{8,13},{9,12},{10,... | collective-permute-start | bytes 147464 | tf_op jit(solution)/shard_map/ppermute | solution.py:181
  54.0 4.1 %collective-permute-start.18 = (f32[96,128]{1,0:T(8,128)S(1)}, f32[96,128]{1,0:T(8,128)S(1)}, u32[]{:S(2)}, u32[]{:S(2)}) collective-permute-start(f32[96,128]{1,0:T(8,128)S(1)} %add_add_fusion), channel_id=1, source_target_pairs={{0,4},{1,5},{2,6},{3,7},{4,0},{5,1},{6,2},{7,3},{8,12},{9,13},{10,... | collective-permute-start | bytes 147464 | tf_op jit(solution)/shard_map/ppermute | solution.py:181
  55.1 4.1 %collective-permute-start.17 = (f32[96,128]{1,0:T(8,128)S(1)}, f32[96,128]{1,0:T(8,128)S(1)}, u32[]{:S(2)}, u32[]{:S(2)}) collective-permute-start(f32[96,128]{1,0:T(8,128)S(1)} %add_add_fusion), channel_id=1, source_target_pairs={{0,1},{1,0},{2,3},{3,2},{4,5},{5,4},{6,7},{7,6},{8,9},{9,8},{10,11... | collective-permute-start | bytes 147464 | tf_op jit(solution)/shard_map/ppermute | solution.py:181
  59.2 1.5 %collective-permute-start.20 = (f32[384,128]{1,0:T(8,128)S(1)}, f32[384,128]{1,0:T(8,128)S(1)}, u32[]{:S(2)}, u32[]{:S(2)}) collective-permute-start(f32[384,128]{1,0:T(8,128)S(1)} %pad_maximum_fusion.own_ref), channel_id=1, source_target_pairs={{0,2},{1,3},{2,0},{3,1},{4,6},{5,7},{6,4},{7,5},{8,10},{9,11},{10,... | collective-permute-start | bytes 589832 | tf_op jit(solution)/shard_map/ppermute | solution.py:181

commit v5 on v2

v5 whole, which is shorter than its diff:
```python
import functools

import jax
import jax.numpy as jnp
from jax import lax
from jax.experimental import pallas as pl
from jax.experimental.pallas import tpu as pltpu
from jax.sharding import PartitionSpec as P

F32 = jnp.float32
BF16 = jnp.bfloat16
SLAB = 8
VMEM = pl.BlockSpec(memory_space=pltpu.VMEM)
SMEM = pl.BlockSpec(memory_space=pltpu.SMEM)
BIG = pltpu.CompilerParams(vmem_limit_bytes=32 * 1024 * 1024)


def halves(value):
    high = value.astype(BF16)
    return high, (value - high.astype(F32)).astype(BF16)


def dot3(left, right, contract):
    dims = (contract, ((), ()))
    lh, ll = left
    rh, rl = right
    out = lax.dot_general(lh, rl, dims, preferred_element_type=F32)
    out += lax.dot_general(ll, rh, dims, preferred_element_type=F32)
    return out + lax.dot_general(lh, rh, dims, preferred_element_type=F32)


def interp_kernel(owners, table_ref, node_ref, interp_ref, near_ref, far_ref, last_ref, grid_scr):
    rows = last_ref.shape[0]
    slots = node_ref.shape[0]
    own = lax.axis_index("fib")
    grid_scr[:slots, :] = dot3(halves(node_ref[...]), halves(interp_ref[...]), ((1,), (0,)))
    near_ref[:rows, :] = grid_scr[:rows, :]
    start = table_ref[0, 0, own]
    for distance in range(1, 3):
        shift = lax.rem(start, SLAB)
        at = pl.multiple_of(start - shift, SLAB)
        wide = grid_scr[pl.ds(at, rows + SLAB), :]
        piece = pltpu.roll(wide, lax.rem(rows + SLAB - shift, rows + SLAB), 0)[:rows, :]
        if distance == 1:
            near_ref[rows:, :] = piece
            far_ref[:rows, :] = piece
        else:
            far_ref[rows:, :] = piece
            last_ref[...] = piece
        start = start + table_ref[distance, 0, lax.rem(own + distance, owners)]


def pick_kernel(rows, per_tile, table_ref, order_ref, order_own_ref, out_ref):
    elements = order_ref.shape[1]
    slots = out_ref.shape[1]
    chip = lax.div(lax.axis_index("fib"), 2)
    rank_at = lax.broadcasted_iota(jnp.int32, (elements, slots), 0)
    slot_at = lax.broadcasted_iota(jnp.int32, (elements, slots), 1)
    row = lax.broadcasted_iota(jnp.int32, (elements, elements), 0)
    for core, order in enumerate((order_ref, order_own_ref)):
        from_slot = jnp.zeros((elements, slots), jnp.bool_)
        start = 0
        for distance in range(slots // rows - 1, -1, -1):
            count = table_ref[distance, 0, 2 * chip + core]
            inside = (rank_at >= start) & (rank_at < start + count)
            from_slot = from_slot | (inside & (slot_at - distance * rows == rank_at - start))
            start = start + count
        place = order[...]
        tile = lax.div(place, jnp.full_like(place, per_tile))
        place = place - tile * per_tile + (tile ^ (2 * chip)) * per_tile
        place = jnp.broadcast_to(place, (elements, elements))
        to_place = jnp.where(place == row, 1.0, 0.0).astype(BF16)
        out_ref[core * elements : (core + 1) * elements, :] = jnp.dot(
            to_place, jnp.where(from_slot, 1.0, 0.0).astype(BF16), preferred_element_type=F32
        )


def order_kernel(pick_ref, own_ref, near_ref, far_ref, last_ref, *outs):
    rows = last_ref.shape[0]
    elements = outs[0].shape[0]
    sources = (
        (near_ref[:rows, :], far_ref[:rows, :], last_ref[...]),
        (own_ref[:rows, :], near_ref[rows:, :], far_ref[rows:, :]),
    )
    for core, pieces in enumerate(sources):
        pick = pick_ref[core * elements : (core + 1) * elements, :].astype(BF16)
        line = jnp.concatenate(pieces, axis=0)
        high = line.astype(BF16)
        rest = line - high.astype(F32)
        mid = rest.astype(BF16)
        low = (rest - mid.astype(F32)).astype(BF16)
        out = jnp.dot(pick, low, preferred_element_type=F32)
        out += jnp.dot(pick, mid, preferred_element_type=F32)
        outs[core][...] = out + jnp.dot(pick, high, preferred_element_type=F32)


def bit_place(order):
    index = 0
    for axis, mask in order:
        index = index * 2 + lax.rem(lax.div(lax.axis_index(axis), mask), 2)
    return index


def image_kernel(mid, *refs):
    field_ref, image_scr = refs[-2:]
    count = 2 ** len(mid)
    outs = refs[-2 - count : -2]
    *block_refs, start_ref = refs[: -2 - count]
    length, width = field_ref.shape
    tile = width // 2
    chip = lax.div(lax.axis_index("fib"), 2)
    each = length // (2 * len(block_refs))
    if len(block_refs) == 1:
        field_ref[...] = block_refs[0][...]
        block_refs = []
    for step, block in enumerate(block_refs):
        for owner in range(2):
            at = pl.multiple_of((2 * (chip ^ step) + owner) * each, each)
            for core in range(2):
                part = (2 * owner + core) * each
                field_ref[pl.ds(at, each), core * tile : (core + 1) * tile] = block[part : part + each, :]
    field = halves(field_ref[...])
    mixed = dot3(field, halves(start_ref[...]), ((0,), (0,)))
    image_scr[...] = dot3(field, halves(mixed), ((1,), (0,)))
    place = bit_place(mid)
    for step, out in enumerate(outs):
        rows = out.shape[0]
        at = pl.multiple_of((place ^ step) * rows, rows)
        out[...] = image_scr[pl.ds(at, rows), :]


def factor_kernel(mid, field_ref, *refs):
    chunk_refs, out_refs, image_scr, work, line_scr = refs[:-5], refs[-5:-3], refs[-3], refs[-2], refs[-1]
    rank = image_scr.shape[1]
    place = bit_place(mid)
    for step, chunk in enumerate(chunk_refs):
        rows = chunk.shape[0]
        at = pl.multiple_of((place ^ step) * rows, rows)
        image_scr[pl.ds(at, rows), :] = chunk[...]
    image = halves(image_scr[...])
    work[:, :rank] = dot3(image, image, ((0,), (0,)))
    work[:, rank:] = dot3(image, halves(field_ref[...]), ((0,), (0,)))
    shape = (1, rank)
    for base in range(0, rank, SLAB):
        left = [work[base + k : base + k + 1, :rank] for k in range(SLAB)]
        right = [work[base + k : base + k + 1, rank:] for k in range(SLAB)]
        entry = [
            [jnp.broadcast_to(left[k][:, base + i : base + i + 1], shape) for i in range(SLAB)]
            for k in range(SLAB)
        ]
        for k in range(SLAB):
            scale = lax.rsqrt(entry[k][k])
            left[k] = left[k] * scale
            right[k] = right[k] * jnp.concatenate([scale] * 2, axis=1)
            factor = {i: entry[k][i] * scale for i in range(k + 1, SLAB)}
            for i in range(k + 1, SLAB):
                for j in range(i, SLAB):
                    entry[i][j] = entry[i][j] - factor[i] * factor[j]
                left[i] = left[i] - factor[i] * left[k]
                right[i] = right[i] - jnp.concatenate([factor[i]] * 2, axis=1) * right[k]
            out_refs[0][base + k : base + k + 1, :] = right[k][:, :rank]
            out_refs[1][base + k : base + k + 1, :] = right[k][:, rank:]
            line_scr[k : k + 1, :rank] = left[k]
            line_scr[k : k + 1, rank:] = right[k]
        after = base + SLAB
        if after < rank:
            line = line_scr[...]
            high = line.astype(BF16).astype(F32)
            rest = line - high
            mid = rest.astype(BF16).astype(F32)
            low = rest - mid
            first = jnp.concatenate([high, high, mid, high, low, mid], axis=0).astype(BF16)
            second = jnp.concatenate([high, mid, high, low, high, mid], axis=0).astype(BF16)
            drop = lax.dot_general(
                first[:, :rank], second, (((0,), (0,)), ((), ())), preferred_element_type=F32
            )
            work[after:, :] = work[after:, :] - drop[after:, :]


def swapped(value, bits, step=1):
    apart = [bit for at, bit in enumerate(reversed(bits)) if step >> at & 1]
    peers = {axis: sum(mask for name, mask in apart if name == axis) for axis in ("fib", "pln")}
    owners, planes = lax.axis_size("fib"), lax.axis_size("pln")
    pairs = []
    for i in range(owners * planes):
        fib, pln = divmod(i, planes)
        if fib % 2:
            pairs.append((i, (fib ^ peers["fib"]) * planes + (pln ^ peers["pln"])))
    return lax.ppermute(value, ("fib", "pln"), pairs)


def masks(axis, low, high):
    out = []
    while low < high:
        out.append((axis, low))
        low *= 2
    return out


def per_device(nodal_values, interp_matrix, count_table, slot_order, start_basis):
    nodes = nodal_values[0, 0]
    table = jnp.transpose(count_table, (2, 0, 1))
    owners = lax.axis_size("fib")
    planes = lax.axis_size("pln")
    window = table.shape[0]
    capacity = nodes.shape[0] // window
    points = interp_matrix.shape[1]
    elements = slot_order.shape[2]
    length, rank = start_basis.shape
    tile = points * elements // length
    odd = range(1, owners, 2)

    order_first = lax.ppermute(slot_order[0], "fib", [(i - 1, i) for i in odd])
    near, far, last = pl.pallas_call(
        functools.partial(interp_kernel, owners),
        out_shape=[jax.ShapeDtypeStruct((n * capacity, points), F32) for n in (2, 2, 1)],
        in_specs=[SMEM, VMEM, VMEM],
        out_specs=[VMEM] * 3,
        scratch_shapes=[pltpu.VMEM((nodes.shape[0] + SLAB, points), F32)],
        compiler_params=BIG,
        name="interp",
    )(table, nodes, interp_matrix)
    far_got = lax.ppermute(far, "fib", [(i, (i + 2) % owners) for i in odd])
    last_got = lax.ppermute(last, "fib", [(i - 1, (i + 2) % owners) for i in odd])
    near_got = lax.ppermute(near, "fib", [(i - 1, i) for i in odd])
    pick = pl.pallas_call(
        functools.partial(pick_kernel, capacity, elements // owners),
        out_shape=jax.ShapeDtypeStruct((2 * elements, capacity * window), F32),
        in_specs=[SMEM, VMEM, VMEM],
        out_specs=VMEM,
        compiler_params=BIG,
        name="pick",
    )(table, order_first, slot_order[0])
    bricks = pl.pallas_call(
        order_kernel,
        out_shape=[jax.ShapeDtypeStruct((elements, points), F32)] * 2,
        in_specs=[VMEM] * 5,
        out_specs=[VMEM] * 2,
        compiler_params=BIG,
        name="order",
    )(pick, near, near_got, far_got, last_got)

    blocks = owners // 2
    chips = masks("fib", 2, owners)[::-1]
    both = jnp.concatenate([b.reshape(blocks, 2 * length // owners, tile) for b in bricks], axis=1)
    got = {step: swapped(both[step], chips, step) for step in range(blocks - 1, 0, -1)}
    got[0] = both[0]
    parts = [got[step] for step in range(blocks)]
    if length // owners % SLAB:
        at = lax.axis_index("fib") // 2 ^ jnp.arange(blocks)
        whole = jnp.stack(parts)[at].reshape(blocks, 2, 2, length // owners, tile)
        parts = [whole.transpose(0, 1, 3, 2, 4).reshape(length, 2 * tile)]

    mid = masks("fib", 2, 4) + masks("pln", 1, planes)
    distant = masks("fib", 4, owners)
    count = 2 ** len(mid)
    chunk = jax.ShapeDtypeStruct((length // count, rank), F32)
    *chunks, field = pl.pallas_call(
        functools.partial(image_kernel, mid),
        out_shape=[chunk] * count + [jax.ShapeDtypeStruct((length, 2 * tile), F32)],
        in_specs=[VMEM] * (len(parts) + 1),
        out_specs=[VMEM] * (count + 1),
        scratch_shapes=[pltpu.VMEM((length, rank), F32)],
        compiler_params=BIG,
        name="image",
    )(*parts, start_basis)
    total = chunks[0]
    for arrived in [swapped(chunks[step], mid, step) for step in range(count - 1, 0, -1)]:
        total = total + arrived
    share = total
    for arrived in [swapped(share, distant, step) for step in range(2 ** len(distant) - 1, 0, -1)]:
        total = total + arrived
    chunks = [total] + [swapped(total, mid, step) for step in range(1, count)]
    first, second = pl.pallas_call(
        functools.partial(factor_kernel, mid),
        out_shape=[jax.ShapeDtypeStruct((rank, tile), F32)] * 2,
        in_specs=[VMEM] * (1 + count),
        out_specs=[VMEM] * 2,
        scratch_shapes=[
            pltpu.VMEM((length, rank), F32),
            pltpu.VMEM((rank, rank + 2 * tile), F32),
            pltpu.VMEM((SLAB, rank + 2 * tile), F32),
        ],
        compiler_params=BIG,
        name="factor",
    )(field, *chunks)
    first_got = lax.ppermute(first, "fib", [(i, i - 1) for i in odd])
    core_values = jnp.where(lax.axis_index("fib") % 2 == 1, second, first_got)
    return core_values[None, None]


def solution(mesh):
    placed = (P("pln", "fib", None, None), P(), P("pln", None, None), P("pln", "fib", None), P())
    return jax.shard_map(
        per_device,
        mesh=mesh,
        in_specs=placed,
        out_specs=P("pln", "fib", None, None),
        check_vma=False,
    )
```

time: 70.5 us -> 93.1 us (1.32)
  waiting for transfers between devices: 12.7 us -> 54.5 us
  blocking collectives: 36.8 us -> 0 us
  starting transfers between devices: 6.85 us -> 22 us
    ppermute x5 -> x21, waiting for transfers between devices: 12.7 us -> 54.5 us  [the longest x1 53.3 us: per_device(): first_got = lax.ppermute(first, 'fib', [(i, i - 1) for i in odd])]
    all_to_all x3 -> x0, blocking collectives: 36.8 us -> none  [the longest x2 20.5 us: plane_exchange(): lax.all_to_all(value, both, split_axis=0, concat_axis=0, axis_index_group...]
    ppermute x5 -> x21, starting transfers between devices: 6.85 us -> 22 us  [the longest x16 10.7 us: swapped(): return lax.ppermute(value, ('fib', 'pln'), pairs)]
    unnamed x10 -> x11, local copies, waits for them, and re-layouts: 3.55 us -> 3.57 us
  transfers between devices with their start and end apart: 5 -> 21, of which waited for: 5 -> 3; matrix products, arithmetic and copies ran while one was open for 0% -> 0% of each run, Pallas kernels for 1% -> 1%
where the time goes in v5:
time: 93.1 us; the launch traced here: 92.4 us
  waiting for transfers between devices  54.5 us (59%)
  starting transfers between devices  22 us (24%)
  Pallas kernels  11 us (12%)
  local copies, waits for them, and re-layouts  3.71 us (4%)
    ppermute x1, waiting for transfers between devices, per_device(): first_got = lax.ppermute(first, 'fib', [(i, i - 1) for i in odd])  53.3 us
    ppermute x16, starting transfers between devices, swapped(): return lax.ppermute(value, ('fib', 'pln'), pairs)  10.7 us
    pallas_call x1, Pallas kernels, per_device(): pl.pallas_call(functools.partial(factor_kernel, mid), out_shape=[jax.Shap...  6.02 us
    ppermute x1, starting transfers between devices, per_device(): lax.ppermute(last, 'fib', [(i - 1, (i + 2) % owners) for i in odd])  5.7 us
    unnamed x11, local copies, waits for them, and re-layouts  3.57 us
    ppermute x1, starting transfers between devices, per_device(): near_got = lax.ppermute(near, 'fib', [(i - 1, i) for i in odd])  2.38 us
  transfers between devices with their start and end apart: 21, of which 3 were waited for; matrix products, arithmetic and copies ran while one was open for 0% of the time, Pallas kernels for 1%

profile of v5, /device:TPU:0, one launch (start us, length us, event | category | flops | bytes accessed | tf_op | source)
XLA Modules:
  0.0 92.4 jit_solution(1543081273589202561)
XLA Ops:
  0.0 0.0 copy-start.4
  0.0 0.0 copy-start
  0.0 1.6 %copy-done = f32[1000,512]{1,0:T(8,128)S(1)} copy-done((f32[1000,512]{1,0:T(8,128)S(1)}, f32[1000,512]{1,0:T(8,128)}, u32[]{:S(2)}) %copy-start) | copy-done | bytes 2048024
  1.6 0.0 copy-start.1
  1.6 1.3 %copy-done.1 = f32[1,1,288,1000]{3,2,1,0:T(8,128)S(1)} copy-done((f32[1,1,288,1000]{3,2,1,0:T(8,128)S(1)}, f32[1,1,288,1000]{3,2,1,0:T(8,128)}, u32[]{:S(2)}) %copy-start.1) | copy-done | bytes 1152024
  2.9 0.0 copy-start.3
  2.9 0.7 copy-done.3
  3.5 1.8 %interp.1 = (f32[192,512]{1,0:T(8,128)S(1)}, f32[192,512]{1,0:T(8,128)S(1)}, f32[96,512]{1,0:T(8,128)S(1)}) custom-call(s32[3,1,16]{2,1,0:T(1,128)S(1)} %bitcast.22, f32[288,1000]{1,0:T(8,128)S(1)} %bitcast.21, f32[1000,512]{1,0:T(8,128)S(1)} %copy-done), custom_call_target="tpu_custom_call" | custom-call | tf_op jit(solution)/shard_map/interp/pallas_call | solution.py:214
  5.4 2.4 %collective-permute-start.1 = (f32[192,512]{1,0:T(8,128)S(1)}, f32[192,512]{1,0:T(8,128)S(1)}, u32[]{:S(2)}, u32[]{:S(2)}) collective-permute-start(f32[192,512]{1,0:T(8,128)S(1)} %get-tuple-element.17.own_ref), channel_id=1, source_target_pairs={{0,2},{4,6},{8,10},{12,14},{16,18},{20,22},{24,26},{28,30},{1,3},{... | collective-permute-start | bytes 1179656 | tf_op jit(solution)/shard_map/ppermute | solution.py:225
  7.8 0.7 collective-permute-start.2
  8.5 5.7 %collective-permute-start.3 = (f32[96,512]{1,0:T(8,128)S(1)}, f32[96,512]{1,0:T(8,128)S(1)}, u32[]{:S(2)}, u32[]{:S(2)}) collective-permute-start(f32[96,512]{1,0:T(8,128)S(1)} %get-tuple-element.19), channel_id=1, source_target_pairs={{0,6},{4,10},{8,14},{12,18},{16,22},{20,26},{24,30},{28,2},{1,7},{... | collective-permute-start | bytes 589832 | tf_op jit(solution)/shard_map/ppermute | solution.py:224
  14.2 0.0 copy-done.4
  14.2 1.3 %collective-permute-start = (s32[1,192]{1,0:T(1,128)S(1)}, s32[1,192]{1,0:T(1,128)S(1)}, u32[]{:S(2)}, u32[]{:S(2)}) collective-permute-start(s32[1,192]{1,0:T(1,128)S(1)} %bitcast.24), channel_id=1, source_target_pairs={{0,2},{4,6},{8,10},{12,14},{16,18},{20,22},{24,26},{28,30},{1,3},{... | collective-permute-start | bytes 2312 | tf_op jit(solution)/shard_map/ppermute | solution.py:213
  15.5 0.8 collective-permute-done.order_ref
  16.3 1.1 %pick.1.pick_ref = f32[384,288]{1,0:T(8,128)S(1)} custom-call(s32[3,1,16]{2,1,0:T(1,128)S(1)} %bitcast.23, s32[1,192]{1,0:T(1,128)S(1)} %collective-permute-done.order_ref, s32[1,192]{1,0:T(1,128)S(1)} %bitcast.25), custom_call_target="tpu_custom_call" | custom-call | tf_op jit(solution)/shard_map/pick/pallas_call | solution.py:226
  17.4 0.4 collective-permute-done.3.last_ref
  17.8 0.0 collective-permute-done.1.near_ref
  17.8 0.0 collective-permute-done.2.far_ref
  17.8 0.8 order.1
  18.7 0.0 copy-start.2
  18.8 0.1 slice_bitcast_fusion
  18.8 0.7 collective-permute-start.10
  19.5 0.7 collective-permute-start.4
  20.2 0.7 collective-permute-start.5
  20.9 0.7 collective-permute-start.6
  21.5 0.7 collective-permute-start.7
  22.2 0.0 collective-permute-done.10.refs_7_
  22.2 0.7 collective-permute-start.8
  22.9 0.0 collective-permute-done.4.refs_1_
  22.9 0.7 collective-permute-start.9
  23.6 0.0 collective-permute-done.5.refs_2_
  23.6 0.0 collective-permute-done.6.refs_3_
  23.6 0.0 collective-permute-done.7.refs_4_
  23.6 0.0 collective-permute-done.8.refs_5_
  23.6 0.0 collective-permute-done.9.refs_6_
  23.6 0.0 copy-done.2
  23.6 1.2 %image.1 = (f32[192,128]{1,0:T(8,128)S(1)}, f32[192,128]{1,0:T(8,128)S(1)}, f32[192,128]{1,0:T(8,128)S(1)}, f32[192,128]{1,0:T(8,128)S(1)}, f32[768,256]{1,0:T(8,128)S(1)}) custom-call(f32[192,128]{1,0:T(8,128)S(1)} %get-tuple-element.36.refs_0_, f32[192,128]{1,0:T(8,128)S(1)} %collective-permute-done.4.refs_1_, ...), custom_call_target="tpu_custom_call" | custom-call | tf_op jit(solution)/shard_map/image/pallas_call | solution.py:258
  24.9 0.7 collective-permute-start.11
  25.6 0.7 collective-permute-start.12
  26.2 0.7 collective-permute-start.13
  26.9 0.0 collective-permute-done.11
  26.9 0.0 collective-permute-done.12
  26.9 0.0 collective-permute-done.13
  27.0 0.7 collective-permute-start.14
  27.6 0.7 collective-permute-start.15
  28.3 0.7 collective-permute-start.16
  29.0 0.0 collective-permute-done.14
  29.0 0.0 collective-permute-done.15
  29.0 0.0 collective-permute-done.16
  29.1 0.7 collective-permute-start.17
  29.7 0.7 collective-permute-start.18
  30.4 0.7 collective-permute-start.19
  31.1 0.0 collective-permute-done.17.refs_1_
  31.1 0.0 collective-permute-done.18.refs_2_
  31.1 0.0 collective-permute-done.19.refs_3_
  31.1 6.0 %factor.1 = (f32[128,128]{1,0:T(8,128)S(1)}, f32[128,128]{1,0:T(8,128)S(1)}) custom-call(f32[768,256]{1,0:T(8,128)S(1)} %get-tuple-element.22.field_ref, f32[192,128]{1,0:T(8,128)S(1)} %add_add_fusion.refs_0_, f32[192,128]{1,0:T(8,128)S(1)} %collective-permute-done.17.refs_1_, f32[192,128]{1,0:T(8,128)S(1)} %collective-permute-done.18.refs_2_, ...), custom_call_target="tpu_custom_call" | custom-call | tf_op jit(solution)/shard_map/factor/pallas_call | solution.py:274
  37.1 1.3 %collective-permute-start.20 = (f32[128,128]{1,0:T(8,128)S(1)}, f32[128,128]{1,0:T(8,128)S(1)}, u32[]{:S(2)}, u32[]{:S(2)}) collective-permute-start(f32[128,128]{1,0:T(8,128)S(1)} %get-tuple-element.28), channel_id=1, source_target_pairs={{2,0},{6,4},{10,8},{14,12},{18,16},{22,20},{26,24},{30,28},{3,1},{... | collective-permute-start | bytes 196616 | tf_op jit(solution)/shard_map/ppermute | solution.py:287
  38.4 53.3 %collective-permute-done.20 = f32[128,128]{1,0:T(8,128)S(1)} collective-permute-done((f32[128,128]{1,0:T(8,128)S(1)}, f32[128,128]{1,0:T(8,128)S(1)}, u32[]{:S(2)}, u32[]{:S(2)}) %collective-permute-start.20) | collective-permute-done | bytes 65568 | tf_op jit(solution)/shard_map/ppermute | solution.py:287
  91.7 0.6 select_bitcast_fusion
  (6 shorter events, 0.2 us)
Async XLA Ops:
  0.0 14.2 %copy-start.4 = (s32[1,1,192]{2,1,0:T(1,128)S(1)}, s32[1,1,192]{2,1,0:T(1,128)}, u32[]{:S(2)}) copy-start(s32[1,1,192]{2,1,0:T(1,128)} %param.8) | copy-start | bytes 2308
  0.0 1.6 %copy-start = (f32[1000,512]{1,0:T(8,128)S(1)}, f32[1000,512]{1,0:T(8,128)}, u32[]{:S(2)}) copy-start(f32[1000,512]{1,0:T(8,128)} %interp_ref.1) | copy-start | bytes 6144004
  1.6 1.3 %copy-start.1 = (f32[1,1,288,1000]{3,2,1,0:T(8,128)S(1)}, f32[1,1,288,1000]{3,2,1,0:T(8,128)}, u32[]{:S(2)}) copy-start(f32[1,1,288,1000]{3,2,1,0:T(8,128)} %param.5) | copy-start | bytes 3456004
  2.9 0.7 copy-start.3
  5.4 12.4 %collective-permute-start.1 = (f32[192,512]{1,0:T(8,128)S(1)}, f32[192,512]{1,0:T(8,128)S(1)}, u32[]{:S(2)}, u32[]{:S(2)}) collective-permute-start(f32[192,512]{1,0:T(8,128)S(1)} %get-tuple-element.17.own_ref), channel_id=1, source_target_pairs={{0,2},{4,6},{8,10},{12,14},{16,18},{20,22},{24,26},{28,30},{1,3},{... | collective-permute-start | bytes 1179656 | tf_op jit(solution)/shard_map/ppermute | solution.py:225
  7.8 10.0 %collective-permute-start.2 = (f32[192,512]{1,0:T(8,128)S(1)}, f32[192,512]{1,0:T(8,128)S(1)}, u32[]{:S(2)}, u32[]{:S(2)}) collective-permute-start(f32[192,512]{1,0:T(8,128)S(1)} %get-tuple-element.18), channel_id=1, source_target_pairs={{2,6},{6,10},{10,14},{14,18},{18,22},{22,26},{26,30},{30,2},{3,7},... | collective-permute-start | bytes 1179656 | tf_op jit(solution)/shard_map/ppermute | solution.py:223
  8.5 9.3 %collective-permute-start.3 = (f32[96,512]{1,0:T(8,128)S(1)}, f32[96,512]{1,0:T(8,128)S(1)}, u32[]{:S(2)}, u32[]{:S(2)}) collective-permute-start(f32[96,512]{1,0:T(8,128)S(1)} %get-tuple-element.19), channel_id=1, source_target_pairs={{0,6},{4,10},{8,14},{12,18},{16,22},{20,26},{24,30},{28,2},{1,7},{... | collective-permute-start | bytes 589832 | tf_op jit(solution)/shard_map/ppermute | solution.py:224
  14.2 2.1 %collective-permute-start = (s32[1,192]{1,0:T(1,128)S(1)}, s32[1,192]{1,0:T(1,128)S(1)}, u32[]{:S(2)}, u32[]{:S(2)}) collective-permute-start(s32[1,192]{1,0:T(1,128)S(1)} %bitcast.24), channel_id=1, source_target_pairs={{0,2},{4,6},{8,10},{12,14},{16,18},{20,22},{24,26},{28,30},{1,3},{... | collective-permute-start | bytes 2312 | tf_op jit(solution)/shard_map/ppermute | solution.py:213
  18.7 5.0 %copy-start.2 = (f32[768,128]{1,0:T(8,128)S(1)}, f32[768,128]{1,0:T(8,128)}, u32[]{:S(2)}) copy-start(f32[768,128]{1,0:T(8,128)} %refs_8_.1) | copy-start | bytes 1179652
  18.8 3.4 %collective-permute-start.10 = (f32[192,128]{1,0:T(8,128)S(1)}, f32[192,128]{1,0:T(8,128)S(1)}, u32[]{:S(2)}, u32[]{:S(2)}) collective-permute-start(f32[192,128]{1,0:T(8,128)S(1)} %get-tuple-element.29), channel_id=1, source_target_pairs={{2,30},{3,31},{6,26},{7,27},{10,22},{11,23},{14,18},{15,19},{18,14... | collective-permute-start | bytes 294920 | tf_op jit(solution)/shard_map/ppermute | solution.py:189
  19.5 3.4 %collective-permute-start.4 = (f32[192,128]{1,0:T(8,128)S(1)}, f32[192,128]{1,0:T(8,128)S(1)}, u32[]{:S(2)}, u32[]{:S(2)}) collective-permute-start(f32[192,128]{1,0:T(8,128)S(1)} %get-tuple-element.35), channel_id=1, source_target_pairs={{2,6},{3,7},{6,2},{7,3},{10,14},{11,15},{14,10},{15,11},{18,22},{1... | collective-permute-start | bytes 294920 | tf_op jit(solution)/shard_map/ppermute | solution.py:189
  20.2 3.4 %collective-permute-start.5 = (f32[192,128]{1,0:T(8,128)S(1)}, f32[192,128]{1,0:T(8,128)S(1)}, u32[]{:S(2)}, u32[]{:S(2)}) collective-permute-start(f32[192,128]{1,0:T(8,128)S(1)} %get-tuple-element.34), channel_id=1, source_target_pairs={{2,10},{3,11},{6,14},{7,15},{10,2},{11,3},{14,6},{15,7},{18,26},{1... | collective-permute-start | bytes 294920 | tf_op jit(solution)/shard_map/ppermute | solution.py:189
  20.9 2.7 %collective-permute-start.6 = (f32[192,128]{1,0:T(8,128)S(1)}, f32[192,128]{1,0:T(8,128)S(1)}, u32[]{:S(2)}, u32[]{:S(2)}) collective-permute-start(f32[192,128]{1,0:T(8,128)S(1)} %get-tuple-element.33), channel_id=1, source_target_pairs={{2,14},{3,15},{6,10},{7,11},{10,6},{11,7},{14,2},{15,3},{18,30},{1... | collective-permute-start | bytes 294920 | tf_op jit(solution)/shard_map/ppermute | solution.py:189
  21.5 2.1 %collective-permute-start.7 = (f32[192,128]{1,0:T(8,128)S(1)}, f32[192,128]{1,0:T(8,128)S(1)}, u32[]{:S(2)}, u32[]{:S(2)}) collective-permute-start(f32[192,128]{1,0:T(8,128)S(1)} %get-tuple-element.32), channel_id=1, source_target_pairs={{2,18},{3,19},{6,22},{7,23},{10,26},{11,27},{14,30},{15,31},{18,2}... | collective-permute-start | bytes 294920 | tf_op jit(solution)/shard_map/ppermute | solution.py:189
  22.2 1.4 %collective-permute-start.8 = (f32[192,128]{1,0:T(8,128)S(1)}, f32[192,128]{1,0:T(8,128)S(1)}, u32[]{:S(2)}, u32[]{:S(2)}) collective-permute-start(f32[192,128]{1,0:T(8,128)S(1)} %get-tuple-element.31), channel_id=1, source_target_pairs={{2,22},{3,23},{6,18},{7,19},{10,30},{11,31},{14,26},{15,27},{18,6}... | collective-permute-start | bytes 294920 | tf_op jit(solution)/shard_map/ppermute | solution.py:189
  22.9 0.7 collective-permute-start.9
  24.9 2.0 %collective-permute-start.11 = (f32[192,128]{1,0:T(8,128)S(1)}, f32[192,128]{1,0:T(8,128)S(1)}, u32[]{:S(2)}, u32[]{:S(2)}) collective-permute-start(f32[192,128]{1,0:T(8,128)S(1)} %get-tuple-element.24), channel_id=1, source_target_pairs={{2,7},{3,6},{6,3},{7,2},{10,15},{11,14},{14,11},{15,10},{18,23},{1... | collective-permute-start | bytes 294920 | tf_op jit(solution)/shard_map/ppermute | solution.py:189
  25.6 1.4 %collective-permute-start.12 = (f32[192,128]{1,0:T(8,128)S(1)}, f32[192,128]{1,0:T(8,128)S(1)}, u32[]{:S(2)}, u32[]{:S(2)}) collective-permute-start(f32[192,128]{1,0:T(8,128)S(1)} %get-tuple-element.25), channel_id=1, source_target_pairs={{2,6},{3,7},{6,2},{7,3},{10,14},{11,15},{14,10},{15,11},{18,22},{1... | collective-permute-start | bytes 294920 | tf_op jit(solution)/shard_map/ppermute | solution.py:189
  26.2 0.7 collective-permute-start.13
  27.0 2.0 %collective-permute-start.14 = (f32[192,128]{1,0:T(8,128)S(1)}, f32[192,128]{1,0:T(8,128)S(1)}, u32[]{:S(2)}, u32[]{:S(2)}) collective-permute-start(f32[192,128]{1,0:T(8,128)S(1)} %add_add_fusion.1), channel_id=1, source_target_pairs={{2,26},{3,27},{6,30},{7,31},{10,18},{11,19},{14,22},{15,23},{18,10... | collective-permute-start | bytes 294920 | tf_op jit(solution)/shard_map/ppermute | solution.py:189
  27.6 1.4 %collective-permute-start.15 = (f32[192,128]{1,0:T(8,128)S(1)}, f32[192,128]{1,0:T(8,128)S(1)}, u32[]{:S(2)}, u32[]{:S(2)}) collective-permute-start(f32[192,128]{1,0:T(8,128)S(1)} %add_add_fusion.1), channel_id=1, source_target_pairs={{2,10},{3,11},{6,14},{7,15},{10,2},{11,3},{14,6},{15,7},{18,26},{1... | collective-permute-start | bytes 294920 | tf_op jit(solution)/shard_map/ppermute | solution.py:189
  28.3 0.7 collective-permute-start.16
  29.1 2.0 %collective-permute-start.17 = (f32[192,128]{1,0:T(8,128)S(1)}, f32[192,128]{1,0:T(8,128)S(1)}, u32[]{:S(2)}, u32[]{:S(2)}) collective-permute-start(f32[192,128]{1,0:T(8,128)S(1)} %add_add_fusion.refs_0_), channel_id=1, source_target_pairs={{2,3},{3,2},{6,7},{7,6},{10,11},{11,10},{14,15},{15,14},{18,19},{1... | collective-permute-start | bytes 294920 | tf_op jit(solution)/shard_map/ppermute | solution.py:189
  29.7 1.4 %collective-permute-start.18 = (f32[192,128]{1,0:T(8,128)S(1)}, f32[192,128]{1,0:T(8,128)S(1)}, u32[]{:S(2)}, u32[]{:S(2)}) collective-permute-start(f32[192,128]{1,0:T(8,128)S(1)} %add_add_fusion.refs_0_), channel_id=1, source_target_pairs={{2,6},{3,7},{6,2},{7,3},{10,14},{11,15},{14,10},{15,11},{18,22},{1... | collective-permute-start | bytes 294920 | tf_op jit(solution)/shard_map/ppermute | solution.py:189
  30.4 0.7 collective-permute-start.19
  37.1 54.6 %collective-permute-start.20 = (f32[128,128]{1,0:T(8,128)S(1)}, f32[128,128]{1,0:T(8,128)S(1)}, u32[]{:S(2)}, u32[]{:S(2)}) collective-permute-start(f32[128,128]{1,0:T(8,128)S(1)} %get-tuple-element.28), channel_id=1, source_target_pairs={{2,0},{6,4},{10,8},{14,12},{18,16},{22,20},{26,24},{30,28},{3,1},{... | collective-permute-start | bytes 196616 | tf_op jit(solution)/shard_map/ppermute | solution.py:287

commit v6 on v5

--- a/solution.py
+++ b/solution.py
@@ -177,6 +177,18 @@
             work[after:, :] = work[after:, :] - drop[after:, :]
 
 
+def choose_kernel(own_ref, got_ref, out_ref):
+    second = lax.rem(lax.axis_index("fib"), 2) == 1
+
+    @pl.when(second)
+    def _():
+        out_ref[...] = own_ref[...]
+
+    @pl.when(jnp.logical_not(second))
+    def _():
+        out_ref[...] = got_ref[...]
+
+
 def swapped(value, bits, step=1):
     apart = [bit for at, bit in enumerate(reversed(bits)) if step >> at & 1]
     peers = {axis: sum(mask for name, mask in apart if name == axis) for axis in ("fib", "pln")}
@@ -184,8 +196,8 @@
     pairs = []
     for i in range(owners * planes):
         fib, pln = divmod(i, planes)
-        if fib % 2:
-            pairs.append((i, (fib ^ peers["fib"]) * planes + (pln ^ peers["pln"])))
+        to = (fib ^ peers["fib"]) * planes + (pln ^ peers["pln"])
+        pairs.append((i, to if fib % 2 else i))
     return lax.ppermute(value, ("fib", "pln"), pairs)
 
 
@@ -208,9 +220,9 @@
     elements = slot_order.shape[2]
     length, rank = start_basis.shape
     tile = points * elements // length
-    odd = range(1, owners, 2)
-
-    order_first = lax.ppermute(slot_order[0], "fib", [(i - 1, i) for i in odd])
+    core_swap = [(i, i ^ 1) for i in range(owners)]
+
+    order_first = lax.ppermute(slot_order[0], "fib", core_swap)
     near, far, last = pl.pallas_call(
         functools.partial(interp_kernel, owners),
         out_shape=[jax.ShapeDtypeStruct((n * capacity, points), F32) for n in (2, 2, 1)],
@@ -220,9 +232,10 @@
         compiler_params=BIG,
         name="interp",
     )(table, nodes, interp_matrix)
-    far_got = lax.ppermute(far, "fib", [(i, (i + 2) % owners) for i in odd])
-    last_got = lax.ppermute(last, "fib", [(i - 1, (i + 2) % owners) for i in odd])
-    near_got = lax.ppermute(near, "fib", [(i - 1, i) for i in odd])
+    far_got = lax.ppermute(far, "fib", [(i, (i + 2) % owners if i % 2 else i) for i in range(owners)])
+    onward = [(i, i - 1 if i % 2 else (i + 3) % owners) for i in range(owners)]
+    last_got = lax.ppermute(last, "fib", onward)
+    near_got = lax.ppermute(near, "fib", core_swap)
     pick = pl.pallas_call(
         functools.partial(pick_kernel, capacity, elements // owners),
         out_shape=jax.ShapeDtypeStruct((2 * elements, capacity * window), F32),
@@ -284,8 +297,13 @@
         compiler_params=BIG,
         name="factor",
     )(field, *chunks)
-    first_got = lax.ppermute(first, "fib", [(i, i - 1) for i in odd])
-    core_values = jnp.where(lax.axis_index("fib") % 2 == 1, second, first_got)
+    core_values = pl.pallas_call(
+        choose_kernel,
+        out_shape=jax.ShapeDtypeStruct((rank, tile), F32),
+        in_specs=[VMEM] * 2,
+        out_specs=VMEM,
+        name="choose",
+    )(second, lax.ppermute(first, "fib", core_swap))
     return core_values[None, None]
 
 

time: 93.1 us -> 92.6 us (level)
  waiting for transfers between devices: 54.5 us -> 5.18 us
  starting transfers between devices: 22 us -> 68.8 us
  Pallas kernels: 11 us -> 12.5 us
  local copies, waits for them, and re-layouts: 3.71 us -> 4.98 us
    ppermute x5, waiting for transfers between devices: 54.5 us -> 5.14 us  [the longest x1 3.09 us: per_device(): last_got = lax.ppermute(last, 'fib', onward)]
    ppermute x5, starting transfers between devices: 11.3 us -> 58.2 us  [the longest x1 52.5 us: per_device(): lax.ppermute(first, 'fib', core_swap)]
    pallas_call x0 -> x1, Pallas kernels: none -> 1.5 us  [per_device(): pl.pallas_call(choose_kernel, out_shape=jax.ShapeDtypeStruct((rank, tile)...]
    unnamed x11 -> x15, local copies, waits for them, and re-layouts: 3.57 us -> 4.84 us
where the time goes in v6:
time: 92.6 us; the launch traced here: 92 us
  starting transfers between devices  68.8 us (74%)
  Pallas kernels  12.5 us (13%)
  waiting for transfers between devices  5.18 us (6%)
  local copies, waits for them, and re-layouts  4.98 us (5%)
    ppermute x1, starting transfers between devices, per_device(): lax.ppermute(first, 'fib', core_swap)  52.5 us
    ppermute x16, starting transfers between devices, swapped(): return lax.ppermute(value, ('fib', 'pln'), pairs)  10.7 us
    pallas_call x1, Pallas kernels, per_device(): pl.pallas_call(functools.partial(factor_kernel, mid), out_shape=[jax.Shap...  6.02 us
    unnamed x15, local copies, waits for them, and re-layouts  4.84 us
    ppermute x1, starting transfers between devices, per_device(): near_got = lax.ppermute(near, 'fib', core_swap)  3.78 us
    ppermute x1, waiting for transfers between devices, per_device(): last_got = lax.ppermute(last, 'fib', onward)  3.09 us
  transfers between devices with their start and end apart: 21, of which 3 were waited for; matrix products, arithmetic and copies ran while one was open for 0% of the time, Pallas kernels for 1%

profile of v6, /device:TPU:0, one launch (start us, length us, event | category | flops | bytes accessed | tf_op | source)
XLA Modules:
  0.0 92.0 jit_solution(10872300390895810768)
XLA Ops:
  0.0 0.0 copy-start.5
  0.0 0.0 copy-start
  0.0 1.6 %copy-done = f32[1000,512]{1,0:T(8,128)S(1)} copy-done((f32[1000,512]{1,0:T(8,128)S(1)}, f32[1000,512]{1,0:T(8,128)}, u32[]{:S(2)}) %copy-start) | copy-done | bytes 2048024
  1.6 0.0 copy-start.1
  1.6 1.3 %copy-done.1 = f32[1,1,288,1000]{3,2,1,0:T(8,128)S(1)} copy-done((f32[1,1,288,1000]{3,2,1,0:T(8,128)S(1)}, f32[1,1,288,1000]{3,2,1,0:T(8,128)}, u32[]{:S(2)}) %copy-start.1) | copy-done | bytes 1152024
  2.9 0.0 copy-start.4
  2.9 0.7 copy-done.4
  3.5 1.8 %interp.1 = (f32[192,512]{1,0:T(8,128)S(1)}, f32[192,512]{1,0:T(8,128)S(1)}, f32[96,512]{1,0:T(8,128)S(1)}) custom-call(s32[3,1,16]{2,1,0:T(1,128)S(1)} %bitcast.21, f32[288,1000]{1,0:T(8,128)S(1)} %bitcast.20, f32[1000,512]{1,0:T(8,128)S(1)} %copy-done), custom_call_target="tpu_custom_call" | custom-call | tf_op jit(solution)/shard_map/interp/pallas_call | solution.py:226
  5.4 0.7 collective-permute-start.2
  6.1 3.8 %collective-permute-start.1 = (f32[192,512]{1,0:T(8,128)S(1)}, f32[192,512]{1,0:T(8,128)S(1)}, u32[]{:S(2)}, u32[]{:S(2)}) collective-permute-start(f32[192,512]{1,0:T(8,128)S(1)} %get-tuple-element.17.own_ref), channel_id=1, source_target_pairs={{0,2},{2,0},{4,6},{6,4},{8,10},{10,8},{12,14},{14,12},{16,18},{18,... | collective-permute-start | bytes 1179656 | tf_op jit(solution)/shard_map/ppermute | solution.py:238
  9.8 1.2 %collective-permute-start.3 = (f32[96,512]{1,0:T(8,128)S(1)}, f32[96,512]{1,0:T(8,128)S(1)}, u32[]{:S(2)}, u32[]{:S(2)}) collective-permute-start(f32[96,512]{1,0:T(8,128)S(1)} %get-tuple-element.19), channel_id=1, source_target_pairs={{0,6},{2,0},{4,10},{6,4},{8,14},{10,8},{12,18},{14,12},{16,22},{18... | collective-permute-start | bytes 589832 | tf_op jit(solution)/shard_map/ppermute | solution.py:237
  11.1 0.0 copy-done.5
  11.1 0.0 collective-permute-start
  11.1 1.1 %collective-permute-done.order_ref = s32[1,192]{1,0:T(1,128)S(1)} collective-permute-done((s32[1,192]{1,0:T(1,128)S(1)}, s32[1,192]{1,0:T(1,128)S(1)}, u32[]{:S(2)}, u32[]{:S(2)}) %collective-permute-start) | collective-permute-done | bytes 800 | tf_op jit(solution)/shard_map/ppermute | solution.py:225
  12.2 1.1 %pick.1.pick_ref = f32[384,288]{1,0:T(8,128)S(1)} custom-call(s32[3,1,16]{2,1,0:T(1,128)S(1)} %bitcast.22, s32[1,192]{1,0:T(1,128)S(1)} %collective-permute-done.order_ref, s32[1,192]{1,0:T(1,128)S(1)} %bitcast.24), custom_call_target="tpu_custom_call" | custom-call | tf_op jit(solution)/shard_map/pick/pallas_call | solution.py:239
  13.3 3.1 %collective-permute-done.3.last_ref = f32[96,512]{1,0:T(8,128)S(1)} collective-permute-done((f32[96,512]{1,0:T(8,128)S(1)}, f32[96,512]{1,0:T(8,128)S(1)}, u32[]{:S(2)}, u32[]{:S(2)}) %collective-permute-start.3) | collective-permute-done | bytes 196640 | tf_op jit(solution)/shard_map/ppermute | solution.py:237
  16.4 0.0 collective-permute-done.2.far_ref
  16.4 0.0 collective-permute-done.1.near_ref
  16.4 0.8 order.1
  17.3 0.0 copy-start.2
  17.4 0.1 slice_bitcast_fusion
  17.5 0.7 collective-permute-start.10
  18.2 0.7 collective-permute-start.9
  18.8 0.7 collective-permute-start.8
  19.5 0.7 collective-permute-start.7
  20.2 0.7 collective-permute-start.6
  20.9 0.0 collective-permute-done.10.refs_7_
  20.9 0.7 collective-permute-start.5
  21.5 0.0 collective-permute-done.9.refs_6_
  21.6 0.7 collective-permute-start.4
  22.2 0.0 collective-permute-done.8.refs_5_
  22.2 0.0 collective-permute-done.7.refs_4_
  22.3 0.0 collective-permute-done.6.refs_3_
  22.3 0.0 collective-permute-done.5.refs_2_
  22.3 0.0 collective-permute-done.4.refs_1_
  22.3 0.0 copy-done.2
  22.3 1.2 %image.1 = (f32[192,128]{1,0:T(8,128)S(1)}, f32[192,128]{1,0:T(8,128)S(1)}, f32[192,128]{1,0:T(8,128)S(1)}, f32[192,128]{1,0:T(8,128)S(1)}, f32[768,256]{1,0:T(8,128)S(1)}) custom-call(f32[192,128]{1,0:T(8,128)S(1)} %get-tuple-element.36.refs_0_, f32[192,128]{1,0:T(8,128)S(1)} %collective-permute-done.4.refs_1_, ...), custom_call_target="tpu_custom_call" | custom-call | tf_op jit(solution)/shard_map/image/pallas_call | solution.py:271
  23.5 0.7 collective-permute-start.11
  24.2 0.7 collective-permute-start.12
  24.9 0.7 collective-permute-start.13
  25.6 0.0 collective-permute-done.11
  25.6 0.0 collective-permute-done.12
  25.6 0.0 collective-permute-done.13
  25.6 0.7 collective-permute-start.16
  26.3 0.7 collective-permute-start.15
  27.0 0.7 collective-permute-start.14
  27.6 0.0 collective-permute-done.16
  27.7 0.0 collective-permute-done.15
  27.7 0.0 collective-permute-done.14
  27.7 0.7 collective-permute-start.19
  28.4 0.7 collective-permute-start.18
  29.1 0.7 collective-permute-start.17
  29.7 0.0 collective-permute-done.19.refs_3_
  29.7 0.0 collective-permute-done.18.refs_2_
  29.8 0.0 collective-permute-done.17.refs_1_
  29.8 6.0 %factor.1 = (f32[128,128]{1,0:T(8,128)S(1)}, f32[128,128]{1,0:T(8,128)S(1)}) custom-call(f32[768,256]{1,0:T(8,128)S(1)} %get-tuple-element.22.field_ref, f32[192,128]{1,0:T(8,128)S(1)} %add_add_fusion.refs_0_, f32[192,128]{1,0:T(8,128)S(1)} %collective-permute-done.17.refs_1_, f32[192,128]{1,0:T(8,128)S(1)} %collective-permute-done.18.refs_2_, ...), custom_call_target="tpu_custom_call" | custom-call | tf_op jit(solution)/shard_map/factor/pallas_call | solution.py:287
  35.8 0.0 copy-start.3
  35.8 0.6 copy-done.3
  36.4 52.5 %collective-permute-start.20 = (f32[128,128]{1,0:T(8,128)S(1)}, f32[128,128]{1,0:T(8,128)S(1)}, u32[]{:S(2)}, u32[]{:S(2)}) collective-permute-start(f32[128,128]{1,0:T(8,128)S(1)} %get-tuple-element.28), channel_id=1, source_target_pairs={{0,2},{2,0},{4,6},{6,4},{8,10},{10,8},{12,14},{14,12},{16,18},{18,... | collective-permute-start | bytes 196616 | tf_op jit(solution)/shard_map/ppermute | solution.py:306
  88.9 0.9 collective-permute-done.20.got_ref
  89.8 0.0 copy-start.6
  89.8 0.6 copy-done.6
  90.4 1.5 %choose.1 = f32[128,128]{1,0:T(8,128)} custom-call(f32[128,128]{1,0:T(8,128)} %copy-done.3, f32[128,128]{1,0:T(8,128)} %copy-done.6), custom_call_target="tpu_custom_call" | custom-call | tf_op jit(solution)/shard_map/choose/pallas_call | solution.py:300
  (6 shorter events, 0.2 us)
Async XLA Ops:
  0.0 11.1 %copy-start.5 = (s32[1,1,192]{2,1,0:T(1,128)S(1)}, s32[1,1,192]{2,1,0:T(1,128)}, u32[]{:S(2)}) copy-start(s32[1,1,192]{2,1,0:T(1,128)} %param.8) | copy-start | bytes 2308
  0.0 1.6 %copy-start = (f32[1000,512]{1,0:T(8,128)S(1)}, f32[1000,512]{1,0:T(8,128)}, u32[]{:S(2)}) copy-start(f32[1000,512]{1,0:T(8,128)} %interp_ref.1) | copy-start | bytes 6144004
  1.6 1.3 %copy-start.1 = (f32[1,1,288,1000]{3,2,1,0:T(8,128)S(1)}, f32[1,1,288,1000]{3,2,1,0:T(8,128)}, u32[]{:S(2)}) copy-start(f32[1,1,288,1000]{3,2,1,0:T(8,128)} %param.5) | copy-start | bytes 3456004
  2.9 0.7 copy-start.4
  5.4 11.1 %collective-permute-start.2 = (f32[192,512]{1,0:T(8,128)S(1)}, f32[192,512]{1,0:T(8,128)S(1)}, u32[]{:S(2)}, u32[]{:S(2)}) collective-permute-start(f32[192,512]{1,0:T(8,128)S(1)} %get-tuple-element.18), channel_id=1, source_target_pairs={{0,0},{2,6},{4,4},{6,10},{8,8},{10,14},{12,12},{14,18},{16,16},{18... | collective-permute-start | bytes 1179656 | tf_op jit(solution)/shard_map/ppermute | solution.py:235
  6.1 10.4 %collective-permute-start.1 = (f32[192,512]{1,0:T(8,128)S(1)}, f32[192,512]{1,0:T(8,128)S(1)}, u32[]{:S(2)}, u32[]{:S(2)}) collective-permute-start(f32[192,512]{1,0:T(8,128)S(1)} %get-tuple-element.17.own_ref), channel_id=1, source_target_pairs={{0,2},{2,0},{4,6},{6,4},{8,10},{10,8},{12,14},{14,12},{16,18},{18,... | collective-permute-start | bytes 1179656 | tf_op jit(solution)/shard_map/ppermute | solution.py:238
  9.8 6.6 %collective-permute-start.3 = (f32[96,512]{1,0:T(8,128)S(1)}, f32[96,512]{1,0:T(8,128)S(1)}, u32[]{:S(2)}, u32[]{:S(2)}) collective-permute-start(f32[96,512]{1,0:T(8,128)S(1)} %get-tuple-element.19), channel_id=1, source_target_pairs={{0,6},{2,0},{4,10},{6,4},{8,14},{10,8},{12,18},{14,12},{16,22},{18... | collective-permute-start | bytes 589832 | tf_op jit(solution)/shard_map/ppermute | solution.py:237
  11.1 1.1 %collective-permute-start = (s32[1,192]{1,0:T(1,128)S(1)}, s32[1,192]{1,0:T(1,128)S(1)}, u32[]{:S(2)}, u32[]{:S(2)}) collective-permute-start(s32[1,192]{1,0:T(1,128)S(1)} %bitcast.23), channel_id=1, source_target_pairs={{0,2},{2,0},{4,6},{6,4},{8,10},{10,8},{12,14},{14,12},{16,18},{18,... | collective-permute-start | bytes 2312 | tf_op jit(solution)/shard_map/ppermute | solution.py:225
  17.3 5.0 %copy-start.2 = (f32[768,128]{1,0:T(8,128)S(1)}, f32[768,128]{1,0:T(8,128)}, u32[]{:S(2)}) copy-start(f32[768,128]{1,0:T(8,128)} %refs_8_.1) | copy-start | bytes 1179652
  17.5 3.4 %collective-permute-start.10 = (f32[192,128]{1,0:T(8,128)S(1)}, f32[192,128]{1,0:T(8,128)S(1)}, u32[]{:S(2)}, u32[]{:S(2)}) collective-permute-start(f32[192,128]{1,0:T(8,128)S(1)} %get-tuple-element.29), channel_id=1, source_target_pairs={{0,0},{1,1},{2,30},{3,31},{4,4},{5,5},{6,26},{7,27},{8,8},{9,9},{1... | collective-permute-start | bytes 294920 | tf_op jit(solution)/shard_map/ppermute | solution.py:201
  18.2 3.4 %collective-permute-start.9 = (f32[192,128]{1,0:T(8,128)S(1)}, f32[192,128]{1,0:T(8,128)S(1)}, u32[]{:S(2)}, u32[]{:S(2)}) collective-permute-start(f32[192,128]{1,0:T(8,128)S(1)} %get-tuple-element.30), channel_id=1, source_target_pairs={{0,0},{1,1},{2,26},{3,27},{4,4},{5,5},{6,30},{7,31},{8,8},{9,9},{1... | collective-permute-start | bytes 294920 | tf_op jit(solution)/shard_map/ppermute | solution.py:201
  18.8 3.4 %collective-permute-start.8 = (f32[192,128]{1,0:T(8,128)S(1)}, f32[192,128]{1,0:T(8,128)S(1)}, u32[]{:S(2)}, u32[]{:S(2)}) collective-permute-start(f32[192,128]{1,0:T(8,128)S(1)} %get-tuple-element.31), channel_id=1, source_target_pairs={{0,0},{1,1},{2,22},{3,23},{4,4},{5,5},{6,18},{7,19},{8,8},{9,9},{1... | collective-permute-start | bytes 294920 | tf_op jit(solution)/shard_map/ppermute | solution.py:201
  19.5 2.7 %collective-permute-start.7 = (f32[192,128]{1,0:T(8,128)S(1)}, f32[192,128]{1,0:T(8,128)S(1)}, u32[]{:S(2)}, u32[]{:S(2)}) collective-permute-start(f32[192,128]{1,0:T(8,128)S(1)} %get-tuple-element.32), channel_id=1, source_target_pairs={{0,0},{1,1},{2,18},{3,19},{4,4},{5,5},{6,22},{7,23},{8,8},{9,9},{1... | collective-permute-start | bytes 294920 | tf_op jit(solution)/shard_map/ppermute | solution.py:201
  20.2 2.1 %collective-permute-start.6 = (f32[192,128]{1,0:T(8,128)S(1)}, f32[192,128]{1,0:T(8,128)S(1)}, u32[]{:S(2)}, u32[]{:S(2)}) collective-permute-start(f32[192,128]{1,0:T(8,128)S(1)} %get-tuple-element.33), channel_id=1, source_target_pairs={{0,0},{1,1},{2,14},{3,15},{4,4},{5,5},{6,10},{7,11},{8,8},{9,9},{1... | collective-permute-start | bytes 294920 | tf_op jit(solution)/shard_map/ppermute | solution.py:201
  20.9 1.4 %collective-permute-start.5 = (f32[192,128]{1,0:T(8,128)S(1)}, f32[192,128]{1,0:T(8,128)S(1)}, u32[]{:S(2)}, u32[]{:S(2)}) collective-permute-start(f32[192,128]{1,0:T(8,128)S(1)} %get-tuple-element.34), channel_id=1, source_target_pairs={{0,0},{1,1},{2,10},{3,11},{4,4},{5,5},{6,14},{7,15},{8,8},{9,9},{1... | collective-permute-start | bytes 294920 | tf_op jit(solution)/shard_map/ppermute | solution.py:201
  21.6 0.7 collective-permute-start.4
  23.5 2.0 %collective-permute-start.11 = (f32[192,128]{1,0:T(8,128)S(1)}, f32[192,128]{1,0:T(8,128)S(1)}, u32[]{:S(2)}, u32[]{:S(2)}) collective-permute-start(f32[192,128]{1,0:T(8,128)S(1)} %get-tuple-element.24), channel_id=1, source_target_pairs={{0,0},{1,1},{2,7},{3,6},{4,4},{5,5},{6,3},{7,2},{8,8},{9,9},{10,15... | collective-permute-start | bytes 294920 | tf_op jit(solution)/shard_map/ppermute | solution.py:201
  24.2 1.4 %collective-permute-start.12 = (f32[192,128]{1,0:T(8,128)S(1)}, f32[192,128]{1,0:T(8,128)S(1)}, u32[]{:S(2)}, u32[]{:S(2)}) collective-permute-start(f32[192,128]{1,0:T(8,128)S(1)} %get-tuple-element.25), channel_id=1, source_target_pairs={{0,0},{1,1},{2,6},{3,7},{4,4},{5,5},{6,2},{7,3},{8,8},{9,9},{10,14... | collective-permute-start | bytes 294920 | tf_op jit(solution)/shard_map/ppermute | solution.py:201
  24.9 0.7 collective-permute-start.13
  25.6 2.0 %collective-permute-start.16 = (f32[192,128]{1,0:T(8,128)S(1)}, f32[192,128]{1,0:T(8,128)S(1)}, u32[]{:S(2)}, u32[]{:S(2)}) collective-permute-start(f32[192,128]{1,0:T(8,128)S(1)} %add_add_fusion.1), channel_id=1, source_target_pairs={{0,0},{1,1},{2,18},{3,19},{4,4},{5,5},{6,22},{7,23},{8,8},{9,9},{1... | collective-permute-start | bytes 294920 | tf_op jit(solution)/shard_map/ppermute | solution.py:201
  26.3 1.4 %collective-permute-start.15 = (f32[192,128]{1,0:T(8,128)S(1)}, f32[192,128]{1,0:T(8,128)S(1)}, u32[]{:S(2)}, u32[]{:S(2)}) collective-permute-start(f32[192,128]{1,0:T(8,128)S(1)} %add_add_fusion.1), channel_id=1, source_target_pairs={{0,0},{1,1},{2,10},{3,11},{4,4},{5,5},{6,14},{7,15},{8,8},{9,9},{1... | collective-permute-start | bytes 294920 | tf_op jit(solution)/shard_map/ppermute | solution.py:201
  27.0 0.7 collective-permute-start.14
  27.7 2.0 %collective-permute-start.19 = (f32[192,128]{1,0:T(8,128)S(1)}, f32[192,128]{1,0:T(8,128)S(1)}, u32[]{:S(2)}, u32[]{:S(2)}) collective-permute-start(f32[192,128]{1,0:T(8,128)S(1)} %add_add_fusion.refs_0_), channel_id=1, source_target_pairs={{0,0},{1,1},{2,7},{3,6},{4,4},{5,5},{6,3},{7,2},{8,8},{9,9},{10,15... | collective-permute-start | bytes 294920 | tf_op jit(solution)/shard_map/ppermute | solution.py:201
  28.4 1.4 %collective-permute-start.18 = (f32[192,128]{1,0:T(8,128)S(1)}, f32[192,128]{1,0:T(8,128)S(1)}, u32[]{:S(2)}, u32[]{:S(2)}) collective-permute-start(f32[192,128]{1,0:T(8,128)S(1)} %add_add_fusion.refs_0_), channel_id=1, source_target_pairs={{0,0},{1,1},{2,6},{3,7},{4,4},{5,5},{6,2},{7,3},{8,8},{9,9},{10,14... | collective-permute-start | bytes 294920 | tf_op jit(solution)/shard_map/ppermute | solution.py:201
  29.1 0.7 collective-permute-start.17
  35.8 0.6 copy-start.3
  36.4 53.4 %collective-permute-start.20 = (f32[128,128]{1,0:T(8,128)S(1)}, f32[128,128]{1,0:T(8,128)S(1)}, u32[]{:S(2)}, u32[]{:S(2)}) collective-permute-start(f32[128,128]{1,0:T(8,128)S(1)} %get-tuple-element.28), channel_id=1, source_target_pairs={{0,2},{2,0},{4,6},{6,4},{8,10},{10,8},{12,14},{14,12},{16,18},{18,... | collective-permute-start | bytes 196616 | tf_op jit(solution)/shard_map/ppermute | solution.py:306
  89.8 0.6 copy-start.6

commit v7 on v5

--- a/solution.py
+++ b/solution.py
@@ -29,12 +29,12 @@
     return out + lax.dot_general(lh, rh, dims, preferred_element_type=F32)
 
 
-def interp_kernel(owners, table_ref, node_ref, interp_ref, near_ref, far_ref, last_ref, grid_scr):
-    rows = last_ref.shape[0]
+def interp_kernel(owners, table_ref, node_ref, interp_ref, zero_ref, one_ref, send_ref, grid_scr):
+    rows = zero_ref.shape[0]
     slots = node_ref.shape[0]
     own = lax.axis_index("fib")
     grid_scr[:slots, :] = dot3(halves(node_ref[...]), halves(interp_ref[...]), ((1,), (0,)))
-    near_ref[:rows, :] = grid_scr[:rows, :]
+    zero_ref[...] = grid_scr[:rows, :]
     start = table_ref[0, 0, own]
     for distance in range(1, 3):
         shift = lax.rem(start, SLAB)
@@ -42,22 +42,25 @@
         wide = grid_scr[pl.ds(at, rows + SLAB), :]
         piece = pltpu.roll(wide, lax.rem(rows + SLAB - shift, rows + SLAB), 0)[:rows, :]
         if distance == 1:
-            near_ref[rows:, :] = piece
-            far_ref[:rows, :] = piece
+            one_ref[...] = piece
+            send_ref[:rows, :] = piece
         else:
-            far_ref[rows:, :] = piece
-            last_ref[...] = piece
+            send_ref[rows:, :] = piece
         start = start + table_ref[distance, 0, lax.rem(own + distance, owners)]
 
-
-def pick_kernel(rows, per_tile, table_ref, order_ref, order_own_ref, out_ref):
+    @pl.when(lax.rem(own, 2) == 0)
+    def _():
+        send_ref[:rows, :] = send_ref[rows:, :]
+
+
+def pick_kernel(rows, per_tile, table_ref, order_ref, order_next_ref, out_ref):
     elements = order_ref.shape[1]
     slots = out_ref.shape[1]
     chip = lax.div(lax.axis_index("fib"), 2)
     rank_at = lax.broadcasted_iota(jnp.int32, (elements, slots), 0)
     slot_at = lax.broadcasted_iota(jnp.int32, (elements, slots), 1)
     row = lax.broadcasted_iota(jnp.int32, (elements, elements), 0)
-    for core, order in enumerate((order_ref, order_own_ref)):
+    for core, order in enumerate((order_ref, order_next_ref)):
         from_slot = jnp.zeros((elements, slots), jnp.bool_)
         start = 0
         for distance in range(slots // rows - 1, -1, -1):
@@ -75,12 +78,12 @@
         )
 
 
-def order_kernel(pick_ref, own_ref, near_ref, far_ref, last_ref, *outs):
-    rows = last_ref.shape[0]
+def order_kernel(pick_ref, zero_ref, one_ref, next_zero_ref, back_ref, back_two_ref, *outs):
+    rows = zero_ref.shape[0]
     elements = outs[0].shape[0]
     sources = (
-        (near_ref[:rows, :], far_ref[:rows, :], last_ref[...]),
-        (own_ref[:rows, :], near_ref[rows:, :], far_ref[rows:, :]),
+        (zero_ref[...], back_ref[:rows, :], back_two_ref[...]),
+        (next_zero_ref[...], one_ref[...], back_ref[rows:, :]),
     )
     for core, pieces in enumerate(sources):
         pick = pick_ref[core * elements : (core + 1) * elements, :].astype(BF16)
@@ -176,16 +179,22 @@
             )
             work[after:, :] = work[after:, :] - drop[after:, :]
 
-
-def swapped(value, bits, step=1):
+    @pl.when(lax.rem(lax.axis_index("fib"), 2) == 1)
+    def _():
+        for out in out_refs:
+            out[...] = jnp.zeros_like(out)
+
+
+def crossed(value, bits, step, to_core):
     apart = [bit for at, bit in enumerate(reversed(bits)) if step >> at & 1]
     peers = {axis: sum(mask for name, mask in apart if name == axis) for axis in ("fib", "pln")}
     owners, planes = lax.axis_size("fib"), lax.axis_size("pln")
     pairs = []
     for i in range(owners * planes):
         fib, pln = divmod(i, planes)
-        if fib % 2:
-            pairs.append((i, (fib ^ peers["fib"]) * planes + (pln ^ peers["pln"])))
+        if fib % 2 != to_core:
+            fib, pln = fib ^ peers["fib"], pln ^ peers["pln"]
+        pairs.append((i, (fib ^ 1) * planes + pln))
     return lax.ppermute(value, ("fib", "pln"), pairs)
 
 
@@ -208,21 +217,22 @@
     elements = slot_order.shape[2]
     length, rank = start_basis.shape
     tile = points * elements // length
-    odd = range(1, owners, 2)
-
-    order_first = lax.ppermute(slot_order[0], "fib", [(i - 1, i) for i in odd])
-    near, far, last = pl.pallas_call(
+    core_swap = [(i, i ^ 1) for i in range(owners)]
+    forward = [(i, (i + 1) % owners) for i in range(owners)]
+
+    order_next = lax.ppermute(slot_order[0], "fib", core_swap)
+    zero, one, send = pl.pallas_call(
         functools.partial(interp_kernel, owners),
-        out_shape=[jax.ShapeDtypeStruct((n * capacity, points), F32) for n in (2, 2, 1)],
+        out_shape=[jax.ShapeDtypeStruct((n * capacity, points), F32) for n in (1, 1, 2)],
         in_specs=[SMEM, VMEM, VMEM],
         out_specs=[VMEM] * 3,
         scratch_shapes=[pltpu.VMEM((nodes.shape[0] + SLAB, points), F32)],
         compiler_params=BIG,
         name="interp",
     )(table, nodes, interp_matrix)
-    far_got = lax.ppermute(far, "fib", [(i, (i + 2) % owners) for i in odd])
-    last_got = lax.ppermute(last, "fib", [(i - 1, (i + 2) % owners) for i in odd])
-    near_got = lax.ppermute(near, "fib", [(i - 1, i) for i in odd])
+    back = lax.ppermute(send, "fib", forward)
+    next_zero = lax.ppermute(zero, "fib", core_swap)
+    back_two = lax.ppermute(back[:capacity], "fib", forward)
     pick = pl.pallas_call(
         functools.partial(pick_kernel, capacity, elements // owners),
         out_shape=jax.ShapeDtypeStruct((2 * elements, capacity * window), F32),
@@ -230,21 +240,20 @@
         out_specs=VMEM,
         compiler_params=BIG,
         name="pick",
-    )(table, order_first, slot_order[0])
+    )(table, slot_order[0], order_next)
     bricks = pl.pallas_call(
         order_kernel,
         out_shape=[jax.ShapeDtypeStruct((elements, points), F32)] * 2,
-        in_specs=[VMEM] * 5,
+        in_specs=[VMEM] * 6,
         out_specs=[VMEM] * 2,
         compiler_params=BIG,
         name="order",
-    )(pick, near, near_got, far_got, last_got)
+    )(pick, zero, one, next_zero, back, back_two)
 
     blocks = owners // 2
     chips = masks("fib", 2, owners)[::-1]
     both = jnp.concatenate([b.reshape(blocks, 2 * length // owners, tile) for b in bricks], axis=1)
-    got = {step: swapped(both[step], chips, step) for step in range(blocks - 1, 0, -1)}
-    got[0] = both[0]
+    got = {step: crossed(both[step], chips, step, 1) for step in range(blocks - 1, -1, -1)}
     parts = [got[step] for step in range(blocks)]
     if length // owners % SLAB:
         at = lax.axis_index("fib") // 2 ^ jnp.arange(blocks)
@@ -264,13 +273,10 @@
         compiler_params=BIG,
         name="image",
     )(*parts, start_basis)
-    total = chunks[0]
-    for arrived in [swapped(chunks[step], mid, step) for step in range(count - 1, 0, -1)]:
-        total = total + arrived
-    share = total
-    for arrived in [swapped(share, distant, step) for step in range(2 ** len(distant) - 1, 0, -1)]:
-        total = total + arrived
-    chunks = [total] + [swapped(total, mid, step) for step in range(1, count)]
+    field = crossed(field, mid, 0, 0)
+    total = sum(crossed(chunks[step], mid, step, 0) for step in range(count - 1, -1, -1))
+    total = sum(crossed(total, distant, step, 1) for step in range(2 ** len(distant) - 1, -1, -1))
+    chunks = [crossed(total, mid, step, 0) for step in range(count)]
     first, second = pl.pallas_call(
         functools.partial(factor_kernel, mid),
         out_shape=[jax.ShapeDtypeStruct((rank, tile), F32)] * 2,
@@ -284,8 +290,7 @@
         compiler_params=BIG,
         name="factor",
     )(field, *chunks)
-    first_got = lax.ppermute(first, "fib", [(i, i - 1) for i in odd])
-    core_values = jnp.where(lax.axis_index("fib") % 2 == 1, second, first_got)
+    core_values = first + lax.ppermute(second, "fib", core_swap)
     return core_values[None, None]
 
 

time: 93.1 us -> 63.8 us (0.69)
  waiting for transfers between devices: 54.5 us -> 26.5 us
    ppermute x21 -> x26, waiting for transfers between devices: 54.5 us -> 26.5 us  [the longest x21 10.9 us: crossed(): return lax.ppermute(value, ('fib', 'pln'), pairs)]
    ppermute x21 -> x26, starting transfers between devices: 22 us -> 21.4 us  [the longest x21 18.1 us: crossed(): return lax.ppermute(value, ('fib', 'pln'), pairs)]
  transfers between devices with their start and end apart: 21 -> 26, of which waited for: 3 -> 15; matrix products, arithmetic and copies ran while one was open for 0% -> 0% of each run, Pallas kernels for 1% -> 2%
where the time goes in v7:
time: 63.8 us; the launch traced here: 63.6 us
  waiting for transfers between devices  26.5 us (42%)
  starting transfers between devices  21.4 us (34%)
  Pallas kernels  11 us (17%)
  local copies, waits for them, and re-layouts  3.73 us (6%)
  other arithmetic  0.68 us (1%)
    ppermute x21, starting transfers between devices, crossed(): return lax.ppermute(value, ('fib', 'pln'), pairs)  18.1 us
    ppermute x21, waiting for transfers between devices, crossed(): return lax.ppermute(value, ('fib', 'pln'), pairs)  10.9 us
    ppermute x1, waiting for transfers between devices, per_device(): back = lax.ppermute(send, 'fib', forward)  7.81 us
    pallas_call x1, Pallas kernels, per_device(): pl.pallas_call(functools.partial(factor_kernel, mid), out_shape=[jax.Shap...  6.02 us
    ppermute x1, waiting for transfers between devices, per_device(): back_two = lax.ppermute(back[:capacity], 'fib', forward)  5.43 us
    unnamed x11, local copies, waits for them, and re-layouts  3.57 us
    ppermute x1, starting transfers between devices, per_device(): next_zero = lax.ppermute(zero, 'fib', core_swap)  2.62 us
    pallas_call x1, Pallas kernels, per_device(): pl.pallas_call(functools.partial(interp_kernel, owners), out_shape=[jax.S...  1.82 us
  transfers between devices with their start and end apart: 26, of which 15 were waited for; matrix products, arithmetic and copies ran while one was open for 0% of the time, Pallas kernels for 2%

profile of v7, /device:TPU:0, one launch (start us, length us, event | category | flops | bytes accessed | tf_op | source)
XLA Modules:
  0.0 63.6 jit_solution(10239052868282705130)
XLA Ops:
  0.0 1.6 %copy-done = f32[1000,512]{1,0:T(8,128)S(1)} copy-done((f32[1000,512]{1,0:T(8,128)S(1)}, f32[1000,512]{1,0:T(8,128)}, u32[]{:S(2)}) %copy-start) | copy-done | bytes 2048024
  1.6 1.3 %copy-done.1 = f32[1,1,288,1000]{3,2,1,0:T(8,128)S(1)} copy-done((f32[1,1,288,1000]{3,2,1,0:T(8,128)S(1)}, f32[1,1,288,1000]{3,2,1,0:T(8,128)}, u32[]{:S(2)}) %copy-start.1) | copy-done | bytes 1152024
  2.9 0.7 %copy-done.3 = s32[1,16,3]{1,0,2:T(1,128)S(1)} copy-done((s32[1,16,3]{1,0,2:T(1,128)S(1)}, s32[1,16,3]{1,0,2:T(1,128)}, u32[]{:S(2)}) %copy-start.3) | copy-done | bytes 216
  3.5 1.8 %interp.1 = (f32[96,512]{1,0:T(8,128)S(1)}, f32[96,512]{1,0:T(8,128)S(1)}, f32[192,512]{1,0:T(8,128)S(1)}) custom-call(s32[3,1,16]{2,1,0:T(1,128)S(1)} %bitcast.22, f32[288,1000]{1,0:T(8,128)S(1)} %bitcast.21, f32[1000,512]{1,0:T(8,128)S(1)} %copy-done), custom_call_target="tpu_custom_call" | custom-call | tf_op jit(solution)/shard_map/interp/pallas_call | solution.py:224
  5.4 0.5 collective-permute-start.2
  5.9 2.6 %collective-permute-start.1 = (f32[96,512]{1,0:T(8,128)S(1)}, f32[96,512]{1,0:T(8,128)S(1)}, u32[]{:S(2)}, u32[]{:S(2)}) collective-permute-start(f32[96,512]{1,0:T(8,128)S(1)} %get-tuple-element.17.zero_ref), channel_id=1, source_target_pairs={{0,2},{2,0},{4,6},{6,4},{8,10},{10,8},{12,14},{14,12},{16,18},{18,... | collective-permute-start | bytes 589832 | tf_op jit(solution)/shard_map/ppermute | solution.py:234
  8.5 7.8 %collective-permute-done.2.back_ref = f32[192,512]{1,0:T(8,128)S(1)} collective-permute-done((f32[192,512]{1,0:T(8,128)S(1)}, f32[192,512]{1,0:T(8,128)S(1)}, u32[]{:S(2)}, u32[]{:S(2)}) %collective-permute-start.2) | collective-permute-done | bytes 393248 | tf_op jit(solution)/shard_map/ppermute | solution.py:233
  16.3 0.1 collective-permute-start.3
  16.4 0.0 copy-done.4
  16.4 0.1 collective-permute-start
  16.5 1.1 %collective-permute-done.order_next_ref = s32[1,192]{1,0:T(1,128)S(1)} collective-permute-done((s32[1,192]{1,0:T(1,128)S(1)}, s32[1,192]{1,0:T(1,128)S(1)}, u32[]{:S(2)}, u32[]{:S(2)}) %collective-permute-start) | collective-permute-done | bytes 800 | tf_op jit(solution)/shard_map/ppermute | solution.py:223
  17.6 1.1 %pick.1.pick_ref = f32[384,288]{1,0:T(8,128)S(1)} custom-call(s32[3,1,16]{2,1,0:T(1,128)S(1)} %bitcast.23, s32[1,192]{1,0:T(1,128)S(1)} %bitcast.25, s32[1,192]{1,0:T(1,128)S(1)} %collective-permute-done.order_next_ref), custom_call_target="tpu_custom_call" | custom-call | tf_op jit(solution)/shard_map/pick/pallas_call | solution.py:236
  18.7 0.0 collective-permute-done.1.next_zero_ref
  18.7 5.4 %collective-permute-done.3.back_two_ref = f32[96,512]{1,0:T(8,128)S(1)} collective-permute-done((f32[96,512]{1,0:T(8,128)S(1)}, f32[96,512]{1,0:T(8,128)S(1)}, u32[]{:S(2)}, u32[]{:S(2)}) %collective-permute-start.3) | collective-permute-done | bytes 196640 | tf_op jit(solution)/shard_map/ppermute | solution.py:235
  24.2 0.8 %order.1 = (f32[192,512]{1,0:T(8,128)S(1)}, f32[192,512]{1,0:T(8,128)S(1)}) custom-call(f32[384,288]{1,0:T(8,128)S(1)} %pick.1.pick_ref, f32[96,512]{1,0:T(8,128)S(1)} %get-tuple-element.17.zero_ref, f32[96,512]{1,0:T(8,128)S(1)} %get-tuple-element.18.one_ref, f32[96,512]{1,0:T(8,128)S(1)} %collective-permute-done.1.next_zero_ref, ...), custom_call_target="tpu_custom_call" | custom-call | tf_op jit(solution)/shard_map/order/pallas_call | solution.py:244
  25.0 0.0 copy-start.2
  25.2 0.1 slice_bitcast_fusion
  25.2 0.1 collective-permute-start.11
  25.3 0.6 collective-permute-start.10
  25.9 0.0 collective-permute-start.9
  25.9 0.0 collective-permute-start.8
  25.9 1.6 %collective-permute-start.7 = (f32[192,128]{1,0:T(8,128)S(1)}, f32[192,128]{1,0:T(8,128)S(1)}, u32[]{:S(2)}, u32[]{:S(2)}) collective-permute-start(f32[192,128]{1,0:T(8,128)S(1)} %get-tuple-element.33), channel_id=1, source_target_pairs={{0,14},{1,15},{2,0},{3,1},{4,10},{5,11},{6,4},{7,5},{8,6},{9,7},{1... | collective-permute-start | bytes 294920 | tf_op jit(solution)/shard_map/ppermute | solution.py:198
  27.5 0.0 collective-permute-done.11.refs_7_
  27.5 2.5 %collective-permute-start.6 = (f32[192,128]{1,0:T(8,128)S(1)}, f32[192,128]{1,0:T(8,128)S(1)}, u32[]{:S(2)}, u32[]{:S(2)}) collective-permute-start(f32[192,128]{1,0:T(8,128)S(1)} %get-tuple-element.34), channel_id=1, source_target_pairs={{0,10},{1,11},{2,0},{3,1},{4,14},{5,15},{6,4},{7,5},{8,2},{9,3},{1... | collective-permute-start | bytes 294920 | tf_op jit(solution)/shard_map/ppermute | solution.py:198
  30.0 0.0 collective-permute-done.10.refs_6_
  30.0 0.0 collective-permute-start.5
  30.0 0.0 collective-permute-done.9.refs_5_
  30.0 2.6 %collective-permute-start.4 = (f32[192,128]{1,0:T(8,128)S(1)}, f32[192,128]{1,0:T(8,128)S(1)}, u32[]{:S(2)}, u32[]{:S(2)}) collective-permute-start(f32[192,128]{1,0:T(8,128)S(1)} %get-tuple-element.36), channel_id=1, source_target_pairs={{0,2},{1,3},{2,0},{3,1},{4,6},{5,7},{6,4},{7,5},{8,10},{9,11},{10,... | collective-permute-start | bytes 294920 | tf_op jit(solution)/shard_map/ppermute | solution.py:198
  32.6 0.0 collective-permute-done.8.refs_4_
  32.7 0.0 collective-permute-done.7.refs_3_
  32.7 0.1 collective-permute-done.6.refs_2_
  32.8 0.2 collective-permute-done.5.refs_1_
  33.0 0.6 collective-permute-done.4.refs_0_
  33.6 1.2 %image.1 = (f32[192,128]{1,0:T(8,128)S(1)}, f32[192,128]{1,0:T(8,128)S(1)}, f32[192,128]{1,0:T(8,128)S(1)}, f32[192,128]{1,0:T(8,128)S(1)}, f32[768,256]{1,0:T(8,128)S(1)}) custom-call(f32[192,128]{1,0:T(8,128)S(1)} %collective-permute-done.4.refs_0_, f32[192,128]{1,0:T(8,128)S(1)} %collective-permute-done.5.refs_1_, ...), custom_call_target="tpu_custom_call" | custom-call | tf_op jit(solution)/shard_map/image/pallas_call | solution.py:267
  34.8 2.3 %collective-permute-start.12 = (f32[768,256]{1,0:T(8,128)S(1)}, f32[768,256]{1,0:T(8,128)S(1)}, u32[]{:S(2)}, u32[]{:S(2)}) collective-permute-start(f32[768,256]{1,0:T(8,128)S(1)} %get-tuple-element.22), channel_id=1, source_target_pairs={{0,2},{1,3},{2,0},{3,1},{4,6},{5,7},{6,4},{7,5},{8,10},{9,11},{10,... | collective-permute-start | bytes 2359304 | tf_op jit(solution)/shard_map/ppermute | solution.py:198
  37.1 0.1 collective-permute-start.13
  37.2 1.4 %collective-permute-start.14 = (f32[192,128]{1,0:T(8,128)S(1)}, f32[192,128]{1,0:T(8,128)S(1)}, u32[]{:S(2)}, u32[]{:S(2)}) collective-permute-start(f32[192,128]{1,0:T(8,128)S(1)} %get-tuple-element.24), channel_id=1, source_target_pairs={{0,2},{1,3},{2,4},{3,5},{4,6},{5,7},{6,0},{7,1},{8,10},{9,11},{10,... | collective-permute-start | bytes 294920 | tf_op jit(solution)/shard_map/ppermute | solution.py:198
  38.6 0.0 collective-permute-start.15
  38.6 0.8 %collective-permute-start.16 = (f32[192,128]{1,0:T(8,128)S(1)}, f32[192,128]{1,0:T(8,128)S(1)}, u32[]{:S(2)}, u32[]{:S(2)}) collective-permute-start(f32[192,128]{1,0:T(8,128)S(1)} %get-tuple-element.26), channel_id=1, source_target_pairs={{0,2},{1,3},{2,0},{3,1},{4,6},{5,7},{6,4},{7,5},{8,10},{9,11},{10,... | collective-permute-start | bytes 294920 | tf_op jit(solution)/shard_map/ppermute | solution.py:198
  39.4 2.8 %collective-permute-done.13 = f32[192,128]{1,0:T(8,128)S(1)} collective-permute-done((f32[192,128]{1,0:T(8,128)S(1)}, f32[192,128]{1,0:T(8,128)S(1)}, u32[]{:S(2)}, u32[]{:S(2)}) %collective-permute-start.13) | collective-permute-done | bytes 98336 | tf_op jit(solution)/shard_map/ppermute | solution.py:198
  42.1 1.6 %collective-permute-done.14 = f32[192,128]{1,0:T(8,128)S(1)} collective-permute-done((f32[192,128]{1,0:T(8,128)S(1)}, f32[192,128]{1,0:T(8,128)S(1)}, u32[]{:S(2)}, u32[]{:S(2)}) %collective-permute-start.14) | collective-permute-done | bytes 98336 | tf_op jit(solution)/shard_map/ppermute | solution.py:198
  43.7 0.0 collective-permute-done.15
  43.7 0.0 collective-permute-done.16
  43.7 0.1 collective-permute-start.20
  43.8 1.1 %collective-permute-start.19 = (f32[192,128]{1,0:T(8,128)S(1)}, f32[192,128]{1,0:T(8,128)S(1)}, u32[]{:S(2)}, u32[]{:S(2)}) collective-permute-start(f32[192,128]{1,0:T(8,128)S(1)} %add_add_fusion.1), channel_id=1, source_target_pairs={{0,18},{1,19},{2,0},{3,1},{4,22},{5,23},{6,4},{7,5},{8,26},{9,27},... | collective-permute-start | bytes 294920 | tf_op jit(solution)/shard_map/ppermute | solution.py:198
  45.0 0.0 collective-permute-start.18
  45.0 1.6 %collective-permute-start.17 = (f32[192,128]{1,0:T(8,128)S(1)}, f32[192,128]{1,0:T(8,128)S(1)}, u32[]{:S(2)}, u32[]{:S(2)}) collective-permute-start(f32[192,128]{1,0:T(8,128)S(1)} %add_add_fusion.1), channel_id=1, source_target_pairs={{0,26},{1,27},{2,0},{3,1},{4,30},{5,31},{6,4},{7,5},{8,18},{9,19},... | collective-permute-start | bytes 294920 | tf_op jit(solution)/shard_map/ppermute | solution.py:198
  46.5 0.0 collective-permute-done.20
  46.5 0.6 %collective-permute-done.19 = f32[192,128]{1,0:T(8,128)S(1)} collective-permute-done((f32[192,128]{1,0:T(8,128)S(1)}, f32[192,128]{1,0:T(8,128)S(1)}, u32[]{:S(2)}, u32[]{:S(2)}) %collective-permute-start.19) | collective-permute-done | bytes 98336 | tf_op jit(solution)/shard_map/ppermute | solution.py:198
  47.2 1.0 %collective-permute-done.18 = f32[192,128]{1,0:T(8,128)S(1)} collective-permute-done((f32[192,128]{1,0:T(8,128)S(1)}, f32[192,128]{1,0:T(8,128)S(1)}, u32[]{:S(2)}, u32[]{:S(2)}) %collective-permute-start.18) | collective-permute-done | bytes 98336 | tf_op jit(solution)/shard_map/ppermute | solution.py:198
  48.2 1.1 %collective-permute-done.17 = f32[192,128]{1,0:T(8,128)S(1)} collective-permute-done((f32[192,128]{1,0:T(8,128)S(1)}, f32[192,128]{1,0:T(8,128)S(1)}, u32[]{:S(2)}, u32[]{:S(2)}) %collective-permute-start.17) | collective-permute-done | bytes 98336 | tf_op jit(solution)/shard_map/ppermute | solution.py:198
  49.3 2.2 %collective-permute-start.24 = (f32[192,128]{1,0:T(8,128)S(1)}, f32[192,128]{1,0:T(8,128)S(1)}, u32[]{:S(2)}, u32[]{:S(2)}) collective-permute-start(f32[192,128]{1,0:T(8,128)S(1)} %add_add_fusion), channel_id=1, source_target_pairs={{0,2},{1,3},{2,5},{3,4},{4,6},{5,7},{6,1},{7,0},{8,10},{9,11},{10,... | collective-permute-start | bytes 294920 | tf_op jit(solution)/shard_map/ppermute | solution.py:198
  51.5 0.1 collective-permute-start.23
  51.5 1.0 %collective-permute-start.22 = (f32[192,128]{1,0:T(8,128)S(1)}, f32[192,128]{1,0:T(8,128)S(1)}, u32[]{:S(2)}, u32[]{:S(2)}) collective-permute-start(f32[192,128]{1,0:T(8,128)S(1)} %add_add_fusion), channel_id=1, source_target_pairs={{0,2},{1,3},{2,1},{3,0},{4,6},{5,7},{6,5},{7,4},{8,10},{9,11},{10,... | collective-permute-start | bytes 294920 | tf_op jit(solution)/shard_map/ppermute | solution.py:198
  52.6 0.1 collective-permute-start.21
  52.7 1.8 %collective-permute-done.24.refs_3_ = f32[192,128]{1,0:T(8,128)S(1)} collective-permute-done((f32[192,128]{1,0:T(8,128)S(1)}, f32[192,128]{1,0:T(8,128)S(1)}, u32[]{:S(2)}, u32[]{:S(2)}) %collective-permute-start.24) | collective-permute-done | bytes 98336 | tf_op jit(solution)/shard_map/ppermute | solution.py:198
  54.5 1.0 %collective-permute-done.23.refs_2_ = f32[192,128]{1,0:T(8,128)S(1)} collective-permute-done((f32[192,128]{1,0:T(8,128)S(1)}, f32[192,128]{1,0:T(8,128)S(1)}, u32[]{:S(2)}, u32[]{:S(2)}) %collective-permute-start.23) | collective-permute-done | bytes 98336 | tf_op jit(solution)/shard_map/ppermute | solution.py:198
  55.5 0.1 collective-permute-done.22.refs_1_
  55.6 0.0 collective-permute-done.21.refs_0_
  55.6 0.0 collective-permute-done.12.field_ref
  55.6 6.0 %factor.1 = (f32[128,128]{1,0:T(8,128)S(1)}, f32[128,128]{1,0:T(8,128)S(1)}) custom-call(f32[768,256]{1,0:T(8,128)S(1)} %collective-permute-done.12.field_ref, f32[192,128]{1,0:T(8,128)S(1)} %collective-permute-done.21.refs_0_, f32[192,128]{1,0:T(8,128)S(1)} %collective-permute-done.22.refs_1_, f32[192,128]{1,0:T(8,128)S(1)} %collective-permute-done.23.refs_2_, ...), custom_call_target="tpu_custom_call" | custom-call | tf_op jit(solution)/shard_map/factor/pallas_call | solution.py:280
  61.6 0.1 collective-permute-start.25
  61.7 1.2 %collective-permute-done.25 = f32[128,128]{1,0:T(8,128)S(1)} collective-permute-done((f32[128,128]{1,0:T(8,128)S(1)}, f32[128,128]{1,0:T(8,128)S(1)}, u32[]{:S(2)}, u32[]{:S(2)}) %collective-permute-start.25) | collective-permute-done | bytes 65568 | tf_op jit(solution)/shard_map/ppermute | solution.py:293
  63.0 0.6 %add_bitcast_fusion = f32[1,1,128,128]{3,2,1,0:T(8,128)} fusion(f32[128,128]{1,0:T(8,128)S(1)} %get-tuple-element.27, f32[128,128]{1,0:T(8,128)S(1)} %collective-permute-done.25), kind=kLoop, calls=%fused_computation.10 | loop fusion | flops 16384 | bytes 196608 | tf_op jit(solution)/shard_map/broadcast_in_dim | solution.py:294
  (12 shorter events, 0.2 us)
Async XLA Ops:
  0.0 16.4 %copy-start.4 = (s32[1,1,192]{2,1,0:T(1,128)S(1)}, s32[1,1,192]{2,1,0:T(1,128)}, u32[]{:S(2)}) copy-start(s32[1,1,192]{2,1,0:T(1,128)} %param.8) | copy-start | bytes 2308
  0.0 1.6 %copy-start = (f32[1000,512]{1,0:T(8,128)S(1)}, f32[1000,512]{1,0:T(8,128)}, u32[]{:S(2)}) copy-start(f32[1000,512]{1,0:T(8,128)} %interp_ref.1) | copy-start | bytes 6144004
  1.6 1.3 %copy-start.1 = (f32[1,1,288,1000]{3,2,1,0:T(8,128)S(1)}, f32[1,1,288,1000]{3,2,1,0:T(8,128)}, u32[]{:S(2)}) copy-start(f32[1,1,288,1000]{3,2,1,0:T(8,128)} %param.5) | copy-start | bytes 3456004
  2.9 0.7 %copy-start.3 = (s32[1,16,3]{1,0,2:T(1,128)S(1)}, s32[1,16,3]{1,0,2:T(1,128)}, u32[]{:S(2)}) copy-start(s32[1,16,3]{1,0,2:T(1,128)} %param.7) | copy-start | bytes 580
  5.4 10.9 %collective-permute-start.2 = (f32[192,512]{1,0:T(8,128)S(1)}, f32[192,512]{1,0:T(8,128)S(1)}, u32[]{:S(2)}, u32[]{:S(2)}) collective-permute-start(f32[192,512]{1,0:T(8,128)S(1)} %get-tuple-element.19), channel_id=1, source_target_pairs={{0,2},{2,4},{4,6},{6,8},{8,10},{10,12},{12,14},{14,16},{16,18},{18... | collective-permute-start | bytes 1179656 | tf_op jit(solution)/shard_map/ppermute | solution.py:233
  5.9 12.9 %collective-permute-start.1 = (f32[96,512]{1,0:T(8,128)S(1)}, f32[96,512]{1,0:T(8,128)S(1)}, u32[]{:S(2)}, u32[]{:S(2)}) collective-permute-start(f32[96,512]{1,0:T(8,128)S(1)} %get-tuple-element.17.zero_ref), channel_id=1, source_target_pairs={{0,2},{2,0},{4,6},{6,4},{8,10},{10,8},{12,14},{14,12},{16,18},{18,... | collective-permute-start | bytes 589832 | tf_op jit(solution)/shard_map/ppermute | solution.py:234
  16.3 7.8 %collective-permute-start.3 = (f32[96,512]{1,0:T(8,128)S(1)}, f32[96,512]{1,0:T(8,128)S(1)}, u32[]{:S(2)}, u32[]{:S(2)}) collective-permute-start(f32[96,512]{1,0:T(8,128)S(1)} %slice.36), channel_id=1, source_target_pairs={{0,2},{2,4},{4,6},{6,8},{8,10},{10,12},{12,14},{14,16},{16,18},{18... | collective-permute-start | bytes 589832 | tf_op jit(solution)/shard_map/ppermute | solution.py:235
  16.4 1.2 %collective-permute-start = (s32[1,192]{1,0:T(1,128)S(1)}, s32[1,192]{1,0:T(1,128)S(1)}, u32[]{:S(2)}, u32[]{:S(2)}) collective-permute-start(s32[1,192]{1,0:T(1,128)S(1)} %bitcast.24), channel_id=1, source_target_pairs={{0,2},{2,0},{4,6},{6,4},{8,10},{10,8},{12,14},{14,12},{16,18},{18,... | collective-permute-start | bytes 2312 | tf_op jit(solution)/shard_map/ppermute | solution.py:223
  25.0 8.6 %copy-start.2 = (f32[768,128]{1,0:T(8,128)S(1)}, f32[768,128]{1,0:T(8,128)}, u32[]{:S(2)}) copy-start(f32[768,128]{1,0:T(8,128)} %refs_8_.1) | copy-start | bytes 1179652
  25.2 2.3 %collective-permute-start.11 = (f32[192,128]{1,0:T(8,128)S(1)}, f32[192,128]{1,0:T(8,128)S(1)}, u32[]{:S(2)}, u32[]{:S(2)}) collective-permute-start(f32[192,128]{1,0:T(8,128)S(1)} %get-tuple-element.29), channel_id=1, source_target_pairs={{0,30},{1,31},{2,0},{3,1},{4,26},{5,27},{6,4},{7,5},{8,22},{9,23},... | collective-permute-start | bytes 294920 | tf_op jit(solution)/shard_map/ppermute | solution.py:198
  25.3 4.7 %collective-permute-start.10 = (f32[192,128]{1,0:T(8,128)S(1)}, f32[192,128]{1,0:T(8,128)S(1)}, u32[]{:S(2)}, u32[]{:S(2)}) collective-permute-start(f32[192,128]{1,0:T(8,128)S(1)} %get-tuple-element.30), channel_id=1, source_target_pairs={{0,26},{1,27},{2,0},{3,1},{4,30},{5,31},{6,4},{7,5},{8,18},{9,19},... | collective-permute-start | bytes 294920 | tf_op jit(solution)/shard_map/ppermute | solution.py:198
  25.9 4.1 %collective-permute-start.9 = (f32[192,128]{1,0:T(8,128)S(1)}, f32[192,128]{1,0:T(8,128)S(1)}, u32[]{:S(2)}, u32[]{:S(2)}) collective-permute-start(f32[192,128]{1,0:T(8,128)S(1)} %get-tuple-element.31), channel_id=1, source_target_pairs={{0,22},{1,23},{2,0},{3,1},{4,18},{5,19},{6,4},{7,5},{8,30},{9,31},... | collective-permute-start | bytes 294920 | tf_op jit(solution)/shard_map/ppermute | solution.py:198
  25.9 6.8 %collective-permute-start.8 = (f32[192,128]{1,0:T(8,128)S(1)}, f32[192,128]{1,0:T(8,128)S(1)}, u32[]{:S(2)}, u32[]{:S(2)}) collective-permute-start(f32[192,128]{1,0:T(8,128)S(1)} %get-tuple-element.32), channel_id=1, source_target_pairs={{0,18},{1,19},{2,0},{3,1},{4,22},{5,23},{6,4},{7,5},{8,26},{9,27},... | collective-permute-start | bytes 294920 | tf_op jit(solution)/shard_map/ppermute | solution.py:198
  25.9 6.8 %collective-permute-start.7 = (f32[192,128]{1,0:T(8,128)S(1)}, f32[192,128]{1,0:T(8,128)S(1)}, u32[]{:S(2)}, u32[]{:S(2)}) collective-permute-start(f32[192,128]{1,0:T(8,128)S(1)} %get-tuple-element.33), channel_id=1, source_target_pairs={{0,14},{1,15},{2,0},{3,1},{4,10},{5,11},{6,4},{7,5},{8,6},{9,7},{1... | collective-permute-start | bytes 294920 | tf_op jit(solution)/shard_map/ppermute | solution.py:198
  27.5 5.3 %collective-permute-start.6 = (f32[192,128]{1,0:T(8,128)S(1)}, f32[192,128]{1,0:T(8,128)S(1)}, u32[]{:S(2)}, u32[]{:S(2)}) collective-permute-start(f32[192,128]{1,0:T(8,128)S(1)} %get-tuple-element.34), channel_id=1, source_target_pairs={{0,10},{1,11},{2,0},{3,1},{4,14},{5,15},{6,4},{7,5},{8,2},{9,3},{1... | collective-permute-start | bytes 294920 | tf_op jit(solution)/shard_map/ppermute | solution.py:198
  30.0 3.0 %collective-permute-start.5 = (f32[192,128]{1,0:T(8,128)S(1)}, f32[192,128]{1,0:T(8,128)S(1)}, u32[]{:S(2)}, u32[]{:S(2)}) collective-permute-start(f32[192,128]{1,0:T(8,128)S(1)} %get-tuple-element.35), channel_id=1, source_target_pairs={{0,6},{1,7},{2,0},{3,1},{4,2},{5,3},{6,4},{7,5},{8,14},{9,15},{10,... | collective-permute-start | bytes 294920 | tf_op jit(solution)/shard_map/ppermute | solution.py:198
  30.0 3.6 %collective-permute-start.4 = (f32[192,128]{1,0:T(8,128)S(1)}, f32[192,128]{1,0:T(8,128)S(1)}, u32[]{:S(2)}, u32[]{:S(2)}) collective-permute-start(f32[192,128]{1,0:T(8,128)S(1)} %get-tuple-element.36), channel_id=1, source_target_pairs={{0,2},{1,3},{2,0},{3,1},{4,6},{5,7},{6,4},{7,5},{8,10},{9,11},{10,... | collective-permute-start | bytes 294920 | tf_op jit(solution)/shard_map/ppermute | solution.py:198
  34.8 20.8 %collective-permute-start.12 = (f32[768,256]{1,0:T(8,128)S(1)}, f32[768,256]{1,0:T(8,128)S(1)}, u32[]{:S(2)}, u32[]{:S(2)}) collective-permute-start(f32[768,256]{1,0:T(8,128)S(1)} %get-tuple-element.22), channel_id=1, source_target_pairs={{0,2},{1,3},{2,0},{3,1},{4,6},{5,7},{6,4},{7,5},{8,10},{9,11},{10,... | collective-permute-start | bytes 2359304 | tf_op jit(solution)/shard_map/ppermute | solution.py:198
  37.1 5.0 %collective-permute-start.13 = (f32[192,128]{1,0:T(8,128)S(1)}, f32[192,128]{1,0:T(8,128)S(1)}, u32[]{:S(2)}, u32[]{:S(2)}) collective-permute-start(f32[192,128]{1,0:T(8,128)S(1)} %get-tuple-element.23), channel_id=1, source_target_pairs={{0,2},{1,3},{2,5},{3,4},{4,6},{5,7},{6,1},{7,0},{8,10},{9,11},{10,... | collective-permute-start | bytes 294920 | tf_op jit(solution)/shard_map/ppermute | solution.py:198
  37.2 6.5 %collective-permute-start.14 = (f32[192,128]{1,0:T(8,128)S(1)}, f32[192,128]{1,0:T(8,128)S(1)}, u32[]{:S(2)}, u32[]{:S(2)}) collective-permute-start(f32[192,128]{1,0:T(8,128)S(1)} %get-tuple-element.24), channel_id=1, source_target_pairs={{0,2},{1,3},{2,4},{3,5},{4,6},{5,7},{6,0},{7,1},{8,10},{9,11},{10,... | collective-permute-start | bytes 294920 | tf_op jit(solution)/shard_map/ppermute | solution.py:198
  38.6 5.1 %collective-permute-start.15 = (f32[192,128]{1,0:T(8,128)S(1)}, f32[192,128]{1,0:T(8,128)S(1)}, u32[]{:S(2)}, u32[]{:S(2)}) collective-permute-start(f32[192,128]{1,0:T(8,128)S(1)} %get-tuple-element.25), channel_id=1, source_target_pairs={{0,2},{1,3},{2,1},{3,0},{4,6},{5,7},{6,5},{7,4},{8,10},{9,11},{10,... | collective-permute-start | bytes 294920 | tf_op jit(solution)/shard_map/ppermute | solution.py:198
  38.6 5.1 %collective-permute-start.16 = (f32[192,128]{1,0:T(8,128)S(1)}, f32[192,128]{1,0:T(8,128)S(1)}, u32[]{:S(2)}, u32[]{:S(2)}) collective-permute-start(f32[192,128]{1,0:T(8,128)S(1)} %get-tuple-element.26), channel_id=1, source_target_pairs={{0,2},{1,3},{2,0},{3,1},{4,6},{5,7},{6,4},{7,5},{8,10},{9,11},{10,... | collective-permute-start | bytes 294920 | tf_op jit(solution)/shard_map/ppermute | solution.py:198
  43.7 2.8 %collective-permute-start.20 = (f32[192,128]{1,0:T(8,128)S(1)}, f32[192,128]{1,0:T(8,128)S(1)}, u32[]{:S(2)}, u32[]{:S(2)}) collective-permute-start(f32[192,128]{1,0:T(8,128)S(1)} %add_add_fusion.1), channel_id=1, source_target_pairs={{0,2},{1,3},{2,0},{3,1},{4,6},{5,7},{6,4},{7,5},{8,10},{9,11},{10,... | collective-permute-start | bytes 294920 | tf_op jit(solution)/shard_map/ppermute | solution.py:198
  43.8 3.4 %collective-permute-start.19 = (f32[192,128]{1,0:T(8,128)S(1)}, f32[192,128]{1,0:T(8,128)S(1)}, u32[]{:S(2)}, u32[]{:S(2)}) collective-permute-start(f32[192,128]{1,0:T(8,128)S(1)} %add_add_fusion.1), channel_id=1, source_target_pairs={{0,18},{1,19},{2,0},{3,1},{4,22},{5,23},{6,4},{7,5},{8,26},{9,27},... | collective-permute-start | bytes 294920 | tf_op jit(solution)/shard_map/ppermute | solution.py:198
  45.0 3.2 %collective-permute-start.18 = (f32[192,128]{1,0:T(8,128)S(1)}, f32[192,128]{1,0:T(8,128)S(1)}, u32[]{:S(2)}, u32[]{:S(2)}) collective-permute-start(f32[192,128]{1,0:T(8,128)S(1)} %add_add_fusion.1), channel_id=1, source_target_pairs={{0,10},{1,11},{2,0},{3,1},{4,14},{5,15},{6,4},{7,5},{8,2},{9,3},{1... | collective-permute-start | bytes 294920 | tf_op jit(solution)/shard_map/ppermute | solution.py:198
  45.0 4.3 %collective-permute-start.17 = (f32[192,128]{1,0:T(8,128)S(1)}, f32[192,128]{1,0:T(8,128)S(1)}, u32[]{:S(2)}, u32[]{:S(2)}) collective-permute-start(f32[192,128]{1,0:T(8,128)S(1)} %add_add_fusion.1), channel_id=1, source_target_pairs={{0,26},{1,27},{2,0},{3,1},{4,30},{5,31},{6,4},{7,5},{8,18},{9,19},... | collective-permute-start | bytes 294920 | tf_op jit(solution)/shard_map/ppermute | solution.py:198
  49.3 5.2 %collective-permute-start.24 = (f32[192,128]{1,0:T(8,128)S(1)}, f32[192,128]{1,0:T(8,128)S(1)}, u32[]{:S(2)}, u32[]{:S(2)}) collective-permute-start(f32[192,128]{1,0:T(8,128)S(1)} %add_add_fusion), channel_id=1, source_target_pairs={{0,2},{1,3},{2,5},{3,4},{4,6},{5,7},{6,1},{7,0},{8,10},{9,11},{10,... | collective-permute-start | bytes 294920 | tf_op jit(solution)/shard_map/ppermute | solution.py:198
  51.5 4.0 %collective-permute-start.23 = (f32[192,128]{1,0:T(8,128)S(1)}, f32[192,128]{1,0:T(8,128)S(1)}, u32[]{:S(2)}, u32[]{:S(2)}) collective-permute-start(f32[192,128]{1,0:T(8,128)S(1)} %add_add_fusion), channel_id=1, source_target_pairs={{0,2},{1,3},{2,4},{3,5},{4,6},{5,7},{6,0},{7,1},{8,10},{9,11},{10,... | collective-permute-start | bytes 294920 | tf_op jit(solution)/shard_map/ppermute | solution.py:198
  51.5 4.1 %collective-permute-start.22 = (f32[192,128]{1,0:T(8,128)S(1)}, f32[192,128]{1,0:T(8,128)S(1)}, u32[]{:S(2)}, u32[]{:S(2)}) collective-permute-start(f32[192,128]{1,0:T(8,128)S(1)} %add_add_fusion), channel_id=1, source_target_pairs={{0,2},{1,3},{2,1},{3,0},{4,6},{5,7},{6,5},{7,4},{8,10},{9,11},{10,... | collective-permute-start | bytes 294920 | tf_op jit(solution)/shard_map/ppermute | solution.py:198
  52.6 3.0 %collective-permute-start.21 = (f32[192,128]{1,0:T(8,128)S(1)}, f32[192,128]{1,0:T(8,128)S(1)}, u32[]{:S(2)}, u32[]{:S(2)}) collective-permute-start(f32[192,128]{1,0:T(8,128)S(1)} %add_add_fusion), channel_id=1, source_target_pairs={{0,2},{1,3},{2,0},{3,1},{4,6},{5,7},{6,4},{7,5},{8,10},{9,11},{10,... | collective-permute-start | bytes 294920 | tf_op jit(solution)/shard_map/ppermute | solution.py:198
  61.6 1.3 %collective-permute-start.25 = (f32[128,128]{1,0:T(8,128)S(1)}, f32[128,128]{1,0:T(8,128)S(1)}, u32[]{:S(2)}, u32[]{:S(2)}) collective-permute-start(f32[128,128]{1,0:T(8,128)S(1)} %get-tuple-element.28), channel_id=1, source_target_pairs={{0,2},{2,0},{4,6},{6,4},{8,10},{10,8},{12,14},{14,12},{16,18},{18,... | collective-permute-start | bytes 196616 | tf_op jit(solution)/shard_map/ppermute | solution.py:293

commit v8 on v7

--- a/solution.py
+++ b/solution.py
@@ -10,6 +10,7 @@
 F32 = jnp.float32
 BF16 = jnp.bfloat16
 SLAB = 8
+KSTEP = 256
 VMEM = pl.BlockSpec(memory_space=pltpu.VMEM)
 SMEM = pl.BlockSpec(memory_space=pltpu.SMEM)
 BIG = pltpu.CompilerParams(vmem_limit_bytes=32 * 1024 * 1024)
@@ -29,11 +30,34 @@
     return out + lax.dot_general(lh, rh, dims, preferred_element_type=F32)
 
 
-def interp_kernel(owners, table_ref, node_ref, interp_ref, zero_ref, one_ref, send_ref, grid_scr):
+def interp_kernel(owners, table_hbm, node_hbm, interp_hbm, swap_ref, one_ref, send_ref, zero_ref, *scratch):
+    grid_scr, node_ref, interp_ref, table_ref, sems = scratch
     rows = zero_ref.shape[0]
-    slots = node_ref.shape[0]
+    slots, depth = node_ref.shape
     own = lax.axis_index("fib")
-    grid_scr[:slots, :] = dot3(halves(node_ref[...]), halves(interp_ref[...]), ((1,), (0,)))
+    copies = [pltpu.make_async_copy(table_hbm, table_ref, sems.at[0])]
+    for part in range(slots // rows):
+        at = pl.ds(part * rows, rows)
+        copies.append(pltpu.make_async_copy(node_hbm.at[at, :], node_ref.at[at, :], sems.at[len(copies)]))
+    steps = [(at, min(KSTEP, depth - at)) for at in range(0, depth, KSTEP)]
+    first = len(copies)
+    for at, size in steps:
+        part = pl.ds(at, size)
+        copies.append(
+            pltpu.make_async_copy(interp_hbm.at[part, :], interp_ref.at[part, :], sems.at[len(copies)])
+        )
+    for copy in copies:
+        copy.start()
+    for copy in copies[:first]:
+        copy.wait()
+    total = None
+    for (at, size), copy in zip(steps, copies[first:]):
+        copy.wait()
+        part = dot3(
+            halves(node_ref[:, at : at + size]), halves(interp_ref[at : at + size, :]), ((1,), (0,))
+        )
+        total = part if total is None else total + part
+    grid_scr[:slots, :] = total
     zero_ref[...] = grid_scr[:rows, :]
     start = table_ref[0, 0, own]
     for distance in range(1, 3):
@@ -47,10 +71,15 @@
         else:
             send_ref[rows:, :] = piece
         start = start + table_ref[distance, 0, lax.rem(own + distance, owners)]
-
-    @pl.when(lax.rem(own, 2) == 0)
+    second = lax.rem(own, 2) == 1
+
+    @pl.when(second)
     def _():
-        send_ref[:rows, :] = send_ref[rows:, :]
+        swap_ref[...] = zero_ref[...]
+
+    @pl.when(jnp.logical_not(second))
+    def _():
+        swap_ref[...] = send_ref[rows:, :]
 
 
 def pick_kernel(rows, per_tile, table_ref, order_ref, order_next_ref, out_ref):
@@ -221,18 +250,26 @@
     forward = [(i, (i + 1) % owners) for i in range(owners)]
 
     order_next = lax.ppermute(slot_order[0], "fib", core_swap)
-    zero, one, send = pl.pallas_call(
+    piece = jax.ShapeDtypeStruct((capacity, points), F32)
+    copies = 1 + window + pl.cdiv(nodes.shape[1], KSTEP)
+    swap, one, send, zero = pl.pallas_call(
         functools.partial(interp_kernel, owners),
-        out_shape=[jax.ShapeDtypeStruct((n * capacity, points), F32) for n in (1, 1, 2)],
-        in_specs=[SMEM, VMEM, VMEM],
-        out_specs=[VMEM] * 3,
-        scratch_shapes=[pltpu.VMEM((nodes.shape[0] + SLAB, points), F32)],
+        out_shape=[piece, piece, jax.ShapeDtypeStruct((2 * capacity, points), F32), piece],
+        in_specs=[pl.BlockSpec(memory_space=pl.ANY)] * 3,
+        out_specs=[VMEM] * 4,
+        scratch_shapes=[
+            pltpu.VMEM((nodes.shape[0] + SLAB, points), F32),
+            pltpu.VMEM(nodes.shape, F32),
+            pltpu.VMEM(interp_matrix.shape, F32),
+            pltpu.SMEM(table.shape, jnp.int32),
+            pltpu.SemaphoreType.DMA((copies,)),
+        ],
         compiler_params=BIG,
         name="interp",
-    )(table, nodes, interp_matrix)
+    )(*(pltpu.with_memory_space_constraint(x, pltpu.HBM) for x in (table, nodes, interp_matrix)))
+    swapped = lax.ppermute(swap, "fib", core_swap)
     back = lax.ppermute(send, "fib", forward)
-    next_zero = lax.ppermute(zero, "fib", core_swap)
-    back_two = lax.ppermute(back[:capacity], "fib", forward)
+    back_two = lax.ppermute(swapped, "fib", forward)
     pick = pl.pallas_call(
         functools.partial(pick_kernel, capacity, elements // owners),
         out_shape=jax.ShapeDtypeStruct((2 * elements, capacity * window), F32),
@@ -248,7 +285,7 @@
         out_specs=[VMEM] * 2,
         compiler_params=BIG,
         name="order",
-    )(pick, zero, one, next_zero, back, back_two)
+    )(pick, zero, one, swapped, back, back_two)
 
     blocks = owners // 2
     chips = masks("fib", 2, owners)[::-1]

time: 63.8 us -> 57.9 us (0.908)
  waiting for transfers between devices: 26.5 us -> 20.5 us
  local copies, waits for them, and re-layouts: 3.73 us -> 0.18 us
  starting transfers between devices: 21.4 us -> 24.1 us
  Pallas kernels: 11 us -> 12.1 us
    ppermute x1, waiting for transfers between devices: 7.81 us -> 0.01 us  [per_device(): back = lax.ppermute(send, 'fib', forward)]
    unnamed x11 -> x7, local copies, waits for them, and re-layouts: 3.57 us -> 0.04 us
    ppermute x2, waiting for transfers between devices: 5.43 us -> 8.2 us  [the longest x1 7.2 us: per_device(): back_two = lax.ppermute(swapped, 'fib', forward)]
    ppermute x21, starting transfers between devices: 18.1 us -> 20.5 us  [crossed(): return lax.ppermute(value, ('fib', 'pln'), pairs)]
    ppermute x1, starting transfers between devices: 0.07 us -> 1.37 us  [per_device(): order_next = lax.ppermute(slot_order[0], 'fib', core_swap)]
    pallas_call x1, Pallas kernels: 1.82 us -> 2.9 us  [per_device(): pl.pallas_call(functools.partial(interp_kernel, owners), out_shape=[piece...]
    ppermute x21, waiting for transfers between devices: 10.9 us -> 10.2 us  [crossed(): return lax.ppermute(value, ('fib', 'pln'), pairs)]
  transfers between devices with their start and end apart: 26 -> 26, of which waited for: 15 -> 14; matrix products, arithmetic and copies ran while one was open for 0% -> 0% of each run, Pallas kernels for 2% -> 2%
where the time goes in v8:
time: 57.9 us; the launch traced here: 57.7 us
  starting transfers between devices  24.1 us (42%)
  waiting for transfers between devices  20.5 us (35%)
  Pallas kernels  12.1 us (21%)
  other arithmetic  0.68 us (1%)
    ppermute x21, starting transfers between devices, crossed(): return lax.ppermute(value, ('fib', 'pln'), pairs)  20.5 us
    ppermute x21, waiting for transfers between devices, crossed(): return lax.ppermute(value, ('fib', 'pln'), pairs)  10.2 us
    ppermute x1, waiting for transfers between devices, per_device(): back_two = lax.ppermute(swapped, 'fib', forward)  7.2 us
    pallas_call x1, Pallas kernels, per_device(): pl.pallas_call(functools.partial(factor_kernel, mid), out_shape=[jax.Shap...  6.02 us
    pallas_call x1, Pallas kernels, per_device(): pl.pallas_call(functools.partial(interp_kernel, owners), out_shape=[piece...  2.9 us
    ppermute x1, starting transfers between devices, per_device(): back_two = lax.ppermute(swapped, 'fib', forward)  1.62 us
    ppermute x1, starting transfers between devices, per_device(): order_next = lax.ppermute(slot_order[0], 'fib', core_swap)  1.37 us
    ppermute x1, waiting for transfers between devices, per_device(): core_values = first + lax.ppermute(second, 'fib', core_swap)  1.24 us
  transfers between devices with their start and end apart: 26, of which 14 were waited for; matrix products, arithmetic and copies ran while one was open for 0% of the time, Pallas kernels for 2%

profile of v8, /device:TPU:0, one launch (start us, length us, event | category | flops | bytes accessed | tf_op | source)
XLA Modules:
  0.0 57.7 jit_solution(5331115553592806176)
XLA Ops:
  0.0 0.0 copy-start.2
  0.0 2.9 %interp.1 = (f32[96,512]{1,0:T(8,128)S(1)}, f32[96,512]{1,0:T(8,128)S(1)}, f32[192,512]{1,0:T(8,128)S(1)}, f32[96,512]{1,0:T(8,128)S(1)}) custom-call(s32[3,1,16]{2,1,0:T(1,128)} %bitcast.21, f32[288,1000]{1,0:T(8,128)} %bitcast.25, f32[1000,512]{1,0:T(8,128)} %interp_hbm.1), custom_call_target="tpu_custom_call" | custom-call | tf_op jit(solution)/shard_map/interp/pallas_call | solution.py:255
  2.9 0.5 collective-permute-start.1
  3.4 0.1 collective-permute-start.2
  3.5 1.0 %collective-permute-done.1.next_zero_ref = f32[96,512]{1,0:T(8,128)S(1)} collective-permute-done((f32[96,512]{1,0:T(8,128)S(1)}, f32[96,512]{1,0:T(8,128)S(1)}, u32[]{:S(2)}, u32[]{:S(2)}) %collective-permute-start.1) | collective-permute-done | bytes 196640 | tf_op jit(solution)/shard_map/ppermute | solution.py:270
  4.5 1.6 %collective-permute-start.3 = (f32[96,512]{1,0:T(8,128)S(1)}, f32[96,512]{1,0:T(8,128)S(1)}, u32[]{:S(2)}, u32[]{:S(2)}) collective-permute-start(f32[96,512]{1,0:T(8,128)S(1)} %collective-permute-done.1.next_zero_ref), channel_id=1, source_target_pairs={{0,2},{2,4},{4,6},{6,8},{8,10},{10,12},{12,14},{14,16},{16,18},{18... | collective-permute-start | bytes 589832 | tf_op jit(solution)/shard_map/ppermute | solution.py:272
  6.1 0.0 copy-done.2
  6.1 1.4 %collective-permute-start = (s32[1,192]{1,0:T(1,128)S(1)}, s32[1,192]{1,0:T(1,128)S(1)}, u32[]{:S(2)}, u32[]{:S(2)}) collective-permute-start(s32[1,192]{1,0:T(1,128)S(1)} %bitcast.23), channel_id=1, source_target_pairs={{0,2},{2,0},{4,6},{6,4},{8,10},{10,8},{12,14},{14,12},{16,18},{18,... | collective-permute-start | bytes 2312 | tf_op jit(solution)/shard_map/ppermute | solution.py:252
  7.5 0.8 %collective-permute-done.order_next_ref = s32[1,192]{1,0:T(1,128)S(1)} collective-permute-done((s32[1,192]{1,0:T(1,128)S(1)}, s32[1,192]{1,0:T(1,128)S(1)}, u32[]{:S(2)}, u32[]{:S(2)}) %collective-permute-start) | collective-permute-done | bytes 800 | tf_op jit(solution)/shard_map/ppermute | solution.py:252
  8.3 0.0 copy-done.1
  8.3 1.1 %pick.1.pick_ref = f32[384,288]{1,0:T(8,128)S(1)} custom-call(s32[3,1,16]{2,1,0:T(1,128)S(1)} %bitcast.22, s32[1,192]{1,0:T(1,128)S(1)} %bitcast.24, s32[1,192]{1,0:T(1,128)S(1)} %collective-permute-done.order_next_ref), custom_call_target="tpu_custom_call" | custom-call | tf_op jit(solution)/shard_map/pick/pallas_call | solution.py:273
  9.4 7.2 %collective-permute-done.3.back_two_ref = f32[96,512]{1,0:T(8,128)S(1)} collective-permute-done((f32[96,512]{1,0:T(8,128)S(1)}, f32[96,512]{1,0:T(8,128)S(1)}, u32[]{:S(2)}, u32[]{:S(2)}) %collective-permute-start.3) | collective-permute-done | bytes 196640 | tf_op jit(solution)/shard_map/ppermute | solution.py:272
  16.6 0.0 collective-permute-done.2.back_ref
  16.6 0.8 %order.1 = (f32[192,512]{1,0:T(8,128)S(1)}, f32[192,512]{1,0:T(8,128)S(1)}) custom-call(f32[384,288]{1,0:T(8,128)S(1)} %pick.1.pick_ref, f32[96,512]{1,0:T(8,128)S(1)} %get-tuple-element.18.zero_ref, f32[96,512]{1,0:T(8,128)S(1)} %get-tuple-element.19.one_ref, f32[96,512]{1,0:T(8,128)S(1)} %collective-permute-done.1.next_zero_ref, ...), custom_call_target="tpu_custom_call" | custom-call | tf_op jit(solution)/shard_map/order/pallas_call | solution.py:281
  17.5 0.0 copy-start
  17.6 0.1 slice_bitcast_fusion
  17.7 0.1 collective-permute-start.11
  17.8 1.8 %collective-permute-start.10 = (f32[192,128]{1,0:T(8,128)S(1)}, f32[192,128]{1,0:T(8,128)S(1)}, u32[]{:S(2)}, u32[]{:S(2)}) collective-permute-start(f32[192,128]{1,0:T(8,128)S(1)} %get-tuple-element.32), channel_id=1, source_target_pairs={{0,26},{1,27},{2,0},{3,1},{4,30},{5,31},{6,4},{7,5},{8,18},{9,19},... | collective-permute-start | bytes 294920 | tf_op jit(solution)/shard_map/ppermute | solution.py:227
  19.5 0.0 collective-permute-start.9
  19.5 0.0 collective-permute-start.8
  19.5 1.6 %collective-permute-start.7 = (f32[192,128]{1,0:T(8,128)S(1)}, f32[192,128]{1,0:T(8,128)S(1)}, u32[]{:S(2)}, u32[]{:S(2)}) collective-permute-start(f32[192,128]{1,0:T(8,128)S(1)} %get-tuple-element.35), channel_id=1, source_target_pairs={{0,14},{1,15},{2,0},{3,1},{4,10},{5,11},{6,4},{7,5},{8,6},{9,7},{1... | collective-permute-start | bytes 294920 | tf_op jit(solution)/shard_map/ppermute | solution.py:227
  21.2 0.0 collective-permute-done.11.refs_7_
  21.2 1.3 %collective-permute-start.6 = (f32[192,128]{1,0:T(8,128)S(1)}, f32[192,128]{1,0:T(8,128)S(1)}, u32[]{:S(2)}, u32[]{:S(2)}) collective-permute-start(f32[192,128]{1,0:T(8,128)S(1)} %get-tuple-element.36), channel_id=1, source_target_pairs={{0,10},{1,11},{2,0},{3,1},{4,14},{5,15},{6,4},{7,5},{8,2},{9,3},{1... | collective-permute-start | bytes 294920 | tf_op jit(solution)/shard_map/ppermute | solution.py:227
  22.5 0.0 collective-permute-done.10.refs_6_
  22.5 0.7 %collective-permute-start.5 = (f32[192,128]{1,0:T(8,128)S(1)}, f32[192,128]{1,0:T(8,128)S(1)}, u32[]{:S(2)}, u32[]{:S(2)}) collective-permute-start(f32[192,128]{1,0:T(8,128)S(1)} %get-tuple-element.37), channel_id=1, source_target_pairs={{0,6},{1,7},{2,0},{3,1},{4,2},{5,3},{6,4},{7,5},{8,14},{9,15},{10,... | collective-permute-start | bytes 294920 | tf_op jit(solution)/shard_map/ppermute | solution.py:227
  23.2 0.0 collective-permute-done.9.refs_5_
  23.2 4.1 %collective-permute-start.4 = (f32[192,128]{1,0:T(8,128)S(1)}, f32[192,128]{1,0:T(8,128)S(1)}, u32[]{:S(2)}, u32[]{:S(2)}) collective-permute-start(f32[192,128]{1,0:T(8,128)S(1)} %get-tuple-element.38), channel_id=1, source_target_pairs={{0,2},{1,3},{2,0},{3,1},{4,6},{5,7},{6,4},{7,5},{8,10},{9,11},{10,... | collective-permute-start | bytes 294920 | tf_op jit(solution)/shard_map/ppermute | solution.py:227
  27.3 0.0 collective-permute-done.8.refs_4_
  27.3 0.0 collective-permute-done.7.refs_3_
  27.3 0.0 collective-permute-done.6.refs_2_
  27.3 0.0 collective-permute-done.5.refs_1_
  27.3 0.9 %collective-permute-done.4.refs_0_ = f32[192,128]{1,0:T(8,128)S(1)} collective-permute-done((f32[192,128]{1,0:T(8,128)S(1)}, f32[192,128]{1,0:T(8,128)S(1)}, u32[]{:S(2)}, u32[]{:S(2)}) %collective-permute-start.4) | collective-permute-done | bytes 98336 | tf_op jit(solution)/shard_map/ppermute | solution.py:227
  28.2 0.0 copy-done
  28.2 1.2 %image.1 = (f32[192,128]{1,0:T(8,128)S(1)}, f32[192,128]{1,0:T(8,128)S(1)}, f32[192,128]{1,0:T(8,128)S(1)}, f32[192,128]{1,0:T(8,128)S(1)}, f32[768,256]{1,0:T(8,128)S(1)}) custom-call(f32[192,128]{1,0:T(8,128)S(1)} %collective-permute-done.4.refs_0_, f32[192,128]{1,0:T(8,128)S(1)} %collective-permute-done.5.refs_1_, ...), custom_call_target="tpu_custom_call" | custom-call | tf_op jit(solution)/shard_map/image/pallas_call | solution.py:304
  29.4 0.4 collective-permute-start.12
  29.9 0.2 collective-permute-start.13
  30.0 2.3 %collective-permute-start.14 = (f32[192,128]{1,0:T(8,128)S(1)}, f32[192,128]{1,0:T(8,128)S(1)}, u32[]{:S(2)}, u32[]{:S(2)}) collective-permute-start(f32[192,128]{1,0:T(8,128)S(1)} %get-tuple-element.26), channel_id=1, source_target_pairs={{0,2},{1,3},{2,4},{3,5},{4,6},{5,7},{6,0},{7,1},{8,10},{9,11},{10,... | collective-permute-start | bytes 294920 | tf_op jit(solution)/shard_map/ppermute | solution.py:227
  32.3 0.0 collective-permute-start.15
  32.3 0.6 %collective-permute-start.16 = (f32[192,128]{1,0:T(8,128)S(1)}, f32[192,128]{1,0:T(8,128)S(1)}, u32[]{:S(2)}, u32[]{:S(2)}) collective-permute-start(f32[192,128]{1,0:T(8,128)S(1)} %get-tuple-element.28), channel_id=1, source_target_pairs={{0,2},{1,3},{2,0},{3,1},{4,6},{5,7},{6,4},{7,5},{8,10},{9,11},{10,... | collective-permute-start | bytes 294920 | tf_op jit(solution)/shard_map/ppermute | solution.py:227
  32.9 1.9 %collective-permute-done.13 = f32[192,128]{1,0:T(8,128)S(1)} collective-permute-done((f32[192,128]{1,0:T(8,128)S(1)}, f32[192,128]{1,0:T(8,128)S(1)}, u32[]{:S(2)}, u32[]{:S(2)}) %collective-permute-start.13) | collective-permute-done | bytes 98336 | tf_op jit(solution)/shard_map/ppermute | solution.py:227
  34.8 1.1 %collective-permute-done.14 = f32[192,128]{1,0:T(8,128)S(1)} collective-permute-done((f32[192,128]{1,0:T(8,128)S(1)}, f32[192,128]{1,0:T(8,128)S(1)}, u32[]{:S(2)}, u32[]{:S(2)}) %collective-permute-start.14) | collective-permute-done | bytes 98336 | tf_op jit(solution)/shard_map/ppermute | solution.py:227
  35.9 0.4 collective-permute-done.15
  36.3 0.0 collective-permute-done.16
  36.4 0.1 collective-permute-start.20
  36.5 2.4 %collective-permute-start.19 = (f32[192,128]{1,0:T(8,128)S(1)}, f32[192,128]{1,0:T(8,128)S(1)}, u32[]{:S(2)}, u32[]{:S(2)}) collective-permute-start(f32[192,128]{1,0:T(8,128)S(1)} %add_add_fusion.1), channel_id=1, source_target_pairs={{0,18},{1,19},{2,0},{3,1},{4,22},{5,23},{6,4},{7,5},{8,26},{9,27},... | collective-permute-start | bytes 294920 | tf_op jit(solution)/shard_map/ppermute | solution.py:227
  38.8 0.0 collective-permute-start.18
  38.8 1.6 %collective-permute-start.17 = (f32[192,128]{1,0:T(8,128)S(1)}, f32[192,128]{1,0:T(8,128)S(1)}, u32[]{:S(2)}, u32[]{:S(2)}) collective-permute-start(f32[192,128]{1,0:T(8,128)S(1)} %add_add_fusion.1), channel_id=1, source_target_pairs={{0,26},{1,27},{2,0},{3,1},{4,30},{5,31},{6,4},{7,5},{8,18},{9,19},... | collective-permute-start | bytes 294920 | tf_op jit(solution)/shard_map/ppermute | solution.py:227
  40.4 0.0 collective-permute-done.20
  40.4 0.6 %collective-permute-done.19 = f32[192,128]{1,0:T(8,128)S(1)} collective-permute-done((f32[192,128]{1,0:T(8,128)S(1)}, f32[192,128]{1,0:T(8,128)S(1)}, u32[]{:S(2)}, u32[]{:S(2)}) %collective-permute-start.19) | collective-permute-done | bytes 98336 | tf_op jit(solution)/shard_map/ppermute | solution.py:227
  41.0 1.0 %collective-permute-done.18 = f32[192,128]{1,0:T(8,128)S(1)} collective-permute-done((f32[192,128]{1,0:T(8,128)S(1)}, f32[192,128]{1,0:T(8,128)S(1)}, u32[]{:S(2)}, u32[]{:S(2)}) %collective-permute-start.18) | collective-permute-done | bytes 98336 | tf_op jit(solution)/shard_map/ppermute | solution.py:227
  42.1 1.1 %collective-permute-done.17 = f32[192,128]{1,0:T(8,128)S(1)} collective-permute-done((f32[192,128]{1,0:T(8,128)S(1)}, f32[192,128]{1,0:T(8,128)S(1)}, u32[]{:S(2)}, u32[]{:S(2)}) %collective-permute-start.17) | collective-permute-done | bytes 98336 | tf_op jit(solution)/shard_map/ppermute | solution.py:227
  43.1 2.1 %collective-permute-start.24 = (f32[192,128]{1,0:T(8,128)S(1)}, f32[192,128]{1,0:T(8,128)S(1)}, u32[]{:S(2)}, u32[]{:S(2)}) collective-permute-start(f32[192,128]{1,0:T(8,128)S(1)} %add_add_fusion), channel_id=1, source_target_pairs={{0,2},{1,3},{2,5},{3,4},{4,6},{5,7},{6,1},{7,0},{8,10},{9,11},{10,... | collective-permute-start | bytes 294920 | tf_op jit(solution)/shard_map/ppermute | solution.py:227
  45.3 0.1 collective-permute-start.23
  45.3 1.1 %collective-permute-start.22 = (f32[192,128]{1,0:T(8,128)S(1)}, f32[192,128]{1,0:T(8,128)S(1)}, u32[]{:S(2)}, u32[]{:S(2)}) collective-permute-start(f32[192,128]{1,0:T(8,128)S(1)} %add_add_fusion), channel_id=1, source_target_pairs={{0,2},{1,3},{2,1},{3,0},{4,6},{5,7},{6,5},{7,4},{8,10},{9,11},{10,... | collective-permute-start | bytes 294920 | tf_op jit(solution)/shard_map/ppermute | solution.py:227
  46.4 0.2 collective-permute-start.21
  46.6 2.1 %collective-permute-done.24.refs_3_ = f32[192,128]{1,0:T(8,128)S(1)} collective-permute-done((f32[192,128]{1,0:T(8,128)S(1)}, f32[192,128]{1,0:T(8,128)S(1)}, u32[]{:S(2)}, u32[]{:S(2)}) %collective-permute-start.24) | collective-permute-done | bytes 98336 | tf_op jit(solution)/shard_map/ppermute | solution.py:227
  48.7 0.6 collective-permute-done.23.refs_2_
  49.3 0.5 collective-permute-done.22.refs_1_
  49.8 0.0 collective-permute-done.21.refs_0_
  49.8 0.0 collective-permute-done.12.field_ref
  49.8 6.0 %factor.1 = (f32[128,128]{1,0:T(8,128)S(1)}, f32[128,128]{1,0:T(8,128)S(1)}) custom-call(f32[768,256]{1,0:T(8,128)S(1)} %collective-permute-done.12.field_ref, f32[192,128]{1,0:T(8,128)S(1)} %collective-permute-done.21.refs_0_, f32[192,128]{1,0:T(8,128)S(1)} %collective-permute-done.22.refs_1_, f32[192,128]{1,0:T(8,128)S(1)} %collective-permute-done.23.refs_2_, ...), custom_call_target="tpu_custom_call" | custom-call | tf_op jit(solution)/shard_map/factor/pallas_call | solution.py:317
  55.8 0.1 collective-permute-start.25
  55.9 1.2 %collective-permute-done.25 = f32[128,128]{1,0:T(8,128)S(1)} collective-permute-done((f32[128,128]{1,0:T(8,128)S(1)}, f32[128,128]{1,0:T(8,128)S(1)}, u32[]{:S(2)}, u32[]{:S(2)}) %collective-permute-start.25) | collective-permute-done | bytes 65568 | tf_op jit(solution)/shard_map/ppermute | solution.py:330
  57.1 0.6 %add_bitcast_fusion = f32[1,1,128,128]{3,2,1,0:T(8,128)} fusion(f32[128,128]{1,0:T(8,128)S(1)} %get-tuple-element.29, f32[128,128]{1,0:T(8,128)S(1)} %collective-permute-done.25), kind=kLoop, calls=%fused_computation.10 | loop fusion | flops 16384 | bytes 196608 | tf_op jit(solution)/shard_map/broadcast_in_dim | solution.py:331
  (7 shorter events, 0.2 us)
Async XLA Ops:
  0.0 8.3 %copy-start.1 = (s32[1,16,3]{1,0,2:T(1,128)S(1)}, s32[1,16,3]{1,0,2:T(1,128)}, u32[]{:S(2)}) copy-start(s32[1,16,3]{1,0,2:T(1,128)} %param.7) | copy-start | bytes 580
  0.0 6.1 %copy-start.2 = (s32[1,1,192]{2,1,0:T(1,128)S(1)}, s32[1,1,192]{2,1,0:T(1,128)}, u32[]{:S(2)}) copy-start(s32[1,1,192]{2,1,0:T(1,128)} %param.8) | copy-start | bytes 2308
  2.9 1.6 %collective-permute-start.1 = (f32[96,512]{1,0:T(8,128)S(1)}, f32[96,512]{1,0:T(8,128)S(1)}, u32[]{:S(2)}, u32[]{:S(2)}) collective-permute-start(f32[96,512]{1,0:T(8,128)S(1)} %get-tuple-element.20), channel_id=1, source_target_pairs={{0,2},{2,0},{4,6},{6,4},{8,10},{10,8},{12,14},{14,12},{16,18},{18,... | collective-permute-start | bytes 589832 | tf_op jit(solution)/shard_map/ppermute | solution.py:270
  3.4 13.2 %collective-permute-start.2 = (f32[192,512]{1,0:T(8,128)S(1)}, f32[192,512]{1,0:T(8,128)S(1)}, u32[]{:S(2)}, u32[]{:S(2)}) collective-permute-start(f32[192,512]{1,0:T(8,128)S(1)} %get-tuple-element.21), channel_id=1, source_target_pairs={{0,2},{2,4},{4,6},{6,8},{8,10},{10,12},{12,14},{14,16},{16,18},{18... | collective-permute-start | bytes 1179656 | tf_op jit(solution)/shard_map/ppermute | solution.py:271
  4.5 12.1 %collective-permute-start.3 = (f32[96,512]{1,0:T(8,128)S(1)}, f32[96,512]{1,0:T(8,128)S(1)}, u32[]{:S(2)}, u32[]{:S(2)}) collective-permute-start(f32[96,512]{1,0:T(8,128)S(1)} %collective-permute-done.1.next_zero_ref), channel_id=1, source_target_pairs={{0,2},{2,4},{4,6},{6,8},{8,10},{10,12},{12,14},{14,16},{16,18},{18... | collective-permute-start | bytes 589832 | tf_op jit(solution)/shard_map/ppermute | solution.py:272
  6.1 2.2 %collective-permute-start = (s32[1,192]{1,0:T(1,128)S(1)}, s32[1,192]{1,0:T(1,128)S(1)}, u32[]{:S(2)}, u32[]{:S(2)}) collective-permute-start(s32[1,192]{1,0:T(1,128)S(1)} %bitcast.23), channel_id=1, source_target_pairs={{0,2},{2,0},{4,6},{6,4},{8,10},{10,8},{12,14},{14,12},{16,18},{18,... | collective-permute-start | bytes 2312 | tf_op jit(solution)/shard_map/ppermute | solution.py:252
  17.5 10.7 %copy-start = (f32[768,128]{1,0:T(8,128)S(1)}, f32[768,128]{1,0:T(8,128)}, u32[]{:S(2)}) copy-start(f32[768,128]{1,0:T(8,128)} %refs_8_.1) | copy-start | bytes 1179652
  17.7 3.5 %collective-permute-start.11 = (f32[192,128]{1,0:T(8,128)S(1)}, f32[192,128]{1,0:T(8,128)S(1)}, u32[]{:S(2)}, u32[]{:S(2)}) collective-permute-start(f32[192,128]{1,0:T(8,128)S(1)} %get-tuple-element.31), channel_id=1, source_target_pairs={{0,30},{1,31},{2,0},{3,1},{4,26},{5,27},{6,4},{7,5},{8,22},{9,23},... | collective-permute-start | bytes 294920 | tf_op jit(solution)/shard_map/ppermute | solution.py:227
  17.8 4.7 %collective-permute-start.10 = (f32[192,128]{1,0:T(8,128)S(1)}, f32[192,128]{1,0:T(8,128)S(1)}, u32[]{:S(2)}, u32[]{:S(2)}) collective-permute-start(f32[192,128]{1,0:T(8,128)S(1)} %get-tuple-element.32), channel_id=1, source_target_pairs={{0,26},{1,27},{2,0},{3,1},{4,30},{5,31},{6,4},{7,5},{8,18},{9,19},... | collective-permute-start | bytes 294920 | tf_op jit(solution)/shard_map/ppermute | solution.py:227
  19.5 3.7 %collective-permute-start.9 = (f32[192,128]{1,0:T(8,128)S(1)}, f32[192,128]{1,0:T(8,128)S(1)}, u32[]{:S(2)}, u32[]{:S(2)}) collective-permute-start(f32[192,128]{1,0:T(8,128)S(1)} %get-tuple-element.33), channel_id=1, source_target_pairs={{0,22},{1,23},{2,0},{3,1},{4,18},{5,19},{6,4},{7,5},{8,30},{9,31},... | collective-permute-start | bytes 294920 | tf_op jit(solution)/shard_map/ppermute | solution.py:227
  19.5 7.7 %collective-permute-start.8 = (f32[192,128]{1,0:T(8,128)S(1)}, f32[192,128]{1,0:T(8,128)S(1)}, u32[]{:S(2)}, u32[]{:S(2)}) collective-permute-start(f32[192,128]{1,0:T(8,128)S(1)} %get-tuple-element.34), channel_id=1, source_target_pairs={{0,18},{1,19},{2,0},{3,1},{4,22},{5,23},{6,4},{7,5},{8,26},{9,27},... | collective-permute-start | bytes 294920 | tf_op jit(solution)/shard_map/ppermute | solution.py:227
  19.5 7.7 %collective-permute-start.7 = (f32[192,128]{1,0:T(8,128)S(1)}, f32[192,128]{1,0:T(8,128)S(1)}, u32[]{:S(2)}, u32[]{:S(2)}) collective-permute-start(f32[192,128]{1,0:T(8,128)S(1)} %get-tuple-element.35), channel_id=1, source_target_pairs={{0,14},{1,15},{2,0},{3,1},{4,10},{5,11},{6,4},{7,5},{8,6},{9,7},{1... | collective-permute-start | bytes 294920 | tf_op jit(solution)/shard_map/ppermute | solution.py:227
  21.2 6.1 %collective-permute-start.6 = (f32[192,128]{1,0:T(8,128)S(1)}, f32[192,128]{1,0:T(8,128)S(1)}, u32[]{:S(2)}, u32[]{:S(2)}) collective-permute-start(f32[192,128]{1,0:T(8,128)S(1)} %get-tuple-element.36), channel_id=1, source_target_pairs={{0,10},{1,11},{2,0},{3,1},{4,14},{5,15},{6,4},{7,5},{8,2},{9,3},{1... | collective-permute-start | bytes 294920 | tf_op jit(solution)/shard_map/ppermute | solution.py:227
  22.5 4.8 %collective-permute-start.5 = (f32[192,128]{1,0:T(8,128)S(1)}, f32[192,128]{1,0:T(8,128)S(1)}, u32[]{:S(2)}, u32[]{:S(2)}) collective-permute-start(f32[192,128]{1,0:T(8,128)S(1)} %get-tuple-element.37), channel_id=1, source_target_pairs={{0,6},{1,7},{2,0},{3,1},{4,2},{5,3},{6,4},{7,5},{8,14},{9,15},{10,... | collective-permute-start | bytes 294920 | tf_op jit(solution)/shard_map/ppermute | solution.py:227
  23.2 5.0 %collective-permute-start.4 = (f32[192,128]{1,0:T(8,128)S(1)}, f32[192,128]{1,0:T(8,128)S(1)}, u32[]{:S(2)}, u32[]{:S(2)}) collective-permute-start(f32[192,128]{1,0:T(8,128)S(1)} %get-tuple-element.38), channel_id=1, source_target_pairs={{0,2},{1,3},{2,0},{3,1},{4,6},{5,7},{6,4},{7,5},{8,10},{9,11},{10,... | collective-permute-start | bytes 294920 | tf_op jit(solution)/shard_map/ppermute | solution.py:227
  29.4 20.3 %collective-permute-start.12 = (f32[768,256]{1,0:T(8,128)S(1)}, f32[768,256]{1,0:T(8,128)S(1)}, u32[]{:S(2)}, u32[]{:S(2)}) collective-permute-start(f32[768,256]{1,0:T(8,128)S(1)} %get-tuple-element.24), channel_id=1, source_target_pairs={{0,2},{1,3},{2,0},{3,1},{4,6},{5,7},{6,4},{7,5},{8,10},{9,11},{10,... | collective-permute-start | bytes 2359304 | tf_op jit(solution)/shard_map/ppermute | solution.py:227
  29.9 4.9 %collective-permute-start.13 = (f32[192,128]{1,0:T(8,128)S(1)}, f32[192,128]{1,0:T(8,128)S(1)}, u32[]{:S(2)}, u32[]{:S(2)}) collective-permute-start(f32[192,128]{1,0:T(8,128)S(1)} %get-tuple-element.25), channel_id=1, source_target_pairs={{0,2},{1,3},{2,5},{3,4},{4,6},{5,7},{6,1},{7,0},{8,10},{9,11},{10,... | collective-permute-start | bytes 294920 | tf_op jit(solution)/shard_map/ppermute | solution.py:227
  30.0 5.9 %collective-permute-start.14 = (f32[192,128]{1,0:T(8,128)S(1)}, f32[192,128]{1,0:T(8,128)S(1)}, u32[]{:S(2)}, u32[]{:S(2)}) collective-permute-start(f32[192,128]{1,0:T(8,128)S(1)} %get-tuple-element.26), channel_id=1, source_target_pairs={{0,2},{1,3},{2,4},{3,5},{4,6},{5,7},{6,0},{7,1},{8,10},{9,11},{10,... | collective-permute-start | bytes 294920 | tf_op jit(solution)/shard_map/ppermute | solution.py:227
  32.3 4.0 %collective-permute-start.15 = (f32[192,128]{1,0:T(8,128)S(1)}, f32[192,128]{1,0:T(8,128)S(1)}, u32[]{:S(2)}, u32[]{:S(2)}) collective-permute-start(f32[192,128]{1,0:T(8,128)S(1)} %get-tuple-element.27), channel_id=1, source_target_pairs={{0,2},{1,3},{2,1},{3,0},{4,6},{5,7},{6,5},{7,4},{8,10},{9,11},{10,... | collective-permute-start | bytes 294920 | tf_op jit(solution)/shard_map/ppermute | solution.py:227
  32.3 4.0 %collective-permute-start.16 = (f32[192,128]{1,0:T(8,128)S(1)}, f32[192,128]{1,0:T(8,128)S(1)}, u32[]{:S(2)}, u32[]{:S(2)}) collective-permute-start(f32[192,128]{1,0:T(8,128)S(1)} %get-tuple-element.28), channel_id=1, source_target_pairs={{0,2},{1,3},{2,0},{3,1},{4,6},{5,7},{6,4},{7,5},{8,10},{9,11},{10,... | collective-permute-start | bytes 294920 | tf_op jit(solution)/shard_map/ppermute | solution.py:227
  36.4 4.0 %collective-permute-start.20 = (f32[192,128]{1,0:T(8,128)S(1)}, f32[192,128]{1,0:T(8,128)S(1)}, u32[]{:S(2)}, u32[]{:S(2)}) collective-permute-start(f32[192,128]{1,0:T(8,128)S(1)} %add_add_fusion.1), channel_id=1, source_target_pairs={{0,2},{1,3},{2,0},{3,1},{4,6},{5,7},{6,4},{7,5},{8,10},{9,11},{10,... | collective-permute-start | bytes 294920 | tf_op jit(solution)/shard_map/ppermute | solution.py:227
  36.5 4.6 %collective-permute-start.19 = (f32[192,128]{1,0:T(8,128)S(1)}, f32[192,128]{1,0:T(8,128)S(1)}, u32[]{:S(2)}, u32[]{:S(2)}) collective-permute-start(f32[192,128]{1,0:T(8,128)S(1)} %add_add_fusion.1), channel_id=1, source_target_pairs={{0,18},{1,19},{2,0},{3,1},{4,22},{5,23},{6,4},{7,5},{8,26},{9,27},... | collective-permute-start | bytes 294920 | tf_op jit(solution)/shard_map/ppermute | solution.py:227
  38.8 3.2 %collective-permute-start.18 = (f32[192,128]{1,0:T(8,128)S(1)}, f32[192,128]{1,0:T(8,128)S(1)}, u32[]{:S(2)}, u32[]{:S(2)}) collective-permute-start(f32[192,128]{1,0:T(8,128)S(1)} %add_add_fusion.1), channel_id=1, source_target_pairs={{0,10},{1,11},{2,0},{3,1},{4,14},{5,15},{6,4},{7,5},{8,2},{9,3},{1... | collective-permute-start | bytes 294920 | tf_op jit(solution)/shard_map/ppermute | solution.py:227
  38.8 4.3 %collective-permute-start.17 = (f32[192,128]{1,0:T(8,128)S(1)}, f32[192,128]{1,0:T(8,128)S(1)}, u32[]{:S(2)}, u32[]{:S(2)}) collective-permute-start(f32[192,128]{1,0:T(8,128)S(1)} %add_add_fusion.1), channel_id=1, source_target_pairs={{0,26},{1,27},{2,0},{3,1},{4,30},{5,31},{6,4},{7,5},{8,18},{9,19},... | collective-permute-start | bytes 294920 | tf_op jit(solution)/shard_map/ppermute | solution.py:227
  43.1 5.6 %collective-permute-start.24 = (f32[192,128]{1,0:T(8,128)S(1)}, f32[192,128]{1,0:T(8,128)S(1)}, u32[]{:S(2)}, u32[]{:S(2)}) collective-permute-start(f32[192,128]{1,0:T(8,128)S(1)} %add_add_fusion), channel_id=1, source_target_pairs={{0,2},{1,3},{2,5},{3,4},{4,6},{5,7},{6,1},{7,0},{8,10},{9,11},{10,... | collective-permute-start | bytes 294920 | tf_op jit(solution)/shard_map/ppermute | solution.py:227
  45.3 4.0 %collective-permute-start.23 = (f32[192,128]{1,0:T(8,128)S(1)}, f32[192,128]{1,0:T(8,128)S(1)}, u32[]{:S(2)}, u32[]{:S(2)}) collective-permute-start(f32[192,128]{1,0:T(8,128)S(1)} %add_add_fusion), channel_id=1, source_target_pairs={{0,2},{1,3},{2,4},{3,5},{4,6},{5,7},{6,0},{7,1},{8,10},{9,11},{10,... | collective-permute-start | bytes 294920 | tf_op jit(solution)/shard_map/ppermute | solution.py:227
  45.3 4.4 %collective-permute-start.22 = (f32[192,128]{1,0:T(8,128)S(1)}, f32[192,128]{1,0:T(8,128)S(1)}, u32[]{:S(2)}, u32[]{:S(2)}) collective-permute-start(f32[192,128]{1,0:T(8,128)S(1)} %add_add_fusion), channel_id=1, source_target_pairs={{0,2},{1,3},{2,1},{3,0},{4,6},{5,7},{6,5},{7,4},{8,10},{9,11},{10,... | collective-permute-start | bytes 294920 | tf_op jit(solution)/shard_map/ppermute | solution.py:227
  46.4 3.3 %collective-permute-start.21 = (f32[192,128]{1,0:T(8,128)S(1)}, f32[192,128]{1,0:T(8,128)S(1)}, u32[]{:S(2)}, u32[]{:S(2)}) collective-permute-start(f32[192,128]{1,0:T(8,128)S(1)} %add_add_fusion), channel_id=1, source_target_pairs={{0,2},{1,3},{2,0},{3,1},{4,6},{5,7},{6,4},{7,5},{8,10},{9,11},{10,... | collective-permute-start | bytes 294920 | tf_op jit(solution)/shard_map/ppermute | solution.py:227
  55.8 1.3 %collective-permute-start.25 = (f32[128,128]{1,0:T(8,128)S(1)}, f32[128,128]{1,0:T(8,128)S(1)}, u32[]{:S(2)}, u32[]{:S(2)}) collective-permute-start(f32[128,128]{1,0:T(8,128)S(1)} %get-tuple-element.30), channel_id=1, source_target_pairs={{0,2},{2,0},{4,6},{6,4},{8,10},{10,8},{12,14},{14,12},{16,18},{18,... | collective-permute-start | bytes 196616 | tf_op jit(solution)/shard_map/ppermute | solution.py:330

commit v9 on v8

--- a/solution.py
+++ b/solution.py
@@ -10,6 +10,7 @@
 F32 = jnp.float32
 BF16 = jnp.bfloat16
 SLAB = 8
+BLOCK = 16
 KSTEP = 256
 VMEM = pl.BlockSpec(memory_space=pltpu.VMEM)
 SMEM = pl.BlockSpec(memory_space=pltpu.SMEM)
@@ -172,39 +173,48 @@
     image = halves(image_scr[...])
     work[:, :rank] = dot3(image, image, ((0,), (0,)))
     work[:, rank:] = dot3(image, halves(field_ref[...]), ((0,), (0,)))
-    shape = (1, rank)
-    for base in range(0, rank, SLAB):
-        left = [work[base + k : base + k + 1, :rank] for k in range(SLAB)]
-        right = [work[base + k : base + k + 1, rank:] for k in range(SLAB)]
-        entry = [
-            [jnp.broadcast_to(left[k][:, base + i : base + i + 1], shape) for i in range(SLAB)]
-            for k in range(SLAB)
-        ]
-        for k in range(SLAB):
-            scale = lax.rsqrt(entry[k][k])
-            left[k] = left[k] * scale
-            right[k] = right[k] * jnp.concatenate([scale] * 2, axis=1)
-            factor = {i: entry[k][i] * scale for i in range(k + 1, SLAB)}
-            for i in range(k + 1, SLAB):
-                for j in range(i, SLAB):
-                    entry[i][j] = entry[i][j] - factor[i] * factor[j]
-                left[i] = left[i] - factor[i] * left[k]
-                right[i] = right[i] - jnp.concatenate([factor[i]] * 2, axis=1) * right[k]
-            out_refs[0][base + k : base + k + 1, :] = right[k][:, :rank]
-            out_refs[1][base + k : base + k + 1, :] = right[k][:, rank:]
-            line_scr[k : k + 1, :rank] = left[k]
-            line_scr[k : k + 1, rank:] = right[k]
-        after = base + SLAB
+    width = work.shape[1]
+
+    def splat(row, lane):
+        return jnp.broadcast_to(row[:, lane : lane + 1], (1, rank))
+
+    def scaled(factor, row):
+        return row * jnp.concatenate([factor] * (width // rank), axis=1)
+
+    for base in range(0, rank, BLOCK):
+        line = [work[base + k : base + k + 1, :] for k in range(BLOCK)]
+        for slab in range(0, BLOCK, SLAB):
+            ahead = base + slab
+            entry = [[splat(line[slab + k], ahead + i) for i in range(SLAB)] for k in range(SLAB)]
+            for k in range(SLAB):
+                scale = lax.rsqrt(entry[k][k])
+                line[slab + k] = scaled(scale, line[slab + k])
+                factor = {i: entry[k][i] * scale for i in range(k + 1, SLAB)}
+                for i in range(k + 1, SLAB):
+                    for j in range(i, SLAB):
+                        entry[i][j] = entry[i][j] - factor[i] * factor[j]
+                    line[slab + i] = line[slab + i] - scaled(factor[i], line[slab + k])
+                row = line[slab + k]
+                for core, out in enumerate(out_refs):
+                    out[ahead + k : ahead + k + 1, :] = row[:, (core + 1) * rank : (core + 2) * rank]
+                line_scr[slab + k : slab + k + 1, :] = row
+            for i in range(slab + SLAB, BLOCK):
+                for k in range(slab, slab + SLAB):
+                    line[i] = line[i] - scaled(splat(line[k], base + i), line[k])
+        after = base + BLOCK
         if after < rank:
-            line = line_scr[...]
-            high = line.astype(BF16).astype(F32)
-            rest = line - high
-            mid = rest.astype(BF16).astype(F32)
-            low = rest - mid
-            first = jnp.concatenate([high, high, mid, high, low, mid], axis=0).astype(BF16)
-            second = jnp.concatenate([high, mid, high, low, high, mid], axis=0).astype(BF16)
+            rows = line_scr[...]
+            high = rows.astype(BF16).astype(F32)
+            rest = rows - high
+            mid_part = rest.astype(BF16).astype(F32)
+            low = rest - mid_part
+            first = jnp.concatenate([x[:, :rank] for x in (high, high, mid_part, high, low, mid_part)], axis=0)
+            second = jnp.concatenate([high, mid_part, high, low, high, mid_part], axis=0)
             drop = lax.dot_general(
-                first[:, :rank], second, (((0,), (0,)), ((), ())), preferred_element_type=F32
+                first.astype(BF16),
+                second.astype(BF16),
+                (((0,), (0,)), ((), ())),
+                preferred_element_type=F32,
             )
             work[after:, :] = work[after:, :] - drop[after:, :]
 
@@ -322,7 +332,7 @@
         scratch_shapes=[
             pltpu.VMEM((length, rank), F32),
             pltpu.VMEM((rank, rank + 2 * tile), F32),
-            pltpu.VMEM((SLAB, rank + 2 * tile), F32),
+            pltpu.VMEM((BLOCK, rank + 2 * tile), F32),
         ],
         compiler_params=BIG,
         name="factor",

time: 57.9 us -> 57.3 us (0.990)
  Pallas kernels: 12.1 us -> 11.5 us
where the time goes in v9:
time: 57.3 us; the launch traced here: 57.2 us
  starting transfers between devices  24.1 us (42%)
  waiting for transfers between devices  20.5 us (36%)
  Pallas kernels  11.5 us (20%)
  other arithmetic  0.68 us (1%)
    ppermute x21, starting transfers between devices, crossed(): return lax.ppermute(value, ('fib', 'pln'), pairs)  20.5 us
    ppermute x21, waiting for transfers between devices, crossed(): return lax.ppermute(value, ('fib', 'pln'), pairs)  10.2 us
    ppermute x1, waiting for transfers between devices, per_device(): back_two = lax.ppermute(swapped, 'fib', forward)  7.2 us
    pallas_call x1, Pallas kernels, per_device(): pl.pallas_call(functools.partial(factor_kernel, mid), out_shape=[jax.Shap...  5.44 us
    pallas_call x1, Pallas kernels, per_device(): pl.pallas_call(functools.partial(interp_kernel, owners), out_shape=[piece...  2.9 us
    ppermute x1, starting transfers between devices, per_device(): back_two = lax.ppermute(swapped, 'fib', forward)  1.62 us
    ppermute x1, starting transfers between devices, per_device(): order_next = lax.ppermute(slot_order[0], 'fib', core_swap)  1.37 us
    ppermute x1, waiting for transfers between devices, per_device(): core_values = first + lax.ppermute(second, 'fib', core_swap)  1.24 us
  transfers between devices with their start and end apart: 26, of which 14 were waited for; matrix products, arithmetic and copies ran while one was open for 0% of the time, Pallas kernels for 2%

profile of v9, /device:TPU:0, one launch (start us, length us, event | category | flops | bytes accessed | tf_op | source)
XLA Modules:
  0.0 57.2 jit_solution(15887952035325367668)
XLA Ops:
  0.0 0.0 copy-start.1
  0.0 2.9 %interp.1 = (f32[96,512]{1,0:T(8,128)S(1)}, f32[96,512]{1,0:T(8,128)S(1)}, f32[192,512]{1,0:T(8,128)S(1)}, f32[96,512]{1,0:T(8,128)S(1)}) custom-call(s32[3,1,16]{2,1,0:T(1,128)} %bitcast.21, f32[288,1000]{1,0:T(8,128)} %bitcast.25, f32[1000,512]{1,0:T(8,128)} %interp_hbm.1), custom_call_target="tpu_custom_call" | custom-call | tf_op jit(solution)/shard_map/interp/pallas_call | solution.py:265
  2.9 0.5 collective-permute-start.1
  3.4 0.1 collective-permute-start.2
  3.5 1.0 %collective-permute-done.1.next_zero_ref = f32[96,512]{1,0:T(8,128)S(1)} collective-permute-done((f32[96,512]{1,0:T(8,128)S(1)}, f32[96,512]{1,0:T(8,128)S(1)}, u32[]{:S(2)}, u32[]{:S(2)}) %collective-permute-start.1) | collective-permute-done | bytes 196640 | tf_op jit(solution)/shard_map/ppermute | solution.py:280
  4.5 1.6 %collective-permute-start.3 = (f32[96,512]{1,0:T(8,128)S(1)}, f32[96,512]{1,0:T(8,128)S(1)}, u32[]{:S(2)}, u32[]{:S(2)}) collective-permute-start(f32[96,512]{1,0:T(8,128)S(1)} %collective-permute-done.1.next_zero_ref), channel_id=1, source_target_pairs={{0,2},{2,4},{4,6},{6,8},{8,10},{10,12},{12,14},{14,16},{16,18},{18... | collective-permute-start | bytes 589832 | tf_op jit(solution)/shard_map/ppermute | solution.py:282
  6.1 0.0 copy-done.2
  6.1 1.4 %collective-permute-start = (s32[1,192]{1,0:T(1,128)S(1)}, s32[1,192]{1,0:T(1,128)S(1)}, u32[]{:S(2)}, u32[]{:S(2)}) collective-permute-start(s32[1,192]{1,0:T(1,128)S(1)} %bitcast.23), channel_id=1, source_target_pairs={{0,2},{2,0},{4,6},{6,4},{8,10},{10,8},{12,14},{14,12},{16,18},{18,... | collective-permute-start | bytes 2312 | tf_op jit(solution)/shard_map/ppermute | solution.py:262
  7.5 0.8 %collective-permute-done.order_next_ref = s32[1,192]{1,0:T(1,128)S(1)} collective-permute-done((s32[1,192]{1,0:T(1,128)S(1)}, s32[1,192]{1,0:T(1,128)S(1)}, u32[]{:S(2)}, u32[]{:S(2)}) %collective-permute-start) | collective-permute-done | bytes 800 | tf_op jit(solution)/shard_map/ppermute | solution.py:262
  8.3 0.0 copy-done.1
  8.3 1.1 %pick.1.pick_ref = f32[384,288]{1,0:T(8,128)S(1)} custom-call(s32[3,1,16]{2,1,0:T(1,128)S(1)} %bitcast.22, s32[1,192]{1,0:T(1,128)S(1)} %bitcast.24, s32[1,192]{1,0:T(1,128)S(1)} %collective-permute-done.order_next_ref), custom_call_target="tpu_custom_call" | custom-call | tf_op jit(solution)/shard_map/pick/pallas_call | solution.py:283
  9.4 7.2 %collective-permute-done.3.back_two_ref = f32[96,512]{1,0:T(8,128)S(1)} collective-permute-done((f32[96,512]{1,0:T(8,128)S(1)}, f32[96,512]{1,0:T(8,128)S(1)}, u32[]{:S(2)}, u32[]{:S(2)}) %collective-permute-start.3) | collective-permute-done | bytes 196640 | tf_op jit(solution)/shard_map/ppermute | solution.py:282
  16.6 0.0 collective-permute-done.2.back_ref
  16.6 0.8 %order.1 = (f32[192,512]{1,0:T(8,128)S(1)}, f32[192,512]{1,0:T(8,128)S(1)}) custom-call(f32[384,288]{1,0:T(8,128)S(1)} %pick.1.pick_ref, f32[96,512]{1,0:T(8,128)S(1)} %get-tuple-element.18.zero_ref, f32[96,512]{1,0:T(8,128)S(1)} %get-tuple-element.19.one_ref, f32[96,512]{1,0:T(8,128)S(1)} %collective-permute-done.1.next_zero_ref, ...), custom_call_target="tpu_custom_call" | custom-call | tf_op jit(solution)/shard_map/order/pallas_call | solution.py:291
  17.5 0.0 copy-start
  17.6 0.1 slice_bitcast_fusion
  17.7 0.1 collective-permute-start.11
  17.8 1.8 %collective-permute-start.10 = (f32[192,128]{1,0:T(8,128)S(1)}, f32[192,128]{1,0:T(8,128)S(1)}, u32[]{:S(2)}, u32[]{:S(2)}) collective-permute-start(f32[192,128]{1,0:T(8,128)S(1)} %get-tuple-element.32), channel_id=1, source_target_pairs={{0,26},{1,27},{2,0},{3,1},{4,30},{5,31},{6,4},{7,5},{8,18},{9,19},... | collective-permute-start | bytes 294920 | tf_op jit(solution)/shard_map/ppermute | solution.py:237
  19.5 0.0 collective-permute-start.9
  19.5 0.0 collective-permute-start.8
  19.5 1.6 %collective-permute-start.7 = (f32[192,128]{1,0:T(8,128)S(1)}, f32[192,128]{1,0:T(8,128)S(1)}, u32[]{:S(2)}, u32[]{:S(2)}) collective-permute-start(f32[192,128]{1,0:T(8,128)S(1)} %get-tuple-element.35), channel_id=1, source_target_pairs={{0,14},{1,15},{2,0},{3,1},{4,10},{5,11},{6,4},{7,5},{8,6},{9,7},{1... | collective-permute-start | bytes 294920 | tf_op jit(solution)/shard_map/ppermute | solution.py:237
  21.2 0.0 collective-permute-done.11.refs_7_
  21.2 1.3 %collective-permute-start.6 = (f32[192,128]{1,0:T(8,128)S(1)}, f32[192,128]{1,0:T(8,128)S(1)}, u32[]{:S(2)}, u32[]{:S(2)}) collective-permute-start(f32[192,128]{1,0:T(8,128)S(1)} %get-tuple-element.36), channel_id=1, source_target_pairs={{0,10},{1,11},{2,0},{3,1},{4,14},{5,15},{6,4},{7,5},{8,2},{9,3},{1... | collective-permute-start | bytes 294920 | tf_op jit(solution)/shard_map/ppermute | solution.py:237
  22.5 0.0 collective-permute-done.10.refs_6_
  22.5 0.7 %collective-permute-start.5 = (f32[192,128]{1,0:T(8,128)S(1)}, f32[192,128]{1,0:T(8,128)S(1)}, u32[]{:S(2)}, u32[]{:S(2)}) collective-permute-start(f32[192,128]{1,0:T(8,128)S(1)} %get-tuple-element.37), channel_id=1, source_target_pairs={{0,6},{1,7},{2,0},{3,1},{4,2},{5,3},{6,4},{7,5},{8,14},{9,15},{10,... | collective-permute-start | bytes 294920 | tf_op jit(solution)/shard_map/ppermute | solution.py:237
  23.2 0.0 collective-permute-done.9.refs_5_
  23.2 4.1 %collective-permute-start.4 = (f32[192,128]{1,0:T(8,128)S(1)}, f32[192,128]{1,0:T(8,128)S(1)}, u32[]{:S(2)}, u32[]{:S(2)}) collective-permute-start(f32[192,128]{1,0:T(8,128)S(1)} %get-tuple-element.38), channel_id=1, source_target_pairs={{0,2},{1,3},{2,0},{3,1},{4,6},{5,7},{6,4},{7,5},{8,10},{9,11},{10,... | collective-permute-start | bytes 294920 | tf_op jit(solution)/shard_map/ppermute | solution.py:237
  27.3 0.0 collective-permute-done.8.refs_4_
  27.3 0.0 collective-permute-done.7.refs_3_
  27.3 0.0 collective-permute-done.6.refs_2_
  27.3 0.0 collective-permute-done.5.refs_1_
  27.3 0.9 %collective-permute-done.4.refs_0_ = f32[192,128]{1,0:T(8,128)S(1)} collective-permute-done((f32[192,128]{1,0:T(8,128)S(1)}, f32[192,128]{1,0:T(8,128)S(1)}, u32[]{:S(2)}, u32[]{:S(2)}) %collective-permute-start.4) | collective-permute-done | bytes 98336 | tf_op jit(solution)/shard_map/ppermute | solution.py:237
  28.2 0.0 copy-done
  28.2 1.2 %image.1 = (f32[192,128]{1,0:T(8,128)S(1)}, f32[192,128]{1,0:T(8,128)S(1)}, f32[192,128]{1,0:T(8,128)S(1)}, f32[192,128]{1,0:T(8,128)S(1)}, f32[768,256]{1,0:T(8,128)S(1)}) custom-call(f32[192,128]{1,0:T(8,128)S(1)} %collective-permute-done.4.refs_0_, f32[192,128]{1,0:T(8,128)S(1)} %collective-permute-done.5.refs_1_, ...), custom_call_target="tpu_custom_call" | custom-call | tf_op jit(solution)/shard_map/image/pallas_call | solution.py:314
  29.4 0.4 collective-permute-start.12
  29.9 0.2 collective-permute-start.13
  30.0 2.3 %collective-permute-start.14 = (f32[192,128]{1,0:T(8,128)S(1)}, f32[192,128]{1,0:T(8,128)S(1)}, u32[]{:S(2)}, u32[]{:S(2)}) collective-permute-start(f32[192,128]{1,0:T(8,128)S(1)} %get-tuple-element.26), channel_id=1, source_target_pairs={{0,2},{1,3},{2,4},{3,5},{4,6},{5,7},{6,0},{7,1},{8,10},{9,11},{10,... | collective-permute-start | bytes 294920 | tf_op jit(solution)/shard_map/ppermute | solution.py:237
  32.3 0.0 collective-permute-start.15
  32.3 0.6 %collective-permute-start.16 = (f32[192,128]{1,0:T(8,128)S(1)}, f32[192,128]{1,0:T(8,128)S(1)}, u32[]{:S(2)}, u32[]{:S(2)}) collective-permute-start(f32[192,128]{1,0:T(8,128)S(1)} %get-tuple-element.28), channel_id=1, source_target_pairs={{0,2},{1,3},{2,0},{3,1},{4,6},{5,7},{6,4},{7,5},{8,10},{9,11},{10,... | collective-permute-start | bytes 294920 | tf_op jit(solution)/shard_map/ppermute | solution.py:237
  32.9 1.9 %collective-permute-done.13 = f32[192,128]{1,0:T(8,128)S(1)} collective-permute-done((f32[192,128]{1,0:T(8,128)S(1)}, f32[192,128]{1,0:T(8,128)S(1)}, u32[]{:S(2)}, u32[]{:S(2)}) %collective-permute-start.13) | collective-permute-done | bytes 98336 | tf_op jit(solution)/shard_map/ppermute | solution.py:237
  34.8 1.1 %collective-permute-done.14 = f32[192,128]{1,0:T(8,128)S(1)} collective-permute-done((f32[192,128]{1,0:T(8,128)S(1)}, f32[192,128]{1,0:T(8,128)S(1)}, u32[]{:S(2)}, u32[]{:S(2)}) %collective-permute-start.14) | collective-permute-done | bytes 98336 | tf_op jit(solution)/shard_map/ppermute | solution.py:237
  35.9 0.4 collective-permute-done.15
  36.3 0.0 collective-permute-done.16
  36.4 0.1 collective-permute-start.20
  36.5 2.4 %collective-permute-start.19 = (f32[192,128]{1,0:T(8,128)S(1)}, f32[192,128]{1,0:T(8,128)S(1)}, u32[]{:S(2)}, u32[]{:S(2)}) collective-permute-start(f32[192,128]{1,0:T(8,128)S(1)} %add_add_fusion.1), channel_id=1, source_target_pairs={{0,18},{1,19},{2,0},{3,1},{4,22},{5,23},{6,4},{7,5},{8,26},{9,27},... | collective-permute-start | bytes 294920 | tf_op jit(solution)/shard_map/ppermute | solution.py:237
  38.8 0.0 collective-permute-start.18
  38.8 1.6 %collective-permute-start.17 = (f32[192,128]{1,0:T(8,128)S(1)}, f32[192,128]{1,0:T(8,128)S(1)}, u32[]{:S(2)}, u32[]{:S(2)}) collective-permute-start(f32[192,128]{1,0:T(8,128)S(1)} %add_add_fusion.1), channel_id=1, source_target_pairs={{0,26},{1,27},{2,0},{3,1},{4,30},{5,31},{6,4},{7,5},{8,18},{9,19},... | collective-permute-start | bytes 294920 | tf_op jit(solution)/shard_map/ppermute | solution.py:237
  40.4 0.0 collective-permute-done.20
  40.4 0.6 %collective-permute-done.19 = f32[192,128]{1,0:T(8,128)S(1)} collective-permute-done((f32[192,128]{1,0:T(8,128)S(1)}, f32[192,128]{1,0:T(8,128)S(1)}, u32[]{:S(2)}, u32[]{:S(2)}) %collective-permute-start.19) | collective-permute-done | bytes 98336 | tf_op jit(solution)/shard_map/ppermute | solution.py:237
  41.0 1.0 %collective-permute-done.18 = f32[192,128]{1,0:T(8,128)S(1)} collective-permute-done((f32[192,128]{1,0:T(8,128)S(1)}, f32[192,128]{1,0:T(8,128)S(1)}, u32[]{:S(2)}, u32[]{:S(2)}) %collective-permute-start.18) | collective-permute-done | bytes 98336 | tf_op jit(solution)/shard_map/ppermute | solution.py:237
  42.1 1.1 %collective-permute-done.17 = f32[192,128]{1,0:T(8,128)S(1)} collective-permute-done((f32[192,128]{1,0:T(8,128)S(1)}, f32[192,128]{1,0:T(8,128)S(1)}, u32[]{:S(2)}, u32[]{:S(2)}) %collective-permute-start.17) | collective-permute-done | bytes 98336 | tf_op jit(solution)/shard_map/ppermute | solution.py:237
  43.1 2.1 %collective-permute-start.24 = (f32[192,128]{1,0:T(8,128)S(1)}, f32[192,128]{1,0:T(8,128)S(1)}, u32[]{:S(2)}, u32[]{:S(2)}) collective-permute-start(f32[192,128]{1,0:T(8,128)S(1)} %add_add_fusion), channel_id=1, source_target_pairs={{0,2},{1,3},{2,5},{3,4},{4,6},{5,7},{6,1},{7,0},{8,10},{9,11},{10,... | collective-permute-start | bytes 294920 | tf_op jit(solution)/shard_map/ppermute | solution.py:237
  45.3 0.1 collective-permute-start.23
  45.3 1.1 %collective-permute-start.22 = (f32[192,128]{1,0:T(8,128)S(1)}, f32[192,128]{1,0:T(8,128)S(1)}, u32[]{:S(2)}, u32[]{:S(2)}) collective-permute-start(f32[192,128]{1,0:T(8,128)S(1)} %add_add_fusion), channel_id=1, source_target_pairs={{0,2},{1,3},{2,1},{3,0},{4,6},{5,7},{6,5},{7,4},{8,10},{9,11},{10,... | collective-permute-start | bytes 294920 | tf_op jit(solution)/shard_map/ppermute | solution.py:237
  46.4 0.2 collective-permute-start.21
  46.6 2.1 %collective-permute-done.24.refs_3_ = f32[192,128]{1,0:T(8,128)S(1)} collective-permute-done((f32[192,128]{1,0:T(8,128)S(1)}, f32[192,128]{1,0:T(8,128)S(1)}, u32[]{:S(2)}, u32[]{:S(2)}) %collective-permute-start.24) | collective-permute-done | bytes 98336 | tf_op jit(solution)/shard_map/ppermute | solution.py:237
  48.7 0.6 collective-permute-done.23.refs_2_
  49.3 0.5 collective-permute-done.22.refs_1_
  49.8 0.0 collective-permute-done.21.refs_0_
  49.8 0.0 collective-permute-done.12.field_ref
  49.8 5.4 %factor.1 = (f32[128,128]{1,0:T(8,128)S(1)}, f32[128,128]{1,0:T(8,128)S(1)}) custom-call(f32[768,256]{1,0:T(8,128)S(1)} %collective-permute-done.12.field_ref, f32[192,128]{1,0:T(8,128)S(1)} %collective-permute-done.21.refs_0_, f32[192,128]{1,0:T(8,128)S(1)} %collective-permute-done.22.refs_1_, f32[192,128]{1,0:T(8,128)S(1)} %collective-permute-done.23.refs_2_, ...), custom_call_target="tpu_custom_call" | custom-call | tf_op jit(solution)/shard_map/factor/pallas_call | solution.py:327
  55.2 0.1 collective-permute-start.25
  55.3 1.2 %collective-permute-done.25 = f32[128,128]{1,0:T(8,128)S(1)} collective-permute-done((f32[128,128]{1,0:T(8,128)S(1)}, f32[128,128]{1,0:T(8,128)S(1)}, u32[]{:S(2)}, u32[]{:S(2)}) %collective-permute-start.25) | collective-permute-done | bytes 65568 | tf_op jit(solution)/shard_map/ppermute | solution.py:340
  56.5 0.6 %add_bitcast_fusion = f32[1,1,128,128]{3,2,1,0:T(8,128)} fusion(f32[128,128]{1,0:T(8,128)S(1)} %get-tuple-element.29, f32[128,128]{1,0:T(8,128)S(1)} %collective-permute-done.25), kind=kLoop, calls=%fused_computation.10 | loop fusion | flops 16384 | bytes 196608 | tf_op jit(solution)/shard_map/broadcast_in_dim | solution.py:341
  (7 shorter events, 0.2 us)
Async XLA Ops:
  0.0 8.3 %copy-start.1 = (s32[1,16,3]{1,0,2:T(1,128)S(1)}, s32[1,16,3]{1,0,2:T(1,128)}, u32[]{:S(2)}) copy-start(s32[1,16,3]{1,0,2:T(1,128)} %param.7) | copy-start | bytes 580
  0.0 6.1 %copy-start.2 = (s32[1,1,192]{2,1,0:T(1,128)S(1)}, s32[1,1,192]{2,1,0:T(1,128)}, u32[]{:S(2)}) copy-start(s32[1,1,192]{2,1,0:T(1,128)} %param.8) | copy-start | bytes 2308
  2.9 1.6 %collective-permute-start.1 = (f32[96,512]{1,0:T(8,128)S(1)}, f32[96,512]{1,0:T(8,128)S(1)}, u32[]{:S(2)}, u32[]{:S(2)}) collective-permute-start(f32[96,512]{1,0:T(8,128)S(1)} %get-tuple-element.20), channel_id=1, source_target_pairs={{0,2},{2,0},{4,6},{6,4},{8,10},{10,8},{12,14},{14,12},{16,18},{18,... | collective-permute-start | bytes 589832 | tf_op jit(solution)/shard_map/ppermute | solution.py:280
  3.4 13.2 %collective-permute-start.2 = (f32[192,512]{1,0:T(8,128)S(1)}, f32[192,512]{1,0:T(8,128)S(1)}, u32[]{:S(2)}, u32[]{:S(2)}) collective-permute-start(f32[192,512]{1,0:T(8,128)S(1)} %get-tuple-element.21), channel_id=1, source_target_pairs={{0,2},{2,4},{4,6},{6,8},{8,10},{10,12},{12,14},{14,16},{16,18},{18... | collective-permute-start | bytes 1179656 | tf_op jit(solution)/shard_map/ppermute | solution.py:281
  4.5 12.1 %collective-permute-start.3 = (f32[96,512]{1,0:T(8,128)S(1)}, f32[96,512]{1,0:T(8,128)S(1)}, u32[]{:S(2)}, u32[]{:S(2)}) collective-permute-start(f32[96,512]{1,0:T(8,128)S(1)} %collective-permute-done.1.next_zero_ref), channel_id=1, source_target_pairs={{0,2},{2,4},{4,6},{6,8},{8,10},{10,12},{12,14},{14,16},{16,18},{18... | collective-permute-start | bytes 589832 | tf_op jit(solution)/shard_map/ppermute | solution.py:282
  6.1 2.2 %collective-permute-start = (s32[1,192]{1,0:T(1,128)S(1)}, s32[1,192]{1,0:T(1,128)S(1)}, u32[]{:S(2)}, u32[]{:S(2)}) collective-permute-start(s32[1,192]{1,0:T(1,128)S(1)} %bitcast.23), channel_id=1, source_target_pairs={{0,2},{2,0},{4,6},{6,4},{8,10},{10,8},{12,14},{14,12},{16,18},{18,... | collective-permute-start | bytes 2312 | tf_op jit(solution)/shard_map/ppermute | solution.py:262
  17.5 10.7 %copy-start = (f32[768,128]{1,0:T(8,128)S(1)}, f32[768,128]{1,0:T(8,128)}, u32[]{:S(2)}) copy-start(f32[768,128]{1,0:T(8,128)} %refs_8_.1) | copy-start | bytes 1179652
  17.7 3.5 %collective-permute-start.11 = (f32[192,128]{1,0:T(8,128)S(1)}, f32[192,128]{1,0:T(8,128)S(1)}, u32[]{:S(2)}, u32[]{:S(2)}) collective-permute-start(f32[192,128]{1,0:T(8,128)S(1)} %get-tuple-element.31), channel_id=1, source_target_pairs={{0,30},{1,31},{2,0},{3,1},{4,26},{5,27},{6,4},{7,5},{8,22},{9,23},... | collective-permute-start | bytes 294920 | tf_op jit(solution)/shard_map/ppermute | solution.py:237
  17.8 4.7 %collective-permute-start.10 = (f32[192,128]{1,0:T(8,128)S(1)}, f32[192,128]{1,0:T(8,128)S(1)}, u32[]{:S(2)}, u32[]{:S(2)}) collective-permute-start(f32[192,128]{1,0:T(8,128)S(1)} %get-tuple-element.32), channel_id=1, source_target_pairs={{0,26},{1,27},{2,0},{3,1},{4,30},{5,31},{6,4},{7,5},{8,18},{9,19},... | collective-permute-start | bytes 294920 | tf_op jit(solution)/shard_map/ppermute | solution.py:237
  19.5 3.7 %collective-permute-start.9 = (f32[192,128]{1,0:T(8,128)S(1)}, f32[192,128]{1,0:T(8,128)S(1)}, u32[]{:S(2)}, u32[]{:S(2)}) collective-permute-start(f32[192,128]{1,0:T(8,128)S(1)} %get-tuple-element.33), channel_id=1, source_target_pairs={{0,22},{1,23},{2,0},{3,1},{4,18},{5,19},{6,4},{7,5},{8,30},{9,31},... | collective-permute-start | bytes 294920 | tf_op jit(solution)/shard_map/ppermute | solution.py:237
  19.5 7.7 %collective-permute-start.8 = (f32[192,128]{1,0:T(8,128)S(1)}, f32[192,128]{1,0:T(8,128)S(1)}, u32[]{:S(2)}, u32[]{:S(2)}) collective-permute-start(f32[192,128]{1,0:T(8,128)S(1)} %get-tuple-element.34), channel_id=1, source_target_pairs={{0,18},{1,19},{2,0},{3,1},{4,22},{5,23},{6,4},{7,5},{8,26},{9,27},... | collective-permute-start | bytes 294920 | tf_op jit(solution)/shard_map/ppermute | solution.py:237
  19.5 7.7 %collective-permute-start.7 = (f32[192,128]{1,0:T(8,128)S(1)}, f32[192,128]{1,0:T(8,128)S(1)}, u32[]{:S(2)}, u32[]{:S(2)}) collective-permute-start(f32[192,128]{1,0:T(8,128)S(1)} %get-tuple-element.35), channel_id=1, source_target_pairs={{0,14},{1,15},{2,0},{3,1},{4,10},{5,11},{6,4},{7,5},{8,6},{9,7},{1... | collective-permute-start | bytes 294920 | tf_op jit(solution)/shard_map/ppermute | solution.py:237
  21.2 6.1 %collective-permute-start.6 = (f32[192,128]{1,0:T(8,128)S(1)}, f32[192,128]{1,0:T(8,128)S(1)}, u32[]{:S(2)}, u32[]{:S(2)}) collective-permute-start(f32[192,128]{1,0:T(8,128)S(1)} %get-tuple-element.36), channel_id=1, source_target_pairs={{0,10},{1,11},{2,0},{3,1},{4,14},{5,15},{6,4},{7,5},{8,2},{9,3},{1... | collective-permute-start | bytes 294920 | tf_op jit(solution)/shard_map/ppermute | solution.py:237
  22.5 4.8 %collective-permute-start.5 = (f32[192,128]{1,0:T(8,128)S(1)}, f32[192,128]{1,0:T(8,128)S(1)}, u32[]{:S(2)}, u32[]{:S(2)}) collective-permute-start(f32[192,128]{1,0:T(8,128)S(1)} %get-tuple-element.37), channel_id=1, source_target_pairs={{0,6},{1,7},{2,0},{3,1},{4,2},{5,3},{6,4},{7,5},{8,14},{9,15},{10,... | collective-permute-start | bytes 294920 | tf_op jit(solution)/shard_map/ppermute | solution.py:237
  23.2 5.0 %collective-permute-start.4 = (f32[192,128]{1,0:T(8,128)S(1)}, f32[192,128]{1,0:T(8,128)S(1)}, u32[]{:S(2)}, u32[]{:S(2)}) collective-permute-start(f32[192,128]{1,0:T(8,128)S(1)} %get-tuple-element.38), channel_id=1, source_target_pairs={{0,2},{1,3},{2,0},{3,1},{4,6},{5,7},{6,4},{7,5},{8,10},{9,11},{10,... | collective-permute-start | bytes 294920 | tf_op jit(solution)/shard_map/ppermute | solution.py:237
  29.4 20.3 %collective-permute-start.12 = (f32[768,256]{1,0:T(8,128)S(1)}, f32[768,256]{1,0:T(8,128)S(1)}, u32[]{:S(2)}, u32[]{:S(2)}) collective-permute-start(f32[768,256]{1,0:T(8,128)S(1)} %get-tuple-element.24), channel_id=1, source_target_pairs={{0,2},{1,3},{2,0},{3,1},{4,6},{5,7},{6,4},{7,5},{8,10},{9,11},{10,... | collective-permute-start | bytes 2359304 | tf_op jit(solution)/shard_map/ppermute | solution.py:237
  29.9 4.9 %collective-permute-start.13 = (f32[192,128]{1,0:T(8,128)S(1)}, f32[192,128]{1,0:T(8,128)S(1)}, u32[]{:S(2)}, u32[]{:S(2)}) collective-permute-start(f32[192,128]{1,0:T(8,128)S(1)} %get-tuple-element.25), channel_id=1, source_target_pairs={{0,2},{1,3},{2,5},{3,4},{4,6},{5,7},{6,1},{7,0},{8,10},{9,11},{10,... | collective-permute-start | bytes 294920 | tf_op jit(solution)/shard_map/ppermute | solution.py:237
  30.0 5.9 %collective-permute-start.14 = (f32[192,128]{1,0:T(8,128)S(1)}, f32[192,128]{1,0:T(8,128)S(1)}, u32[]{:S(2)}, u32[]{:S(2)}) collective-permute-start(f32[192,128]{1,0:T(8,128)S(1)} %get-tuple-element.26), channel_id=1, source_target_pairs={{0,2},{1,3},{2,4},{3,5},{4,6},{5,7},{6,0},{7,1},{8,10},{9,11},{10,... | collective-permute-start | bytes 294920 | tf_op jit(solution)/shard_map/ppermute | solution.py:237
  32.3 4.0 %collective-permute-start.15 = (f32[192,128]{1,0:T(8,128)S(1)}, f32[192,128]{1,0:T(8,128)S(1)}, u32[]{:S(2)}, u32[]{:S(2)}) collective-permute-start(f32[192,128]{1,0:T(8,128)S(1)} %get-tuple-element.27), channel_id=1, source_target_pairs={{0,2},{1,3},{2,1},{3,0},{4,6},{5,7},{6,5},{7,4},{8,10},{9,11},{10,... | collective-permute-start | bytes 294920 | tf_op jit(solution)/shard_map/ppermute | solution.py:237
  32.3 4.0 %collective-permute-start.16 = (f32[192,128]{1,0:T(8,128)S(1)}, f32[192,128]{1,0:T(8,128)S(1)}, u32[]{:S(2)}, u32[]{:S(2)}) collective-permute-start(f32[192,128]{1,0:T(8,128)S(1)} %get-tuple-element.28), channel_id=1, source_target_pairs={{0,2},{1,3},{2,0},{3,1},{4,6},{5,7},{6,4},{7,5},{8,10},{9,11},{10,... | collective-permute-start | bytes 294920 | tf_op jit(solution)/shard_map/ppermute | solution.py:237
  36.4 4.0 %collective-permute-start.20 = (f32[192,128]{1,0:T(8,128)S(1)}, f32[192,128]{1,0:T(8,128)S(1)}, u32[]{:S(2)}, u32[]{:S(2)}) collective-permute-start(f32[192,128]{1,0:T(8,128)S(1)} %add_add_fusion.1), channel_id=1, source_target_pairs={{0,2},{1,3},{2,0},{3,1},{4,6},{5,7},{6,4},{7,5},{8,10},{9,11},{10,... | collective-permute-start | bytes 294920 | tf_op jit(solution)/shard_map/ppermute | solution.py:237
  36.5 4.6 %collective-permute-start.19 = (f32[192,128]{1,0:T(8,128)S(1)}, f32[192,128]{1,0:T(8,128)S(1)}, u32[]{:S(2)}, u32[]{:S(2)}) collective-permute-start(f32[192,128]{1,0:T(8,128)S(1)} %add_add_fusion.1), channel_id=1, source_target_pairs={{0,18},{1,19},{2,0},{3,1},{4,22},{5,23},{6,4},{7,5},{8,26},{9,27},... | collective-permute-start | bytes 294920 | tf_op jit(solution)/shard_map/ppermute | solution.py:237
  38.8 3.2 %collective-permute-start.18 = (f32[192,128]{1,0:T(8,128)S(1)}, f32[192,128]{1,0:T(8,128)S(1)}, u32[]{:S(2)}, u32[]{:S(2)}) collective-permute-start(f32[192,128]{1,0:T(8,128)S(1)} %add_add_fusion.1), channel_id=1, source_target_pairs={{0,10},{1,11},{2,0},{3,1},{4,14},{5,15},{6,4},{7,5},{8,2},{9,3},{1... | collective-permute-start | bytes 294920 | tf_op jit(solution)/shard_map/ppermute | solution.py:237
  38.8 4.3 %collective-permute-start.17 = (f32[192,128]{1,0:T(8,128)S(1)}, f32[192,128]{1,0:T(8,128)S(1)}, u32[]{:S(2)}, u32[]{:S(2)}) collective-permute-start(f32[192,128]{1,0:T(8,128)S(1)} %add_add_fusion.1), channel_id=1, source_target_pairs={{0,26},{1,27},{2,0},{3,1},{4,30},{5,31},{6,4},{7,5},{8,18},{9,19},... | collective-permute-start | bytes 294920 | tf_op jit(solution)/shard_map/ppermute | solution.py:237
  43.1 5.6 %collective-permute-start.24 = (f32[192,128]{1,0:T(8,128)S(1)}, f32[192,128]{1,0:T(8,128)S(1)}, u32[]{:S(2)}, u32[]{:S(2)}) collective-permute-start(f32[192,128]{1,0:T(8,128)S(1)} %add_add_fusion), channel_id=1, source_target_pairs={{0,2},{1,3},{2,5},{3,4},{4,6},{5,7},{6,1},{7,0},{8,10},{9,11},{10,... | collective-permute-start | bytes 294920 | tf_op jit(solution)/shard_map/ppermute | solution.py:237
  45.3 4.0 %collective-permute-start.23 = (f32[192,128]{1,0:T(8,128)S(1)}, f32[192,128]{1,0:T(8,128)S(1)}, u32[]{:S(2)}, u32[]{:S(2)}) collective-permute-start(f32[192,128]{1,0:T(8,128)S(1)} %add_add_fusion), channel_id=1, source_target_pairs={{0,2},{1,3},{2,4},{3,5},{4,6},{5,7},{6,0},{7,1},{8,10},{9,11},{10,... | collective-permute-start | bytes 294920 | tf_op jit(solution)/shard_map/ppermute | solution.py:237
  45.3 4.4 %collective-permute-start.22 = (f32[192,128]{1,0:T(8,128)S(1)}, f32[192,128]{1,0:T(8,128)S(1)}, u32[]{:S(2)}, u32[]{:S(2)}) collective-permute-start(f32[192,128]{1,0:T(8,128)S(1)} %add_add_fusion), channel_id=1, source_target_pairs={{0,2},{1,3},{2,1},{3,0},{4,6},{5,7},{6,5},{7,4},{8,10},{9,11},{10,... | collective-permute-start | bytes 294920 | tf_op jit(solution)/shard_map/ppermute | solution.py:237
  46.4 3.3 %collective-permute-start.21 = (f32[192,128]{1,0:T(8,128)S(1)}, f32[192,128]{1,0:T(8,128)S(1)}, u32[]{:S(2)}, u32[]{:S(2)}) collective-permute-start(f32[192,128]{1,0:T(8,128)S(1)} %add_add_fusion), channel_id=1, source_target_pairs={{0,2},{1,3},{2,0},{3,1},{4,6},{5,7},{6,4},{7,5},{8,10},{9,11},{10,... | collective-permute-start | bytes 294920 | tf_op jit(solution)/shard_map/ppermute | solution.py:237
  55.2 1.3 %collective-permute-start.25 = (f32[128,128]{1,0:T(8,128)S(1)}, f32[128,128]{1,0:T(8,128)S(1)}, u32[]{:S(2)}, u32[]{:S(2)}) collective-permute-start(f32[128,128]{1,0:T(8,128)S(1)} %get-tuple-element.30), channel_id=1, source_target_pairs={{0,2},{2,0},{4,6},{6,4},{8,10},{10,8},{12,14},{14,12},{16,18},{18,... | collective-permute-start | bytes 196616 | tf_op jit(solution)/shard_map/ppermute | solution.py:340

commit v10 on v9

--- a/solution.py
+++ b/solution.py
@@ -26,6 +26,11 @@
     dims = (contract, ((), ()))
     lh, ll = left
     rh, rl = right
+    (lk,), (rk,) = contract
+    if lh.shape[lk] % 128 == 0:
+        longer_left = jnp.concatenate([lh, ll, lh], axis=lk)
+        longer_right = jnp.concatenate([rl, rh, rh], axis=rk)
+        return lax.dot_general(longer_left, longer_right, dims, preferred_element_type=F32)
     out = lax.dot_general(lh, rl, dims, preferred_element_type=F32)
     out += lax.dot_general(ll, rh, dims, preferred_element_type=F32)
     return out + lax.dot_general(lh, rh, dims, preferred_element_type=F32)
@@ -83,7 +88,7 @@
         swap_ref[...] = send_ref[rows:, :]
 
 
-def pick_kernel(rows, per_tile, table_ref, order_ref, order_next_ref, out_ref):
+def pick_kernel(rows, per_tile, table_ref, order_ref, order_next_ref, start_ref, out_ref, high_ref, low_ref):
     elements = order_ref.shape[1]
     slots = out_ref.shape[1]
     chip = lax.div(lax.axis_index("fib"), 2)
@@ -105,7 +110,8 @@
         to_place = jnp.where(place == row, 1.0, 0.0).astype(BF16)
         out_ref[core * elements : (core + 1) * elements, :] = jnp.dot(
             to_place, jnp.where(from_slot, 1.0, 0.0).astype(BF16), preferred_element_type=F32
-        )
+        ).astype(BF16)
+    high_ref[...], low_ref[...] = halves(start_ref[...].T)
 
 
 def order_kernel(pick_ref, zero_ref, one_ref, next_zero_ref, back_ref, back_two_ref, *outs):
@@ -116,14 +122,9 @@
         (next_zero_ref[...], one_ref[...], back_ref[rows:, :]),
     )
     for core, pieces in enumerate(sources):
-        pick = pick_ref[core * elements : (core + 1) * elements, :].astype(BF16)
-        line = jnp.concatenate(pieces, axis=0)
-        high = line.astype(BF16)
-        rest = line - high.astype(F32)
-        mid = rest.astype(BF16)
-        low = (rest - mid.astype(F32)).astype(BF16)
+        pick = pick_ref[core * elements : (core + 1) * elements, :]
+        high, low = halves(jnp.concatenate(pieces, axis=0))
         out = jnp.dot(pick, low, preferred_element_type=F32)
-        out += jnp.dot(pick, mid, preferred_element_type=F32)
         outs[core][...] = out + jnp.dot(pick, high, preferred_element_type=F32)
 
 
@@ -138,7 +139,7 @@
     field_ref, image_scr = refs[-2:]
     count = 2 ** len(mid)
     outs = refs[-2 - count : -2]
-    *block_refs, start_ref = refs[: -2 - count]
+    *block_refs, high_ref, low_ref = refs[: -2 - count]
     length, width = field_ref.shape
     tile = width // 2
     chip = lax.div(lax.axis_index("fib"), 2)
@@ -153,8 +154,8 @@
                 part = (2 * owner + core) * each
                 field_ref[pl.ds(at, each), core * tile : (core + 1) * tile] = block[part : part + each, :]
     field = halves(field_ref[...])
-    mixed = dot3(field, halves(start_ref[...]), ((0,), (0,)))
-    image_scr[...] = dot3(field, halves(mixed), ((1,), (0,)))
+    mixed = dot3((high_ref[...], low_ref[...]), field, ((1,), (0,)))
+    image_scr[...] = dot3(field, halves(mixed), ((1,), (1,)))
     place = bit_place(mid)
     for step, out in enumerate(outs):
         rows = out.shape[0]
@@ -162,7 +163,11 @@
         out[...] = image_scr[pl.ds(at, rows), :]
 
 
-def factor_kernel(mid, field_ref, *refs):
+def split_kernel(value_ref, high_ref, low_ref):
+    high_ref[...], low_ref[...] = halves(value_ref[...])
+
+
+def factor_kernel(mid, high_ref, low_ref, *refs):
     chunk_refs, out_refs, image_scr, work, line_scr = refs[:-5], refs[-5:-3], refs[-3], refs[-2], refs[-1]
     rank = image_scr.shape[1]
     place = bit_place(mid)
@@ -172,7 +177,7 @@
         image_scr[pl.ds(at, rows), :] = chunk[...]
     image = halves(image_scr[...])
     work[:, :rank] = dot3(image, image, ((0,), (0,)))
-    work[:, rank:] = dot3(image, halves(field_ref[...]), ((0,), (0,)))
+    work[:, rank:] = dot3(image, (high_ref[...], low_ref[...]), ((0,), (0,)))
     width = work.shape[1]
 
     def splat(row, lane):
@@ -280,14 +285,15 @@
     swapped = lax.ppermute(swap, "fib", core_swap)
     back = lax.ppermute(send, "fib", forward)
     back_two = lax.ppermute(swapped, "fib", forward)
-    pick = pl.pallas_call(
+    basis = jax.ShapeDtypeStruct((rank, length), BF16)
+    pick, *basis_parts = pl.pallas_call(
         functools.partial(pick_kernel, capacity, elements // owners),
-        out_shape=jax.ShapeDtypeStruct((2 * elements, capacity * window), F32),
-        in_specs=[SMEM, VMEM, VMEM],
-        out_specs=VMEM,
+        out_shape=[jax.ShapeDtypeStruct((2 * elements, capacity * window), BF16), basis, basis],
+        in_specs=[SMEM, VMEM, VMEM, VMEM],
+        out_specs=[VMEM] * 3,
         compiler_params=BIG,
         name="pick",
-    )(table, slot_order[0], order_next)
+    )(table, slot_order[0], order_next, start_basis)
     bricks = pl.pallas_call(
         order_kernel,
         out_shape=[jax.ShapeDtypeStruct((elements, points), F32)] * 2,
@@ -314,20 +320,28 @@
     *chunks, field = pl.pallas_call(
         functools.partial(image_kernel, mid),
         out_shape=[chunk] * count + [jax.ShapeDtypeStruct((length, 2 * tile), F32)],
-        in_specs=[VMEM] * (len(parts) + 1),
+        in_specs=[VMEM] * (len(parts) + 2),
         out_specs=[VMEM] * (count + 1),
         scratch_shapes=[pltpu.VMEM((length, rank), F32)],
         compiler_params=BIG,
         name="image",
-    )(*parts, start_basis)
-    field = crossed(field, mid, 0, 0)
+    )(*parts, *basis_parts)
+    field_part = jax.ShapeDtypeStruct((length, 2 * tile), BF16)
+    field_halves = pl.pallas_call(
+        split_kernel,
+        out_shape=[field_part] * 2,
+        in_specs=[VMEM],
+        out_specs=[VMEM] * 2,
+        compiler_params=BIG,
+        name="split",
+    )(crossed(field, mid, 0, 0))
     total = sum(crossed(chunks[step], mid, step, 0) for step in range(count - 1, -1, -1))
     total = sum(crossed(total, distant, step, 1) for step in range(2 ** len(distant) - 1, -1, -1))
     chunks = [crossed(total, mid, step, 0) for step in range(count)]
     first, second = pl.pallas_call(
         functools.partial(factor_kernel, mid),
         out_shape=[jax.ShapeDtypeStruct((rank, tile), F32)] * 2,
-        in_specs=[VMEM] * (1 + count),
+        in_specs=[VMEM] * (2 + count),
         out_specs=[VMEM] * 2,
         scratch_shapes=[
             pltpu.VMEM((length, rank), F32),
@@ -336,7 +350,7 @@
         ],
         compiler_params=BIG,
         name="factor",
-    )(field, *chunks)
+    )(*field_halves, *chunks)
     core_values = first + lax.ppermute(second, "fib", core_swap)
     return core_values[None, None]
 

time: 57.3 us -> 57.1 us (level)
  no operation moved by 1% of the time
where the time goes in v10:
time: 57.1 us; the launch traced here: 57 us
  starting transfers between devices  24.1 us (42%)
  waiting for transfers between devices  20.3 us (36%)
  Pallas kernels  11.5 us (20%)
  other arithmetic  0.69 us (1%)
    ppermute x21, starting transfers between devices, crossed(): return lax.ppermute(value, ('fib', 'pln'), pairs)  20.5 us
    ppermute x21, waiting for transfers between devices, crossed(): return lax.ppermute(value, ('fib', 'pln'), pairs)  10.1 us
    ppermute x1, waiting for transfers between devices, per_device(): back_two = lax.ppermute(swapped, 'fib', forward)  7.2 us
    pallas_call x1, Pallas kernels, per_device(): pl.pallas_call(functools.partial(factor_kernel, mid), out_shape=[jax.Shap...  5.44 us
    pallas_call x1, Pallas kernels, per_device(): pl.pallas_call(functools.partial(interp_kernel, owners), out_shape=[piece...  3.04 us
    ppermute x1, starting transfers between devices, per_device(): back_two = lax.ppermute(swapped, 'fib', forward)  1.6 us
    ppermute x1, starting transfers between devices, per_device(): order_next = lax.ppermute(slot_order[0], 'fib', core_swap)  1.37 us
    ppermute x1, waiting for transfers between devices, per_device(): core_values = first + lax.ppermute(second, 'fib', core_swap)  1.24 us
  transfers between devices with their start and end apart: 26, of which 14 were waited for; matrix products, arithmetic and copies ran while one was open for 0% of the time, Pallas kernels for 2%

profile of v10, /device:TPU:0, one launch (start us, length us, event | category | flops | bytes accessed | tf_op | source)
XLA Modules:
  0.0 57.0 jit_solution(18272883891779294845)
XLA Ops:
  0.0 0.0 copy-start.1
  0.0 3.0 %interp.1 = (f32[96,512]{1,0:T(8,128)S(1)}, f32[96,512]{1,0:T(8,128)S(1)}, f32[192,512]{1,0:T(8,128)S(1)}, f32[96,512]{1,0:T(8,128)S(1)}) custom-call(s32[3,1,16]{2,1,0:T(1,128)} %bitcast.21, f32[288,1000]{1,0:T(8,128)} %bitcast.25, f32[1000,512]{1,0:T(8,128)} %interp_hbm.1), custom_call_target="tpu_custom_call" | custom-call | tf_op jit(solution)/shard_map/interp/pallas_call | solution.py:270
  3.1 0.5 collective-permute-start.1
  3.6 0.1 collective-permute-start.2
  3.6 1.0 %collective-permute-done.1.next_zero_ref = f32[96,512]{1,0:T(8,128)S(1)} collective-permute-done((f32[96,512]{1,0:T(8,128)S(1)}, f32[96,512]{1,0:T(8,128)S(1)}, u32[]{:S(2)}, u32[]{:S(2)}) %collective-permute-start.1) | collective-permute-done | bytes 196640 | tf_op jit(solution)/shard_map/ppermute | solution.py:285
  4.6 1.6 %collective-permute-start.3 = (f32[96,512]{1,0:T(8,128)S(1)}, f32[96,512]{1,0:T(8,128)S(1)}, u32[]{:S(2)}, u32[]{:S(2)}) collective-permute-start(f32[96,512]{1,0:T(8,128)S(1)} %collective-permute-done.1.next_zero_ref), channel_id=1, source_target_pairs={{0,2},{2,4},{4,6},{6,8},{8,10},{10,12},{12,14},{14,16},{16,18},{18... | collective-permute-start | bytes 589832 | tf_op jit(solution)/shard_map/ppermute | solution.py:287
  6.2 0.0 copy-done.2
  6.2 1.4 %collective-permute-start = (s32[1,192]{1,0:T(1,128)S(1)}, s32[1,192]{1,0:T(1,128)S(1)}, u32[]{:S(2)}, u32[]{:S(2)}) collective-permute-start(s32[1,192]{1,0:T(1,128)S(1)} %bitcast.23), channel_id=1, source_target_pairs={{0,2},{2,0},{4,6},{6,4},{8,10},{10,8},{12,14},{14,12},{16,18},{18,... | collective-permute-start | bytes 2312 | tf_op jit(solution)/shard_map/ppermute | solution.py:267
  7.6 0.8 %collective-permute-done.order_next_ref = s32[1,192]{1,0:T(1,128)S(1)} collective-permute-done((s32[1,192]{1,0:T(1,128)S(1)}, s32[1,192]{1,0:T(1,128)S(1)}, u32[]{:S(2)}, u32[]{:S(2)}) %collective-permute-start) | collective-permute-done | bytes 800 | tf_op jit(solution)/shard_map/ppermute | solution.py:267
  8.4 0.0 copy-done.1
  8.4 0.0 copy-done
  8.4 1.1 %pick.1 = (bf16[384,288]{1,0:T(8,128)(2,1)S(1)}, bf16[128,768]{1,0:T(8,128)(2,1)S(1)}, bf16[128,768]{1,0:T(8,128)(2,1)S(1)}) custom-call(s32[3,1,16]{2,1,0:T(1,128)S(1)} %bitcast.22, s32[1,192]{1,0:T(1,128)S(1)} %bitcast.24, s32[1,192]{1,0:T(1,128)S(1)} %collective-permute-done.order_next_ref, f32[768,128]{1,0:T(8,128)S(1)} %copy-done), custom_call_target="tpu_custom_call" | custom-call | tf_op jit(solution)/shard_map/pick/pallas_call | solution.py:289
  9.6 7.2 %collective-permute-done.3.back_two_ref = f32[96,512]{1,0:T(8,128)S(1)} collective-permute-done((f32[96,512]{1,0:T(8,128)S(1)}, f32[96,512]{1,0:T(8,128)S(1)}, u32[]{:S(2)}, u32[]{:S(2)}) %collective-permute-start.3) | collective-permute-done | bytes 196640 | tf_op jit(solution)/shard_map/ppermute | solution.py:287
  16.8 0.0 collective-permute-done.2.back_ref
  16.8 0.6 %order.1 = (f32[192,512]{1,0:T(8,128)S(1)}, f32[192,512]{1,0:T(8,128)S(1)}) custom-call(bf16[384,288]{1,0:T(8,128)(2,1)S(1)} %get-tuple-element.23.pick_ref, f32[96,512]{1,0:T(8,128)S(1)} %get-tuple-element.24.zero_ref, f32[96,512]{1,0:T(8,128)S(1)} %get-tuple-element.25.one_ref, f32[96,512]{1,0:T(8,128)S(1)} %collective-permute-done.1.next_zero_ref, ...), custom_call_target="tpu_custom_call" | custom-call | tf_op jit(solution)/shard_map/order/pallas_call | solution.py:297
  17.5 0.1 slice_bitcast_fusion
  17.6 0.1 collective-permute-start.11
  17.6 1.8 %collective-permute-start.10 = (f32[192,128]{1,0:T(8,128)S(1)}, f32[192,128]{1,0:T(8,128)S(1)}, u32[]{:S(2)}, u32[]{:S(2)}) collective-permute-start(f32[192,128]{1,0:T(8,128)S(1)} %get-tuple-element.42), channel_id=1, source_target_pairs={{0,26},{1,27},{2,0},{3,1},{4,30},{5,31},{6,4},{7,5},{8,18},{9,19},... | collective-permute-start | bytes 294920 | tf_op jit(solution)/shard_map/ppermute | solution.py:242
  19.4 0.0 collective-permute-start.9
  19.4 0.0 collective-permute-start.8
  19.4 1.6 %collective-permute-start.7 = (f32[192,128]{1,0:T(8,128)S(1)}, f32[192,128]{1,0:T(8,128)S(1)}, u32[]{:S(2)}, u32[]{:S(2)}) collective-permute-start(f32[192,128]{1,0:T(8,128)S(1)} %get-tuple-element.45), channel_id=1, source_target_pairs={{0,14},{1,15},{2,0},{3,1},{4,10},{5,11},{6,4},{7,5},{8,6},{9,7},{1... | collective-permute-start | bytes 294920 | tf_op jit(solution)/shard_map/ppermute | solution.py:242
  21.1 0.0 collective-permute-done.11.refs_7_
  21.1 1.3 %collective-permute-start.6 = (f32[192,128]{1,0:T(8,128)S(1)}, f32[192,128]{1,0:T(8,128)S(1)}, u32[]{:S(2)}, u32[]{:S(2)}) collective-permute-start(f32[192,128]{1,0:T(8,128)S(1)} %get-tuple-element.46), channel_id=1, source_target_pairs={{0,10},{1,11},{2,0},{3,1},{4,14},{5,15},{6,4},{7,5},{8,2},{9,3},{1... | collective-permute-start | bytes 294920 | tf_op jit(solution)/shard_map/ppermute | solution.py:242
  22.4 0.0 collective-permute-done.10.refs_6_
  22.4 0.7 %collective-permute-start.5 = (f32[192,128]{1,0:T(8,128)S(1)}, f32[192,128]{1,0:T(8,128)S(1)}, u32[]{:S(2)}, u32[]{:S(2)}) collective-permute-start(f32[192,128]{1,0:T(8,128)S(1)} %get-tuple-element.47), channel_id=1, source_target_pairs={{0,6},{1,7},{2,0},{3,1},{4,2},{5,3},{6,4},{7,5},{8,14},{9,15},{10,... | collective-permute-start | bytes 294920 | tf_op jit(solution)/shard_map/ppermute | solution.py:242
  23.1 0.0 collective-permute-done.9.refs_5_
  23.1 4.1 %collective-permute-start.4 = (f32[192,128]{1,0:T(8,128)S(1)}, f32[192,128]{1,0:T(8,128)S(1)}, u32[]{:S(2)}, u32[]{:S(2)}) collective-permute-start(f32[192,128]{1,0:T(8,128)S(1)} %get-tuple-element.48), channel_id=1, source_target_pairs={{0,2},{1,3},{2,0},{3,1},{4,6},{5,7},{6,4},{7,5},{8,10},{9,11},{10,... | collective-permute-start | bytes 294920 | tf_op jit(solution)/shard_map/ppermute | solution.py:242
  27.2 0.0 collective-permute-done.8.refs_4_
  27.2 0.0 collective-permute-done.7.refs_3_
  27.2 0.0 collective-permute-done.6.refs_2_
  27.2 0.0 collective-permute-done.5.refs_1_
  27.2 0.9 %collective-permute-done.4.refs_0_ = f32[192,128]{1,0:T(8,128)S(1)} collective-permute-done((f32[192,128]{1,0:T(8,128)S(1)}, f32[192,128]{1,0:T(8,128)S(1)}, u32[]{:S(2)}, u32[]{:S(2)}) %collective-permute-start.4) | collective-permute-done | bytes 98336 | tf_op jit(solution)/shard_map/ppermute | solution.py:242
  28.1 1.1 %image.1 = (f32[192,128]{1,0:T(8,128)S(1)}, f32[192,128]{1,0:T(8,128)S(1)}, f32[192,128]{1,0:T(8,128)S(1)}, f32[192,128]{1,0:T(8,128)S(1)}, f32[768,256]{1,0:T(8,128)S(1)}) custom-call(f32[192,128]{1,0:T(8,128)S(1)} %collective-permute-done.4.refs_0_, f32[192,128]{1,0:T(8,128)S(1)} %collective-permute-done.5.refs_1_, ...), custom_call_target="tpu_custom_call" | custom-call | tf_op jit(solution)/shard_map/image/pallas_call | solution.py:320
  29.2 0.4 collective-permute-start.12
  29.7 0.1 collective-permute-start.13
  29.8 2.3 %collective-permute-start.14 = (f32[192,128]{1,0:T(8,128)S(1)}, f32[192,128]{1,0:T(8,128)S(1)}, u32[]{:S(2)}, u32[]{:S(2)}) collective-permute-start(f32[192,128]{1,0:T(8,128)S(1)} %get-tuple-element.36), channel_id=1, source_target_pairs={{0,2},{1,3},{2,4},{3,5},{4,6},{5,7},{6,0},{7,1},{8,10},{9,11},{10,... | collective-permute-start | bytes 294920 | tf_op jit(solution)/shard_map/ppermute | solution.py:242
  32.1 0.0 collective-permute-start.15
  32.1 0.6 %collective-permute-start.16 = (f32[192,128]{1,0:T(8,128)S(1)}, f32[192,128]{1,0:T(8,128)S(1)}, u32[]{:S(2)}, u32[]{:S(2)}) collective-permute-start(f32[192,128]{1,0:T(8,128)S(1)} %get-tuple-element.38), channel_id=1, source_target_pairs={{0,2},{1,3},{2,0},{3,1},{4,6},{5,7},{6,4},{7,5},{8,10},{9,11},{10,... | collective-permute-start | bytes 294920 | tf_op jit(solution)/shard_map/ppermute | solution.py:242
  32.7 1.9 %collective-permute-done.13 = f32[192,128]{1,0:T(8,128)S(1)} collective-permute-done((f32[192,128]{1,0:T(8,128)S(1)}, f32[192,128]{1,0:T(8,128)S(1)}, u32[]{:S(2)}, u32[]{:S(2)}) %collective-permute-start.13) | collective-permute-done | bytes 98336 | tf_op jit(solution)/shard_map/ppermute | solution.py:242
  34.6 1.1 %collective-permute-done.14 = f32[192,128]{1,0:T(8,128)S(1)} collective-permute-done((f32[192,128]{1,0:T(8,128)S(1)}, f32[192,128]{1,0:T(8,128)S(1)}, u32[]{:S(2)}, u32[]{:S(2)}) %collective-permute-start.14) | collective-permute-done | bytes 98336 | tf_op jit(solution)/shard_map/ppermute | solution.py:242
  35.7 0.4 collective-permute-done.15
  36.1 0.0 collective-permute-done.16
  36.2 0.1 collective-permute-start.20
  36.2 2.4 %collective-permute-start.19 = (f32[192,128]{1,0:T(8,128)S(1)}, f32[192,128]{1,0:T(8,128)S(1)}, u32[]{:S(2)}, u32[]{:S(2)}) collective-permute-start(f32[192,128]{1,0:T(8,128)S(1)} %add_add_fusion.1), channel_id=1, source_target_pairs={{0,18},{1,19},{2,0},{3,1},{4,22},{5,23},{6,4},{7,5},{8,26},{9,27},... | collective-permute-start | bytes 294920 | tf_op jit(solution)/shard_map/ppermute | solution.py:242
  38.6 0.0 collective-permute-start.18
  38.6 1.6 %collective-permute-start.17 = (f32[192,128]{1,0:T(8,128)S(1)}, f32[192,128]{1,0:T(8,128)S(1)}, u32[]{:S(2)}, u32[]{:S(2)}) collective-permute-start(f32[192,128]{1,0:T(8,128)S(1)} %add_add_fusion.1), channel_id=1, source_target_pairs={{0,26},{1,27},{2,0},{3,1},{4,30},{5,31},{6,4},{7,5},{8,18},{9,19},... | collective-permute-start | bytes 294920 | tf_op jit(solution)/shard_map/ppermute | solution.py:242
  40.2 0.0 collective-permute-done.20
  40.2 0.6 %collective-permute-done.19 = f32[192,128]{1,0:T(8,128)S(1)} collective-permute-done((f32[192,128]{1,0:T(8,128)S(1)}, f32[192,128]{1,0:T(8,128)S(1)}, u32[]{:S(2)}, u32[]{:S(2)}) %collective-permute-start.19) | collective-permute-done | bytes 98336 | tf_op jit(solution)/shard_map/ppermute | solution.py:242
  40.8 1.0 %collective-permute-done.18 = f32[192,128]{1,0:T(8,128)S(1)} collective-permute-done((f32[192,128]{1,0:T(8,128)S(1)}, f32[192,128]{1,0:T(8,128)S(1)}, u32[]{:S(2)}, u32[]{:S(2)}) %collective-permute-start.18) | collective-permute-done | bytes 98336 | tf_op jit(solution)/shard_map/ppermute | solution.py:242
  41.9 1.1 %collective-permute-done.17 = f32[192,128]{1,0:T(8,128)S(1)} collective-permute-done((f32[192,128]{1,0:T(8,128)S(1)}, f32[192,128]{1,0:T(8,128)S(1)}, u32[]{:S(2)}, u32[]{:S(2)}) %collective-permute-start.17) | collective-permute-done | bytes 98336 | tf_op jit(solution)/shard_map/ppermute | solution.py:242
  42.9 2.1 %collective-permute-start.24 = (f32[192,128]{1,0:T(8,128)S(1)}, f32[192,128]{1,0:T(8,128)S(1)}, u32[]{:S(2)}, u32[]{:S(2)}) collective-permute-start(f32[192,128]{1,0:T(8,128)S(1)} %add_add_fusion), channel_id=1, source_target_pairs={{0,2},{1,3},{2,5},{3,4},{4,6},{5,7},{6,1},{7,0},{8,10},{9,11},{10,... | collective-permute-start | bytes 294920 | tf_op jit(solution)/shard_map/ppermute | solution.py:242
  45.1 0.1 collective-permute-start.23
  45.1 1.1 %collective-permute-start.22 = (f32[192,128]{1,0:T(8,128)S(1)}, f32[192,128]{1,0:T(8,128)S(1)}, u32[]{:S(2)}, u32[]{:S(2)}) collective-permute-start(f32[192,128]{1,0:T(8,128)S(1)} %add_add_fusion), channel_id=1, source_target_pairs={{0,2},{1,3},{2,1},{3,0},{4,6},{5,7},{6,5},{7,4},{8,10},{9,11},{10,... | collective-permute-start | bytes 294920 | tf_op jit(solution)/shard_map/ppermute | solution.py:242
  46.2 0.2 collective-permute-start.21
  46.4 0.0 collective-permute-done.12.value_ref
  46.4 0.1 split.1
  46.6 2.0 %collective-permute-done.24.refs_3_ = f32[192,128]{1,0:T(8,128)S(1)} collective-permute-done((f32[192,128]{1,0:T(8,128)S(1)}, f32[192,128]{1,0:T(8,128)S(1)}, u32[]{:S(2)}, u32[]{:S(2)}) %collective-permute-start.24) | collective-permute-done | bytes 98336 | tf_op jit(solution)/shard_map/ppermute | solution.py:242
  48.5 0.6 collective-permute-done.23.refs_2_
  49.1 0.5 collective-permute-done.22.refs_1_
  49.6 0.0 collective-permute-done.21.refs_0_
  49.6 5.4 %factor.1 = (f32[128,128]{1,0:T(8,128)S(1)}, f32[128,128]{1,0:T(8,128)S(1)}) custom-call(bf16[768,256]{1,0:T(8,128)(2,1)S(1)} %get-tuple-element.33.high_ref, bf16[768,256]{1,0:T(8,128)(2,1)S(1)} %get-tuple-element.34.low_ref, f32[192,128]{1,0:T(8,128)S(1)} %collective-permute-done.21.refs_0_, f32[192,128]{1,0:T(8,128)S(1)} %collective-permute-done.22.refs_1_, ...), custom_call_target="tpu_custom_call" | custom-call | tf_op jit(solution)/shard_map/factor/pallas_call | solution.py:341
  55.0 0.1 collective-permute-start.25
  55.1 1.2 %collective-permute-done.25 = f32[128,128]{1,0:T(8,128)S(1)} collective-permute-done((f32[128,128]{1,0:T(8,128)S(1)}, f32[128,128]{1,0:T(8,128)S(1)}, u32[]{:S(2)}, u32[]{:S(2)}) %collective-permute-start.25) | collective-permute-done | bytes 65568 | tf_op jit(solution)/shard_map/ppermute | solution.py:354
  56.3 0.6 %add_bitcast_fusion = f32[1,1,128,128]{3,2,1,0:T(8,128)} fusion(f32[128,128]{1,0:T(8,128)S(1)} %get-tuple-element.39, f32[128,128]{1,0:T(8,128)S(1)} %collective-permute-done.25), kind=kLoop, calls=%fused_computation.10 | loop fusion | flops 16384 | bytes 196608 | tf_op jit(solution)/shard_map/broadcast_in_dim | solution.py:355
  (8 shorter events, 0.2 us)
Async XLA Ops:
  0.0 8.4 %copy-start.1 = (s32[1,16,3]{1,0,2:T(1,128)S(1)}, s32[1,16,3]{1,0,2:T(1,128)}, u32[]{:S(2)}) copy-start(s32[1,16,3]{1,0,2:T(1,128)} %param.7) | copy-start | bytes 580
  0.0 6.2 %copy-start.2 = (s32[1,1,192]{2,1,0:T(1,128)S(1)}, s32[1,1,192]{2,1,0:T(1,128)}, u32[]{:S(2)}) copy-start(s32[1,1,192]{2,1,0:T(1,128)} %param.8) | copy-start | bytes 2308
  0.0 8.4 %copy-start = (f32[768,128]{1,0:T(8,128)S(1)}, f32[768,128]{1,0:T(8,128)}, u32[]{:S(2)}) copy-start(f32[768,128]{1,0:T(8,128)} %start_ref.1) | copy-start | bytes 1179652
  3.1 1.6 %collective-permute-start.1 = (f32[96,512]{1,0:T(8,128)S(1)}, f32[96,512]{1,0:T(8,128)S(1)}, u32[]{:S(2)}, u32[]{:S(2)}) collective-permute-start(f32[96,512]{1,0:T(8,128)S(1)} %get-tuple-element.26), channel_id=1, source_target_pairs={{0,2},{2,0},{4,6},{6,4},{8,10},{10,8},{12,14},{14,12},{16,18},{18,... | collective-permute-start | bytes 589832 | tf_op jit(solution)/shard_map/ppermute | solution.py:285
  3.6 13.2 %collective-permute-start.2 = (f32[192,512]{1,0:T(8,128)S(1)}, f32[192,512]{1,0:T(8,128)S(1)}, u32[]{:S(2)}, u32[]{:S(2)}) collective-permute-start(f32[192,512]{1,0:T(8,128)S(1)} %get-tuple-element.27), channel_id=1, source_target_pairs={{0,2},{2,4},{4,6},{6,8},{8,10},{10,12},{12,14},{14,16},{16,18},{18... | collective-permute-start | bytes 1179656 | tf_op jit(solution)/shard_map/ppermute | solution.py:286
  4.6 12.1 %collective-permute-start.3 = (f32[96,512]{1,0:T(8,128)S(1)}, f32[96,512]{1,0:T(8,128)S(1)}, u32[]{:S(2)}, u32[]{:S(2)}) collective-permute-start(f32[96,512]{1,0:T(8,128)S(1)} %collective-permute-done.1.next_zero_ref), channel_id=1, source_target_pairs={{0,2},{2,4},{4,6},{6,8},{8,10},{10,12},{12,14},{14,16},{16,18},{18... | collective-permute-start | bytes 589832 | tf_op jit(solution)/shard_map/ppermute | solution.py:287
  6.2 2.2 %collective-permute-start = (s32[1,192]{1,0:T(1,128)S(1)}, s32[1,192]{1,0:T(1,128)S(1)}, u32[]{:S(2)}, u32[]{:S(2)}) collective-permute-start(s32[1,192]{1,0:T(1,128)S(1)} %bitcast.23), channel_id=1, source_target_pairs={{0,2},{2,0},{4,6},{6,4},{8,10},{10,8},{12,14},{14,12},{16,18},{18,... | collective-permute-start | bytes 2312 | tf_op jit(solution)/shard_map/ppermute | solution.py:267
  17.6 3.5 %collective-permute-start.11 = (f32[192,128]{1,0:T(8,128)S(1)}, f32[192,128]{1,0:T(8,128)S(1)}, u32[]{:S(2)}, u32[]{:S(2)}) collective-permute-start(f32[192,128]{1,0:T(8,128)S(1)} %get-tuple-element.41), channel_id=1, source_target_pairs={{0,30},{1,31},{2,0},{3,1},{4,26},{5,27},{6,4},{7,5},{8,22},{9,23},... | collective-permute-start | bytes 294920 | tf_op jit(solution)/shard_map/ppermute | solution.py:242
  17.6 4.7 %collective-permute-start.10 = (f32[192,128]{1,0:T(8,128)S(1)}, f32[192,128]{1,0:T(8,128)S(1)}, u32[]{:S(2)}, u32[]{:S(2)}) collective-permute-start(f32[192,128]{1,0:T(8,128)S(1)} %get-tuple-element.42), channel_id=1, source_target_pairs={{0,26},{1,27},{2,0},{3,1},{4,30},{5,31},{6,4},{7,5},{8,18},{9,19},... | collective-permute-start | bytes 294920 | tf_op jit(solution)/shard_map/ppermute | solution.py:242
  19.4 3.7 %collective-permute-start.9 = (f32[192,128]{1,0:T(8,128)S(1)}, f32[192,128]{1,0:T(8,128)S(1)}, u32[]{:S(2)}, u32[]{:S(2)}) collective-permute-start(f32[192,128]{1,0:T(8,128)S(1)} %get-tuple-element.43), channel_id=1, source_target_pairs={{0,22},{1,23},{2,0},{3,1},{4,18},{5,19},{6,4},{7,5},{8,30},{9,31},... | collective-permute-start | bytes 294920 | tf_op jit(solution)/shard_map/ppermute | solution.py:242
  19.4 7.7 %collective-permute-start.8 = (f32[192,128]{1,0:T(8,128)S(1)}, f32[192,128]{1,0:T(8,128)S(1)}, u32[]{:S(2)}, u32[]{:S(2)}) collective-permute-start(f32[192,128]{1,0:T(8,128)S(1)} %get-tuple-element.44), channel_id=1, source_target_pairs={{0,18},{1,19},{2,0},{3,1},{4,22},{5,23},{6,4},{7,5},{8,26},{9,27},... | collective-permute-start | bytes 294920 | tf_op jit(solution)/shard_map/ppermute | solution.py:242
  19.4 7.7 %collective-permute-start.7 = (f32[192,128]{1,0:T(8,128)S(1)}, f32[192,128]{1,0:T(8,128)S(1)}, u32[]{:S(2)}, u32[]{:S(2)}) collective-permute-start(f32[192,128]{1,0:T(8,128)S(1)} %get-tuple-element.45), channel_id=1, source_target_pairs={{0,14},{1,15},{2,0},{3,1},{4,10},{5,11},{6,4},{7,5},{8,6},{9,7},{1... | collective-permute-start | bytes 294920 | tf_op jit(solution)/shard_map/ppermute | solution.py:242
  21.1 6.1 %collective-permute-start.6 = (f32[192,128]{1,0:T(8,128)S(1)}, f32[192,128]{1,0:T(8,128)S(1)}, u32[]{:S(2)}, u32[]{:S(2)}) collective-permute-start(f32[192,128]{1,0:T(8,128)S(1)} %get-tuple-element.46), channel_id=1, source_target_pairs={{0,10},{1,11},{2,0},{3,1},{4,14},{5,15},{6,4},{7,5},{8,2},{9,3},{1... | collective-permute-start | bytes 294920 | tf_op jit(solution)/shard_map/ppermute | solution.py:242
  22.4 4.8 %collective-permute-start.5 = (f32[192,128]{1,0:T(8,128)S(1)}, f32[192,128]{1,0:T(8,128)S(1)}, u32[]{:S(2)}, u32[]{:S(2)}) collective-permute-start(f32[192,128]{1,0:T(8,128)S(1)} %get-tuple-element.47), channel_id=1, source_target_pairs={{0,6},{1,7},{2,0},{3,1},{4,2},{5,3},{6,4},{7,5},{8,14},{9,15},{10,... | collective-permute-start | bytes 294920 | tf_op jit(solution)/shard_map/ppermute | solution.py:242
  23.1 5.0 %collective-permute-start.4 = (f32[192,128]{1,0:T(8,128)S(1)}, f32[192,128]{1,0:T(8,128)S(1)}, u32[]{:S(2)}, u32[]{:S(2)}) collective-permute-start(f32[192,128]{1,0:T(8,128)S(1)} %get-tuple-element.48), channel_id=1, source_target_pairs={{0,2},{1,3},{2,0},{3,1},{4,6},{5,7},{6,4},{7,5},{8,10},{9,11},{10,... | collective-permute-start | bytes 294920 | tf_op jit(solution)/shard_map/ppermute | solution.py:242
  29.2 17.2 %collective-permute-start.12 = (f32[768,256]{1,0:T(8,128)S(1)}, f32[768,256]{1,0:T(8,128)S(1)}, u32[]{:S(2)}, u32[]{:S(2)}) collective-permute-start(f32[768,256]{1,0:T(8,128)S(1)} %get-tuple-element.32), channel_id=1, source_target_pairs={{0,2},{1,3},{2,0},{3,1},{4,6},{5,7},{6,4},{7,5},{8,10},{9,11},{10,... | collective-permute-start | bytes 2359304 | tf_op jit(solution)/shard_map/ppermute | solution.py:242
  29.7 4.9 %collective-permute-start.13 = (f32[192,128]{1,0:T(8,128)S(1)}, f32[192,128]{1,0:T(8,128)S(1)}, u32[]{:S(2)}, u32[]{:S(2)}) collective-permute-start(f32[192,128]{1,0:T(8,128)S(1)} %get-tuple-element.35), channel_id=1, source_target_pairs={{0,2},{1,3},{2,5},{3,4},{4,6},{5,7},{6,1},{7,0},{8,10},{9,11},{10,... | collective-permute-start | bytes 294920 | tf_op jit(solution)/shard_map/ppermute | solution.py:242
  29.8 5.9 %collective-permute-start.14 = (f32[192,128]{1,0:T(8,128)S(1)}, f32[192,128]{1,0:T(8,128)S(1)}, u32[]{:S(2)}, u32[]{:S(2)}) collective-permute-start(f32[192,128]{1,0:T(8,128)S(1)} %get-tuple-element.36), channel_id=1, source_target_pairs={{0,2},{1,3},{2,4},{3,5},{4,6},{5,7},{6,0},{7,1},{8,10},{9,11},{10,... | collective-permute-start | bytes 294920 | tf_op jit(solution)/shard_map/ppermute | solution.py:242
  32.1 4.0 %collective-permute-start.15 = (f32[192,128]{1,0:T(8,128)S(1)}, f32[192,128]{1,0:T(8,128)S(1)}, u32[]{:S(2)}, u32[]{:S(2)}) collective-permute-start(f32[192,128]{1,0:T(8,128)S(1)} %get-tuple-element.37), channel_id=1, source_target_pairs={{0,2},{1,3},{2,1},{3,0},{4,6},{5,7},{6,5},{7,4},{8,10},{9,11},{10,... | collective-permute-start | bytes 294920 | tf_op jit(solution)/shard_map/ppermute | solution.py:242
  32.1 4.0 %collective-permute-start.16 = (f32[192,128]{1,0:T(8,128)S(1)}, f32[192,128]{1,0:T(8,128)S(1)}, u32[]{:S(2)}, u32[]{:S(2)}) collective-permute-start(f32[192,128]{1,0:T(8,128)S(1)} %get-tuple-element.38), channel_id=1, source_target_pairs={{0,2},{1,3},{2,0},{3,1},{4,6},{5,7},{6,4},{7,5},{8,10},{9,11},{10,... | collective-permute-start | bytes 294920 | tf_op jit(solution)/shard_map/ppermute | solution.py:242
  36.2 4.1 %collective-permute-start.20 = (f32[192,128]{1,0:T(8,128)S(1)}, f32[192,128]{1,0:T(8,128)S(1)}, u32[]{:S(2)}, u32[]{:S(2)}) collective-permute-start(f32[192,128]{1,0:T(8,128)S(1)} %add_add_fusion.1), channel_id=1, source_target_pairs={{0,2},{1,3},{2,0},{3,1},{4,6},{5,7},{6,4},{7,5},{8,10},{9,11},{10,... | collective-permute-start | bytes 294920 | tf_op jit(solution)/shard_map/ppermute | solution.py:242
  36.2 4.6 %collective-permute-start.19 = (f32[192,128]{1,0:T(8,128)S(1)}, f32[192,128]{1,0:T(8,128)S(1)}, u32[]{:S(2)}, u32[]{:S(2)}) collective-permute-start(f32[192,128]{1,0:T(8,128)S(1)} %add_add_fusion.1), channel_id=1, source_target_pairs={{0,18},{1,19},{2,0},{3,1},{4,22},{5,23},{6,4},{7,5},{8,26},{9,27},... | collective-permute-start | bytes 294920 | tf_op jit(solution)/shard_map/ppermute | solution.py:242
  38.6 3.2 %collective-permute-start.18 = (f32[192,128]{1,0:T(8,128)S(1)}, f32[192,128]{1,0:T(8,128)S(1)}, u32[]{:S(2)}, u32[]{:S(2)}) collective-permute-start(f32[192,128]{1,0:T(8,128)S(1)} %add_add_fusion.1), channel_id=1, source_target_pairs={{0,10},{1,11},{2,0},{3,1},{4,14},{5,15},{6,4},{7,5},{8,2},{9,3},{1... | collective-permute-start | bytes 294920 | tf_op jit(solution)/shard_map/ppermute | solution.py:242
  38.6 4.3 %collective-permute-start.17 = (f32[192,128]{1,0:T(8,128)S(1)}, f32[192,128]{1,0:T(8,128)S(1)}, u32[]{:S(2)}, u32[]{:S(2)}) collective-permute-start(f32[192,128]{1,0:T(8,128)S(1)} %add_add_fusion.1), channel_id=1, source_target_pairs={{0,26},{1,27},{2,0},{3,1},{4,30},{5,31},{6,4},{7,5},{8,18},{9,19},... | collective-permute-start | bytes 294920 | tf_op jit(solution)/shard_map/ppermute | solution.py:242
  42.9 5.6 %collective-permute-start.24 = (f32[192,128]{1,0:T(8,128)S(1)}, f32[192,128]{1,0:T(8,128)S(1)}, u32[]{:S(2)}, u32[]{:S(2)}) collective-permute-start(f32[192,128]{1,0:T(8,128)S(1)} %add_add_fusion), channel_id=1, source_target_pairs={{0,2},{1,3},{2,5},{3,4},{4,6},{5,7},{6,1},{7,0},{8,10},{9,11},{10,... | collective-permute-start | bytes 294920 | tf_op jit(solution)/shard_map/ppermute | solution.py:242
  45.1 4.0 %collective-permute-start.23 = (f32[192,128]{1,0:T(8,128)S(1)}, f32[192,128]{1,0:T(8,128)S(1)}, u32[]{:S(2)}, u32[]{:S(2)}) collective-permute-start(f32[192,128]{1,0:T(8,128)S(1)} %add_add_fusion), channel_id=1, source_target_pairs={{0,2},{1,3},{2,4},{3,5},{4,6},{5,7},{6,0},{7,1},{8,10},{9,11},{10,... | collective-permute-start | bytes 294920 | tf_op jit(solution)/shard_map/ppermute | solution.py:242
  45.1 4.4 %collective-permute-start.22 = (f32[192,128]{1,0:T(8,128)S(1)}, f32[192,128]{1,0:T(8,128)S(1)}, u32[]{:S(2)}, u32[]{:S(2)}) collective-permute-start(f32[192,128]{1,0:T(8,128)S(1)} %add_add_fusion), channel_id=1, source_target_pairs={{0,2},{1,3},{2,1},{3,0},{4,6},{5,7},{6,5},{7,4},{8,10},{9,11},{10,... | collective-permute-start | bytes 294920 | tf_op jit(solution)/shard_map/ppermute | solution.py:242
  46.2 3.3 %collective-permute-start.21 = (f32[192,128]{1,0:T(8,128)S(1)}, f32[192,128]{1,0:T(8,128)S(1)}, u32[]{:S(2)}, u32[]{:S(2)}) collective-permute-start(f32[192,128]{1,0:T(8,128)S(1)} %add_add_fusion), channel_id=1, source_target_pairs={{0,2},{1,3},{2,0},{3,1},{4,6},{5,7},{6,4},{7,5},{8,10},{9,11},{10,... | collective-permute-start | bytes 294920 | tf_op jit(solution)/shard_map/ppermute | solution.py:242
  55.0 1.3 %collective-permute-start.25 = (f32[128,128]{1,0:T(8,128)S(1)}, f32[128,128]{1,0:T(8,128)S(1)}, u32[]{:S(2)}, u32[]{:S(2)}) collective-permute-start(f32[128,128]{1,0:T(8,128)S(1)} %get-tuple-element.40), channel_id=1, source_target_pairs={{0,2},{2,0},{4,6},{6,4},{8,10},{10,8},{12,14},{14,12},{16,18},{18,... | collective-permute-start | bytes 196616 | tf_op jit(solution)/shard_map/ppermute | solution.py:354

commit v11 on v10

--- a/solution.py
+++ b/solution.py
@@ -175,7 +175,8 @@
         rows = chunk.shape[0]
         at = pl.multiple_of((place ^ step) * rows, rows)
         image_scr[pl.ds(at, rows), :] = chunk[...]
-    image = halves(image_scr[...])
+    image = image_scr[...]
+    image = halves(image * lax.rsqrt(jnp.sum(image * image, axis=0, keepdims=True)))
     work[:, :rank] = dot3(image, image, ((0,), (0,)))
     work[:, rank:] = dot3(image, (high_ref[...], low_ref[...]), ((0,), (0,)))
     width = work.shape[1]
@@ -191,18 +192,21 @@
         for slab in range(0, BLOCK, SLAB):
             ahead = base + slab
             entry = [[splat(line[slab + k], ahead + i) for i in range(SLAB)] for k in range(SLAB)]
-            for k in range(SLAB):
-                scale = lax.rsqrt(entry[k][k])
-                line[slab + k] = scaled(scale, line[slab + k])
-                factor = {i: entry[k][i] * scale for i in range(k + 1, SLAB)}
-                for i in range(k + 1, SLAB):
-                    for j in range(i, SLAB):
-                        entry[i][j] = entry[i][j] - factor[i] * factor[j]
-                    line[slab + i] = line[slab + i] - scaled(factor[i], line[slab + k])
-                row = line[slab + k]
-                for core, out in enumerate(out_refs):
-                    out[ahead + k : ahead + k + 1, :] = row[:, (core + 1) * rank : (core + 2) * rank]
-                line_scr[slab + k : slab + k + 1, :] = row
+            for k in range(0, SLAB, 2):
+                p, q, r = entry[k][k], entry[k][k + 1], entry[k + 1][k + 1]
+                root = lax.rsqrt(p)
+                scales = (root, lax.rsqrt(p * r - q * q) * (p * root))
+                for n, scale in zip((k, k + 1), scales):
+                    row = scaled(scale, line[slab + n])
+                    factor = {i: entry[n][i] * scale for i in range(n + 1, SLAB)}
+                    for i in range(n + 1, SLAB):
+                        for j in range(i, SLAB):
+                            entry[i][j] = entry[i][j] - factor[i] * factor[j]
+                        line[slab + i] = line[slab + i] - scaled(factor[i], row)
+                    line[slab + n] = row
+                    for core, out in enumerate(out_refs):
+                        out[ahead + n : ahead + n + 1, :] = row[:, (core + 1) * rank : (core + 2) * rank]
+                    line_scr[slab + n : slab + n + 1, :] = row
             for i in range(slab + SLAB, BLOCK):
                 for k in range(slab, slab + SLAB):
                     line[i] = line[i] - scaled(splat(line[k], base + i), line[k])
@@ -314,7 +318,7 @@
         parts = [whole.transpose(0, 1, 3, 2, 4).reshape(length, 2 * tile)]
 
     mid = masks("fib", 2, 4) + masks("pln", 1, planes)
-    distant = masks("fib", 4, owners)
+    distant = masks("fib", 4, owners)[::-1]
     count = 2 ** len(mid)
     chunk = jax.ShapeDtypeStruct((length // count, rank), F32)
     *chunks, field = pl.pallas_call(

time: 57.1 us -> 56.7 us (level)
  transfers between devices with their start and end apart: 26 -> 26, of which waited for: 14 -> 13; matrix products, arithmetic and copies ran while one was open for 0% -> 0% of each run, Pallas kernels for 2% -> 2%
where the time goes in v11:
time: 56.7 us; the launch traced here: 56.6 us
  starting transfers between devices  24.4 us (43%)
  waiting for transfers between devices  19.8 us (35%)
  Pallas kernels  11.4 us (20%)
  other arithmetic  0.69 us (1%)
    ppermute x21, starting transfers between devices, crossed(): return lax.ppermute(value, ('fib', 'pln'), pairs)  20.7 us
    ppermute x21, waiting for transfers between devices, crossed(): return lax.ppermute(value, ('fib', 'pln'), pairs)  9.52 us
    ppermute x1, waiting for transfers between devices, per_device(): back_two = lax.ppermute(swapped, 'fib', forward)  7.2 us
    pallas_call x1, Pallas kernels, per_device(): pl.pallas_call(functools.partial(factor_kernel, mid), out_shape=[jax.Shap...  5.41 us
    pallas_call x1, Pallas kernels, per_device(): pl.pallas_call(functools.partial(interp_kernel, owners), out_shape=[piece...  3.04 us
    ppermute x1, starting transfers between devices, per_device(): back_two = lax.ppermute(swapped, 'fib', forward)  1.6 us
    ppermute x1, starting transfers between devices, per_device(): order_next = lax.ppermute(slot_order[0], 'fib', core_swap)  1.37 us
    ppermute x1, waiting for transfers between devices, per_device(): core_values = first + lax.ppermute(second, 'fib', core_swap)  1.24 us
  transfers between devices with their start and end apart: 26, of which 13 were waited for; matrix products, arithmetic and copies ran while one was open for 0% of the time, Pallas kernels for 2%

profile of v11, /device:TPU:0, one launch (start us, length us, event | category | flops | bytes accessed | tf_op | source)
XLA Modules:
  0.0 56.6 jit_solution(2662383481461903842)
XLA Ops:
  0.0 0.0 copy-start.2
  0.0 3.0 %interp.1 = (f32[96,512]{1,0:T(8,128)S(1)}, f32[96,512]{1,0:T(8,128)S(1)}, f32[192,512]{1,0:T(8,128)S(1)}, f32[96,512]{1,0:T(8,128)S(1)}) custom-call(s32[3,1,16]{2,1,0:T(1,128)} %bitcast.21, f32[288,1000]{1,0:T(8,128)} %bitcast.25, f32[1000,512]{1,0:T(8,128)} %interp_hbm.1), custom_call_target="tpu_custom_call" | custom-call | tf_op jit(solution)/shard_map/interp/pallas_call | solution.py:274
  3.1 0.5 collective-permute-start.1
  3.6 0.1 collective-permute-start.2
  3.6 1.0 %collective-permute-done.1.next_zero_ref = f32[96,512]{1,0:T(8,128)S(1)} collective-permute-done((f32[96,512]{1,0:T(8,128)S(1)}, f32[96,512]{1,0:T(8,128)S(1)}, u32[]{:S(2)}, u32[]{:S(2)}) %collective-permute-start.1) | collective-permute-done | bytes 196640 | tf_op jit(solution)/shard_map/ppermute | solution.py:289
  4.6 1.6 %collective-permute-start.3 = (f32[96,512]{1,0:T(8,128)S(1)}, f32[96,512]{1,0:T(8,128)S(1)}, u32[]{:S(2)}, u32[]{:S(2)}) collective-permute-start(f32[96,512]{1,0:T(8,128)S(1)} %collective-permute-done.1.next_zero_ref), channel_id=1, source_target_pairs={{0,2},{2,4},{4,6},{6,8},{8,10},{10,12},{12,14},{14,16},{16,18},{18... | collective-permute-start | bytes 589832 | tf_op jit(solution)/shard_map/ppermute | solution.py:291
  6.2 0.0 copy-done.2
  6.2 1.4 %collective-permute-start = (s32[1,192]{1,0:T(1,128)S(1)}, s32[1,192]{1,0:T(1,128)S(1)}, u32[]{:S(2)}, u32[]{:S(2)}) collective-permute-start(s32[1,192]{1,0:T(1,128)S(1)} %bitcast.23), channel_id=1, source_target_pairs={{0,2},{2,0},{4,6},{6,4},{8,10},{10,8},{12,14},{14,12},{16,18},{18,... | collective-permute-start | bytes 2312 | tf_op jit(solution)/shard_map/ppermute | solution.py:271
  7.6 0.8 %collective-permute-done.order_next_ref = s32[1,192]{1,0:T(1,128)S(1)} collective-permute-done((s32[1,192]{1,0:T(1,128)S(1)}, s32[1,192]{1,0:T(1,128)S(1)}, u32[]{:S(2)}, u32[]{:S(2)}) %collective-permute-start) | collective-permute-done | bytes 800 | tf_op jit(solution)/shard_map/ppermute | solution.py:271
  8.4 0.0 copy-done.1
  8.4 0.0 copy-done
  8.4 1.1 %pick.1 = (bf16[384,288]{1,0:T(8,128)(2,1)S(1)}, bf16[128,768]{1,0:T(8,128)(2,1)S(1)}, bf16[128,768]{1,0:T(8,128)(2,1)S(1)}) custom-call(s32[3,1,16]{2,1,0:T(1,128)S(1)} %bitcast.22, s32[1,192]{1,0:T(1,128)S(1)} %bitcast.24, s32[1,192]{1,0:T(1,128)S(1)} %collective-permute-done.order_next_ref, f32[768,128]{1,0:T(8,128)S(1)} %copy-done), custom_call_target="tpu_custom_call" | custom-call | tf_op jit(solution)/shard_map/pick/pallas_call | solution.py:293
  9.6 7.2 %collective-permute-done.3.back_two_ref = f32[96,512]{1,0:T(8,128)S(1)} collective-permute-done((f32[96,512]{1,0:T(8,128)S(1)}, f32[96,512]{1,0:T(8,128)S(1)}, u32[]{:S(2)}, u32[]{:S(2)}) %collective-permute-start.3) | collective-permute-done | bytes 196640 | tf_op jit(solution)/shard_map/ppermute | solution.py:291
  16.8 0.0 collective-permute-done.2.back_ref
  16.8 0.6 %order.1 = (f32[192,512]{1,0:T(8,128)S(1)}, f32[192,512]{1,0:T(8,128)S(1)}) custom-call(bf16[384,288]{1,0:T(8,128)(2,1)S(1)} %get-tuple-element.23.pick_ref, f32[96,512]{1,0:T(8,128)S(1)} %get-tuple-element.24.zero_ref, f32[96,512]{1,0:T(8,128)S(1)} %get-tuple-element.25.one_ref, f32[96,512]{1,0:T(8,128)S(1)} %collective-permute-done.1.next_zero_ref, ...), custom_call_target="tpu_custom_call" | custom-call | tf_op jit(solution)/shard_map/order/pallas_call | solution.py:301
  17.5 0.1 slice_bitcast_fusion
  17.6 0.1 collective-permute-start.11
  17.6 1.8 %collective-permute-start.10 = (f32[192,128]{1,0:T(8,128)S(1)}, f32[192,128]{1,0:T(8,128)S(1)}, u32[]{:S(2)}, u32[]{:S(2)}) collective-permute-start(f32[192,128]{1,0:T(8,128)S(1)} %get-tuple-element.42), channel_id=1, source_target_pairs={{0,26},{1,27},{2,0},{3,1},{4,30},{5,31},{6,4},{7,5},{8,18},{9,19},... | collective-permute-start | bytes 294920 | tf_op jit(solution)/shard_map/ppermute | solution.py:246
  19.4 0.0 collective-permute-start.9
  19.4 0.0 collective-permute-start.8
  19.4 1.6 %collective-permute-start.7 = (f32[192,128]{1,0:T(8,128)S(1)}, f32[192,128]{1,0:T(8,128)S(1)}, u32[]{:S(2)}, u32[]{:S(2)}) collective-permute-start(f32[192,128]{1,0:T(8,128)S(1)} %get-tuple-element.45), channel_id=1, source_target_pairs={{0,14},{1,15},{2,0},{3,1},{4,10},{5,11},{6,4},{7,5},{8,6},{9,7},{1... | collective-permute-start | bytes 294920 | tf_op jit(solution)/shard_map/ppermute | solution.py:246
  21.1 0.0 collective-permute-done.11.refs_7_
  21.1 1.3 %collective-permute-start.6 = (f32[192,128]{1,0:T(8,128)S(1)}, f32[192,128]{1,0:T(8,128)S(1)}, u32[]{:S(2)}, u32[]{:S(2)}) collective-permute-start(f32[192,128]{1,0:T(8,128)S(1)} %get-tuple-element.46), channel_id=1, source_target_pairs={{0,10},{1,11},{2,0},{3,1},{4,14},{5,15},{6,4},{7,5},{8,2},{9,3},{1... | collective-permute-start | bytes 294920 | tf_op jit(solution)/shard_map/ppermute | solution.py:246
  22.4 0.0 collective-permute-done.10.refs_6_
  22.4 0.7 %collective-permute-start.5 = (f32[192,128]{1,0:T(8,128)S(1)}, f32[192,128]{1,0:T(8,128)S(1)}, u32[]{:S(2)}, u32[]{:S(2)}) collective-permute-start(f32[192,128]{1,0:T(8,128)S(1)} %get-tuple-element.47), channel_id=1, source_target_pairs={{0,6},{1,7},{2,0},{3,1},{4,2},{5,3},{6,4},{7,5},{8,14},{9,15},{10,... | collective-permute-start | bytes 294920 | tf_op jit(solution)/shard_map/ppermute | solution.py:246
  23.1 0.0 collective-permute-done.9.refs_5_
  23.1 4.1 %collective-permute-start.4 = (f32[192,128]{1,0:T(8,128)S(1)}, f32[192,128]{1,0:T(8,128)S(1)}, u32[]{:S(2)}, u32[]{:S(2)}) collective-permute-start(f32[192,128]{1,0:T(8,128)S(1)} %get-tuple-element.48), channel_id=1, source_target_pairs={{0,2},{1,3},{2,0},{3,1},{4,6},{5,7},{6,4},{7,5},{8,10},{9,11},{10,... | collective-permute-start | bytes 294920 | tf_op jit(solution)/shard_map/ppermute | solution.py:246
  27.2 0.0 collective-permute-done.8.refs_4_
  27.2 0.0 collective-permute-done.7.refs_3_
  27.2 0.0 collective-permute-done.6.refs_2_
  27.2 0.0 collective-permute-done.5.refs_1_
  27.2 0.9 %collective-permute-done.4.refs_0_ = f32[192,128]{1,0:T(8,128)S(1)} collective-permute-done((f32[192,128]{1,0:T(8,128)S(1)}, f32[192,128]{1,0:T(8,128)S(1)}, u32[]{:S(2)}, u32[]{:S(2)}) %collective-permute-start.4) | collective-permute-done | bytes 98336 | tf_op jit(solution)/shard_map/ppermute | solution.py:246
  28.1 1.1 %image.1 = (f32[192,128]{1,0:T(8,128)S(1)}, f32[192,128]{1,0:T(8,128)S(1)}, f32[192,128]{1,0:T(8,128)S(1)}, f32[192,128]{1,0:T(8,128)S(1)}, f32[768,256]{1,0:T(8,128)S(1)}) custom-call(f32[192,128]{1,0:T(8,128)S(1)} %collective-permute-done.4.refs_0_, f32[192,128]{1,0:T(8,128)S(1)} %collective-permute-done.5.refs_1_, ...), custom_call_target="tpu_custom_call" | custom-call | tf_op jit(solution)/shard_map/image/pallas_call | solution.py:324
  29.2 0.4 collective-permute-start.12
  29.7 0.1 collective-permute-start.13
  29.8 2.3 %collective-permute-start.14 = (f32[192,128]{1,0:T(8,128)S(1)}, f32[192,128]{1,0:T(8,128)S(1)}, u32[]{:S(2)}, u32[]{:S(2)}) collective-permute-start(f32[192,128]{1,0:T(8,128)S(1)} %get-tuple-element.36), channel_id=1, source_target_pairs={{0,2},{1,3},{2,4},{3,5},{4,6},{5,7},{6,0},{7,1},{8,10},{9,11},{10,... | collective-permute-start | bytes 294920 | tf_op jit(solution)/shard_map/ppermute | solution.py:246
  32.1 0.0 collective-permute-start.15
  32.1 0.6 %collective-permute-start.16 = (f32[192,128]{1,0:T(8,128)S(1)}, f32[192,128]{1,0:T(8,128)S(1)}, u32[]{:S(2)}, u32[]{:S(2)}) collective-permute-start(f32[192,128]{1,0:T(8,128)S(1)} %get-tuple-element.38), channel_id=1, source_target_pairs={{0,2},{1,3},{2,0},{3,1},{4,6},{5,7},{6,4},{7,5},{8,10},{9,11},{10,... | collective-permute-start | bytes 294920 | tf_op jit(solution)/shard_map/ppermute | solution.py:246
  32.7 1.9 %collective-permute-done.13 = f32[192,128]{1,0:T(8,128)S(1)} collective-permute-done((f32[192,128]{1,0:T(8,128)S(1)}, f32[192,128]{1,0:T(8,128)S(1)}, u32[]{:S(2)}, u32[]{:S(2)}) %collective-permute-start.13) | collective-permute-done | bytes 98336 | tf_op jit(solution)/shard_map/ppermute | solution.py:246
  34.6 1.1 %collective-permute-done.14 = f32[192,128]{1,0:T(8,128)S(1)} collective-permute-done((f32[192,128]{1,0:T(8,128)S(1)}, f32[192,128]{1,0:T(8,128)S(1)}, u32[]{:S(2)}, u32[]{:S(2)}) %collective-permute-start.14) | collective-permute-done | bytes 98336 | tf_op jit(solution)/shard_map/ppermute | solution.py:246
  35.7 0.4 collective-permute-done.15
  36.1 0.0 collective-permute-done.16
  36.2 0.1 collective-permute-start.20
  36.2 1.5 %collective-permute-start.19 = (f32[192,128]{1,0:T(8,128)S(1)}, f32[192,128]{1,0:T(8,128)S(1)}, u32[]{:S(2)}, u32[]{:S(2)}) collective-permute-start(f32[192,128]{1,0:T(8,128)S(1)} %add_add_fusion.1), channel_id=1, source_target_pairs={{0,10},{1,11},{2,0},{3,1},{4,14},{5,15},{6,4},{7,5},{8,2},{9,3},{1... | collective-permute-start | bytes 294920 | tf_op jit(solution)/shard_map/ppermute | solution.py:246
  37.7 1.0 %collective-permute-start.18 = (f32[192,128]{1,0:T(8,128)S(1)}, f32[192,128]{1,0:T(8,128)S(1)}, u32[]{:S(2)}, u32[]{:S(2)}) collective-permute-start(f32[192,128]{1,0:T(8,128)S(1)} %add_add_fusion.1), channel_id=1, source_target_pairs={{0,18},{1,19},{2,0},{3,1},{4,22},{5,23},{6,4},{7,5},{8,26},{9,27},... | collective-permute-start | bytes 294920 | tf_op jit(solution)/shard_map/ppermute | solution.py:246
  38.7 1.5 %collective-permute-start.17 = (f32[192,128]{1,0:T(8,128)S(1)}, f32[192,128]{1,0:T(8,128)S(1)}, u32[]{:S(2)}, u32[]{:S(2)}) collective-permute-start(f32[192,128]{1,0:T(8,128)S(1)} %add_add_fusion.1), channel_id=1, source_target_pairs={{0,26},{1,27},{2,0},{3,1},{4,30},{5,31},{6,4},{7,5},{8,18},{9,19},... | collective-permute-start | bytes 294920 | tf_op jit(solution)/shard_map/ppermute | solution.py:246
  40.2 0.0 collective-permute-done.20
  40.2 0.0 collective-permute-done.19
  40.2 0.8 %collective-permute-done.18 = f32[192,128]{1,0:T(8,128)S(1)} collective-permute-done((f32[192,128]{1,0:T(8,128)S(1)}, f32[192,128]{1,0:T(8,128)S(1)}, u32[]{:S(2)}, u32[]{:S(2)}) %collective-permute-start.18) | collective-permute-done | bytes 98336 | tf_op jit(solution)/shard_map/ppermute | solution.py:246
  41.0 1.4 %collective-permute-done.17 = f32[192,128]{1,0:T(8,128)S(1)} collective-permute-done((f32[192,128]{1,0:T(8,128)S(1)}, f32[192,128]{1,0:T(8,128)S(1)}, u32[]{:S(2)}, u32[]{:S(2)}) %collective-permute-start.17) | collective-permute-done | bytes 98336 | tf_op jit(solution)/shard_map/ppermute | solution.py:246
  42.4 2.3 %collective-permute-start.24 = (f32[192,128]{1,0:T(8,128)S(1)}, f32[192,128]{1,0:T(8,128)S(1)}, u32[]{:S(2)}, u32[]{:S(2)}) collective-permute-start(f32[192,128]{1,0:T(8,128)S(1)} %add_add_fusion), channel_id=1, source_target_pairs={{0,2},{1,3},{2,5},{3,4},{4,6},{5,7},{6,1},{7,0},{8,10},{9,11},{10,... | collective-permute-start | bytes 294920 | tf_op jit(solution)/shard_map/ppermute | solution.py:246
  44.8 0.1 collective-permute-start.23
  44.9 1.1 %collective-permute-start.22 = (f32[192,128]{1,0:T(8,128)S(1)}, f32[192,128]{1,0:T(8,128)S(1)}, u32[]{:S(2)}, u32[]{:S(2)}) collective-permute-start(f32[192,128]{1,0:T(8,128)S(1)} %add_add_fusion), channel_id=1, source_target_pairs={{0,2},{1,3},{2,1},{3,0},{4,6},{5,7},{6,5},{7,4},{8,10},{9,11},{10,... | collective-permute-start | bytes 294920 | tf_op jit(solution)/shard_map/ppermute | solution.py:246
  46.0 0.2 collective-permute-start.21
  46.1 0.0 collective-permute-done.12.value_ref
  46.2 0.1 split.1
  46.3 1.9 %collective-permute-done.24.refs_3_ = f32[192,128]{1,0:T(8,128)S(1)} collective-permute-done((f32[192,128]{1,0:T(8,128)S(1)}, f32[192,128]{1,0:T(8,128)S(1)}, u32[]{:S(2)}, u32[]{:S(2)}) %collective-permute-start.24) | collective-permute-done | bytes 98336 | tf_op jit(solution)/shard_map/ppermute | solution.py:246
  48.2 0.6 %collective-permute-done.23.refs_2_ = f32[192,128]{1,0:T(8,128)S(1)} collective-permute-done((f32[192,128]{1,0:T(8,128)S(1)}, f32[192,128]{1,0:T(8,128)S(1)}, u32[]{:S(2)}, u32[]{:S(2)}) %collective-permute-start.23) | collective-permute-done | bytes 98336 | tf_op jit(solution)/shard_map/ppermute | solution.py:246
  48.8 0.4 collective-permute-done.22.refs_1_
  49.2 0.0 collective-permute-done.21.refs_0_
  49.2 5.4 %factor.1 = (f32[128,128]{1,0:T(8,128)S(1)}, f32[128,128]{1,0:T(8,128)S(1)}) custom-call(bf16[768,256]{1,0:T(8,128)(2,1)S(1)} %get-tuple-element.33.high_ref, bf16[768,256]{1,0:T(8,128)(2,1)S(1)} %get-tuple-element.34.low_ref, f32[192,128]{1,0:T(8,128)S(1)} %collective-permute-done.21.refs_0_, f32[192,128]{1,0:T(8,128)S(1)} %collective-permute-done.22.refs_1_, ...), custom_call_target="tpu_custom_call" | custom-call | tf_op jit(solution)/shard_map/factor/pallas_call | solution.py:345
  54.6 0.1 collective-permute-start.25
  54.7 1.2 %collective-permute-done.25 = f32[128,128]{1,0:T(8,128)S(1)} collective-permute-done((f32[128,128]{1,0:T(8,128)S(1)}, f32[128,128]{1,0:T(8,128)S(1)}, u32[]{:S(2)}, u32[]{:S(2)}) %collective-permute-start.25) | collective-permute-done | bytes 65568 | tf_op jit(solution)/shard_map/ppermute | solution.py:358
  56.0 0.6 %add_bitcast_fusion = f32[1,1,128,128]{3,2,1,0:T(8,128)} fusion(f32[128,128]{1,0:T(8,128)S(1)} %get-tuple-element.39, f32[128,128]{1,0:T(8,128)S(1)} %collective-permute-done.25), kind=kLoop, calls=%fused_computation.10 | loop fusion | flops 16384 | bytes 196608 | tf_op jit(solution)/shard_map/broadcast_in_dim | solution.py:359
  (8 shorter events, 0.2 us)
Async XLA Ops:
  0.0 8.4 %copy-start.1 = (s32[1,16,3]{1,0,2:T(1,128)S(1)}, s32[1,16,3]{1,0,2:T(1,128)}, u32[]{:S(2)}) copy-start(s32[1,16,3]{1,0,2:T(1,128)} %param.7) | copy-start | bytes 580
  0.0 6.2 %copy-start.2 = (s32[1,1,192]{2,1,0:T(1,128)S(1)}, s32[1,1,192]{2,1,0:T(1,128)}, u32[]{:S(2)}) copy-start(s32[1,1,192]{2,1,0:T(1,128)} %param.8) | copy-start | bytes 2308
  0.0 8.4 %copy-start = (f32[768,128]{1,0:T(8,128)S(1)}, f32[768,128]{1,0:T(8,128)}, u32[]{:S(2)}) copy-start(f32[768,128]{1,0:T(8,128)} %start_ref.1) | copy-start | bytes 1179652
  3.1 1.6 %collective-permute-start.1 = (f32[96,512]{1,0:T(8,128)S(1)}, f32[96,512]{1,0:T(8,128)S(1)}, u32[]{:S(2)}, u32[]{:S(2)}) collective-permute-start(f32[96,512]{1,0:T(8,128)S(1)} %get-tuple-element.26), channel_id=1, source_target_pairs={{0,2},{2,0},{4,6},{6,4},{8,10},{10,8},{12,14},{14,12},{16,18},{18,... | collective-permute-start | bytes 589832 | tf_op jit(solution)/shard_map/ppermute | solution.py:289
  3.6 13.2 %collective-permute-start.2 = (f32[192,512]{1,0:T(8,128)S(1)}, f32[192,512]{1,0:T(8,128)S(1)}, u32[]{:S(2)}, u32[]{:S(2)}) collective-permute-start(f32[192,512]{1,0:T(8,128)S(1)} %get-tuple-element.27), channel_id=1, source_target_pairs={{0,2},{2,4},{4,6},{6,8},{8,10},{10,12},{12,14},{14,16},{16,18},{18... | collective-permute-start | bytes 1179656 | tf_op jit(solution)/shard_map/ppermute | solution.py:290
  4.6 12.1 %collective-permute-start.3 = (f32[96,512]{1,0:T(8,128)S(1)}, f32[96,512]{1,0:T(8,128)S(1)}, u32[]{:S(2)}, u32[]{:S(2)}) collective-permute-start(f32[96,512]{1,0:T(8,128)S(1)} %collective-permute-done.1.next_zero_ref), channel_id=1, source_target_pairs={{0,2},{2,4},{4,6},{6,8},{8,10},{10,12},{12,14},{14,16},{16,18},{18... | collective-permute-start | bytes 589832 | tf_op jit(solution)/shard_map/ppermute | solution.py:291
  6.2 2.2 %collective-permute-start = (s32[1,192]{1,0:T(1,128)S(1)}, s32[1,192]{1,0:T(1,128)S(1)}, u32[]{:S(2)}, u32[]{:S(2)}) collective-permute-start(s32[1,192]{1,0:T(1,128)S(1)} %bitcast.23), channel_id=1, source_target_pairs={{0,2},{2,0},{4,6},{6,4},{8,10},{10,8},{12,14},{14,12},{16,18},{18,... | collective-permute-start | bytes 2312 | tf_op jit(solution)/shard_map/ppermute | solution.py:271
  17.6 3.5 %collective-permute-start.11 = (f32[192,128]{1,0:T(8,128)S(1)}, f32[192,128]{1,0:T(8,128)S(1)}, u32[]{:S(2)}, u32[]{:S(2)}) collective-permute-start(f32[192,128]{1,0:T(8,128)S(1)} %get-tuple-element.41), channel_id=1, source_target_pairs={{0,30},{1,31},{2,0},{3,1},{4,26},{5,27},{6,4},{7,5},{8,22},{9,23},... | collective-permute-start | bytes 294920 | tf_op jit(solution)/shard_map/ppermute | solution.py:246
  17.6 4.7 %collective-permute-start.10 = (f32[192,128]{1,0:T(8,128)S(1)}, f32[192,128]{1,0:T(8,128)S(1)}, u32[]{:S(2)}, u32[]{:S(2)}) collective-permute-start(f32[192,128]{1,0:T(8,128)S(1)} %get-tuple-element.42), channel_id=1, source_target_pairs={{0,26},{1,27},{2,0},{3,1},{4,30},{5,31},{6,4},{7,5},{8,18},{9,19},... | collective-permute-start | bytes 294920 | tf_op jit(solution)/shard_map/ppermute | solution.py:246
  19.4 3.7 %collective-permute-start.9 = (f32[192,128]{1,0:T(8,128)S(1)}, f32[192,128]{1,0:T(8,128)S(1)}, u32[]{:S(2)}, u32[]{:S(2)}) collective-permute-start(f32[192,128]{1,0:T(8,128)S(1)} %get-tuple-element.43), channel_id=1, source_target_pairs={{0,22},{1,23},{2,0},{3,1},{4,18},{5,19},{6,4},{7,5},{8,30},{9,31},... | collective-permute-start | bytes 294920 | tf_op jit(solution)/shard_map/ppermute | solution.py:246
  19.4 7.7 %collective-permute-start.8 = (f32[192,128]{1,0:T(8,128)S(1)}, f32[192,128]{1,0:T(8,128)S(1)}, u32[]{:S(2)}, u32[]{:S(2)}) collective-permute-start(f32[192,128]{1,0:T(8,128)S(1)} %get-tuple-element.44), channel_id=1, source_target_pairs={{0,18},{1,19},{2,0},{3,1},{4,22},{5,23},{6,4},{7,5},{8,26},{9,27},... | collective-permute-start | bytes 294920 | tf_op jit(solution)/shard_map/ppermute | solution.py:246
  19.4 7.7 %collective-permute-start.7 = (f32[192,128]{1,0:T(8,128)S(1)}, f32[192,128]{1,0:T(8,128)S(1)}, u32[]{:S(2)}, u32[]{:S(2)}) collective-permute-start(f32[192,128]{1,0:T(8,128)S(1)} %get-tuple-element.45), channel_id=1, source_target_pairs={{0,14},{1,15},{2,0},{3,1},{4,10},{5,11},{6,4},{7,5},{8,6},{9,7},{1... | collective-permute-start | bytes 294920 | tf_op jit(solution)/shard_map/ppermute | solution.py:246
  21.1 6.1 %collective-permute-start.6 = (f32[192,128]{1,0:T(8,128)S(1)}, f32[192,128]{1,0:T(8,128)S(1)}, u32[]{:S(2)}, u32[]{:S(2)}) collective-permute-start(f32[192,128]{1,0:T(8,128)S(1)} %get-tuple-element.46), channel_id=1, source_target_pairs={{0,10},{1,11},{2,0},{3,1},{4,14},{5,15},{6,4},{7,5},{8,2},{9,3},{1... | collective-permute-start | bytes 294920 | tf_op jit(solution)/shard_map/ppermute | solution.py:246
  22.4 4.8 %collective-permute-start.5 = (f32[192,128]{1,0:T(8,128)S(1)}, f32[192,128]{1,0:T(8,128)S(1)}, u32[]{:S(2)}, u32[]{:S(2)}) collective-permute-start(f32[192,128]{1,0:T(8,128)S(1)} %get-tuple-element.47), channel_id=1, source_target_pairs={{0,6},{1,7},{2,0},{3,1},{4,2},{5,3},{6,4},{7,5},{8,14},{9,15},{10,... | collective-permute-start | bytes 294920 | tf_op jit(solution)/shard_map/ppermute | solution.py:246
  23.1 5.0 %collective-permute-start.4 = (f32[192,128]{1,0:T(8,128)S(1)}, f32[192,128]{1,0:T(8,128)S(1)}, u32[]{:S(2)}, u32[]{:S(2)}) collective-permute-start(f32[192,128]{1,0:T(8,128)S(1)} %get-tuple-element.48), channel_id=1, source_target_pairs={{0,2},{1,3},{2,0},{3,1},{4,6},{5,7},{6,4},{7,5},{8,10},{9,11},{10,... | collective-permute-start | bytes 294920 | tf_op jit(solution)/shard_map/ppermute | solution.py:246
  29.2 16.9 %collective-permute-start.12 = (f32[768,256]{1,0:T(8,128)S(1)}, f32[768,256]{1,0:T(8,128)S(1)}, u32[]{:S(2)}, u32[]{:S(2)}) collective-permute-start(f32[768,256]{1,0:T(8,128)S(1)} %get-tuple-element.32), channel_id=1, source_target_pairs={{0,2},{1,3},{2,0},{3,1},{4,6},{5,7},{6,4},{7,5},{8,10},{9,11},{10,... | collective-permute-start | bytes 2359304 | tf_op jit(solution)/shard_map/ppermute | solution.py:246
  29.7 4.9 %collective-permute-start.13 = (f32[192,128]{1,0:T(8,128)S(1)}, f32[192,128]{1,0:T(8,128)S(1)}, u32[]{:S(2)}, u32[]{:S(2)}) collective-permute-start(f32[192,128]{1,0:T(8,128)S(1)} %get-tuple-element.35), channel_id=1, source_target_pairs={{0,2},{1,3},{2,5},{3,4},{4,6},{5,7},{6,1},{7,0},{8,10},{9,11},{10,... | collective-permute-start | bytes 294920 | tf_op jit(solution)/shard_map/ppermute | solution.py:246
  29.8 5.9 %collective-permute-start.14 = (f32[192,128]{1,0:T(8,128)S(1)}, f32[192,128]{1,0:T(8,128)S(1)}, u32[]{:S(2)}, u32[]{:S(2)}) collective-permute-start(f32[192,128]{1,0:T(8,128)S(1)} %get-tuple-element.36), channel_id=1, source_target_pairs={{0,2},{1,3},{2,4},{3,5},{4,6},{5,7},{6,0},{7,1},{8,10},{9,11},{10,... | collective-permute-start | bytes 294920 | tf_op jit(solution)/shard_map/ppermute | solution.py:246
  32.1 4.0 %collective-permute-start.15 = (f32[192,128]{1,0:T(8,128)S(1)}, f32[192,128]{1,0:T(8,128)S(1)}, u32[]{:S(2)}, u32[]{:S(2)}) collective-permute-start(f32[192,128]{1,0:T(8,128)S(1)} %get-tuple-element.37), channel_id=1, source_target_pairs={{0,2},{1,3},{2,1},{3,0},{4,6},{5,7},{6,5},{7,4},{8,10},{9,11},{10,... | collective-permute-start | bytes 294920 | tf_op jit(solution)/shard_map/ppermute | solution.py:246
  32.1 4.0 %collective-permute-start.16 = (f32[192,128]{1,0:T(8,128)S(1)}, f32[192,128]{1,0:T(8,128)S(1)}, u32[]{:S(2)}, u32[]{:S(2)}) collective-permute-start(f32[192,128]{1,0:T(8,128)S(1)} %get-tuple-element.38), channel_id=1, source_target_pairs={{0,2},{1,3},{2,0},{3,1},{4,6},{5,7},{6,4},{7,5},{8,10},{9,11},{10,... | collective-permute-start | bytes 294920 | tf_op jit(solution)/shard_map/ppermute | solution.py:246
  36.2 4.0 %collective-permute-start.20 = (f32[192,128]{1,0:T(8,128)S(1)}, f32[192,128]{1,0:T(8,128)S(1)}, u32[]{:S(2)}, u32[]{:S(2)}) collective-permute-start(f32[192,128]{1,0:T(8,128)S(1)} %add_add_fusion.1), channel_id=1, source_target_pairs={{0,2},{1,3},{2,0},{3,1},{4,6},{5,7},{6,4},{7,5},{8,10},{9,11},{10,... | collective-permute-start | bytes 294920 | tf_op jit(solution)/shard_map/ppermute | solution.py:246
  36.2 4.0 %collective-permute-start.19 = (f32[192,128]{1,0:T(8,128)S(1)}, f32[192,128]{1,0:T(8,128)S(1)}, u32[]{:S(2)}, u32[]{:S(2)}) collective-permute-start(f32[192,128]{1,0:T(8,128)S(1)} %add_add_fusion.1), channel_id=1, source_target_pairs={{0,10},{1,11},{2,0},{3,1},{4,14},{5,15},{6,4},{7,5},{8,2},{9,3},{1... | collective-permute-start | bytes 294920 | tf_op jit(solution)/shard_map/ppermute | solution.py:246
  37.7 3.2 %collective-permute-start.18 = (f32[192,128]{1,0:T(8,128)S(1)}, f32[192,128]{1,0:T(8,128)S(1)}, u32[]{:S(2)}, u32[]{:S(2)}) collective-permute-start(f32[192,128]{1,0:T(8,128)S(1)} %add_add_fusion.1), channel_id=1, source_target_pairs={{0,18},{1,19},{2,0},{3,1},{4,22},{5,23},{6,4},{7,5},{8,26},{9,27},... | collective-permute-start | bytes 294920 | tf_op jit(solution)/shard_map/ppermute | solution.py:246
  38.7 3.7 %collective-permute-start.17 = (f32[192,128]{1,0:T(8,128)S(1)}, f32[192,128]{1,0:T(8,128)S(1)}, u32[]{:S(2)}, u32[]{:S(2)}) collective-permute-start(f32[192,128]{1,0:T(8,128)S(1)} %add_add_fusion.1), channel_id=1, source_target_pairs={{0,26},{1,27},{2,0},{3,1},{4,30},{5,31},{6,4},{7,5},{8,18},{9,19},... | collective-permute-start | bytes 294920 | tf_op jit(solution)/shard_map/ppermute | solution.py:246
  42.4 5.8 %collective-permute-start.24 = (f32[192,128]{1,0:T(8,128)S(1)}, f32[192,128]{1,0:T(8,128)S(1)}, u32[]{:S(2)}, u32[]{:S(2)}) collective-permute-start(f32[192,128]{1,0:T(8,128)S(1)} %add_add_fusion), channel_id=1, source_target_pairs={{0,2},{1,3},{2,5},{3,4},{4,6},{5,7},{6,1},{7,0},{8,10},{9,11},{10,... | collective-permute-start | bytes 294920 | tf_op jit(solution)/shard_map/ppermute | solution.py:246
  44.8 4.0 %collective-permute-start.23 = (f32[192,128]{1,0:T(8,128)S(1)}, f32[192,128]{1,0:T(8,128)S(1)}, u32[]{:S(2)}, u32[]{:S(2)}) collective-permute-start(f32[192,128]{1,0:T(8,128)S(1)} %add_add_fusion), channel_id=1, source_target_pairs={{0,2},{1,3},{2,4},{3,5},{4,6},{5,7},{6,0},{7,1},{8,10},{9,11},{10,... | collective-permute-start | bytes 294920 | tf_op jit(solution)/shard_map/ppermute | solution.py:246
  44.9 4.4 %collective-permute-start.22 = (f32[192,128]{1,0:T(8,128)S(1)}, f32[192,128]{1,0:T(8,128)S(1)}, u32[]{:S(2)}, u32[]{:S(2)}) collective-permute-start(f32[192,128]{1,0:T(8,128)S(1)} %add_add_fusion), channel_id=1, source_target_pairs={{0,2},{1,3},{2,1},{3,0},{4,6},{5,7},{6,5},{7,4},{8,10},{9,11},{10,... | collective-permute-start | bytes 294920 | tf_op jit(solution)/shard_map/ppermute | solution.py:246
  46.0 3.3 %collective-permute-start.21 = (f32[192,128]{1,0:T(8,128)S(1)}, f32[192,128]{1,0:T(8,128)S(1)}, u32[]{:S(2)}, u32[]{:S(2)}) collective-permute-start(f32[192,128]{1,0:T(8,128)S(1)} %add_add_fusion), channel_id=1, source_target_pairs={{0,2},{1,3},{2,0},{3,1},{4,6},{5,7},{6,4},{7,5},{8,10},{9,11},{10,... | collective-permute-start | bytes 294920 | tf_op jit(solution)/shard_map/ppermute | solution.py:246
  54.6 1.3 %collective-permute-start.25 = (f32[128,128]{1,0:T(8,128)S(1)}, f32[128,128]{1,0:T(8,128)S(1)}, u32[]{:S(2)}, u32[]{:S(2)}) collective-permute-start(f32[128,128]{1,0:T(8,128)S(1)} %get-tuple-element.40), channel_id=1, source_target_pairs={{0,2},{2,0},{4,6},{6,4},{8,10},{10,8},{12,14},{14,12},{16,18},{18,... | collective-permute-start | bytes 196616 | tf_op jit(solution)/shard_map/ppermute | solution.py:358

commit v12 on v11

--- a/solution.py
+++ b/solution.py
@@ -36,7 +36,7 @@
     return out + lax.dot_general(lh, rh, dims, preferred_element_type=F32)
 
 
-def interp_kernel(owners, table_hbm, node_hbm, interp_hbm, swap_ref, one_ref, send_ref, zero_ref, *scratch):
+def interp_kernel(owners, table_hbm, node_hbm, interp_hbm, zero_ref, one_ref, two_ref, *scratch):
     grid_scr, node_ref, interp_ref, table_ref, sems = scratch
     rows = zero_ref.shape[0]
     slots, depth = node_ref.shape
@@ -71,26 +71,14 @@
         at = pl.multiple_of(start - shift, SLAB)
         wide = grid_scr[pl.ds(at, rows + SLAB), :]
         piece = pltpu.roll(wide, lax.rem(rows + SLAB - shift, rows + SLAB), 0)[:rows, :]
-        if distance == 1:
-            one_ref[...] = piece
-            send_ref[:rows, :] = piece
-        else:
-            send_ref[rows:, :] = piece
+        (one_ref, two_ref)[distance - 1][...] = piece
         start = start + table_ref[distance, 0, lax.rem(own + distance, owners)]
-    second = lax.rem(own, 2) == 1
-
-    @pl.when(second)
-    def _():
-        swap_ref[...] = zero_ref[...]
-
-    @pl.when(jnp.logical_not(second))
-    def _():
-        swap_ref[...] = send_ref[rows:, :]
-
-
-def pick_kernel(rows, per_tile, table_ref, order_ref, order_next_ref, start_ref, out_ref, high_ref, low_ref):
+
+
+def pick_kernel(rows, per_tile, table_ref, order_ref, order_next_ref, start_ref, *refs):
     elements = order_ref.shape[1]
-    slots = out_ref.shape[1]
+    *outs, high_ref, low_ref = refs
+    slots = outs[0].shape[1]
     chip = lax.div(lax.axis_index("fib"), 2)
     rank_at = lax.broadcasted_iota(jnp.int32, (elements, slots), 0)
     slot_at = lax.broadcasted_iota(jnp.int32, (elements, slots), 1)
@@ -108,24 +96,17 @@
         place = place - tile * per_tile + (tile ^ (2 * chip)) * per_tile
         place = jnp.broadcast_to(place, (elements, elements))
         to_place = jnp.where(place == row, 1.0, 0.0).astype(BF16)
-        out_ref[core * elements : (core + 1) * elements, :] = jnp.dot(
+        outs[core][...] = jnp.dot(
             to_place, jnp.where(from_slot, 1.0, 0.0).astype(BF16), preferred_element_type=F32
         ).astype(BF16)
     high_ref[...], low_ref[...] = halves(start_ref[...].T)
 
 
-def order_kernel(pick_ref, zero_ref, one_ref, next_zero_ref, back_ref, back_two_ref, *outs):
-    rows = zero_ref.shape[0]
-    elements = outs[0].shape[0]
-    sources = (
-        (zero_ref[...], back_ref[:rows, :], back_two_ref[...]),
-        (next_zero_ref[...], one_ref[...], back_ref[rows:, :]),
-    )
-    for core, pieces in enumerate(sources):
-        pick = pick_ref[core * elements : (core + 1) * elements, :]
-        high, low = halves(jnp.concatenate(pieces, axis=0))
-        out = jnp.dot(pick, low, preferred_element_type=F32)
-        outs[core][...] = out + jnp.dot(pick, high, preferred_element_type=F32)
+def order_kernel(pick_ref, *refs):
+    *pieces, out_ref = refs
+    high, low = halves(jnp.concatenate([piece[...] for piece in pieces], axis=0))
+    out = jnp.dot(pick_ref[...], low, preferred_element_type=F32)
+    out_ref[...] = out + jnp.dot(pick_ref[...], high, preferred_element_type=F32)
 
 
 def bit_place(order):
@@ -143,16 +124,15 @@
     length, width = field_ref.shape
     tile = width // 2
     chip = lax.div(lax.axis_index("fib"), 2)
-    each = length // (2 * len(block_refs))
+    each = length // len(block_refs)
     if len(block_refs) == 1:
         field_ref[...] = block_refs[0][...]
         block_refs = []
-    for step, block in enumerate(block_refs):
-        for owner in range(2):
-            at = pl.multiple_of((2 * (chip ^ step) + owner) * each, each)
-            for core in range(2):
-                part = (2 * owner + core) * each
-                field_ref[pl.ds(at, each), core * tile : (core + 1) * tile] = block[part : part + each, :]
+    for n, block in enumerate(block_refs):
+        owner, step = divmod(n, len(block_refs) // 2)
+        at = pl.multiple_of((2 * (chip ^ step) + owner) * each, each)
+        for core in range(2):
+            field_ref[pl.ds(at, each), core * tile : (core + 1) * tile] = block[core * each : (core + 1) * each, :]
     field = halves(field_ref[...])
     mixed = dot3((high_ref[...], low_ref[...]), field, ((1,), (0,)))
     image_scr[...] = dot3(field, halves(mixed), ((1,), (1,)))
@@ -271,11 +251,11 @@
     order_next = lax.ppermute(slot_order[0], "fib", core_swap)
     piece = jax.ShapeDtypeStruct((capacity, points), F32)
     copies = 1 + window + pl.cdiv(nodes.shape[1], KSTEP)
-    swap, one, send, zero = pl.pallas_call(
+    zero, one, two = pl.pallas_call(
         functools.partial(interp_kernel, owners),
-        out_shape=[piece, piece, jax.ShapeDtypeStruct((2 * capacity, points), F32), piece],
+        out_shape=[piece] * 3,
         in_specs=[pl.BlockSpec(memory_space=pl.ANY)] * 3,
-        out_specs=[VMEM] * 4,
+        out_specs=[VMEM] * 3,
         scratch_shapes=[
             pltpu.VMEM((nodes.shape[0] + SLAB, points), F32),
             pltpu.VMEM(nodes.shape, F32),
@@ -286,36 +266,42 @@
         compiler_params=BIG,
         name="interp",
     )(*(pltpu.with_memory_space_constraint(x, pltpu.HBM) for x in (table, nodes, interp_matrix)))
-    swapped = lax.ppermute(swap, "fib", core_swap)
-    back = lax.ppermute(send, "fib", forward)
-    back_two = lax.ppermute(swapped, "fib", forward)
+    back = lax.ppermute(two, "fib", forward)
+    next_zero = lax.ppermute(zero, "fib", core_swap)
+    back_one = lax.ppermute(one, "fib", forward)
+    back_two = lax.ppermute(back, "fib", forward)
     basis = jax.ShapeDtypeStruct((rank, length), BF16)
-    pick, *basis_parts = pl.pallas_call(
+    first_pick, second_pick, *basis_parts = pl.pallas_call(
         functools.partial(pick_kernel, capacity, elements // owners),
-        out_shape=[jax.ShapeDtypeStruct((2 * elements, capacity * window), BF16), basis, basis],
+        out_shape=[jax.ShapeDtypeStruct((elements, capacity * window), BF16)] * 2 + [basis] * 2,
         in_specs=[SMEM, VMEM, VMEM, VMEM],
-        out_specs=[VMEM] * 3,
+        out_specs=[VMEM] * 4,
         compiler_params=BIG,
         name="pick",
     )(table, slot_order[0], order_next, start_basis)
-    bricks = pl.pallas_call(
+    order = pl.pallas_call(
         order_kernel,
-        out_shape=[jax.ShapeDtypeStruct((elements, points), F32)] * 2,
-        in_specs=[VMEM] * 6,
-        out_specs=[VMEM] * 2,
+        out_shape=jax.ShapeDtypeStruct((elements, points), F32),
+        in_specs=[VMEM] * (1 + window),
+        out_specs=VMEM,
         compiler_params=BIG,
         name="order",
-    )(pick, zero, one, swapped, back, back_two)
+    )
 
     blocks = owners // 2
     chips = masks("fib", 2, owners)[::-1]
-    both = jnp.concatenate([b.reshape(blocks, 2 * length // owners, tile) for b in bricks], axis=1)
-    got = {step: crossed(both[step], chips, step, 1) for step in range(blocks - 1, -1, -1)}
-    parts = [got[step] for step in range(blocks)]
+    parts = [None] * owners
+    for owner, brick in (
+        (1, order(second_pick, next_zero, one, back)),
+        (0, order(first_pick, zero, back_one, back_two)),
+    ):
+        brick = brick.reshape(blocks, 2 * length // owners, tile)
+        for step in range(blocks - 1, -1, -1):
+            parts[owner * blocks + step] = crossed(brick[step], chips, step, 1)
     if length // owners % SLAB:
         at = lax.axis_index("fib") // 2 ^ jnp.arange(blocks)
-        whole = jnp.stack(parts)[at].reshape(blocks, 2, 2, length // owners, tile)
-        parts = [whole.transpose(0, 1, 3, 2, 4).reshape(length, 2 * tile)]
+        whole = jnp.stack(parts).reshape(2, blocks, 2, length // owners, tile)[:, at]
+        parts = [whole.transpose(1, 0, 3, 2, 4).reshape(length, 2 * tile)]
 
     mid = masks("fib", 2, 4) + masks("pln", 1, planes)
     distant = masks("fib", 4, owners)[::-1]

time: 56.7 us -> 63.7 us (1.12)
  starting transfers between devices: 24.4 us -> 29.5 us
  waiting for transfers between devices: 19.8 us -> 21.4 us
    ppermute x21 -> x29, starting transfers between devices: 20.7 us -> 25.8 us  [crossed(): return lax.ppermute(value, ('fib', 'pln'), pairs)]
    ppermute x21 -> x29, waiting for transfers between devices: 9.52 us -> 11.8 us  [crossed(): return lax.ppermute(value, ('fib', 'pln'), pairs)]
    ppermute x3 -> x4, starting transfers between devices: 2.19 us -> 3.62 us  [the longest x1 2.6 us: per_device(): next_zero = lax.ppermute(zero, 'fib', core_swap)]
    ppermute x1, starting transfers between devices: 1.37 us -> 0.01 us  [per_device(): order_next = lax.ppermute(slot_order[0], 'fib', core_swap)]
    ppermute x3 -> x4, waiting for transfers between devices: 8.21 us -> 7.72 us  [the longest x1 4.27 us: per_device(): back_two = lax.ppermute(back, 'fib', forward)]
  transfers between devices with their start and end apart: 26 -> 35, of which waited for: 13 -> 14; matrix products, arithmetic and copies ran while one was open for 0% -> 0% of each run, Pallas kernels for 2% -> 3%
where the time goes in v12:
time: 63.7 us; the launch traced here: 63.6 us
  starting transfers between devices  29.5 us (46%)
  waiting for transfers between devices  21.4 us (34%)
  Pallas kernels  11.6 us (18%)
  other arithmetic  0.69 us (1%)
    ppermute x29, starting transfers between devices, crossed(): return lax.ppermute(value, ('fib', 'pln'), pairs)  25.8 us
    ppermute x29, waiting for transfers between devices, crossed(): return lax.ppermute(value, ('fib', 'pln'), pairs)  11.8 us
    pallas_call x1, Pallas kernels, per_device(): pl.pallas_call(functools.partial(factor_kernel, mid), out_shape=[jax.Shap...  5.42 us
    ppermute x1, waiting for transfers between devices, per_device(): back_two = lax.ppermute(back, 'fib', forward)  4.27 us
    ppermute x1, waiting for transfers between devices, per_device(): back = lax.ppermute(two, 'fib', forward)  3.44 us
    pallas_call x1, Pallas kernels, per_device(): pl.pallas_call(functools.partial(interp_kernel, owners), out_shape=[piece...  3.01 us
    ppermute x1, starting transfers between devices, per_device(): next_zero = lax.ppermute(zero, 'fib', core_swap)  2.6 us
  transfers between devices with their start and end apart: 35, of which 14 were waited for; matrix products, arithmetic and copies ran while one was open for 0% of the time, Pallas kernels for 3%

profile of v12, /device:TPU:0, one launch (start us, length us, event | category | flops | bytes accessed | tf_op | source)
XLA Modules:
  0.0 63.6 jit_solution(2439278639054649293)
XLA Ops:
  0.0 3.0 %interp.1 = (f32[96,512]{1,0:T(8,128)S(1)}, f32[96,512]{1,0:T(8,128)S(1)}, f32[96,512]{1,0:T(8,128)S(1)}) custom-call(s32[3,1,16]{2,1,0:T(1,128)} %bitcast.5, f32[288,1000]{1,0:T(8,128)} %bitcast.9, f32[1000,512]{1,0:T(8,128)} %interp_hbm.1), custom_call_target="tpu_custom_call" | custom-call | tf_op jit(solution)/shard_map/interp/pallas_call | solution.py:254
  3.0 0.5 collective-permute-start.2
  3.5 2.6 %collective-permute-start.12 = (f32[96,512]{1,0:T(8,128)S(1)}, f32[96,512]{1,0:T(8,128)S(1)}, u32[]{:S(2)}, u32[]{:S(2)}) collective-permute-start(f32[96,512]{1,0:T(8,128)S(1)} %get-tuple-element.22.refs_0_), channel_id=1, source_target_pairs={{0,2},{2,0},{4,6},{6,4},{8,10},{10,8},{12,14},{14,12},{16,18},{18,... | collective-permute-start | bytes 589832 | tf_op jit(solution)/shard_map/ppermute | solution.py:270
  6.1 0.0 collective-permute-start
  6.1 0.5 collective-permute-start.1
  6.7 0.6 collective-permute-done.order_next_ref
  7.3 1.1 %pick.1 = (bf16[192,288]{1,0:T(8,128)(2,1)S(1)}, bf16[192,288]{1,0:T(8,128)(2,1)S(1)}, bf16[128,768]{1,0:T(8,128)(2,1)S(1)}, bf16[128,768]{1,0:T(8,128)(2,1)S(1)}) custom-call(s32[3,1,16]{2,1,0:T(1,128)S(1)} %bitcast.6, s32[1,192]{1,0:T(1,128)S(1)} %bitcast.8, s32[1,192]{1,0:T(1,128)S(1)} %collective-permute-done.order_next_ref, f32[768,128]{1,0:T(8,128)S(1)} %copy-done), custom_call_target="tpu_custom_call" | custom-call | tf_op jit(solution)/shard_map/pick/pallas_call | solution.py:274
  8.4 3.4 %collective-permute-done.2.refs_2_ = f32[96,512]{1,0:T(8,128)S(1)} collective-permute-done((f32[96,512]{1,0:T(8,128)S(1)}, f32[96,512]{1,0:T(8,128)S(1)}, u32[]{:S(2)}, u32[]{:S(2)}) %collective-permute-start.2) | collective-permute-done | bytes 196640 | tf_op jit(solution)/shard_map/ppermute | solution.py:269
  11.9 0.4 order.3
  12.3 0.1 collective-permute-start.13
  12.5 1.5 %collective-permute-start.14 = (f32[96,128]{1,0:T(8,128)S(1)}, f32[96,128]{1,0:T(8,128)S(1)}, u32[]{:S(2)}, u32[]{:S(2)}) collective-permute-start(f32[96,128]{1,0:T(8,128)S(1)} %squeeze.66), channel_id=1, source_target_pairs={{0,6},{1,7},{2,0},{3,1},{4,2},{5,3},{6,4},{7,5},{8,14},{9,15},{10,... | collective-permute-start | bytes 147464 | tf_op jit(solution)/shard_map/ppermute | solution.py:226
  13.9 0.0 collective-permute-done.1.refs_1_
  14.0 1.5 %collective-permute-start.16 = (f32[96,128]{1,0:T(8,128)S(1)}, f32[96,128]{1,0:T(8,128)S(1)}, u32[]{:S(2)}, u32[]{:S(2)}) collective-permute-start(f32[96,128]{1,0:T(8,128)S(1)} %squeeze.68), channel_id=1, source_target_pairs={{0,14},{1,15},{2,0},{3,1},{4,10},{5,11},{6,4},{7,5},{8,6},{9,7},{1... | collective-permute-start | bytes 147464 | tf_op jit(solution)/shard_map/ppermute | solution.py:226
  15.5 4.3 %collective-permute-done.3.refs_2_ = f32[96,512]{1,0:T(8,128)S(1)} collective-permute-done((f32[96,512]{1,0:T(8,128)S(1)}, f32[96,512]{1,0:T(8,128)S(1)}, u32[]{:S(2)}, u32[]{:S(2)}) %collective-permute-start.3) | collective-permute-done | bytes 196640 | tf_op jit(solution)/shard_map/ppermute | solution.py:272
  19.8 0.0 collective-permute-start.17
  19.8 0.4 order.2
  20.2 0.0 collective-permute-done.13.refs_8_
  20.2 0.1 collective-permute-start.18
  20.3 0.6 collective-permute-start.19
  20.9 1.3 %collective-permute-start.20 = (f32[96,128]{1,0:T(8,128)S(1)}, f32[96,128]{1,0:T(8,128)S(1)}, u32[]{:S(2)}, u32[]{:S(2)}) collective-permute-start(f32[96,128]{1,0:T(8,128)S(1)} %squeeze.72), channel_id=1, source_target_pairs={{0,30},{1,31},{2,0},{3,1},{4,26},{5,27},{6,4},{7,5},{8,22},{9,23},... | collective-permute-start | bytes 147464 | tf_op jit(solution)/shard_map/ppermute | solution.py:226
  22.2 0.0 collective-permute-done.16.refs_11_
  22.2 0.0 collective-permute-start.4
  22.2 0.0 collective-permute-done.17.refs_12_
  22.3 0.3 collective-permute-start.5
  22.6 0.0 collective-permute-done.18.refs_13_
  22.6 2.6 %collective-permute-start.6 = (f32[96,128]{1,0:T(8,128)S(1)}, f32[96,128]{1,0:T(8,128)S(1)}, u32[]{:S(2)}, u32[]{:S(2)}) collective-permute-start(f32[96,128]{1,0:T(8,128)S(1)} %squeeze.59), channel_id=1, source_target_pairs={{0,10},{1,11},{2,0},{3,1},{4,14},{5,15},{6,4},{7,5},{8,2},{9,3},{1... | collective-permute-start | bytes 147464 | tf_op jit(solution)/shard_map/ppermute | solution.py:226
  25.2 1.6 %collective-permute-start.7 = (f32[96,128]{1,0:T(8,128)S(1)}, f32[96,128]{1,0:T(8,128)S(1)}, u32[]{:S(2)}, u32[]{:S(2)}) collective-permute-start(f32[96,128]{1,0:T(8,128)S(1)} %squeeze.60), channel_id=1, source_target_pairs={{0,14},{1,15},{2,0},{3,1},{4,10},{5,11},{6,4},{7,5},{8,6},{9,7},{1... | collective-permute-start | bytes 147464 | tf_op jit(solution)/shard_map/ppermute | solution.py:226
  26.8 1.5 %collective-permute-start.8 = (f32[96,128]{1,0:T(8,128)S(1)}, f32[96,128]{1,0:T(8,128)S(1)}, u32[]{:S(2)}, u32[]{:S(2)}) collective-permute-start(f32[96,128]{1,0:T(8,128)S(1)} %squeeze.61), channel_id=1, source_target_pairs={{0,18},{1,19},{2,0},{3,1},{4,22},{5,23},{6,4},{7,5},{8,26},{9,27},... | collective-permute-start | bytes 147464 | tf_op jit(solution)/shard_map/ppermute | solution.py:226
  28.3 0.0 collective-permute-done.4.refs_0_
  28.3 0.9 %collective-permute-start.9 = (f32[96,128]{1,0:T(8,128)S(1)}, f32[96,128]{1,0:T(8,128)S(1)}, u32[]{:S(2)}, u32[]{:S(2)}) collective-permute-start(f32[96,128]{1,0:T(8,128)S(1)} %squeeze.62), channel_id=1, source_target_pairs={{0,22},{1,23},{2,0},{3,1},{4,18},{5,19},{6,4},{7,5},{8,30},{9,31},... | collective-permute-start | bytes 147464 | tf_op jit(solution)/shard_map/ppermute | solution.py:226
  29.2 0.0 collective-permute-done.5.refs_1_
  29.2 1.2 %collective-permute-start.10 = (f32[96,128]{1,0:T(8,128)S(1)}, f32[96,128]{1,0:T(8,128)S(1)}, u32[]{:S(2)}, u32[]{:S(2)}) collective-permute-start(f32[96,128]{1,0:T(8,128)S(1)} %squeeze.63), channel_id=1, source_target_pairs={{0,26},{1,27},{2,0},{3,1},{4,30},{5,31},{6,4},{7,5},{8,18},{9,19},... | collective-permute-start | bytes 147464 | tf_op jit(solution)/shard_map/ppermute | solution.py:226
  30.4 1.0 %collective-permute-start.11 = (f32[96,128]{1,0:T(8,128)S(1)}, f32[96,128]{1,0:T(8,128)S(1)}, u32[]{:S(2)}, u32[]{:S(2)}) collective-permute-start(f32[96,128]{1,0:T(8,128)S(1)} %squeeze.64), channel_id=1, source_target_pairs={{0,30},{1,31},{2,0},{3,1},{4,26},{5,27},{6,4},{7,5},{8,22},{9,23},... | collective-permute-start | bytes 147464 | tf_op jit(solution)/shard_map/ppermute | solution.py:226
  31.4 0.0 collective-permute-done.7.refs_3_
  31.4 0.0 collective-permute-done.8.refs_4_
  31.4 0.0 collective-permute-done.9.refs_5_
  31.4 0.8 %collective-permute-done.10.refs_6_ = f32[96,128]{1,0:T(8,128)S(1)} collective-permute-done((f32[96,128]{1,0:T(8,128)S(1)}, f32[96,128]{1,0:T(8,128)S(1)}, u32[]{:S(2)}, u32[]{:S(2)}) %collective-permute-start.10) | collective-permute-done | bytes 49184 | tf_op jit(solution)/shard_map/ppermute | solution.py:226
  32.2 1.0 %collective-permute-done.11.refs_7_ = f32[96,128]{1,0:T(8,128)S(1)} collective-permute-done((f32[96,128]{1,0:T(8,128)S(1)}, f32[96,128]{1,0:T(8,128)S(1)}, u32[]{:S(2)}, u32[]{:S(2)}) %collective-permute-start.11) | collective-permute-done | bytes 49184 | tf_op jit(solution)/shard_map/ppermute | solution.py:226
  33.1 1.1 %image.1 = (f32[192,128]{1,0:T(8,128)S(1)}, f32[192,128]{1,0:T(8,128)S(1)}, f32[192,128]{1,0:T(8,128)S(1)}, f32[192,128]{1,0:T(8,128)S(1)}, f32[768,256]{1,0:T(8,128)S(1)}) custom-call(f32[96,128]{1,0:T(8,128)S(1)} %collective-permute-done.4.refs_0_, f32[96,128]{1,0:T(8,128)S(1)} %collective-permute-done.5.refs_1_, ...), custom_call_target="tpu_custom_call" | custom-call | tf_op jit(solution)/shard_map/image/pallas_call | solution.py:310
  34.3 2.9 %collective-permute-start.21 = (f32[768,256]{1,0:T(8,128)S(1)}, f32[768,256]{1,0:T(8,128)S(1)}, u32[]{:S(2)}, u32[]{:S(2)}) collective-permute-start(f32[768,256]{1,0:T(8,128)S(1)} %get-tuple-element.28), channel_id=1, source_target_pairs={{0,2},{1,3},{2,0},{3,1},{4,6},{5,7},{6,4},{7,5},{8,10},{9,11},{10,... | collective-permute-start | bytes 2359304 | tf_op jit(solution)/shard_map/ppermute | solution.py:226
  37.2 0.1 collective-permute-start.22
  37.3 2.3 %collective-permute-start.23 = (f32[192,128]{1,0:T(8,128)S(1)}, f32[192,128]{1,0:T(8,128)S(1)}, u32[]{:S(2)}, u32[]{:S(2)}) collective-permute-start(f32[192,128]{1,0:T(8,128)S(1)} %get-tuple-element.32), channel_id=1, source_target_pairs={{0,2},{1,3},{2,4},{3,5},{4,6},{5,7},{6,0},{7,1},{8,10},{9,11},{10,... | collective-permute-start | bytes 294920 | tf_op jit(solution)/shard_map/ppermute | solution.py:226
  39.6 0.1 collective-permute-start.25
  39.7 2.4 %collective-permute-done.22 = f32[192,128]{1,0:T(8,128)S(1)} collective-permute-done((f32[192,128]{1,0:T(8,128)S(1)}, f32[192,128]{1,0:T(8,128)S(1)}, u32[]{:S(2)}, u32[]{:S(2)}) %collective-permute-start.22) | collective-permute-done | bytes 98336 | tf_op jit(solution)/shard_map/ppermute | solution.py:226
  42.1 1.9 %collective-permute-done.23 = f32[192,128]{1,0:T(8,128)S(1)} collective-permute-done((f32[192,128]{1,0:T(8,128)S(1)}, f32[192,128]{1,0:T(8,128)S(1)}, u32[]{:S(2)}, u32[]{:S(2)}) %collective-permute-start.23) | collective-permute-done | bytes 98336 | tf_op jit(solution)/shard_map/ppermute | solution.py:226
  44.0 0.0 collective-permute-done.24
  44.0 0.0 collective-permute-done.25
  44.1 0.1 collective-permute-start.29
  44.1 0.8 %collective-permute-start.28 = (f32[192,128]{1,0:T(8,128)S(1)}, f32[192,128]{1,0:T(8,128)S(1)}, u32[]{:S(2)}, u32[]{:S(2)}) collective-permute-start(f32[192,128]{1,0:T(8,128)S(1)} %add_add_fusion.1), channel_id=1, source_target_pairs={{0,10},{1,11},{2,0},{3,1},{4,14},{5,15},{6,4},{7,5},{8,2},{9,3},{1... | collective-permute-start | bytes 294920 | tf_op jit(solution)/shard_map/ppermute | solution.py:226
  44.9 1.6 %collective-permute-start.26 = (f32[192,128]{1,0:T(8,128)S(1)}, f32[192,128]{1,0:T(8,128)S(1)}, u32[]{:S(2)}, u32[]{:S(2)}) collective-permute-start(f32[192,128]{1,0:T(8,128)S(1)} %add_add_fusion.1), channel_id=1, source_target_pairs={{0,26},{1,27},{2,0},{3,1},{4,30},{5,31},{6,4},{7,5},{8,18},{9,19},... | collective-permute-start | bytes 294920 | tf_op jit(solution)/shard_map/ppermute | solution.py:226
  46.6 0.6 collective-permute-done.28
  47.1 1.0 %collective-permute-done.27 = f32[192,128]{1,0:T(8,128)S(1)} collective-permute-done((f32[192,128]{1,0:T(8,128)S(1)}, f32[192,128]{1,0:T(8,128)S(1)}, u32[]{:S(2)}, u32[]{:S(2)}) %collective-permute-start.27) | collective-permute-done | bytes 98336 | tf_op jit(solution)/shard_map/ppermute | solution.py:226
  48.1 1.1 %collective-permute-done.26 = f32[192,128]{1,0:T(8,128)S(1)} collective-permute-done((f32[192,128]{1,0:T(8,128)S(1)}, f32[192,128]{1,0:T(8,128)S(1)}, u32[]{:S(2)}, u32[]{:S(2)}) %collective-permute-start.26) | collective-permute-done | bytes 98336 | tf_op jit(solution)/shard_map/ppermute | solution.py:226
  49.2 2.6 %collective-permute-start.33 = (f32[192,128]{1,0:T(8,128)S(1)}, f32[192,128]{1,0:T(8,128)S(1)}, u32[]{:S(2)}, u32[]{:S(2)}) collective-permute-start(f32[192,128]{1,0:T(8,128)S(1)} %add_add_fusion), channel_id=1, source_target_pairs={{0,2},{1,3},{2,5},{3,4},{4,6},{5,7},{6,1},{7,0},{8,10},{9,11},{10,... | collective-permute-start | bytes 294920 | tf_op jit(solution)/shard_map/ppermute | solution.py:226
  51.8 0.1 collective-permute-start.32
  51.9 1.1 %collective-permute-start.31 = (f32[192,128]{1,0:T(8,128)S(1)}, f32[192,128]{1,0:T(8,128)S(1)}, u32[]{:S(2)}, u32[]{:S(2)}) collective-permute-start(f32[192,128]{1,0:T(8,128)S(1)} %add_add_fusion), channel_id=1, source_target_pairs={{0,2},{1,3},{2,1},{3,0},{4,6},{5,7},{6,5},{7,4},{8,10},{9,11},{10,... | collective-permute-start | bytes 294920 | tf_op jit(solution)/shard_map/ppermute | solution.py:226
  53.0 0.1 split.1
  53.1 2.0 %collective-permute-done.33.refs_3_ = f32[192,128]{1,0:T(8,128)S(1)} collective-permute-done((f32[192,128]{1,0:T(8,128)S(1)}, f32[192,128]{1,0:T(8,128)S(1)}, u32[]{:S(2)}, u32[]{:S(2)}) %collective-permute-start.33) | collective-permute-done | bytes 98336 | tf_op jit(solution)/shard_map/ppermute | solution.py:226
  55.2 0.7 %collective-permute-done.32.refs_2_ = f32[192,128]{1,0:T(8,128)S(1)} collective-permute-done((f32[192,128]{1,0:T(8,128)S(1)}, f32[192,128]{1,0:T(8,128)S(1)}, u32[]{:S(2)}, u32[]{:S(2)}) %collective-permute-start.32) | collective-permute-done | bytes 98336 | tf_op jit(solution)/shard_map/ppermute | solution.py:226
  55.9 0.3 collective-permute-done.31.refs_1_
  56.2 5.4 %factor.1 = (f32[128,128]{1,0:T(8,128)S(1)}, f32[128,128]{1,0:T(8,128)S(1)}) custom-call(bf16[768,256]{1,0:T(8,128)(2,1)S(1)} %get-tuple-element.29.high_ref, bf16[768,256]{1,0:T(8,128)(2,1)S(1)} %get-tuple-element.30.low_ref, f32[192,128]{1,0:T(8,128)S(1)} %collective-permute-done.30.refs_0_, f32[192,128]{1,0:T(8,128)S(1)} %collective-permute-done.31.refs_1_, ...), custom_call_target="tpu_custom_call" | custom-call | tf_op jit(solution)/shard_map/factor/pallas_call | solution.py:331
  61.6 0.1 collective-permute-start.34
  61.7 1.2 %collective-permute-done.34 = f32[128,128]{1,0:T(8,128)S(1)} collective-permute-done((f32[128,128]{1,0:T(8,128)S(1)}, f32[128,128]{1,0:T(8,128)S(1)}, u32[]{:S(2)}, u32[]{:S(2)}) %collective-permute-start.34) | collective-permute-done | bytes 65568 | tf_op jit(solution)/shard_map/ppermute | solution.py:344
  62.9 0.6 %add_bitcast_fusion = f32[1,1,128,128]{3,2,1,0:T(8,128)} fusion(f32[128,128]{1,0:T(8,128)S(1)} %get-tuple-element.35, f32[128,128]{1,0:T(8,128)S(1)} %collective-permute-done.34), kind=kLoop, calls=%fused_computation.2 | loop fusion | flops 16384 | bytes 196608 | tf_op jit(solution)/shard_map/broadcast_in_dim | solution.py:345
  (40 shorter events, 0.2 us)
Async XLA Ops:
  0.0 7.3 %copy-start.1 = (s32[1,16,3]{1,0,2:T(1,128)S(1)}, s32[1,16,3]{1,0,2:T(1,128)}, u32[]{:S(2)}) copy-start(s32[1,16,3]{1,0,2:T(1,128)} %param.7) | copy-start | bytes 580
  0.0 6.1 %copy-start.2 = (s32[1,1,192]{2,1,0:T(1,128)S(1)}, s32[1,1,192]{2,1,0:T(1,128)}, u32[]{:S(2)}) copy-start(s32[1,1,192]{2,1,0:T(1,128)} %param.8) | copy-start | bytes 2308
  0.0 7.3 %copy-start = (f32[768,128]{1,0:T(8,128)S(1)}, f32[768,128]{1,0:T(8,128)}, u32[]{:S(2)}) copy-start(f32[768,128]{1,0:T(8,128)} %start_ref.1) | copy-start | bytes 1179652
  3.0 8.8 %collective-permute-start.2 = (f32[96,512]{1,0:T(8,128)S(1)}, f32[96,512]{1,0:T(8,128)S(1)}, u32[]{:S(2)}, u32[]{:S(2)}) collective-permute-start(f32[96,512]{1,0:T(8,128)S(1)} %get-tuple-element.24), channel_id=1, source_target_pairs={{0,2},{2,4},{4,6},{6,8},{8,10},{10,12},{12,14},{14,16},{16,18},{18... | collective-permute-start | bytes 589832 | tf_op jit(solution)/shard_map/ppermute | solution.py:269
  3.5 8.3 %collective-permute-start.12 = (f32[96,512]{1,0:T(8,128)S(1)}, f32[96,512]{1,0:T(8,128)S(1)}, u32[]{:S(2)}, u32[]{:S(2)}) collective-permute-start(f32[96,512]{1,0:T(8,128)S(1)} %get-tuple-element.22.refs_0_), channel_id=1, source_target_pairs={{0,2},{2,0},{4,6},{6,4},{8,10},{10,8},{12,14},{14,12},{16,18},{18,... | collective-permute-start | bytes 589832 | tf_op jit(solution)/shard_map/ppermute | solution.py:270
  6.1 1.1 %collective-permute-start = (s32[1,192]{1,0:T(1,128)S(1)}, s32[1,192]{1,0:T(1,128)S(1)}, u32[]{:S(2)}, u32[]{:S(2)}) collective-permute-start(s32[1,192]{1,0:T(1,128)S(1)} %bitcast.7), channel_id=1, source_target_pairs={{0,2},{2,0},{4,6},{6,4},{8,10},{10,8},{12,14},{14,12},{16,18},{18,... | collective-permute-start | bytes 2312 | tf_op jit(solution)/shard_map/ppermute | solution.py:251
  6.1 7.8 %collective-permute-start.1 = (f32[96,512]{1,0:T(8,128)S(1)}, f32[96,512]{1,0:T(8,128)S(1)}, u32[]{:S(2)}, u32[]{:S(2)}) collective-permute-start(f32[96,512]{1,0:T(8,128)S(1)} %get-tuple-element.23.refs_1_), channel_id=1, source_target_pairs={{0,2},{2,4},{4,6},{6,8},{8,10},{10,12},{12,14},{14,16},{16,18},{18... | collective-permute-start | bytes 589832 | tf_op jit(solution)/shard_map/ppermute | solution.py:271
  11.9 7.9 %collective-permute-start.3 = (f32[96,512]{1,0:T(8,128)S(1)}, f32[96,512]{1,0:T(8,128)S(1)}, u32[]{:S(2)}, u32[]{:S(2)}) collective-permute-start(f32[96,512]{1,0:T(8,128)S(1)} %collective-permute-done.2.refs_2_), channel_id=1, source_target_pairs={{0,2},{2,4},{4,6},{6,8},{8,10},{10,12},{12,14},{14,16},{16,18},{18... | collective-permute-start | bytes 589832 | tf_op jit(solution)/shard_map/ppermute | solution.py:272
  12.3 7.9 %collective-permute-start.13 = (f32[96,128]{1,0:T(8,128)S(1)}, f32[96,128]{1,0:T(8,128)S(1)}, u32[]{:S(2)}, u32[]{:S(2)}) collective-permute-start(f32[96,128]{1,0:T(8,128)S(1)} %squeeze.65), channel_id=1, source_target_pairs={{0,2},{1,3},{2,0},{3,1},{4,6},{5,7},{6,4},{7,5},{8,10},{9,11},{10,... | collective-permute-start | bytes 147464 | tf_op jit(solution)/shard_map/ppermute | solution.py:226
  12.5 7.8 %collective-permute-start.14 = (f32[96,128]{1,0:T(8,128)S(1)}, f32[96,128]{1,0:T(8,128)S(1)}, u32[]{:S(2)}, u32[]{:S(2)}) collective-permute-start(f32[96,128]{1,0:T(8,128)S(1)} %squeeze.66), channel_id=1, source_target_pairs={{0,6},{1,7},{2,0},{3,1},{4,2},{5,3},{6,4},{7,5},{8,14},{9,15},{10,... | collective-permute-start | bytes 147464 | tf_op jit(solution)/shard_map/ppermute | solution.py:226
  13.9 7.0 %collective-permute-start.15 = (f32[96,128]{1,0:T(8,128)S(1)}, f32[96,128]{1,0:T(8,128)S(1)}, u32[]{:S(2)}, u32[]{:S(2)}) collective-permute-start(f32[96,128]{1,0:T(8,128)S(1)} %squeeze.67), channel_id=1, source_target_pairs={{0,10},{1,11},{2,0},{3,1},{4,14},{5,15},{6,4},{7,5},{8,2},{9,3},{1... | collective-permute-start | bytes 147464 | tf_op jit(solution)/shard_map/ppermute | solution.py:226
  14.0 8.3 %collective-permute-start.16 = (f32[96,128]{1,0:T(8,128)S(1)}, f32[96,128]{1,0:T(8,128)S(1)}, u32[]{:S(2)}, u32[]{:S(2)}) collective-permute-start(f32[96,128]{1,0:T(8,128)S(1)} %squeeze.68), channel_id=1, source_target_pairs={{0,14},{1,15},{2,0},{3,1},{4,10},{5,11},{6,4},{7,5},{8,6},{9,7},{1... | collective-permute-start | bytes 147464 | tf_op jit(solution)/shard_map/ppermute | solution.py:226
  19.8 2.5 %collective-permute-start.17 = (f32[96,128]{1,0:T(8,128)S(1)}, f32[96,128]{1,0:T(8,128)S(1)}, u32[]{:S(2)}, u32[]{:S(2)}) collective-permute-start(f32[96,128]{1,0:T(8,128)S(1)} %squeeze.69), channel_id=1, source_target_pairs={{0,18},{1,19},{2,0},{3,1},{4,22},{5,23},{6,4},{7,5},{8,26},{9,27},... | collective-permute-start | bytes 147464 | tf_op jit(solution)/shard_map/ppermute | solution.py:226
  20.2 2.4 %collective-permute-start.18 = (f32[96,128]{1,0:T(8,128)S(1)}, f32[96,128]{1,0:T(8,128)S(1)}, u32[]{:S(2)}, u32[]{:S(2)}) collective-permute-start(f32[96,128]{1,0:T(8,128)S(1)} %squeeze.70), channel_id=1, source_target_pairs={{0,22},{1,23},{2,0},{3,1},{4,18},{5,19},{6,4},{7,5},{8,30},{9,31},... | collective-permute-start | bytes 147464 | tf_op jit(solution)/shard_map/ppermute | solution.py:226
  20.3 4.9 %collective-permute-start.19 = (f32[96,128]{1,0:T(8,128)S(1)}, f32[96,128]{1,0:T(8,128)S(1)}, u32[]{:S(2)}, u32[]{:S(2)}) collective-permute-start(f32[96,128]{1,0:T(8,128)S(1)} %squeeze.71), channel_id=1, source_target_pairs={{0,26},{1,27},{2,0},{3,1},{4,30},{5,31},{6,4},{7,5},{8,18},{9,19},... | collective-permute-start | bytes 147464 | tf_op jit(solution)/shard_map/ppermute | solution.py:226
  20.9 5.9 %collective-permute-start.20 = (f32[96,128]{1,0:T(8,128)S(1)}, f32[96,128]{1,0:T(8,128)S(1)}, u32[]{:S(2)}, u32[]{:S(2)}) collective-permute-start(f32[96,128]{1,0:T(8,128)S(1)} %squeeze.72), channel_id=1, source_target_pairs={{0,30},{1,31},{2,0},{3,1},{4,26},{5,27},{6,4},{7,5},{8,22},{9,23},... | collective-permute-start | bytes 147464 | tf_op jit(solution)/shard_map/ppermute | solution.py:226
  22.2 6.1 %collective-permute-start.4 = (f32[96,128]{1,0:T(8,128)S(1)}, f32[96,128]{1,0:T(8,128)S(1)}, u32[]{:S(2)}, u32[]{:S(2)}) collective-permute-start(f32[96,128]{1,0:T(8,128)S(1)} %squeeze.57), channel_id=1, source_target_pairs={{0,2},{1,3},{2,0},{3,1},{4,6},{5,7},{6,4},{7,5},{8,10},{9,11},{10,... | collective-permute-start | bytes 147464 | tf_op jit(solution)/shard_map/ppermute | solution.py:226
  22.3 7.0 %collective-permute-start.5 = (f32[96,128]{1,0:T(8,128)S(1)}, f32[96,128]{1,0:T(8,128)S(1)}, u32[]{:S(2)}, u32[]{:S(2)}) collective-permute-start(f32[96,128]{1,0:T(8,128)S(1)} %squeeze.58), channel_id=1, source_target_pairs={{0,6},{1,7},{2,0},{3,1},{4,2},{5,3},{6,4},{7,5},{8,14},{9,15},{10,... | collective-permute-start | bytes 147464 | tf_op jit(solution)/shard_map/ppermute | solution.py:226
  22.6 7.8 %collective-permute-start.6 = (f32[96,128]{1,0:T(8,128)S(1)}, f32[96,128]{1,0:T(8,128)S(1)}, u32[]{:S(2)}, u32[]{:S(2)}) collective-permute-start(f32[96,128]{1,0:T(8,128)S(1)} %squeeze.59), channel_id=1, source_target_pairs={{0,10},{1,11},{2,0},{3,1},{4,14},{5,15},{6,4},{7,5},{8,2},{9,3},{1... | collective-permute-start | bytes 147464 | tf_op jit(solution)/shard_map/ppermute | solution.py:226
  25.2 6.2 %collective-permute-start.7 = (f32[96,128]{1,0:T(8,128)S(1)}, f32[96,128]{1,0:T(8,128)S(1)}, u32[]{:S(2)}, u32[]{:S(2)}) collective-permute-start(f32[96,128]{1,0:T(8,128)S(1)} %squeeze.60), channel_id=1, source_target_pairs={{0,14},{1,15},{2,0},{3,1},{4,10},{5,11},{6,4},{7,5},{8,6},{9,7},{1... | collective-permute-start | bytes 147464 | tf_op jit(solution)/shard_map/ppermute | solution.py:226
  26.8 4.6 %collective-permute-start.8 = (f32[96,128]{1,0:T(8,128)S(1)}, f32[96,128]{1,0:T(8,128)S(1)}, u32[]{:S(2)}, u32[]{:S(2)}) collective-permute-start(f32[96,128]{1,0:T(8,128)S(1)} %squeeze.61), channel_id=1, source_target_pairs={{0,18},{1,19},{2,0},{3,1},{4,22},{5,23},{6,4},{7,5},{8,26},{9,27},... | collective-permute-start | bytes 147464 | tf_op jit(solution)/shard_map/ppermute | solution.py:226
  28.3 3.1 %collective-permute-start.9 = (f32[96,128]{1,0:T(8,128)S(1)}, f32[96,128]{1,0:T(8,128)S(1)}, u32[]{:S(2)}, u32[]{:S(2)}) collective-permute-start(f32[96,128]{1,0:T(8,128)S(1)} %squeeze.62), channel_id=1, source_target_pairs={{0,22},{1,23},{2,0},{3,1},{4,18},{5,19},{6,4},{7,5},{8,30},{9,31},... | collective-permute-start | bytes 147464 | tf_op jit(solution)/shard_map/ppermute | solution.py:226
  29.2 2.9 %collective-permute-start.10 = (f32[96,128]{1,0:T(8,128)S(1)}, f32[96,128]{1,0:T(8,128)S(1)}, u32[]{:S(2)}, u32[]{:S(2)}) collective-permute-start(f32[96,128]{1,0:T(8,128)S(1)} %squeeze.63), channel_id=1, source_target_pairs={{0,26},{1,27},{2,0},{3,1},{4,30},{5,31},{6,4},{7,5},{8,18},{9,19},... | collective-permute-start | bytes 147464 | tf_op jit(solution)/shard_map/ppermute | solution.py:226
  30.4 2.7 %collective-permute-start.11 = (f32[96,128]{1,0:T(8,128)S(1)}, f32[96,128]{1,0:T(8,128)S(1)}, u32[]{:S(2)}, u32[]{:S(2)}) collective-permute-start(f32[96,128]{1,0:T(8,128)S(1)} %squeeze.64), channel_id=1, source_target_pairs={{0,30},{1,31},{2,0},{3,1},{4,26},{5,27},{6,4},{7,5},{8,22},{9,23},... | collective-permute-start | bytes 147464 | tf_op jit(solution)/shard_map/ppermute | solution.py:226
  34.3 18.7 %collective-permute-start.21 = (f32[768,256]{1,0:T(8,128)S(1)}, f32[768,256]{1,0:T(8,128)S(1)}, u32[]{:S(2)}, u32[]{:S(2)}) collective-permute-start(f32[768,256]{1,0:T(8,128)S(1)} %get-tuple-element.28), channel_id=1, source_target_pairs={{0,2},{1,3},{2,0},{3,1},{4,6},{5,7},{6,4},{7,5},{8,10},{9,11},{10,... | collective-permute-start | bytes 2359304 | tf_op jit(solution)/shard_map/ppermute | solution.py:226
  37.2 4.9 %collective-permute-start.22 = (f32[192,128]{1,0:T(8,128)S(1)}, f32[192,128]{1,0:T(8,128)S(1)}, u32[]{:S(2)}, u32[]{:S(2)}) collective-permute-start(f32[192,128]{1,0:T(8,128)S(1)} %get-tuple-element.31), channel_id=1, source_target_pairs={{0,2},{1,3},{2,5},{3,4},{4,6},{5,7},{6,1},{7,0},{8,10},{9,11},{10,... | collective-permute-start | bytes 294920 | tf_op jit(solution)/shard_map/ppermute | solution.py:226
  37.3 6.8 %collective-permute-start.23 = (f32[192,128]{1,0:T(8,128)S(1)}, f32[192,128]{1,0:T(8,128)S(1)}, u32[]{:S(2)}, u32[]{:S(2)}) collective-permute-start(f32[192,128]{1,0:T(8,128)S(1)} %get-tuple-element.32), channel_id=1, source_target_pairs={{0,2},{1,3},{2,4},{3,5},{4,6},{5,7},{6,0},{7,1},{8,10},{9,11},{10,... | collective-permute-start | bytes 294920 | tf_op jit(solution)/shard_map/ppermute | solution.py:226
  39.6 4.5 %collective-permute-start.24 = (f32[192,128]{1,0:T(8,128)S(1)}, f32[192,128]{1,0:T(8,128)S(1)}, u32[]{:S(2)}, u32[]{:S(2)}) collective-permute-start(f32[192,128]{1,0:T(8,128)S(1)} %get-tuple-element.33), channel_id=1, source_target_pairs={{0,2},{1,3},{2,1},{3,0},{4,6},{5,7},{6,5},{7,4},{8,10},{9,11},{10,... | collective-permute-start | bytes 294920 | tf_op jit(solution)/shard_map/ppermute | solution.py:226
  39.6 4.5 %collective-permute-start.25 = (f32[192,128]{1,0:T(8,128)S(1)}, f32[192,128]{1,0:T(8,128)S(1)}, u32[]{:S(2)}, u32[]{:S(2)}) collective-permute-start(f32[192,128]{1,0:T(8,128)S(1)} %get-tuple-element.34), channel_id=1, source_target_pairs={{0,2},{1,3},{2,0},{3,1},{4,6},{5,7},{6,4},{7,5},{8,10},{9,11},{10,... | collective-permute-start | bytes 294920 | tf_op jit(solution)/shard_map/ppermute | solution.py:226
  44.1 2.5 %collective-permute-start.29 = (f32[192,128]{1,0:T(8,128)S(1)}, f32[192,128]{1,0:T(8,128)S(1)}, u32[]{:S(2)}, u32[]{:S(2)}) collective-permute-start(f32[192,128]{1,0:T(8,128)S(1)} %add_add_fusion.1), channel_id=1, source_target_pairs={{0,2},{1,3},{2,0},{3,1},{4,6},{5,7},{6,4},{7,5},{8,10},{9,11},{10,... | collective-permute-start | bytes 294920 | tf_op jit(solution)/shard_map/ppermute | solution.py:226
  44.1 3.0 %collective-permute-start.28 = (f32[192,128]{1,0:T(8,128)S(1)}, f32[192,128]{1,0:T(8,128)S(1)}, u32[]{:S(2)}, u32[]{:S(2)}) collective-permute-start(f32[192,128]{1,0:T(8,128)S(1)} %add_add_fusion.1), channel_id=1, source_target_pairs={{0,10},{1,11},{2,0},{3,1},{4,14},{5,15},{6,4},{7,5},{8,2},{9,3},{1... | collective-permute-start | bytes 294920 | tf_op jit(solution)/shard_map/ppermute | solution.py:226
  44.9 3.2 %collective-permute-start.27 = (f32[192,128]{1,0:T(8,128)S(1)}, f32[192,128]{1,0:T(8,128)S(1)}, u32[]{:S(2)}, u32[]{:S(2)}) collective-permute-start(f32[192,128]{1,0:T(8,128)S(1)} %add_add_fusion.1), channel_id=1, source_target_pairs={{0,18},{1,19},{2,0},{3,1},{4,22},{5,23},{6,4},{7,5},{8,26},{9,27},... | collective-permute-start | bytes 294920 | tf_op jit(solution)/shard_map/ppermute | solution.py:226
  44.9 4.3 %collective-permute-start.26 = (f32[192,128]{1,0:T(8,128)S(1)}, f32[192,128]{1,0:T(8,128)S(1)}, u32[]{:S(2)}, u32[]{:S(2)}) collective-permute-start(f32[192,128]{1,0:T(8,128)S(1)} %add_add_fusion.1), channel_id=1, source_target_pairs={{0,26},{1,27},{2,0},{3,1},{4,30},{5,31},{6,4},{7,5},{8,18},{9,19},... | collective-permute-start | bytes 294920 | tf_op jit(solution)/shard_map/ppermute | solution.py:226
  49.2 5.9 %collective-permute-start.33 = (f32[192,128]{1,0:T(8,128)S(1)}, f32[192,128]{1,0:T(8,128)S(1)}, u32[]{:S(2)}, u32[]{:S(2)}) collective-permute-start(f32[192,128]{1,0:T(8,128)S(1)} %add_add_fusion), channel_id=1, source_target_pairs={{0,2},{1,3},{2,5},{3,4},{4,6},{5,7},{6,1},{7,0},{8,10},{9,11},{10,... | collective-permute-start | bytes 294920 | tf_op jit(solution)/shard_map/ppermute | solution.py:226
  51.8 4.0 %collective-permute-start.32 = (f32[192,128]{1,0:T(8,128)S(1)}, f32[192,128]{1,0:T(8,128)S(1)}, u32[]{:S(2)}, u32[]{:S(2)}) collective-permute-start(f32[192,128]{1,0:T(8,128)S(1)} %add_add_fusion), channel_id=1, source_target_pairs={{0,2},{1,3},{2,4},{3,5},{4,6},{5,7},{6,0},{7,1},{8,10},{9,11},{10,... | collective-permute-start | bytes 294920 | tf_op jit(solution)/shard_map/ppermute | solution.py:226
  51.9 4.3 %collective-permute-start.31 = (f32[192,128]{1,0:T(8,128)S(1)}, f32[192,128]{1,0:T(8,128)S(1)}, u32[]{:S(2)}, u32[]{:S(2)}) collective-permute-start(f32[192,128]{1,0:T(8,128)S(1)} %add_add_fusion), channel_id=1, source_target_pairs={{0,2},{1,3},{2,1},{3,0},{4,6},{5,7},{6,5},{7,4},{8,10},{9,11},{10,... | collective-permute-start | bytes 294920 | tf_op jit(solution)/shard_map/ppermute | solution.py:226
  53.0 3.2 %collective-permute-start.30 = (f32[192,128]{1,0:T(8,128)S(1)}, f32[192,128]{1,0:T(8,128)S(1)}, u32[]{:S(2)}, u32[]{:S(2)}) collective-permute-start(f32[192,128]{1,0:T(8,128)S(1)} %add_add_fusion), channel_id=1, source_target_pairs={{0,2},{1,3},{2,0},{3,1},{4,6},{5,7},{6,4},{7,5},{8,10},{9,11},{10,... | collective-permute-start | bytes 294920 | tf_op jit(solution)/shard_map/ppermute | solution.py:226
  61.6 1.3 %collective-permute-start.34 = (f32[128,128]{1,0:T(8,128)S(1)}, f32[128,128]{1,0:T(8,128)S(1)}, u32[]{:S(2)}, u32[]{:S(2)}) collective-permute-start(f32[128,128]{1,0:T(8,128)S(1)} %get-tuple-element.36), channel_id=1, source_target_pairs={{0,2},{2,0},{4,6},{6,4},{8,10},{10,8},{12,14},{14,12},{16,18},{18,... | collective-permute-start | bytes 196616 | tf_op jit(solution)/shard_map/ppermute | solution.py:344

commit v13 on v11

--- a/solution.py
+++ b/solution.py
@@ -330,6 +330,8 @@
         compiler_params=BIG,
         name="image",
     )(*parts, *basis_parts)
+    total = sum(crossed(chunks[step], mid, step, 0) for step in range(count - 1, -1, -1))
+    field, total = lax.optimization_barrier((field, total))
     field_part = jax.ShapeDtypeStruct((length, 2 * tile), BF16)
     field_halves = pl.pallas_call(
         split_kernel,
@@ -339,7 +341,6 @@
         compiler_params=BIG,
         name="split",
     )(crossed(field, mid, 0, 0))
-    total = sum(crossed(chunks[step], mid, step, 0) for step in range(count - 1, -1, -1))
     total = sum(crossed(total, distant, step, 1) for step in range(2 ** len(distant) - 1, -1, -1))
     chunks = [crossed(total, mid, step, 0) for step in range(count)]
     first, second = pl.pallas_call(

time: 56.7 us -> 56.2 us (level)
  starting transfers between devices: 24.4 us -> 23.5 us
    ppermute x21, starting transfers between devices: 20.7 us -> 19.8 us  [crossed(): return lax.ppermute(value, ('fib', 'pln'), pairs)]
where the time goes in v13:
time: 56.2 us; the launch traced here: 56 us
  starting transfers between devices  23.5 us (42%)
  waiting for transfers between devices  20.1 us (36%)
  Pallas kernels  11.4 us (20%)
  other arithmetic  0.68 us (1%)
    ppermute x21, starting transfers between devices, crossed(): return lax.ppermute(value, ('fib', 'pln'), pairs)  19.8 us
    ppermute x21, waiting for transfers between devices, crossed(): return lax.ppermute(value, ('fib', 'pln'), pairs)  9.85 us
    ppermute x1, waiting for transfers between devices, per_device(): back_two = lax.ppermute(swapped, 'fib', forward)  7.2 us
    pallas_call x1, Pallas kernels, per_device(): pl.pallas_call(functools.partial(factor_kernel, mid), out_shape=[jax.Shap...  5.42 us
    pallas_call x1, Pallas kernels, per_device(): pl.pallas_call(functools.partial(interp_kernel, owners), out_shape=[piece...  3.04 us
    ppermute x1, starting transfers between devices, per_device(): back_two = lax.ppermute(swapped, 'fib', forward)  1.6 us
    ppermute x1, starting transfers between devices, per_device(): order_next = lax.ppermute(slot_order[0], 'fib', core_swap)  1.37 us
    ppermute x1, waiting for transfers between devices, per_device(): core_values = first + lax.ppermute(second, 'fib', core_swap)  1.24 us
  transfers between devices with their start and end apart: 26, of which 13 were waited for; matrix products, arithmetic and copies ran while one was open for 0% of the time, Pallas kernels for 2%

profile of v13, /device:TPU:0, one launch (start us, length us, event | category | flops | bytes accessed | tf_op | source)
XLA Modules:
  0.0 56.0 jit_solution(10360915728424772397)
XLA Ops:
  0.0 0.0 copy-start.1
  0.0 3.0 %interp.1 = (f32[96,512]{1,0:T(8,128)S(1)}, f32[96,512]{1,0:T(8,128)S(1)}, f32[192,512]{1,0:T(8,128)S(1)}, f32[96,512]{1,0:T(8,128)S(1)}) custom-call(s32[3,1,16]{2,1,0:T(1,128)} %bitcast.21, f32[288,1000]{1,0:T(8,128)} %bitcast.25, f32[1000,512]{1,0:T(8,128)} %interp_hbm.1), custom_call_target="tpu_custom_call" | custom-call | tf_op jit(solution)/shard_map/interp/pallas_call | solution.py:274
  3.1 0.5 collective-permute-start.1
  3.6 0.1 collective-permute-start.2
  3.6 1.0 %collective-permute-done.1.next_zero_ref = f32[96,512]{1,0:T(8,128)S(1)} collective-permute-done((f32[96,512]{1,0:T(8,128)S(1)}, f32[96,512]{1,0:T(8,128)S(1)}, u32[]{:S(2)}, u32[]{:S(2)}) %collective-permute-start.1) | collective-permute-done | bytes 196640 | tf_op jit(solution)/shard_map/ppermute | solution.py:289
  4.6 1.6 %collective-permute-start.3 = (f32[96,512]{1,0:T(8,128)S(1)}, f32[96,512]{1,0:T(8,128)S(1)}, u32[]{:S(2)}, u32[]{:S(2)}) collective-permute-start(f32[96,512]{1,0:T(8,128)S(1)} %collective-permute-done.1.next_zero_ref), channel_id=1, source_target_pairs={{0,2},{2,4},{4,6},{6,8},{8,10},{10,12},{12,14},{14,16},{16,18},{18... | collective-permute-start | bytes 589832 | tf_op jit(solution)/shard_map/ppermute | solution.py:291
  6.2 0.0 copy-done.2
  6.2 1.4 %collective-permute-start = (s32[1,192]{1,0:T(1,128)S(1)}, s32[1,192]{1,0:T(1,128)S(1)}, u32[]{:S(2)}, u32[]{:S(2)}) collective-permute-start(s32[1,192]{1,0:T(1,128)S(1)} %bitcast.23), channel_id=1, source_target_pairs={{0,2},{2,0},{4,6},{6,4},{8,10},{10,8},{12,14},{14,12},{16,18},{18,... | collective-permute-start | bytes 2312 | tf_op jit(solution)/shard_map/ppermute | solution.py:271
  7.6 0.8 %collective-permute-done.order_next_ref = s32[1,192]{1,0:T(1,128)S(1)} collective-permute-done((s32[1,192]{1,0:T(1,128)S(1)}, s32[1,192]{1,0:T(1,128)S(1)}, u32[]{:S(2)}, u32[]{:S(2)}) %collective-permute-start) | collective-permute-done | bytes 800 | tf_op jit(solution)/shard_map/ppermute | solution.py:271
  8.4 0.0 copy-done.1
  8.4 0.0 copy-done
  8.4 1.1 %pick.1 = (bf16[384,288]{1,0:T(8,128)(2,1)S(1)}, bf16[128,768]{1,0:T(8,128)(2,1)S(1)}, bf16[128,768]{1,0:T(8,128)(2,1)S(1)}) custom-call(s32[3,1,16]{2,1,0:T(1,128)S(1)} %bitcast.22, s32[1,192]{1,0:T(1,128)S(1)} %bitcast.24, s32[1,192]{1,0:T(1,128)S(1)} %collective-permute-done.order_next_ref, f32[768,128]{1,0:T(8,128)S(1)} %copy-done), custom_call_target="tpu_custom_call" | custom-call | tf_op jit(solution)/shard_map/pick/pallas_call | solution.py:293
  9.6 7.2 %collective-permute-done.3.back_two_ref = f32[96,512]{1,0:T(8,128)S(1)} collective-permute-done((f32[96,512]{1,0:T(8,128)S(1)}, f32[96,512]{1,0:T(8,128)S(1)}, u32[]{:S(2)}, u32[]{:S(2)}) %collective-permute-start.3) | collective-permute-done | bytes 196640 | tf_op jit(solution)/shard_map/ppermute | solution.py:291
  16.8 0.0 collective-permute-done.2.back_ref
  16.8 0.6 %order.1 = (f32[192,512]{1,0:T(8,128)S(1)}, f32[192,512]{1,0:T(8,128)S(1)}) custom-call(bf16[384,288]{1,0:T(8,128)(2,1)S(1)} %get-tuple-element.25.pick_ref, f32[96,512]{1,0:T(8,128)S(1)} %get-tuple-element.26.zero_ref, f32[96,512]{1,0:T(8,128)S(1)} %get-tuple-element.27.one_ref, f32[96,512]{1,0:T(8,128)S(1)} %collective-permute-done.1.next_zero_ref, ...), custom_call_target="tpu_custom_call" | custom-call | tf_op jit(solution)/shard_map/order/pallas_call | solution.py:301
  17.5 0.1 slice_bitcast_fusion
  17.6 0.1 collective-permute-start.11
  17.6 1.8 %collective-permute-start.10 = (f32[192,128]{1,0:T(8,128)S(1)}, f32[192,128]{1,0:T(8,128)S(1)}, u32[]{:S(2)}, u32[]{:S(2)}) collective-permute-start(f32[192,128]{1,0:T(8,128)S(1)} %get-tuple-element.46), channel_id=1, source_target_pairs={{0,26},{1,27},{2,0},{3,1},{4,30},{5,31},{6,4},{7,5},{8,18},{9,19},... | collective-permute-start | bytes 294920 | tf_op jit(solution)/shard_map/ppermute | solution.py:246
  19.4 0.0 collective-permute-start.9
  19.4 0.0 collective-permute-start.8
  19.4 1.6 %collective-permute-start.7 = (f32[192,128]{1,0:T(8,128)S(1)}, f32[192,128]{1,0:T(8,128)S(1)}, u32[]{:S(2)}, u32[]{:S(2)}) collective-permute-start(f32[192,128]{1,0:T(8,128)S(1)} %get-tuple-element.49), channel_id=1, source_target_pairs={{0,14},{1,15},{2,0},{3,1},{4,10},{5,11},{6,4},{7,5},{8,6},{9,7},{1... | collective-permute-start | bytes 294920 | tf_op jit(solution)/shard_map/ppermute | solution.py:246
  21.1 0.0 collective-permute-done.11.refs_7_
  21.1 1.3 %collective-permute-start.6 = (f32[192,128]{1,0:T(8,128)S(1)}, f32[192,128]{1,0:T(8,128)S(1)}, u32[]{:S(2)}, u32[]{:S(2)}) collective-permute-start(f32[192,128]{1,0:T(8,128)S(1)} %get-tuple-element.50), channel_id=1, source_target_pairs={{0,10},{1,11},{2,0},{3,1},{4,14},{5,15},{6,4},{7,5},{8,2},{9,3},{1... | collective-permute-start | bytes 294920 | tf_op jit(solution)/shard_map/ppermute | solution.py:246
  22.4 0.0 collective-permute-done.10.refs_6_
  22.4 0.7 %collective-permute-start.5 = (f32[192,128]{1,0:T(8,128)S(1)}, f32[192,128]{1,0:T(8,128)S(1)}, u32[]{:S(2)}, u32[]{:S(2)}) collective-permute-start(f32[192,128]{1,0:T(8,128)S(1)} %get-tuple-element.51), channel_id=1, source_target_pairs={{0,6},{1,7},{2,0},{3,1},{4,2},{5,3},{6,4},{7,5},{8,14},{9,15},{10,... | collective-permute-start | bytes 294920 | tf_op jit(solution)/shard_map/ppermute | solution.py:246
  23.1 0.0 collective-permute-done.9.refs_5_
  23.1 4.1 %collective-permute-start.4 = (f32[192,128]{1,0:T(8,128)S(1)}, f32[192,128]{1,0:T(8,128)S(1)}, u32[]{:S(2)}, u32[]{:S(2)}) collective-permute-start(f32[192,128]{1,0:T(8,128)S(1)} %get-tuple-element.52), channel_id=1, source_target_pairs={{0,2},{1,3},{2,0},{3,1},{4,6},{5,7},{6,4},{7,5},{8,10},{9,11},{10,... | collective-permute-start | bytes 294920 | tf_op jit(solution)/shard_map/ppermute | solution.py:246
  27.2 0.0 collective-permute-done.8.refs_4_
  27.2 0.0 collective-permute-done.7.refs_3_
  27.2 0.0 collective-permute-done.6.refs_2_
  27.2 0.0 collective-permute-done.5.refs_1_
  27.2 0.9 %collective-permute-done.4.refs_0_ = f32[192,128]{1,0:T(8,128)S(1)} collective-permute-done((f32[192,128]{1,0:T(8,128)S(1)}, f32[192,128]{1,0:T(8,128)S(1)}, u32[]{:S(2)}, u32[]{:S(2)}) %collective-permute-start.4) | collective-permute-done | bytes 98336 | tf_op jit(solution)/shard_map/ppermute | solution.py:246
  28.1 1.1 %image.1 = (f32[192,128]{1,0:T(8,128)S(1)}, f32[192,128]{1,0:T(8,128)S(1)}, f32[192,128]{1,0:T(8,128)S(1)}, f32[192,128]{1,0:T(8,128)S(1)}, f32[768,256]{1,0:T(8,128)S(1)}) custom-call(f32[192,128]{1,0:T(8,128)S(1)} %collective-permute-done.4.refs_0_, f32[192,128]{1,0:T(8,128)S(1)} %collective-permute-done.5.refs_1_, ...), custom_call_target="tpu_custom_call" | custom-call | tf_op jit(solution)/shard_map/image/pallas_call | solution.py:324
  29.2 0.4 collective-permute-start.12
  29.7 2.1 %collective-permute-start.13 = (f32[192,128]{1,0:T(8,128)S(1)}, f32[192,128]{1,0:T(8,128)S(1)}, u32[]{:S(2)}, u32[]{:S(2)}) collective-permute-start(f32[192,128]{1,0:T(8,128)S(1)} %get-tuple-element.36), channel_id=1, source_target_pairs={{0,2},{1,3},{2,4},{3,5},{4,6},{5,7},{6,0},{7,1},{8,10},{9,11},{10,... | collective-permute-start | bytes 294920 | tf_op jit(solution)/shard_map/ppermute | solution.py:246
  31.7 0.0 collective-permute-start.14
  31.7 0.6 %collective-permute-start.15 = (f32[192,128]{1,0:T(8,128)S(1)}, f32[192,128]{1,0:T(8,128)S(1)}, u32[]{:S(2)}, u32[]{:S(2)}) collective-permute-start(f32[192,128]{1,0:T(8,128)S(1)} %get-tuple-element.38), channel_id=1, source_target_pairs={{0,2},{1,3},{2,0},{3,1},{4,6},{5,7},{6,4},{7,5},{8,10},{9,11},{10,... | collective-permute-start | bytes 294920 | tf_op jit(solution)/shard_map/ppermute | solution.py:246
  32.3 1.9 %collective-permute-done.12 = f32[192,128]{1,0:T(8,128)S(1)} collective-permute-done((f32[192,128]{1,0:T(8,128)S(1)}, f32[192,128]{1,0:T(8,128)S(1)}, u32[]{:S(2)}, u32[]{:S(2)}) %collective-permute-start.12) | collective-permute-done | bytes 98336 | tf_op jit(solution)/shard_map/ppermute | solution.py:246
  34.2 1.1 %collective-permute-done.13 = f32[192,128]{1,0:T(8,128)S(1)} collective-permute-done((f32[192,128]{1,0:T(8,128)S(1)}, f32[192,128]{1,0:T(8,128)S(1)}, u32[]{:S(2)}, u32[]{:S(2)}) %collective-permute-start.13) | collective-permute-done | bytes 98336 | tf_op jit(solution)/shard_map/ppermute | solution.py:246
  35.4 0.4 collective-permute-done.14
  35.8 0.0 collective-permute-done.15
  35.8 0.1 collective-permute-start.16
  35.9 0.5 collective-permute-start.20
  36.4 0.2 collective-permute-start.19
  36.6 1.4 %collective-permute-start.18 = (f32[192,128]{1,0:T(8,128)S(1)}, f32[192,128]{1,0:T(8,128)S(1)}, u32[]{:S(2)}, u32[]{:S(2)}) collective-permute-start(f32[192,128]{1,0:T(8,128)S(1)} %add_add_fusion.1), channel_id=1, source_target_pairs={{0,18},{1,19},{2,0},{3,1},{4,22},{5,23},{6,4},{7,5},{8,26},{9,27},... | collective-permute-start | bytes 294920 | tf_op jit(solution)/shard_map/ppermute | solution.py:246
  38.0 1.1 %collective-permute-start.17 = (f32[192,128]{1,0:T(8,128)S(1)}, f32[192,128]{1,0:T(8,128)S(1)}, u32[]{:S(2)}, u32[]{:S(2)}) collective-permute-start(f32[192,128]{1,0:T(8,128)S(1)} %add_add_fusion.1), channel_id=1, source_target_pairs={{0,26},{1,27},{2,0},{3,1},{4,30},{5,31},{6,4},{7,5},{8,18},{9,19},... | collective-permute-start | bytes 294920 | tf_op jit(solution)/shard_map/ppermute | solution.py:246
  39.1 0.0 collective-permute-done.20
  39.1 0.0 collective-permute-done.19
  39.1 1.1 %collective-permute-done.18 = f32[192,128]{1,0:T(8,128)S(1)} collective-permute-done((f32[192,128]{1,0:T(8,128)S(1)}, f32[192,128]{1,0:T(8,128)S(1)}, u32[]{:S(2)}, u32[]{:S(2)}) %collective-permute-start.18) | collective-permute-done | bytes 98336 | tf_op jit(solution)/shard_map/ppermute | solution.py:246
  40.2 1.1 %collective-permute-done.17 = f32[192,128]{1,0:T(8,128)S(1)} collective-permute-done((f32[192,128]{1,0:T(8,128)S(1)}, f32[192,128]{1,0:T(8,128)S(1)}, u32[]{:S(2)}, u32[]{:S(2)}) %collective-permute-start.17) | collective-permute-done | bytes 98336 | tf_op jit(solution)/shard_map/ppermute | solution.py:246
  41.3 2.7 %collective-permute-start.24 = (f32[192,128]{1,0:T(8,128)S(1)}, f32[192,128]{1,0:T(8,128)S(1)}, u32[]{:S(2)}, u32[]{:S(2)}) collective-permute-start(f32[192,128]{1,0:T(8,128)S(1)} %add_add_fusion), channel_id=1, source_target_pairs={{0,2},{1,3},{2,5},{3,4},{4,6},{5,7},{6,1},{7,0},{8,10},{9,11},{10,... | collective-permute-start | bytes 294920 | tf_op jit(solution)/shard_map/ppermute | solution.py:246
  44.0 0.1 collective-permute-start.23
  44.1 1.0 %collective-permute-start.22 = (f32[192,128]{1,0:T(8,128)S(1)}, f32[192,128]{1,0:T(8,128)S(1)}, u32[]{:S(2)}, u32[]{:S(2)}) collective-permute-start(f32[192,128]{1,0:T(8,128)S(1)} %add_add_fusion), channel_id=1, source_target_pairs={{0,2},{1,3},{2,1},{3,0},{4,6},{5,7},{6,5},{7,4},{8,10},{9,11},{10,... | collective-permute-start | bytes 294920 | tf_op jit(solution)/shard_map/ppermute | solution.py:246
  45.1 0.1 collective-permute-start.21
  45.2 0.0 collective-permute-done.16.value_ref
  45.2 0.1 split.1
  45.4 2.2 %collective-permute-done.24.refs_3_ = f32[192,128]{1,0:T(8,128)S(1)} collective-permute-done((f32[192,128]{1,0:T(8,128)S(1)}, f32[192,128]{1,0:T(8,128)S(1)}, u32[]{:S(2)}, u32[]{:S(2)}) %collective-permute-start.24) | collective-permute-done | bytes 98336 | tf_op jit(solution)/shard_map/ppermute | solution.py:246
  47.6 0.4 collective-permute-done.23.refs_2_
  48.1 0.6 %collective-permute-done.22.refs_1_ = f32[192,128]{1,0:T(8,128)S(1)} collective-permute-done((f32[192,128]{1,0:T(8,128)S(1)}, f32[192,128]{1,0:T(8,128)S(1)}, u32[]{:S(2)}, u32[]{:S(2)}) %collective-permute-start.22) | collective-permute-done | bytes 98336 | tf_op jit(solution)/shard_map/ppermute | solution.py:246
  48.6 0.0 collective-permute-done.21.refs_0_
  48.6 5.4 %factor.1 = (f32[128,128]{1,0:T(8,128)S(1)}, f32[128,128]{1,0:T(8,128)S(1)}) custom-call(bf16[768,256]{1,0:T(8,128)(2,1)S(1)} %get-tuple-element.40.high_ref, bf16[768,256]{1,0:T(8,128)(2,1)S(1)} %get-tuple-element.41.low_ref, f32[192,128]{1,0:T(8,128)S(1)} %collective-permute-done.21.refs_0_, f32[192,128]{1,0:T(8,128)S(1)} %collective-permute-done.22.refs_1_, ...), custom_call_target="tpu_custom_call" | custom-call | tf_op jit(solution)/shard_map/factor/pallas_call | solution.py:346
  54.1 0.1 collective-permute-start.25
  54.1 1.2 %collective-permute-done.25 = f32[128,128]{1,0:T(8,128)S(1)} collective-permute-done((f32[128,128]{1,0:T(8,128)S(1)}, f32[128,128]{1,0:T(8,128)S(1)}, u32[]{:S(2)}, u32[]{:S(2)}) %collective-permute-start.25) | collective-permute-done | bytes 65568 | tf_op jit(solution)/shard_map/ppermute | solution.py:359
  55.4 0.6 %add_bitcast_fusion = f32[1,1,128,128]{3,2,1,0:T(8,128)} fusion(f32[128,128]{1,0:T(8,128)S(1)} %get-tuple-element.43, f32[128,128]{1,0:T(8,128)S(1)} %collective-permute-done.25), kind=kLoop, calls=%fused_computation.10 | loop fusion | flops 16384 | bytes 196608 | tf_op jit(solution)/shard_map/broadcast_in_dim | solution.py:360
  (8 shorter events, 0.2 us)
Async XLA Ops:
  0.0 8.4 %copy-start.1 = (s32[1,16,3]{1,0,2:T(1,128)S(1)}, s32[1,16,3]{1,0,2:T(1,128)}, u32[]{:S(2)}) copy-start(s32[1,16,3]{1,0,2:T(1,128)} %param.7) | copy-start | bytes 580
  0.0 6.2 %copy-start.2 = (s32[1,1,192]{2,1,0:T(1,128)S(1)}, s32[1,1,192]{2,1,0:T(1,128)}, u32[]{:S(2)}) copy-start(s32[1,1,192]{2,1,0:T(1,128)} %param.8) | copy-start | bytes 2308
  0.0 8.4 %copy-start = (f32[768,128]{1,0:T(8,128)S(1)}, f32[768,128]{1,0:T(8,128)}, u32[]{:S(2)}) copy-start(f32[768,128]{1,0:T(8,128)} %start_ref.1) | copy-start | bytes 1179652
  3.1 1.6 %collective-permute-start.1 = (f32[96,512]{1,0:T(8,128)S(1)}, f32[96,512]{1,0:T(8,128)S(1)}, u32[]{:S(2)}, u32[]{:S(2)}) collective-permute-start(f32[96,512]{1,0:T(8,128)S(1)} %get-tuple-element.28), channel_id=1, source_target_pairs={{0,2},{2,0},{4,6},{6,4},{8,10},{10,8},{12,14},{14,12},{16,18},{18,... | collective-permute-start | bytes 589832 | tf_op jit(solution)/shard_map/ppermute | solution.py:289
  3.6 13.2 %collective-permute-start.2 = (f32[192,512]{1,0:T(8,128)S(1)}, f32[192,512]{1,0:T(8,128)S(1)}, u32[]{:S(2)}, u32[]{:S(2)}) collective-permute-start(f32[192,512]{1,0:T(8,128)S(1)} %get-tuple-element.29), channel_id=1, source_target_pairs={{0,2},{2,4},{4,6},{6,8},{8,10},{10,12},{12,14},{14,16},{16,18},{18... | collective-permute-start | bytes 1179656 | tf_op jit(solution)/shard_map/ppermute | solution.py:290
  4.6 12.1 %collective-permute-start.3 = (f32[96,512]{1,0:T(8,128)S(1)}, f32[96,512]{1,0:T(8,128)S(1)}, u32[]{:S(2)}, u32[]{:S(2)}) collective-permute-start(f32[96,512]{1,0:T(8,128)S(1)} %collective-permute-done.1.next_zero_ref), channel_id=1, source_target_pairs={{0,2},{2,4},{4,6},{6,8},{8,10},{10,12},{12,14},{14,16},{16,18},{18... | collective-permute-start | bytes 589832 | tf_op jit(solution)/shard_map/ppermute | solution.py:291
  6.2 2.2 %collective-permute-start = (s32[1,192]{1,0:T(1,128)S(1)}, s32[1,192]{1,0:T(1,128)S(1)}, u32[]{:S(2)}, u32[]{:S(2)}) collective-permute-start(s32[1,192]{1,0:T(1,128)S(1)} %bitcast.23), channel_id=1, source_target_pairs={{0,2},{2,0},{4,6},{6,4},{8,10},{10,8},{12,14},{14,12},{16,18},{18,... | collective-permute-start | bytes 2312 | tf_op jit(solution)/shard_map/ppermute | solution.py:271
  17.6 3.5 %collective-permute-start.11 = (f32[192,128]{1,0:T(8,128)S(1)}, f32[192,128]{1,0:T(8,128)S(1)}, u32[]{:S(2)}, u32[]{:S(2)}) collective-permute-start(f32[192,128]{1,0:T(8,128)S(1)} %get-tuple-element.45), channel_id=1, source_target_pairs={{0,30},{1,31},{2,0},{3,1},{4,26},{5,27},{6,4},{7,5},{8,22},{9,23},... | collective-permute-start | bytes 294920 | tf_op jit(solution)/shard_map/ppermute | solution.py:246
  17.6 4.7 %collective-permute-start.10 = (f32[192,128]{1,0:T(8,128)S(1)}, f32[192,128]{1,0:T(8,128)S(1)}, u32[]{:S(2)}, u32[]{:S(2)}) collective-permute-start(f32[192,128]{1,0:T(8,128)S(1)} %get-tuple-element.46), channel_id=1, source_target_pairs={{0,26},{1,27},{2,0},{3,1},{4,30},{5,31},{6,4},{7,5},{8,18},{9,19},... | collective-permute-start | bytes 294920 | tf_op jit(solution)/shard_map/ppermute | solution.py:246
  19.4 3.7 %collective-permute-start.9 = (f32[192,128]{1,0:T(8,128)S(1)}, f32[192,128]{1,0:T(8,128)S(1)}, u32[]{:S(2)}, u32[]{:S(2)}) collective-permute-start(f32[192,128]{1,0:T(8,128)S(1)} %get-tuple-element.47), channel_id=1, source_target_pairs={{0,22},{1,23},{2,0},{3,1},{4,18},{5,19},{6,4},{7,5},{8,30},{9,31},... | collective-permute-start | bytes 294920 | tf_op jit(solution)/shard_map/ppermute | solution.py:246
  19.4 7.7 %collective-permute-start.8 = (f32[192,128]{1,0:T(8,128)S(1)}, f32[192,128]{1,0:T(8,128)S(1)}, u32[]{:S(2)}, u32[]{:S(2)}) collective-permute-start(f32[192,128]{1,0:T(8,128)S(1)} %get-tuple-element.48), channel_id=1, source_target_pairs={{0,18},{1,19},{2,0},{3,1},{4,22},{5,23},{6,4},{7,5},{8,26},{9,27},... | collective-permute-start | bytes 294920 | tf_op jit(solution)/shard_map/ppermute | solution.py:246
  19.4 7.7 %collective-permute-start.7 = (f32[192,128]{1,0:T(8,128)S(1)}, f32[192,128]{1,0:T(8,128)S(1)}, u32[]{:S(2)}, u32[]{:S(2)}) collective-permute-start(f32[192,128]{1,0:T(8,128)S(1)} %get-tuple-element.49), channel_id=1, source_target_pairs={{0,14},{1,15},{2,0},{3,1},{4,10},{5,11},{6,4},{7,5},{8,6},{9,7},{1... | collective-permute-start | bytes 294920 | tf_op jit(solution)/shard_map/ppermute | solution.py:246
  21.1 6.1 %collective-permute-start.6 = (f32[192,128]{1,0:T(8,128)S(1)}, f32[192,128]{1,0:T(8,128)S(1)}, u32[]{:S(2)}, u32[]{:S(2)}) collective-permute-start(f32[192,128]{1,0:T(8,128)S(1)} %get-tuple-element.50), channel_id=1, source_target_pairs={{0,10},{1,11},{2,0},{3,1},{4,14},{5,15},{6,4},{7,5},{8,2},{9,3},{1... | collective-permute-start | bytes 294920 | tf_op jit(solution)/shard_map/ppermute | solution.py:246
  22.4 4.8 %collective-permute-start.5 = (f32[192,128]{1,0:T(8,128)S(1)}, f32[192,128]{1,0:T(8,128)S(1)}, u32[]{:S(2)}, u32[]{:S(2)}) collective-permute-start(f32[192,128]{1,0:T(8,128)S(1)} %get-tuple-element.51), channel_id=1, source_target_pairs={{0,6},{1,7},{2,0},{3,1},{4,2},{5,3},{6,4},{7,5},{8,14},{9,15},{10,... | collective-permute-start | bytes 294920 | tf_op jit(solution)/shard_map/ppermute | solution.py:246
  23.1 5.0 %collective-permute-start.4 = (f32[192,128]{1,0:T(8,128)S(1)}, f32[192,128]{1,0:T(8,128)S(1)}, u32[]{:S(2)}, u32[]{:S(2)}) collective-permute-start(f32[192,128]{1,0:T(8,128)S(1)} %get-tuple-element.52), channel_id=1, source_target_pairs={{0,2},{1,3},{2,0},{3,1},{4,6},{5,7},{6,4},{7,5},{8,10},{9,11},{10,... | collective-permute-start | bytes 294920 | tf_op jit(solution)/shard_map/ppermute | solution.py:246
  29.2 5.0 %collective-permute-start.12 = (f32[192,128]{1,0:T(8,128)S(1)}, f32[192,128]{1,0:T(8,128)S(1)}, u32[]{:S(2)}, u32[]{:S(2)}) collective-permute-start(f32[192,128]{1,0:T(8,128)S(1)} %get-tuple-element.35), channel_id=1, source_target_pairs={{0,2},{1,3},{2,5},{3,4},{4,6},{5,7},{6,1},{7,0},{8,10},{9,11},{10,... | collective-permute-start | bytes 294920 | tf_op jit(solution)/shard_map/ppermute | solution.py:246
  29.7 5.7 %collective-permute-start.13 = (f32[192,128]{1,0:T(8,128)S(1)}, f32[192,128]{1,0:T(8,128)S(1)}, u32[]{:S(2)}, u32[]{:S(2)}) collective-permute-start(f32[192,128]{1,0:T(8,128)S(1)} %get-tuple-element.36), channel_id=1, source_target_pairs={{0,2},{1,3},{2,4},{3,5},{4,6},{5,7},{6,0},{7,1},{8,10},{9,11},{10,... | collective-permute-start | bytes 294920 | tf_op jit(solution)/shard_map/ppermute | solution.py:246
  31.7 4.0 %collective-permute-start.14 = (f32[192,128]{1,0:T(8,128)S(1)}, f32[192,128]{1,0:T(8,128)S(1)}, u32[]{:S(2)}, u32[]{:S(2)}) collective-permute-start(f32[192,128]{1,0:T(8,128)S(1)} %get-tuple-element.37), channel_id=1, source_target_pairs={{0,2},{1,3},{2,1},{3,0},{4,6},{5,7},{6,5},{7,4},{8,10},{9,11},{10,... | collective-permute-start | bytes 294920 | tf_op jit(solution)/shard_map/ppermute | solution.py:246
  31.7 4.0 %collective-permute-start.15 = (f32[192,128]{1,0:T(8,128)S(1)}, f32[192,128]{1,0:T(8,128)S(1)}, u32[]{:S(2)}, u32[]{:S(2)}) collective-permute-start(f32[192,128]{1,0:T(8,128)S(1)} %get-tuple-element.38), channel_id=1, source_target_pairs={{0,2},{1,3},{2,0},{3,1},{4,6},{5,7},{6,4},{7,5},{8,10},{9,11},{10,... | collective-permute-start | bytes 294920 | tf_op jit(solution)/shard_map/ppermute | solution.py:246
  35.8 9.5 %collective-permute-start.16 = (f32[768,256]{1,0:T(8,128)S(1)}, f32[768,256]{1,0:T(8,128)S(1)}, u32[]{:S(2)}, u32[]{:S(2)}) collective-permute-start(f32[768,256]{1,0:T(8,128)S(1)} %get-tuple-element.39), channel_id=1, source_target_pairs={{0,2},{1,3},{2,0},{3,1},{4,6},{5,7},{6,4},{7,5},{8,10},{9,11},{10,... | collective-permute-start | bytes 2359304 | tf_op jit(solution)/shard_map/ppermute | solution.py:246
  35.9 3.2 %collective-permute-start.20 = (f32[192,128]{1,0:T(8,128)S(1)}, f32[192,128]{1,0:T(8,128)S(1)}, u32[]{:S(2)}, u32[]{:S(2)}) collective-permute-start(f32[192,128]{1,0:T(8,128)S(1)} %add_add_fusion.1), channel_id=1, source_target_pairs={{0,2},{1,3},{2,0},{3,1},{4,6},{5,7},{6,4},{7,5},{8,10},{9,11},{10,... | collective-permute-start | bytes 294920 | tf_op jit(solution)/shard_map/ppermute | solution.py:246
  36.4 2.7 %collective-permute-start.19 = (f32[192,128]{1,0:T(8,128)S(1)}, f32[192,128]{1,0:T(8,128)S(1)}, u32[]{:S(2)}, u32[]{:S(2)}) collective-permute-start(f32[192,128]{1,0:T(8,128)S(1)} %add_add_fusion.1), channel_id=1, source_target_pairs={{0,10},{1,11},{2,0},{3,1},{4,14},{5,15},{6,4},{7,5},{8,2},{9,3},{1... | collective-permute-start | bytes 294920 | tf_op jit(solution)/shard_map/ppermute | solution.py:246
  36.6 3.6 %collective-permute-start.18 = (f32[192,128]{1,0:T(8,128)S(1)}, f32[192,128]{1,0:T(8,128)S(1)}, u32[]{:S(2)}, u32[]{:S(2)}) collective-permute-start(f32[192,128]{1,0:T(8,128)S(1)} %add_add_fusion.1), channel_id=1, source_target_pairs={{0,18},{1,19},{2,0},{3,1},{4,22},{5,23},{6,4},{7,5},{8,26},{9,27},... | collective-permute-start | bytes 294920 | tf_op jit(solution)/shard_map/ppermute | solution.py:246
  38.0 3.4 %collective-permute-start.17 = (f32[192,128]{1,0:T(8,128)S(1)}, f32[192,128]{1,0:T(8,128)S(1)}, u32[]{:S(2)}, u32[]{:S(2)}) collective-permute-start(f32[192,128]{1,0:T(8,128)S(1)} %add_add_fusion.1), channel_id=1, source_target_pairs={{0,26},{1,27},{2,0},{3,1},{4,30},{5,31},{6,4},{7,5},{8,18},{9,19},... | collective-permute-start | bytes 294920 | tf_op jit(solution)/shard_map/ppermute | solution.py:246
  41.3 6.3 %collective-permute-start.24 = (f32[192,128]{1,0:T(8,128)S(1)}, f32[192,128]{1,0:T(8,128)S(1)}, u32[]{:S(2)}, u32[]{:S(2)}) collective-permute-start(f32[192,128]{1,0:T(8,128)S(1)} %add_add_fusion), channel_id=1, source_target_pairs={{0,2},{1,3},{2,5},{3,4},{4,6},{5,7},{6,1},{7,0},{8,10},{9,11},{10,... | collective-permute-start | bytes 294920 | tf_op jit(solution)/shard_map/ppermute | solution.py:246
  44.0 4.0 %collective-permute-start.23 = (f32[192,128]{1,0:T(8,128)S(1)}, f32[192,128]{1,0:T(8,128)S(1)}, u32[]{:S(2)}, u32[]{:S(2)}) collective-permute-start(f32[192,128]{1,0:T(8,128)S(1)} %add_add_fusion), channel_id=1, source_target_pairs={{0,2},{1,3},{2,4},{3,5},{4,6},{5,7},{6,0},{7,1},{8,10},{9,11},{10,... | collective-permute-start | bytes 294920 | tf_op jit(solution)/shard_map/ppermute | solution.py:246
  44.1 4.6 %collective-permute-start.22 = (f32[192,128]{1,0:T(8,128)S(1)}, f32[192,128]{1,0:T(8,128)S(1)}, u32[]{:S(2)}, u32[]{:S(2)}) collective-permute-start(f32[192,128]{1,0:T(8,128)S(1)} %add_add_fusion), channel_id=1, source_target_pairs={{0,2},{1,3},{2,1},{3,0},{4,6},{5,7},{6,5},{7,4},{8,10},{9,11},{10,... | collective-permute-start | bytes 294920 | tf_op jit(solution)/shard_map/ppermute | solution.py:246
  45.1 3.5 %collective-permute-start.21 = (f32[192,128]{1,0:T(8,128)S(1)}, f32[192,128]{1,0:T(8,128)S(1)}, u32[]{:S(2)}, u32[]{:S(2)}) collective-permute-start(f32[192,128]{1,0:T(8,128)S(1)} %add_add_fusion), channel_id=1, source_target_pairs={{0,2},{1,3},{2,0},{3,1},{4,6},{5,7},{6,4},{7,5},{8,10},{9,11},{10,... | collective-permute-start | bytes 294920 | tf_op jit(solution)/shard_map/ppermute | solution.py:246
  54.1 1.3 %collective-permute-start.25 = (f32[128,128]{1,0:T(8,128)S(1)}, f32[128,128]{1,0:T(8,128)S(1)}, u32[]{:S(2)}, u32[]{:S(2)}) collective-permute-start(f32[128,128]{1,0:T(8,128)S(1)} %get-tuple-element.44), channel_id=1, source_target_pairs={{0,2},{2,0},{4,6},{6,4},{8,10},{10,8},{12,14},{14,12},{16,18},{18,... | collective-permute-start | bytes 196616 | tf_op jit(solution)/shard_map/ppermute | solution.py:359

commit v14 on v13

--- a/solution.py
+++ b/solution.py
@@ -11,7 +11,7 @@
 BF16 = jnp.bfloat16
 SLAB = 8
 BLOCK = 16
-KSTEP = 256
+KSTEP = 128
 VMEM = pl.BlockSpec(memory_space=pltpu.VMEM)
 SMEM = pl.BlockSpec(memory_space=pltpu.SMEM)
 BIG = pltpu.CompilerParams(vmem_limit_bytes=32 * 1024 * 1024)
@@ -214,11 +214,9 @@
         if after < rank:
             rows = line_scr[...]
             high = rows.astype(BF16).astype(F32)
-            rest = rows - high
-            mid_part = rest.astype(BF16).astype(F32)
-            low = rest - mid_part
-            first = jnp.concatenate([x[:, :rank] for x in (high, high, mid_part, high, low, mid_part)], axis=0)
-            second = jnp.concatenate([high, mid_part, high, low, high, mid_part], axis=0)
+            low = rows - high
+            first = jnp.concatenate([x[:, :rank] for x in (high, high, low)], axis=0)
+            second = jnp.concatenate([high, low, high], axis=0)
             drop = lax.dot_general(
                 first.astype(BF16),
                 second.astype(BF16),

time: 56.2 us -> 56.6 us (level)
  no operation moved by 1% of the time
where the time goes in v14:
time: 56.6 us; the launch traced here: 56.5 us
  starting transfers between devices  23.5 us (42%)
  waiting for transfers between devices  20.1 us (36%)
  Pallas kernels  11.9 us (21%)
  other arithmetic  0.68 us (1%)
    ppermute x21, starting transfers between devices, crossed(): return lax.ppermute(value, ('fib', 'pln'), pairs)  19.8 us
    ppermute x21, waiting for transfers between devices, crossed(): return lax.ppermute(value, ('fib', 'pln'), pairs)  9.85 us
    ppermute x1, waiting for transfers between devices, per_device(): back_two = lax.ppermute(swapped, 'fib', forward)  7.2 us
    pallas_call x1, Pallas kernels, per_device(): pl.pallas_call(functools.partial(factor_kernel, mid), out_shape=[jax.Shap...  5.4 us
    pallas_call x1, Pallas kernels, per_device(): pl.pallas_call(functools.partial(interp_kernel, owners), out_shape=[piece...  3.48 us
    ppermute x1, starting transfers between devices, per_device(): back_two = lax.ppermute(swapped, 'fib', forward)  1.6 us
    ppermute x1, starting transfers between devices, per_device(): order_next = lax.ppermute(slot_order[0], 'fib', core_swap)  1.37 us
    ppermute x1, waiting for transfers between devices, per_device(): core_values = first + lax.ppermute(second, 'fib', core_swap)  1.24 us
  transfers between devices with their start and end apart: 26, of which 13 were waited for; matrix products, arithmetic and copies ran while one was open for 0% of the time, Pallas kernels for 2%

profile of v14, /device:TPU:0, one launch (start us, length us, event | category | flops | bytes accessed | tf_op | source)
XLA Modules:
  0.0 56.5 jit_solution(16715479896260293943)
XLA Ops:
  0.0 0.0 copy-start.1
  0.0 3.5 %interp.1 = (f32[96,512]{1,0:T(8,128)S(1)}, f32[96,512]{1,0:T(8,128)S(1)}, f32[192,512]{1,0:T(8,128)S(1)}, f32[96,512]{1,0:T(8,128)S(1)}) custom-call(s32[3,1,16]{2,1,0:T(1,128)} %bitcast.21, f32[288,1000]{1,0:T(8,128)} %bitcast.25, f32[1000,512]{1,0:T(8,128)} %interp_hbm.1), custom_call_target="tpu_custom_call" | custom-call | tf_op jit(solution)/shard_map/interp/pallas_call | solution.py:272
  3.5 0.5 collective-permute-start.1
  4.0 0.1 collective-permute-start.2
  4.1 1.0 %collective-permute-done.1.next_zero_ref = f32[96,512]{1,0:T(8,128)S(1)} collective-permute-done((f32[96,512]{1,0:T(8,128)S(1)}, f32[96,512]{1,0:T(8,128)S(1)}, u32[]{:S(2)}, u32[]{:S(2)}) %collective-permute-start.1) | collective-permute-done | bytes 196640 | tf_op jit(solution)/shard_map/ppermute | solution.py:287
  5.1 1.6 %collective-permute-start.3 = (f32[96,512]{1,0:T(8,128)S(1)}, f32[96,512]{1,0:T(8,128)S(1)}, u32[]{:S(2)}, u32[]{:S(2)}) collective-permute-start(f32[96,512]{1,0:T(8,128)S(1)} %collective-permute-done.1.next_zero_ref), channel_id=1, source_target_pairs={{0,2},{2,4},{4,6},{6,8},{8,10},{10,12},{12,14},{14,16},{16,18},{18... | collective-permute-start | bytes 589832 | tf_op jit(solution)/shard_map/ppermute | solution.py:289
  6.7 0.0 copy-done.2
  6.7 1.4 %collective-permute-start = (s32[1,192]{1,0:T(1,128)S(1)}, s32[1,192]{1,0:T(1,128)S(1)}, u32[]{:S(2)}, u32[]{:S(2)}) collective-permute-start(s32[1,192]{1,0:T(1,128)S(1)} %bitcast.23), channel_id=1, source_target_pairs={{0,2},{2,0},{4,6},{6,4},{8,10},{10,8},{12,14},{14,12},{16,18},{18,... | collective-permute-start | bytes 2312 | tf_op jit(solution)/shard_map/ppermute | solution.py:269
  8.1 0.8 %collective-permute-done.order_next_ref = s32[1,192]{1,0:T(1,128)S(1)} collective-permute-done((s32[1,192]{1,0:T(1,128)S(1)}, s32[1,192]{1,0:T(1,128)S(1)}, u32[]{:S(2)}, u32[]{:S(2)}) %collective-permute-start) | collective-permute-done | bytes 800 | tf_op jit(solution)/shard_map/ppermute | solution.py:269
  8.9 0.0 copy-done.1
  8.9 0.0 copy-done
  8.9 1.1 %pick.1 = (bf16[384,288]{1,0:T(8,128)(2,1)S(1)}, bf16[128,768]{1,0:T(8,128)(2,1)S(1)}, bf16[128,768]{1,0:T(8,128)(2,1)S(1)}) custom-call(s32[3,1,16]{2,1,0:T(1,128)S(1)} %bitcast.22, s32[1,192]{1,0:T(1,128)S(1)} %bitcast.24, s32[1,192]{1,0:T(1,128)S(1)} %collective-permute-done.order_next_ref, f32[768,128]{1,0:T(8,128)S(1)} %copy-done), custom_call_target="tpu_custom_call" | custom-call | tf_op jit(solution)/shard_map/pick/pallas_call | solution.py:291
  10.0 7.2 %collective-permute-done.3.back_two_ref = f32[96,512]{1,0:T(8,128)S(1)} collective-permute-done((f32[96,512]{1,0:T(8,128)S(1)}, f32[96,512]{1,0:T(8,128)S(1)}, u32[]{:S(2)}, u32[]{:S(2)}) %collective-permute-start.3) | collective-permute-done | bytes 196640 | tf_op jit(solution)/shard_map/ppermute | solution.py:289
  17.2 0.0 collective-permute-done.2.back_ref
  17.2 0.6 %order.1 = (f32[192,512]{1,0:T(8,128)S(1)}, f32[192,512]{1,0:T(8,128)S(1)}) custom-call(bf16[384,288]{1,0:T(8,128)(2,1)S(1)} %get-tuple-element.25.pick_ref, f32[96,512]{1,0:T(8,128)S(1)} %get-tuple-element.26.zero_ref, f32[96,512]{1,0:T(8,128)S(1)} %get-tuple-element.27.one_ref, f32[96,512]{1,0:T(8,128)S(1)} %collective-permute-done.1.next_zero_ref, ...), custom_call_target="tpu_custom_call" | custom-call | tf_op jit(solution)/shard_map/order/pallas_call | solution.py:299
  18.0 0.1 slice_bitcast_fusion
  18.0 0.1 collective-permute-start.11
  18.1 1.8 %collective-permute-start.10 = (f32[192,128]{1,0:T(8,128)S(1)}, f32[192,128]{1,0:T(8,128)S(1)}, u32[]{:S(2)}, u32[]{:S(2)}) collective-permute-start(f32[192,128]{1,0:T(8,128)S(1)} %get-tuple-element.46), channel_id=1, source_target_pairs={{0,26},{1,27},{2,0},{3,1},{4,30},{5,31},{6,4},{7,5},{8,18},{9,19},... | collective-permute-start | bytes 294920 | tf_op jit(solution)/shard_map/ppermute | solution.py:244
  19.9 0.0 collective-permute-start.9
  19.9 0.0 collective-permute-start.8
  19.9 1.6 %collective-permute-start.7 = (f32[192,128]{1,0:T(8,128)S(1)}, f32[192,128]{1,0:T(8,128)S(1)}, u32[]{:S(2)}, u32[]{:S(2)}) collective-permute-start(f32[192,128]{1,0:T(8,128)S(1)} %get-tuple-element.49), channel_id=1, source_target_pairs={{0,14},{1,15},{2,0},{3,1},{4,10},{5,11},{6,4},{7,5},{8,6},{9,7},{1... | collective-permute-start | bytes 294920 | tf_op jit(solution)/shard_map/ppermute | solution.py:244
  21.5 0.0 collective-permute-done.11.refs_7_
  21.5 1.3 %collective-permute-start.6 = (f32[192,128]{1,0:T(8,128)S(1)}, f32[192,128]{1,0:T(8,128)S(1)}, u32[]{:S(2)}, u32[]{:S(2)}) collective-permute-start(f32[192,128]{1,0:T(8,128)S(1)} %get-tuple-element.50), channel_id=1, source_target_pairs={{0,10},{1,11},{2,0},{3,1},{4,14},{5,15},{6,4},{7,5},{8,2},{9,3},{1... | collective-permute-start | bytes 294920 | tf_op jit(solution)/shard_map/ppermute | solution.py:244
  22.8 0.0 collective-permute-done.10.refs_6_
  22.8 0.7 %collective-permute-start.5 = (f32[192,128]{1,0:T(8,128)S(1)}, f32[192,128]{1,0:T(8,128)S(1)}, u32[]{:S(2)}, u32[]{:S(2)}) collective-permute-start(f32[192,128]{1,0:T(8,128)S(1)} %get-tuple-element.51), channel_id=1, source_target_pairs={{0,6},{1,7},{2,0},{3,1},{4,2},{5,3},{6,4},{7,5},{8,14},{9,15},{10,... | collective-permute-start | bytes 294920 | tf_op jit(solution)/shard_map/ppermute | solution.py:244
  23.5 0.0 collective-permute-done.9.refs_5_
  23.5 4.1 %collective-permute-start.4 = (f32[192,128]{1,0:T(8,128)S(1)}, f32[192,128]{1,0:T(8,128)S(1)}, u32[]{:S(2)}, u32[]{:S(2)}) collective-permute-start(f32[192,128]{1,0:T(8,128)S(1)} %get-tuple-element.52), channel_id=1, source_target_pairs={{0,2},{1,3},{2,0},{3,1},{4,6},{5,7},{6,4},{7,5},{8,10},{9,11},{10,... | collective-permute-start | bytes 294920 | tf_op jit(solution)/shard_map/ppermute | solution.py:244
  27.6 0.0 collective-permute-done.8.refs_4_
  27.6 0.0 collective-permute-done.7.refs_3_
  27.6 0.0 collective-permute-done.6.refs_2_
  27.6 0.0 collective-permute-done.5.refs_1_
  27.6 0.9 %collective-permute-done.4.refs_0_ = f32[192,128]{1,0:T(8,128)S(1)} collective-permute-done((f32[192,128]{1,0:T(8,128)S(1)}, f32[192,128]{1,0:T(8,128)S(1)}, u32[]{:S(2)}, u32[]{:S(2)}) %collective-permute-start.4) | collective-permute-done | bytes 98336 | tf_op jit(solution)/shard_map/ppermute | solution.py:244
  28.5 1.1 %image.1 = (f32[192,128]{1,0:T(8,128)S(1)}, f32[192,128]{1,0:T(8,128)S(1)}, f32[192,128]{1,0:T(8,128)S(1)}, f32[192,128]{1,0:T(8,128)S(1)}, f32[768,256]{1,0:T(8,128)S(1)}) custom-call(f32[192,128]{1,0:T(8,128)S(1)} %collective-permute-done.4.refs_0_, f32[192,128]{1,0:T(8,128)S(1)} %collective-permute-done.5.refs_1_, ...), custom_call_target="tpu_custom_call" | custom-call | tf_op jit(solution)/shard_map/image/pallas_call | solution.py:322
  29.7 0.4 collective-permute-start.12
  30.1 2.1 %collective-permute-start.13 = (f32[192,128]{1,0:T(8,128)S(1)}, f32[192,128]{1,0:T(8,128)S(1)}, u32[]{:S(2)}, u32[]{:S(2)}) collective-permute-start(f32[192,128]{1,0:T(8,128)S(1)} %get-tuple-element.36), channel_id=1, source_target_pairs={{0,2},{1,3},{2,4},{3,5},{4,6},{5,7},{6,0},{7,1},{8,10},{9,11},{10,... | collective-permute-start | bytes 294920 | tf_op jit(solution)/shard_map/ppermute | solution.py:244
  32.2 0.0 collective-permute-start.14
  32.2 0.6 %collective-permute-start.15 = (f32[192,128]{1,0:T(8,128)S(1)}, f32[192,128]{1,0:T(8,128)S(1)}, u32[]{:S(2)}, u32[]{:S(2)}) collective-permute-start(f32[192,128]{1,0:T(8,128)S(1)} %get-tuple-element.38), channel_id=1, source_target_pairs={{0,2},{1,3},{2,0},{3,1},{4,6},{5,7},{6,4},{7,5},{8,10},{9,11},{10,... | collective-permute-start | bytes 294920 | tf_op jit(solution)/shard_map/ppermute | solution.py:244
  32.8 1.9 %collective-permute-done.12 = f32[192,128]{1,0:T(8,128)S(1)} collective-permute-done((f32[192,128]{1,0:T(8,128)S(1)}, f32[192,128]{1,0:T(8,128)S(1)}, u32[]{:S(2)}, u32[]{:S(2)}) %collective-permute-start.12) | collective-permute-done | bytes 98336 | tf_op jit(solution)/shard_map/ppermute | solution.py:244
  34.7 1.1 %collective-permute-done.13 = f32[192,128]{1,0:T(8,128)S(1)} collective-permute-done((f32[192,128]{1,0:T(8,128)S(1)}, f32[192,128]{1,0:T(8,128)S(1)}, u32[]{:S(2)}, u32[]{:S(2)}) %collective-permute-start.13) | collective-permute-done | bytes 98336 | tf_op jit(solution)/shard_map/ppermute | solution.py:244
  35.8 0.4 collective-permute-done.14
  36.2 0.0 collective-permute-done.15
  36.2 0.1 collective-permute-start.16
  36.3 0.5 collective-permute-start.20
  36.8 0.2 collective-permute-start.19
  37.1 1.4 %collective-permute-start.18 = (f32[192,128]{1,0:T(8,128)S(1)}, f32[192,128]{1,0:T(8,128)S(1)}, u32[]{:S(2)}, u32[]{:S(2)}) collective-permute-start(f32[192,128]{1,0:T(8,128)S(1)} %add_add_fusion.1), channel_id=1, source_target_pairs={{0,18},{1,19},{2,0},{3,1},{4,22},{5,23},{6,4},{7,5},{8,26},{9,27},... | collective-permute-start | bytes 294920 | tf_op jit(solution)/shard_map/ppermute | solution.py:244
  38.4 1.1 %collective-permute-start.17 = (f32[192,128]{1,0:T(8,128)S(1)}, f32[192,128]{1,0:T(8,128)S(1)}, u32[]{:S(2)}, u32[]{:S(2)}) collective-permute-start(f32[192,128]{1,0:T(8,128)S(1)} %add_add_fusion.1), channel_id=1, source_target_pairs={{0,26},{1,27},{2,0},{3,1},{4,30},{5,31},{6,4},{7,5},{8,18},{9,19},... | collective-permute-start | bytes 294920 | tf_op jit(solution)/shard_map/ppermute | solution.py:244
  39.6 0.0 collective-permute-done.20
  39.6 0.0 collective-permute-done.19
  39.6 1.1 %collective-permute-done.18 = f32[192,128]{1,0:T(8,128)S(1)} collective-permute-done((f32[192,128]{1,0:T(8,128)S(1)}, f32[192,128]{1,0:T(8,128)S(1)}, u32[]{:S(2)}, u32[]{:S(2)}) %collective-permute-start.18) | collective-permute-done | bytes 98336 | tf_op jit(solution)/shard_map/ppermute | solution.py:244
  40.6 1.1 %collective-permute-done.17 = f32[192,128]{1,0:T(8,128)S(1)} collective-permute-done((f32[192,128]{1,0:T(8,128)S(1)}, f32[192,128]{1,0:T(8,128)S(1)}, u32[]{:S(2)}, u32[]{:S(2)}) %collective-permute-start.17) | collective-permute-done | bytes 98336 | tf_op jit(solution)/shard_map/ppermute | solution.py:244
  41.8 2.7 %collective-permute-start.24 = (f32[192,128]{1,0:T(8,128)S(1)}, f32[192,128]{1,0:T(8,128)S(1)}, u32[]{:S(2)}, u32[]{:S(2)}) collective-permute-start(f32[192,128]{1,0:T(8,128)S(1)} %add_add_fusion), channel_id=1, source_target_pairs={{0,2},{1,3},{2,5},{3,4},{4,6},{5,7},{6,1},{7,0},{8,10},{9,11},{10,... | collective-permute-start | bytes 294920 | tf_op jit(solution)/shard_map/ppermute | solution.py:244
  44.5 0.1 collective-permute-start.23
  44.5 1.0 %collective-permute-start.22 = (f32[192,128]{1,0:T(8,128)S(1)}, f32[192,128]{1,0:T(8,128)S(1)}, u32[]{:S(2)}, u32[]{:S(2)}) collective-permute-start(f32[192,128]{1,0:T(8,128)S(1)} %add_add_fusion), channel_id=1, source_target_pairs={{0,2},{1,3},{2,1},{3,0},{4,6},{5,7},{6,5},{7,4},{8,10},{9,11},{10,... | collective-permute-start | bytes 294920 | tf_op jit(solution)/shard_map/ppermute | solution.py:244
  45.6 0.1 collective-permute-start.21
  45.7 0.0 collective-permute-done.16.value_ref
  45.7 0.1 split.1
  45.8 2.2 %collective-permute-done.24.refs_3_ = f32[192,128]{1,0:T(8,128)S(1)} collective-permute-done((f32[192,128]{1,0:T(8,128)S(1)}, f32[192,128]{1,0:T(8,128)S(1)}, u32[]{:S(2)}, u32[]{:S(2)}) %collective-permute-start.24) | collective-permute-done | bytes 98336 | tf_op jit(solution)/shard_map/ppermute | solution.py:244
  48.1 0.4 collective-permute-done.23.refs_2_
  48.5 0.6 %collective-permute-done.22.refs_1_ = f32[192,128]{1,0:T(8,128)S(1)} collective-permute-done((f32[192,128]{1,0:T(8,128)S(1)}, f32[192,128]{1,0:T(8,128)S(1)}, u32[]{:S(2)}, u32[]{:S(2)}) %collective-permute-start.22) | collective-permute-done | bytes 98336 | tf_op jit(solution)/shard_map/ppermute | solution.py:244
  49.1 0.0 collective-permute-done.21.refs_0_
  49.1 5.4 %factor.1 = (f32[128,128]{1,0:T(8,128)S(1)}, f32[128,128]{1,0:T(8,128)S(1)}) custom-call(bf16[768,256]{1,0:T(8,128)(2,1)S(1)} %get-tuple-element.40.high_ref, bf16[768,256]{1,0:T(8,128)(2,1)S(1)} %get-tuple-element.41.low_ref, f32[192,128]{1,0:T(8,128)S(1)} %collective-permute-done.21.refs_0_, f32[192,128]{1,0:T(8,128)S(1)} %collective-permute-done.22.refs_1_, ...), custom_call_target="tpu_custom_call" | custom-call | tf_op jit(solution)/shard_map/factor/pallas_call | solution.py:344
  54.5 0.1 collective-permute-start.25
  54.6 1.2 %collective-permute-done.25 = f32[128,128]{1,0:T(8,128)S(1)} collective-permute-done((f32[128,128]{1,0:T(8,128)S(1)}, f32[128,128]{1,0:T(8,128)S(1)}, u32[]{:S(2)}, u32[]{:S(2)}) %collective-permute-start.25) | collective-permute-done | bytes 65568 | tf_op jit(solution)/shard_map/ppermute | solution.py:357
  55.8 0.6 %add_bitcast_fusion = f32[1,1,128,128]{3,2,1,0:T(8,128)} fusion(f32[128,128]{1,0:T(8,128)S(1)} %get-tuple-element.43, f32[128,128]{1,0:T(8,128)S(1)} %collective-permute-done.25), kind=kLoop, calls=%fused_computation.10 | loop fusion | flops 16384 | bytes 196608 | tf_op jit(solution)/shard_map/broadcast_in_dim | solution.py:358
  (8 shorter events, 0.2 us)
Async XLA Ops:
  0.0 8.9 %copy-start.1 = (s32[1,16,3]{1,0,2:T(1,128)S(1)}, s32[1,16,3]{1,0,2:T(1,128)}, u32[]{:S(2)}) copy-start(s32[1,16,3]{1,0,2:T(1,128)} %param.7) | copy-start | bytes 580
  0.0 6.7 %copy-start.2 = (s32[1,1,192]{2,1,0:T(1,128)S(1)}, s32[1,1,192]{2,1,0:T(1,128)}, u32[]{:S(2)}) copy-start(s32[1,1,192]{2,1,0:T(1,128)} %param.8) | copy-start | bytes 2308
  0.0 8.9 %copy-start = (f32[768,128]{1,0:T(8,128)S(1)}, f32[768,128]{1,0:T(8,128)}, u32[]{:S(2)}) copy-start(f32[768,128]{1,0:T(8,128)} %start_ref.1) | copy-start | bytes 1179652
  3.5 1.6 %collective-permute-start.1 = (f32[96,512]{1,0:T(8,128)S(1)}, f32[96,512]{1,0:T(8,128)S(1)}, u32[]{:S(2)}, u32[]{:S(2)}) collective-permute-start(f32[96,512]{1,0:T(8,128)S(1)} %get-tuple-element.28), channel_id=1, source_target_pairs={{0,2},{2,0},{4,6},{6,4},{8,10},{10,8},{12,14},{14,12},{16,18},{18,... | collective-permute-start | bytes 589832 | tf_op jit(solution)/shard_map/ppermute | solution.py:287
  4.0 13.2 %collective-permute-start.2 = (f32[192,512]{1,0:T(8,128)S(1)}, f32[192,512]{1,0:T(8,128)S(1)}, u32[]{:S(2)}, u32[]{:S(2)}) collective-permute-start(f32[192,512]{1,0:T(8,128)S(1)} %get-tuple-element.29), channel_id=1, source_target_pairs={{0,2},{2,4},{4,6},{6,8},{8,10},{10,12},{12,14},{14,16},{16,18},{18... | collective-permute-start | bytes 1179656 | tf_op jit(solution)/shard_map/ppermute | solution.py:288
  5.1 12.1 %collective-permute-start.3 = (f32[96,512]{1,0:T(8,128)S(1)}, f32[96,512]{1,0:T(8,128)S(1)}, u32[]{:S(2)}, u32[]{:S(2)}) collective-permute-start(f32[96,512]{1,0:T(8,128)S(1)} %collective-permute-done.1.next_zero_ref), channel_id=1, source_target_pairs={{0,2},{2,4},{4,6},{6,8},{8,10},{10,12},{12,14},{14,16},{16,18},{18... | collective-permute-start | bytes 589832 | tf_op jit(solution)/shard_map/ppermute | solution.py:289
  6.7 2.2 %collective-permute-start = (s32[1,192]{1,0:T(1,128)S(1)}, s32[1,192]{1,0:T(1,128)S(1)}, u32[]{:S(2)}, u32[]{:S(2)}) collective-permute-start(s32[1,192]{1,0:T(1,128)S(1)} %bitcast.23), channel_id=1, source_target_pairs={{0,2},{2,0},{4,6},{6,4},{8,10},{10,8},{12,14},{14,12},{16,18},{18,... | collective-permute-start | bytes 2312 | tf_op jit(solution)/shard_map/ppermute | solution.py:269
  18.0 3.5 %collective-permute-start.11 = (f32[192,128]{1,0:T(8,128)S(1)}, f32[192,128]{1,0:T(8,128)S(1)}, u32[]{:S(2)}, u32[]{:S(2)}) collective-permute-start(f32[192,128]{1,0:T(8,128)S(1)} %get-tuple-element.45), channel_id=1, source_target_pairs={{0,30},{1,31},{2,0},{3,1},{4,26},{5,27},{6,4},{7,5},{8,22},{9,23},... | collective-permute-start | bytes 294920 | tf_op jit(solution)/shard_map/ppermute | solution.py:244
  18.1 4.7 %collective-permute-start.10 = (f32[192,128]{1,0:T(8,128)S(1)}, f32[192,128]{1,0:T(8,128)S(1)}, u32[]{:S(2)}, u32[]{:S(2)}) collective-permute-start(f32[192,128]{1,0:T(8,128)S(1)} %get-tuple-element.46), channel_id=1, source_target_pairs={{0,26},{1,27},{2,0},{3,1},{4,30},{5,31},{6,4},{7,5},{8,18},{9,19},... | collective-permute-start | bytes 294920 | tf_op jit(solution)/shard_map/ppermute | solution.py:244
  19.9 3.7 %collective-permute-start.9 = (f32[192,128]{1,0:T(8,128)S(1)}, f32[192,128]{1,0:T(8,128)S(1)}, u32[]{:S(2)}, u32[]{:S(2)}) collective-permute-start(f32[192,128]{1,0:T(8,128)S(1)} %get-tuple-element.47), channel_id=1, source_target_pairs={{0,22},{1,23},{2,0},{3,1},{4,18},{5,19},{6,4},{7,5},{8,30},{9,31},... | collective-permute-start | bytes 294920 | tf_op jit(solution)/shard_map/ppermute | solution.py:244
  19.9 7.7 %collective-permute-start.8 = (f32[192,128]{1,0:T(8,128)S(1)}, f32[192,128]{1,0:T(8,128)S(1)}, u32[]{:S(2)}, u32[]{:S(2)}) collective-permute-start(f32[192,128]{1,0:T(8,128)S(1)} %get-tuple-element.48), channel_id=1, source_target_pairs={{0,18},{1,19},{2,0},{3,1},{4,22},{5,23},{6,4},{7,5},{8,26},{9,27},... | collective-permute-start | bytes 294920 | tf_op jit(solution)/shard_map/ppermute | solution.py:244
  19.9 7.7 %collective-permute-start.7 = (f32[192,128]{1,0:T(8,128)S(1)}, f32[192,128]{1,0:T(8,128)S(1)}, u32[]{:S(2)}, u32[]{:S(2)}) collective-permute-start(f32[192,128]{1,0:T(8,128)S(1)} %get-tuple-element.49), channel_id=1, source_target_pairs={{0,14},{1,15},{2,0},{3,1},{4,10},{5,11},{6,4},{7,5},{8,6},{9,7},{1... | collective-permute-start | bytes 294920 | tf_op jit(solution)/shard_map/ppermute | solution.py:244
  21.5 6.1 %collective-permute-start.6 = (f32[192,128]{1,0:T(8,128)S(1)}, f32[192,128]{1,0:T(8,128)S(1)}, u32[]{:S(2)}, u32[]{:S(2)}) collective-permute-start(f32[192,128]{1,0:T(8,128)S(1)} %get-tuple-element.50), channel_id=1, source_target_pairs={{0,10},{1,11},{2,0},{3,1},{4,14},{5,15},{6,4},{7,5},{8,2},{9,3},{1... | collective-permute-start | bytes 294920 | tf_op jit(solution)/shard_map/ppermute | solution.py:244
  22.8 4.8 %collective-permute-start.5 = (f32[192,128]{1,0:T(8,128)S(1)}, f32[192,128]{1,0:T(8,128)S(1)}, u32[]{:S(2)}, u32[]{:S(2)}) collective-permute-start(f32[192,128]{1,0:T(8,128)S(1)} %get-tuple-element.51), channel_id=1, source_target_pairs={{0,6},{1,7},{2,0},{3,1},{4,2},{5,3},{6,4},{7,5},{8,14},{9,15},{10,... | collective-permute-start | bytes 294920 | tf_op jit(solution)/shard_map/ppermute | solution.py:244
  23.5 5.0 %collective-permute-start.4 = (f32[192,128]{1,0:T(8,128)S(1)}, f32[192,128]{1,0:T(8,128)S(1)}, u32[]{:S(2)}, u32[]{:S(2)}) collective-permute-start(f32[192,128]{1,0:T(8,128)S(1)} %get-tuple-element.52), channel_id=1, source_target_pairs={{0,2},{1,3},{2,0},{3,1},{4,6},{5,7},{6,4},{7,5},{8,10},{9,11},{10,... | collective-permute-start | bytes 294920 | tf_op jit(solution)/shard_map/ppermute | solution.py:244
  29.7 5.0 %collective-permute-start.12 = (f32[192,128]{1,0:T(8,128)S(1)}, f32[192,128]{1,0:T(8,128)S(1)}, u32[]{:S(2)}, u32[]{:S(2)}) collective-permute-start(f32[192,128]{1,0:T(8,128)S(1)} %get-tuple-element.35), channel_id=1, source_target_pairs={{0,2},{1,3},{2,5},{3,4},{4,6},{5,7},{6,1},{7,0},{8,10},{9,11},{10,... | collective-permute-start | bytes 294920 | tf_op jit(solution)/shard_map/ppermute | solution.py:244
  30.1 5.7 %collective-permute-start.13 = (f32[192,128]{1,0:T(8,128)S(1)}, f32[192,128]{1,0:T(8,128)S(1)}, u32[]{:S(2)}, u32[]{:S(2)}) collective-permute-start(f32[192,128]{1,0:T(8,128)S(1)} %get-tuple-element.36), channel_id=1, source_target_pairs={{0,2},{1,3},{2,4},{3,5},{4,6},{5,7},{6,0},{7,1},{8,10},{9,11},{10,... | collective-permute-start | bytes 294920 | tf_op jit(solution)/shard_map/ppermute | solution.py:244
  32.2 4.0 %collective-permute-start.14 = (f32[192,128]{1,0:T(8,128)S(1)}, f32[192,128]{1,0:T(8,128)S(1)}, u32[]{:S(2)}, u32[]{:S(2)}) collective-permute-start(f32[192,128]{1,0:T(8,128)S(1)} %get-tuple-element.37), channel_id=1, source_target_pairs={{0,2},{1,3},{2,1},{3,0},{4,6},{5,7},{6,5},{7,4},{8,10},{9,11},{10,... | collective-permute-start | bytes 294920 | tf_op jit(solution)/shard_map/ppermute | solution.py:244
  32.2 4.0 %collective-permute-start.15 = (f32[192,128]{1,0:T(8,128)S(1)}, f32[192,128]{1,0:T(8,128)S(1)}, u32[]{:S(2)}, u32[]{:S(2)}) collective-permute-start(f32[192,128]{1,0:T(8,128)S(1)} %get-tuple-element.38), channel_id=1, source_target_pairs={{0,2},{1,3},{2,0},{3,1},{4,6},{5,7},{6,4},{7,5},{8,10},{9,11},{10,... | collective-permute-start | bytes 294920 | tf_op jit(solution)/shard_map/ppermute | solution.py:244
  36.2 9.4 %collective-permute-start.16 = (f32[768,256]{1,0:T(8,128)S(1)}, f32[768,256]{1,0:T(8,128)S(1)}, u32[]{:S(2)}, u32[]{:S(2)}) collective-permute-start(f32[768,256]{1,0:T(8,128)S(1)} %get-tuple-element.39), channel_id=1, source_target_pairs={{0,2},{1,3},{2,0},{3,1},{4,6},{5,7},{6,4},{7,5},{8,10},{9,11},{10,... | collective-permute-start | bytes 2359304 | tf_op jit(solution)/shard_map/ppermute | solution.py:244
  36.3 3.2 %collective-permute-start.20 = (f32[192,128]{1,0:T(8,128)S(1)}, f32[192,128]{1,0:T(8,128)S(1)}, u32[]{:S(2)}, u32[]{:S(2)}) collective-permute-start(f32[192,128]{1,0:T(8,128)S(1)} %add_add_fusion.1), channel_id=1, source_target_pairs={{0,2},{1,3},{2,0},{3,1},{4,6},{5,7},{6,4},{7,5},{8,10},{9,11},{10,... | collective-permute-start | bytes 294920 | tf_op jit(solution)/shard_map/ppermute | solution.py:244
  36.8 2.7 %collective-permute-start.19 = (f32[192,128]{1,0:T(8,128)S(1)}, f32[192,128]{1,0:T(8,128)S(1)}, u32[]{:S(2)}, u32[]{:S(2)}) collective-permute-start(f32[192,128]{1,0:T(8,128)S(1)} %add_add_fusion.1), channel_id=1, source_target_pairs={{0,10},{1,11},{2,0},{3,1},{4,14},{5,15},{6,4},{7,5},{8,2},{9,3},{1... | collective-permute-start | bytes 294920 | tf_op jit(solution)/shard_map/ppermute | solution.py:244
  37.1 3.6 %collective-permute-start.18 = (f32[192,128]{1,0:T(8,128)S(1)}, f32[192,128]{1,0:T(8,128)S(1)}, u32[]{:S(2)}, u32[]{:S(2)}) collective-permute-start(f32[192,128]{1,0:T(8,128)S(1)} %add_add_fusion.1), channel_id=1, source_target_pairs={{0,18},{1,19},{2,0},{3,1},{4,22},{5,23},{6,4},{7,5},{8,26},{9,27},... | collective-permute-start | bytes 294920 | tf_op jit(solution)/shard_map/ppermute | solution.py:244
  38.4 3.4 %collective-permute-start.17 = (f32[192,128]{1,0:T(8,128)S(1)}, f32[192,128]{1,0:T(8,128)S(1)}, u32[]{:S(2)}, u32[]{:S(2)}) collective-permute-start(f32[192,128]{1,0:T(8,128)S(1)} %add_add_fusion.1), channel_id=1, source_target_pairs={{0,26},{1,27},{2,0},{3,1},{4,30},{5,31},{6,4},{7,5},{8,18},{9,19},... | collective-permute-start | bytes 294920 | tf_op jit(solution)/shard_map/ppermute | solution.py:244
  41.8 6.3 %collective-permute-start.24 = (f32[192,128]{1,0:T(8,128)S(1)}, f32[192,128]{1,0:T(8,128)S(1)}, u32[]{:S(2)}, u32[]{:S(2)}) collective-permute-start(f32[192,128]{1,0:T(8,128)S(1)} %add_add_fusion), channel_id=1, source_target_pairs={{0,2},{1,3},{2,5},{3,4},{4,6},{5,7},{6,1},{7,0},{8,10},{9,11},{10,... | collective-permute-start | bytes 294920 | tf_op jit(solution)/shard_map/ppermute | solution.py:244
  44.5 4.0 %collective-permute-start.23 = (f32[192,128]{1,0:T(8,128)S(1)}, f32[192,128]{1,0:T(8,128)S(1)}, u32[]{:S(2)}, u32[]{:S(2)}) collective-permute-start(f32[192,128]{1,0:T(8,128)S(1)} %add_add_fusion), channel_id=1, source_target_pairs={{0,2},{1,3},{2,4},{3,5},{4,6},{5,7},{6,0},{7,1},{8,10},{9,11},{10,... | collective-permute-start | bytes 294920 | tf_op jit(solution)/shard_map/ppermute | solution.py:244
  44.5 4.6 %collective-permute-start.22 = (f32[192,128]{1,0:T(8,128)S(1)}, f32[192,128]{1,0:T(8,128)S(1)}, u32[]{:S(2)}, u32[]{:S(2)}) collective-permute-start(f32[192,128]{1,0:T(8,128)S(1)} %add_add_fusion), channel_id=1, source_target_pairs={{0,2},{1,3},{2,1},{3,0},{4,6},{5,7},{6,5},{7,4},{8,10},{9,11},{10,... | collective-permute-start | bytes 294920 | tf_op jit(solution)/shard_map/ppermute | solution.py:244
  45.6 3.5 %collective-permute-start.21 = (f32[192,128]{1,0:T(8,128)S(1)}, f32[192,128]{1,0:T(8,128)S(1)}, u32[]{:S(2)}, u32[]{:S(2)}) collective-permute-start(f32[192,128]{1,0:T(8,128)S(1)} %add_add_fusion), channel_id=1, source_target_pairs={{0,2},{1,3},{2,0},{3,1},{4,6},{5,7},{6,4},{7,5},{8,10},{9,11},{10,... | collective-permute-start | bytes 294920 | tf_op jit(solution)/shard_map/ppermute | solution.py:244
  54.5 1.3 %collective-permute-start.25 = (f32[128,128]{1,0:T(8,128)S(1)}, f32[128,128]{1,0:T(8,128)S(1)}, u32[]{:S(2)}, u32[]{:S(2)}) collective-permute-start(f32[128,128]{1,0:T(8,128)S(1)} %get-tuple-element.44), channel_id=1, source_target_pairs={{0,2},{2,0},{4,6},{6,4},{8,10},{10,8},{12,14},{14,12},{16,18},{18,... | collective-permute-start | bytes 196616 | tf_op jit(solution)/shard_map/ppermute | solution.py:357
